TPU v7x, 32 devices: a whole 2x2x4 slice. The times are simulated.
32 devices in a mesh: dp: 4 (over x, core), space: 8 (over z, y).
Axes of the slice: x: 2, y: 2, z: 4, core: 2. Of those that a mesh axis runs over, the one named last changes fastest.
Arguments:
- volume: bfloat16 [4, 64, 32, 2048], P('dp', 'space'), may hold values from -6 to 6
- weight_first: bfloat16 [1728, 128], P('dp'), may hold values from -0.15625 to 0.15625
- weight_second: bfloat16 [3456, 256], P('dp'), may hold values from -0.109375 to 0.109375
- cotangent: bfloat16 [4, 16, 8, 2048], P('dp', 'space'), may hold values from -6 to 6
Outputs:
- activations: bfloat16 [4, 16, 8, 2048], P('dp', 'space')
- input_gradient: bfloat16 [4, 64, 32, 2048], P('dp', 'space')
- first_gradient: float32 [1728, 128], P('dp')
- second_gradient: float32 [3456, 256], P('dp')
All inputs are finite; a program needn't handle non-finite values.
Results may differ from a plain program's by a relative error of at most 0.012.
Values may be sent and summed in bfloat16 or wider, within the bound.
No kernel may reach another device: no remote copies, remote signals or barrier semaphores. Data moves between devices by JAX's collectives and lax.ppermute only.
A program may use at most 64 MiB of HBM per device.

v0:
```python
import functools

import jax
import jax.numpy as jnp
from jax import lax
from jax.experimental import pallas as pl
from jax.experimental.pallas import tpu as pltpu
from jax.sharding import PartitionSpec as P

LEAK_SLOPE = 0.2
F32 = jnp.float32
BF16 = jnp.bfloat16
VMEM_LIMIT = 48 * 1024 * 1024


def activate(values):
    small = jnp.exp(-jnp.abs(values))
    return LEAK_SLOPE * values + (1.0 - LEAK_SLOPE) * (
        jnp.maximum(values, 0.0) + jnp.log(1.0 + small)
    )


def activate_slope(values):
    small = jnp.exp(-jnp.abs(values))
    inverse = 1.0 / (1.0 + small)
    return LEAK_SLOPE + (1.0 - LEAK_SLOPE) * jnp.where(
        values >= 0.0, inverse, small * inverse
    )


def block_row(rows, width):
    return lax.broadcasted_iota(jnp.int32, (rows, width), 0) % 8


def from_before(block):
    moved = pltpu.roll(block, 1, 0)
    return jnp.where(block_row(*block.shape) == 0, 0.0, moved)


def from_after(block):
    moved = pltpu.roll(block, block.shape[0] - 1, 0)
    return jnp.where(block_row(*block.shape) == 7, 0.0, moved)


def call(kernel, out_shape, scratch, *operands, smem=(), flops=0, aliases=None):
    nbytes = sum(a.size * a.dtype.itemsize for a in (*operands, *jax.tree.leaves(out_shape)))
    specs = [pl.BlockSpec(memory_space=pltpu.SMEM)] * len(smem)
    specs += [pl.BlockSpec(memory_space=pltpu.VMEM)] * len(operands)
    return pl.pallas_call(
        kernel,
        out_shape=out_shape,
        in_specs=specs,
        out_specs=jax.tree.map(lambda _: pl.BlockSpec(memory_space=pltpu.VMEM), out_shape),
        scratch_shapes=scratch,
        compiler_params=pltpu.CompilerParams(vmem_limit_bytes=VMEM_LIMIT),
        cost_estimate=pl.CostEstimate(flops=flops, bytes_accessed=nbytes, transcendentals=0),
    )(*smem, *operands)


def sds(shape, dtype):
    return jax.ShapeDtypeStruct(shape, dtype)


def sort_kernel(planes, in_ref, out_ref, wide):
    pairs = wide.shape[0]
    for plane in range(planes):
        for pair in range(pairs):
            wide[pair] = in_ref[plane, :, pair * 128 : (pair + 1) * 128].astype(F32)
        classes = [
            wide[:, pl.ds(r, 8, stride=4), :].reshape(pairs * 8, 128) for r in range(4)
        ]
        before = from_before(classes[3])
        for tap, (even, odd) in enumerate(
            ((before, classes[1]), (classes[0], classes[2]), (classes[1], classes[3]))
        ):
            both = jnp.concatenate(
                [even.reshape(pairs, 1, 8, 128), odd.reshape(pairs, 1, 8, 128)], axis=1
            )
            out_ref[plane, tap] = both.reshape(pairs * 16, 128).astype(BF16)


def sorted_planes(volume):
    planes, rows, width = volume.shape
    pairs = width // 128
    return call(
        functools.partial(sort_kernel, planes),
        sds((planes, 3, pairs * 16, 128), BF16),
        [pltpu.VMEM((pairs, rows, 128), F32)],
        volume,
    )


def put_rows(dst, pieces, offsets):
    rows = pieces[0].shape[0]
    for index, piece in enumerate(pieces):
        dst[pl.ds(pl.multiple_of(offsets[index], 16), rows), :] = piece[...]


def gather_taps(columns, sorted_ref, halo_ref, first, count, base):
    planes = sorted_ref.shape[0]
    rows = sorted_ref.shape[2]
    halo = halo_ref.shape[0]
    for cell in range(count):
        at = base + cell * rows
        for a in range(3):
            plane = 2 * (first + cell) - 1 + a
            for e in range(3):
                source = halo_ref.at[plane + halo, e] if plane < 0 else sorted_ref.at[plane, e]
                left = (a * 3 + e) * 256
                columns[at : at + 16, left : left + 128] = jnp.zeros((16, 128), BF16)
                columns[at + 16 : at + rows, left : left + 128] = source[0 : rows - 16, :]
                columns[at : at + rows, left + 128 : left + 256] = source[...]


def forward_first_kernel(
    offsets, alive, sorted_ref, halo_ref, w0, w1, w2, w3,
    slope_ref, windows_ref, sorted_halo, wide, columns, whole, padded, hidden,
):
    halo = halo_ref.shape[0]
    planes = sorted_ref.shape[0]
    rows = sorted_ref.shape[2]
    cells = planes // 2
    sort_kernel(halo, halo_ref, sorted_halo, wide)
    put_rows(whole, (w0, w1, w2, w3), offsets)
    for tap in range(9):
        padded[tap * 256 : tap * 256 + 64, :] = jnp.zeros((64, 128), BF16)
        padded[tap * 256 + 64 : (tap + 1) * 256, :] = whole[tap * 192 : (tap + 1) * 192, :]
    gather_taps(columns, sorted_ref, sorted_halo, -1, cells + 1, 0)
    linear = jnp.dot(columns[...], padded[...], preferred_element_type=F32)
    slope_ref[...] = activate_slope(linear[rows:])
    hidden[...] = activate(linear).reshape(hidden.shape)
    hidden[0] = hidden[0] * alive[0]
    pairs = rows // 16
    half = pairs // 2
    for out in range(cells // 2):
        for a in range(3):
            plane = 2 * out + a
            for e in range(3):
                for f in range(3):
                    block = hidden[plane, :, 0 if f == 1 else 1, 0 if e == 1 else 1]
                    block = block.reshape(half * 8, 128)
                    if e == 0:
                        block = from_before(block)
                    if f == 0:
                        block = jnp.concatenate(
                            [jnp.zeros((8, 128), F32), block[: half * 8 - 8]], axis=0
                        )
                    left = ((a * 3 + e) * 3 + f) * 128
                    windows_ref[out * half * 8 : (out + 1) * half * 8, left : left + 128] = (
                        block.astype(BF16)
                    )


def forward_first(sorted_volume, halo, shards, offsets, alive):
    planes, _, rows, _ = sorted_volume.shape
    cells = planes // 2
    shard = shards[0].shape[0]
    pairs = rows // 16
    return call(
        forward_first_kernel,
        (sds((cells * rows, 128), F32), sds((cells * rows // 8, 27 * 128), BF16)),
        [
            pltpu.VMEM((halo.shape[0], 3, rows, 128), BF16),
            pltpu.VMEM((pairs, halo.shape[1], 128), F32),
            pltpu.VMEM(((cells + 1) * rows, 9 * 256), BF16),
            pltpu.VMEM((4 * shard, 128), BF16),
            pltpu.VMEM((9 * 256, 128), BF16),
            pltpu.VMEM((cells + 1, pairs // 2, 2, 2, 8, 128), F32),
        ],
        sorted_volume, halo, *shards,
        smem=(offsets, alive),
        flops=2 * (cells + 1) * rows * 9 * 256 * 128,
    )


def forward_second_kernel(
    offsets, windows_ref, cot_ref, w0, w1, w2, w3,
    act_ref, delta_ref, g0, g1, g2, g3, whole, total,
):
    put_rows(whole, (w0, w1, w2, w3), offsets)
    linear = jnp.dot(windows_ref[...], whole[...], preferred_element_type=F32)
    outs, _, width = cot_ref.shape
    features = linear.shape[1]
    count = width // features
    acted = activate(linear)
    slope = activate_slope(linear)
    deltas = []
    for out in range(outs):
        base = out * count * 8
        act_ref[out] = jnp.concatenate(
            [acted[base + q * 8 : base + (q + 1) * 8] for q in range(count)], axis=1
        ).astype(BF16)
        cot = cot_ref[out].astype(F32)
        deltas.append(
            jnp.concatenate(
                [cot[:, q * features : (q + 1) * features] for q in range(count)], axis=0
            )
        )
    delta = (jnp.concatenate(deltas, axis=0) * slope).astype(BF16)
    delta_ref[...] = delta
    total[...] = lax.dot_general(
        windows_ref[...], delta, (((0,), (0,)), ((), ())), preferred_element_type=F32
    ).astype(BF16)
    rows = g0.shape[0]
    for index, piece in enumerate((g0, g1, g2, g3)):
        piece[...] = total[pl.ds(pl.multiple_of(offsets[index], 16), rows), :]


def forward_second(windows, cot, shards, offsets):
    rows, features = shards[0].shape
    piece = sds((rows, features), BF16)
    return call(
        forward_second_kernel,
        (sds(cot.shape, BF16), sds((windows.shape[0], features), BF16), piece, piece, piece, piece),
        [pltpu.VMEM((4 * rows, features), BF16), pltpu.VMEM((4 * rows, features), BF16)],
        windows, cot, *shards,
        smem=(offsets,),
        flops=4 * windows.shape[0] * 4 * rows * features,
    )


def back_second_kernel(offsets, delta_ref, w0, w1, w2, w3, rim_ref, spread_ref, whole, product):
    put_rows(whole, (w0, w1, w2, w3), offsets)
    product[...] = lax.dot_general(
        delta_ref[...], whole[...], (((1,), (1,)), ((), ())), preferred_element_type=F32
    )
    cells, half = spread_ref.shape[0], spread_ref.shape[1]
    size = half * 8

    def term(out, a, e, f):
        left = ((a * 3 + e) * 3 + f) * 128
        block = product[out * size : (out + 1) * size, left : left + 128]
        if f == 0:
            block = jnp.concatenate([block[8:], jnp.zeros((8, 128), F32)], axis=0)
        if e == 0:
            block = from_after(block)
        return block

    for plane in range(-1, cells):
        taps = [
            (out, a) for out in range(cells // 2) for a in range(3) if 2 * out - 1 + a == plane
        ]
        for column in range(2):
            for row in range(2):
                sums = sum(
                    term(out, a, e, f)
                    for out, a in taps
                    for e in ((0, 2) if row else (1,))
                    for f in ((0, 2) if column else (1,))
                ).reshape(half, 8, 128)
                if plane < 0:
                    rim_ref[:, column, row] = sums
                else:
                    spread_ref[plane, :, column, row] = sums


def back_second(delta, shards, offsets, cells):
    rows, features = shards[0].shape
    half = delta.shape[0] // (cells // 2) // 8
    return call(
        back_second_kernel,
        (sds((half, 2, 2, 8, 128), F32), sds((cells, half, 2, 2, 8, 128), F32)),
        [pltpu.VMEM((4 * rows, features), BF16), pltpu.VMEM((delta.shape[0], 4 * rows), F32)],
        delta, *shards,
        smem=(offsets,),
        flops=2 * delta.shape[0] * 4 * rows * features,
    )


def back_first_kernel(
    offsets, spread_ref, rim_ref, slope_ref, sorted_ref, halo_ref,
    delta_ref, g0, g1, g2, g3, sorted_halo, wide, columns, total,
):
    rows = sorted_ref.shape[2]
    cells = sorted_ref.shape[0] // 2
    sort_kernel(1, halo_ref, sorted_halo, wide)
    gather_taps(columns, sorted_ref, sorted_halo, 0, cells, 0)
    last = (cells - 1) * rows
    delta_ref[:last, :] = (spread_ref[:last, :] * slope_ref[:last, :]).astype(BF16)
    delta_ref[last:, :] = (
        (spread_ref[last:, :] + rim_ref[...].astype(F32)) * slope_ref[last:, :]
    ).astype(BF16)
    flipped = jnp.transpose(delta_ref[...].astype(F32)).astype(BF16)
    tally = jnp.dot(flipped, columns[...], preferred_element_type=F32)
    for tap in range(9):
        turned = jnp.transpose(tally[:, tap * 256 : (tap + 1) * 256])
        total[tap * 192 : (tap + 1) * 192, :] = turned[64:].astype(BF16)
    size = g0.shape[0]
    for index, piece in enumerate((g0, g1, g2, g3)):
        piece[...] = total[pl.ds(pl.multiple_of(offsets[index], 16), size), :]


def back_first(spread, rim, slope, sorted_volume, halo, offsets, shard):
    planes, _, rows, _ = sorted_volume.shape
    cells = planes // 2
    piece = sds((shard, 128), BF16)
    return call(
        back_first_kernel,
        (sds((cells * rows, 128), BF16), piece, piece, piece, piece),
        [
            pltpu.VMEM((1, 3, rows, 128), BF16),
            pltpu.VMEM((rows // 16, halo.shape[1], 128), F32),
            pltpu.VMEM((cells * rows, 9 * 256), BF16),
            pltpu.VMEM((4 * shard, 128), BF16),
        ],
        spread, rim, slope, sorted_volume, halo,
        smem=(offsets,),
        flops=2 * cells * rows * 9 * 256 * 128,
    )


def back_input_kernel(
    offsets, delta_ref, w0, w1, w2, w3, rim_ref, last_ref, out_ref, whole, turned, pairs, product, wide
):
    put_rows(whole, (w0, w1, w2, w3), offsets)
    for tap in range(9):
        top = tap * 128
        turned[top : top + 128, 0:128] = whole[tap * 192 + 64 : (tap + 1) * 192, :]
        turned[top : top + 64, 128:256] = jnp.zeros((64, 128), BF16)
        turned[top + 64 : top + 128, 128:256] = whole[tap * 192 : tap * 192 + 64, :]
    planes, side, width = out_ref.shape
    cells = planes // 2
    rows = delta_ref.shape[0] // cells
    groups = rows // 16
    for cell in range(cells):
        at = cell * rows
        pairs[at : at + rows, 0:128] = delta_ref[at : at + rows, :]
        pairs[at : at + rows - 16, 128:256] = delta_ref[at + 16 : at + rows, :]
        pairs[at + rows - 16 : at + rows, 128:256] = jnp.zeros((16, 128), BF16)
    product[...] = lax.dot_general(
        pairs[...], turned[...], (((1,), (1,)), ((), ())), preferred_element_type=F32
    ).reshape(product.shape)

    def part(cell, a, e, parity):
        left = (a * 3 + e) * 128
        return product[cell * groups : (cell + 1) * groups, parity, :, left : left + 128]

    def after(block):
        flat = block.reshape(groups * 8, 128)
        return from_after(flat).reshape(groups, 8, 128)

    for plane in range(-1, planes):
        taps = [(o, a) for o in range(cells) for a in range(3) if 2 * o - 1 + a == plane]
        wide[:, pl.ds(0, 8, stride=4), :] = sum(part(o, a, 1, 0) for o, a in taps)
        wide[:, pl.ds(1, 8, stride=4), :] = sum(
            part(o, a, 2, 0) + part(o, a, 0, 1) for o, a in taps
        )
        wide[:, pl.ds(2, 8, stride=4), :] = sum(part(o, a, 1, 1) for o, a in taps)
        wide[:, pl.ds(3, 8, stride=4), :] = sum(part(o, a, 2, 1) for o, a in taps) + after(
            sum(part(o, a, 0, 0) for o, a in taps)
        )
        for group in range(groups):
            lanes = slice(group * 128, (group + 1) * 128)
            block = wide[group]
            if plane < 0:
                rim_ref[:, lanes] = block.astype(BF16)
            else:
                out_ref[plane, :, lanes] = block.astype(BF16)
            if plane == planes - 1:
                last_ref[:, lanes] = block


def back_input(delta, shards, offsets, shape):
    planes, side, width = shape
    shard = shards[0].shape[0]
    rows = delta.shape[0]
    return call(
        back_input_kernel,
        (sds((side, width), BF16), sds((side, width), F32), sds(shape, BF16)),
        [
            pltpu.VMEM((4 * shard, 128), BF16),
            pltpu.VMEM((9 * 128, 256), BF16),
            pltpu.VMEM((rows, 256), BF16),
            pltpu.VMEM((rows // 16, 2, 8, 9 * 128), F32),
            pltpu.VMEM((width // 128, side, 128), F32),
        ],
        delta, *shards,
        smem=(offsets,),
        flops=2 * rows * 9 * 128 * 256,
    )


def close_kernel(whole_ref, last_ref, rim_ref, out_ref):
    del whole_ref
    out_ref[0] = (last_ref[...] + rim_ref[...].astype(F32)).astype(BF16)


def close_input(whole, last, rim):
    planes, side, width = whole.shape
    flat = pl.BlockSpec((side, width), lambda i: (0, 0))
    return pl.pallas_call(
        close_kernel,
        grid=(1,),
        out_shape=sds(whole.shape, BF16),
        in_specs=[pl.BlockSpec(memory_space=pl.ANY), flat, flat],
        out_specs=pl.BlockSpec((1, side, width), lambda i: (planes - 1, 0, 0)),
        input_output_aliases={0: 0},
        cost_estimate=pl.CostEstimate(
            flops=0, bytes_accessed=side * width * 8, transcendentals=0
        ),
    )(whole, last, rim)


def pack_kernel(order, *refs):
    (s0, s1, s2, f0, f1, f2, *outs, flat) = refs
    rows = s0.shape[0]
    second = s0[...].astype(F32) + s1[...].astype(F32) + s2[...].astype(F32)
    lanes = second.shape[1] // 128
    for lane in range(lanes):
        flat[lane * rows : (lane + 1) * rows, :] = second[:, lane * 128 : (lane + 1) * 128].astype(BF16)
    top = lanes * rows
    small = f0.shape[0]
    first = f0[...].astype(F32) + f1[...].astype(F32) + f2[...].astype(F32)
    flat[top : top + small, :] = first.astype(BF16)
    rest = flat.shape[0] - top - small
    if rest:
        flat[top + small :, :] = jnp.zeros((rest, 128), BF16)
    size = outs[0].shape[0]
    for index, out in enumerate(outs):
        out[...] = flat[pl.ds(pl.multiple_of(order[index] * size, 16), size), :]


def unpack_kernel(scale_first, scale_second, order, *refs):
    *chunks, first_ref, second_ref, flat = refs
    size = chunks[0].shape[0]
    for index, chunk in enumerate(chunks):
        flat[pl.ds(pl.multiple_of(order[index] * size, 16), size), :] = chunk[...]
    rows, features = second_ref.shape
    for lane in range(features // 128):
        second_ref[:, lane * 128 : (lane + 1) * 128] = (
            flat[lane * rows : (lane + 1) * rows, :].astype(F32) * scale_second
        )
    top = rows * (features // 128)
    first_ref[...] = flat[top : top + first_ref.shape[0], :].astype(F32) * scale_first


def total(pieces):
    return sum(piece.astype(F32) for piece in pieces)


def swap(value, axis, bits):
    size = lax.axis_size(axis)
    return lax.ppermute(value, axis, [(i, i ^ bits) for i in range(size)])


def shifted(value, axis, by):
    size = lax.axis_size(axis)
    pairs = [(i, i + by) for i in range(size) if 0 <= i + by < size]
    return lax.ppermute(value, axis, pairs)


def sum_over_space(chunks):
    count = len(chunks)
    if count == 1:
        return chunks
    group = min(8, count)
    partial = []
    for high in range(0, count, group):
        got = [chunks[high]] + [swap(chunks[high + k], "space", k) for k in range(1, group)]
        partial.append(total(got).astype(BF16))
    if count > group:
        partial = sum_over_space_high(partial, group)
    sums = [None] * count
    for high in range(count // group):
        sums[high * group] = partial[high]
        for k in range(1, group):
            sums[high * group + k] = swap(partial[high], "space", k)
    return sums


def sum_over_space_high(chunks, stride):
    count = len(chunks)
    got = [chunks[0]] + [swap(chunks[k], "space", k * stride) for k in range(1, count)]
    mine = total(got).astype(BF16)
    return [mine] + [swap(mine, "space", k * stride) for k in range(1, count)]


def local(volume, weight_first, weight_second, cotangent):
    samples, planes, side, width = volume.shape
    data = lax.axis_index("dp")
    place = lax.axis_index("space")
    spaces = lax.axis_size("space")
    small, big = weight_first.shape[0], weight_second.shape[0]
    partners = jnp.arange(4, dtype=jnp.int32) ^ data
    offsets_first = partners * small
    offsets_second = partners * big
    alive = (place > 0).astype(F32).reshape(1)
    order = jnp.arange(spaces, dtype=jnp.int32) ^ place

    inputs = volume.reshape(planes, side, width)
    halo = shifted(inputs[planes - 3 :], "space", 1)
    first_x = swap(weight_first, "dp", 2)
    first_core = swap(weight_first, "dp", 1)
    second_x = swap(weight_second, "dp", 2)
    second_core = swap(weight_second, "dp", 1)
    first_far = swap(first_x, "dp", 1)
    second_far = swap(second_x, "dp", 1)
    shards_first = (weight_first, first_core, first_x, first_far)
    shards_second = (weight_second, second_core, second_x, second_far)

    sorted_volume = sorted_planes(inputs)
    slope, windows = forward_first(sorted_volume, halo, shards_first, offsets_first, alive)
    cot = cotangent.reshape(cotangent.shape[1:])
    activations, delta_second, *second = forward_second(windows, cot, shards_second, offsets_second)
    second_sum = second[2].astype(F32) + swap(second[3], "dp", 1).astype(F32)
    second_here = swap(second[1], "dp", 1)
    second_there = swap(second_sum.astype(BF16), "dp", 2)

    cells = planes // 2
    rim, spread = back_second(delta_second, shards_second, offsets_second, cells)
    rim = shifted(rim.reshape(-1, 128).astype(BF16), "space", -1)
    delta_first, *first = back_first(
        spread.reshape(-1, 128), rim, slope, sorted_volume, halo[2:], offsets_first, small
    )
    first_sum = first[2].astype(F32) + swap(first[3], "dp", 1).astype(F32)
    first_here = swap(first[1], "dp", 1)
    first_there = swap(first_sum.astype(BF16), "dp", 2)

    last_rim, last, gradient = back_input(delta_first, shards_first, offsets_first, inputs.shape)
    last_rim = shifted(last_rim, "space", -1)
    input_gradient = close_input(gradient, last, last_rim)

    lanes = weight_second.shape[1] // 128
    rows = lanes * big + small
    size = -(-rows // (16 * spaces)) * 16
    chunk = sds((size, 128), BF16)
    chunks = call(
        pack_kernel,
        (chunk,) * spaces,
        [pltpu.VMEM((size * spaces, 128), BF16)],
        second[0], second_here, second_there, first[0], first_here, first_there,
        smem=(order,),
    )
    sums = sum_over_space(list(chunks))
    cells_first = samples * lax.axis_size("dp") * cells * spaces * (side // 2) ** 2
    cells_second = cells_first // 8
    first_gradient, second_gradient = call(
        functools.partial(unpack_kernel, float(cells_first) ** -0.5, float(cells_second) ** -0.5),
        (sds(weight_first.shape, F32), sds(weight_second.shape, F32)),
        [pltpu.VMEM((size * spaces, 128), BF16)],
        *sums,
        smem=(order,),
    )
    return (
        activations.reshape(cotangent.shape),
        input_gradient.reshape(volume.shape),
        first_gradient,
        second_gradient,
    )


def solution(mesh):
    return jax.shard_map(
        local,
        mesh=mesh,
        in_specs=(
            P("dp", "space", None, None),
            P("dp", None),
            P("dp", None),
            P("dp", "space", None, None),
        ),
        out_specs=(
            P("dp", "space", None, None),
            P("dp", "space", None, None),
            P("dp", None),
            P("dp", None),
        ),
        check_vma=False,
    )
```

profile of v0, /device:TPU:0, one launch (start us, length us, event | category | flops | bytes accessed | tf_op | source)
XLA Modules:
  0.0 89.8 jit_solution(1543206538355289338)
XLA Ops:
  0.6 3.0 %collective-permute-start.5 = (bf16[864,256]{1,0:T(8,128)(2,1)}, bf16[864,256]{1,0:T(8,128)(2,1)S(1)}, u32[]{:S(2)}, u32[]{:S(2)}) collective-permute-start(bf16[864,256]{1,0:T(8,128)(2,1)} %w0.6), channel_id=1, source_target_pairs={{0,16},{8,24},{16,0},{24,8},{1,17},{9,25},{17,1},{25,9},{2,18},{10... | collective-permute-start | bytes 1327112 | tf_op jit(solution)/shard_map/ppermute | solution.py:443
  3.6 1.0 %slice_bitcast_fusion = bf16[3,32,2048]{2,1,0:T(8,128)(2,1)S(1)} fusion(bf16[1,8,32,2048]{3,2,1,0:T(8,128)(2,1)} %param.4), kind=kLoop, calls=%fused_computation.1 | loop fusion | bytes 786432 | tf_op jit(solution)/shard_map/slice | solution.py:491
  4.7 3.4 %collective-permute-start = (bf16[3,32,2048]{2,1,0:T(8,128)(2,1)S(1)}, bf16[3,32,2048]{2,1,0:T(8,128)(2,1)S(1)}, u32[]{:S(2)}, u32[]{:S(2)}) collective-permute-start(bf16[3,32,2048]{2,1,0:T(8,128)(2,1)S(1)} %slice_bitcast_fusion), channel_id=1, source_target_pairs={{0,1},{1,2},{2,3},{3,4},{4,5},{5,6},{6,7},{8,9},{9,10},{10,11},{11... | collective-permute-start | bytes 1179656 | tf_op jit(solution)/shard_map/ppermute | solution.py:449
  8.1 0.1 collective-permute-start.4
  8.2 5.8 %collective-permute-done.5.w2 = bf16[864,256]{1,0:T(8,128)(2,1)S(1)} collective-permute-done((bf16[864,256]{1,0:T(8,128)(2,1)}, bf16[864,256]{1,0:T(8,128)(2,1)S(1)}, u32[]{:S(2)}, u32[]{:S(2)}) %collective-permute-start.5) | collective-permute-done | bytes 442400 | tf_op jit(solution)/shard_map/ppermute | solution.py:443
  14.0 1.7 %collective-permute-start.2 = (bf16[432,128]{1,0:T(8,128)(2,1)}, bf16[432,128]{1,0:T(8,128)(2,1)S(1)}, u32[]{:S(2)}, u32[]{:S(2)}) collective-permute-start(bf16[432,128]{1,0:T(8,128)(2,1)} %w0.7), channel_id=1, source_target_pairs={{0,16},{8,24},{16,0},{24,8},{1,17},{9,25},{17,1},{25,9},{2,18},{10... | collective-permute-start | bytes 331784 | tf_op jit(solution)/shard_map/ppermute | solution.py:443
  15.8 0.2 collective-permute-start.1
  16.0 1.2 %copy-done = bf16[1,8,32,2048]{3,2,1,0:T(8,128)(2,1)S(1)} copy-done((bf16[1,8,32,2048]{3,2,1,0:T(8,128)(2,1)S(1)}, bf16[1,8,32,2048]{3,2,1,0:T(8,128)(2,1)}, u32[]{:S(2)}) %copy-start) | copy-done | bytes 1048600
  17.2 0.3 shard_map.75.sorted_ref
  17.6 2.1 %collective-permute-done.2.w2 = bf16[432,128]{1,0:T(8,128)(2,1)S(1)} collective-permute-done((bf16[432,128]{1,0:T(8,128)(2,1)}, bf16[432,128]{1,0:T(8,128)(2,1)S(1)}, u32[]{:S(2)}, u32[]{:S(2)}) %collective-permute-start.2) | collective-permute-done | bytes 110624 | tf_op jit(solution)/shard_map/ppermute | solution.py:443
  19.7 1.3 %collective-permute-done.3.w3 = bf16[432,128]{1,0:T(8,128)(2,1)S(1)} collective-permute-done((bf16[432,128]{1,0:T(8,128)(2,1)S(1)}, bf16[432,128]{1,0:T(8,128)(2,1)S(1)}, u32[]{:S(2)}, u32[]{:S(2)}) %collective-permute-start.3) | collective-permute-done | bytes 110624 | tf_op jit(solution)/shard_map/ppermute | solution.py:443
  21.0 2.8 %shard_map.76 = (f32[1024,128]{1,0:T(8,128)S(1)}, bf16[128,3456]{1,0:T(8,128)(2,1)S(1)}) custom-call(s32[4]{0:T(128)S(1)} %fusion.offsets, f32[1]{0:T(128)} %bitcast.alive, bf16[8,3,256,128]{3,2,1,0:T(8,128)(2,1)S(1)} %shard_map.75.sorted_ref, bf16[3,32,2048]{2,1,0:T(8,128)(2,1)S(1)} %collective-permute-done.halo_ref, bf16[432,128]{1,0:T(8,128)(2,1)S(1)} %copy-done.4, ...), custom_call_target="tpu_custom_call" | custom-call | flops 754974720 | bytes 3817472 | tf_op jit(solution)/shard_map/pallas_call | solution.py:49
  23.9 2.9 %shard_map.77 = (bf16[2,8,2048]{2,1,0:T(8,128)(2,1)}, bf16[128,256]{1,0:T(8,128)(2,1)S(1)}, bf16[864,256]{1,0:T(8,128)(2,1)S(1)}, bf16[864,256]{1,0:T(8,128)(2,1...) custom-call(s32[4]{0:T(128)S(1)} %fusion.1.offsets, ...), custom_call_target="tpu_custom_call" | custom-call | flops 452984832 | bytes 4620288 | tf_op jit(solution)/shard_map/pallas_call | solution.py:49
  26.8 0.2 collective-permute-start.10
  27.0 1.4 %shard_map.78 = (f32[8,2,2,8,128]{4,3,2,1,0:T(8,128)S(1)}, f32[4,8,2,2,8,128]{5,4,3,2,1,0:T(8,128)S(1)}) custom-call(s32[4]{0:T(128)S(1)} %fusion.1.offsets, bf16[128,256]{1,0:T(8,128)(2,1)S(1)} %get-tuple-element.34.delta_ref, bf16[864,256]{1,0:T(8,128)(2,1)S(1)} %copy-done.1, bf16[864,256]{1,0:T(8,128)(2,1)S(1)} %collective-permute-done.4.w1, ...), custom_call_target="tpu_custom_call" | custom-call | flops 226492416 | bytes 2490368 | tf_op jit(solution)/shard_map/pallas_call | solution.py:49
  28.4 1.3 %collective-permute-start.7 = (bf16[256,128]{1,0:T(8,128)(2,1)S(1)}, bf16[256,128]{1,0:T(8,128)(2,1)S(1)}, u32[]{:S(2)}, u32[]{:S(2)}) collective-permute-start(bf16[256,128]{1,0:T(8,128)(2,1)S(1)} %bitcast.13), channel_id=1, source_target_pairs={{1,0},{2,1},{3,2},{4,3},{5,4},{6,5},{7,6},{9,8},{10,9},{11,10},{12... | collective-permute-start | bytes 196616 | tf_op jit(solution)/shard_map/ppermute | solution.py:449
  29.7 0.4 collective-permute-start.9
  30.1 4.5 %collective-permute-done.7.rim_ref = bf16[256,128]{1,0:T(8,128)(2,1)S(1)} collective-permute-done((bf16[256,128]{1,0:T(8,128)(2,1)S(1)}, bf16[256,128]{1,0:T(8,128)(2,1)S(1)}, u32[]{:S(2)}, u32[]{:S(2)}) %collective-permute-start.7) | collective-permute-done | bytes 65568 | tf_op jit(solution)/shard_map/ppermute | solution.py:449
  34.7 1.9 %shard_map.79 = (bf16[1024,128]{1,0:T(8,128)(2,1)S(1)}, bf16[432,128]{1,0:T(8,128)(2,1)S(1)}, bf16[432,128]{1,0:T(8,128)(2,1)S(1)}, bf16[432,128]{1,0:T(8,128)(2,1)S(1)}, bf16[432,128]{1,0:T(8,128)(2,1)S(1)}) custom-call(s32[4]{0:T(128)S(1)} %fusion.offsets, f32[1024,128]{1,0:T(8,128)S(1)} %bitcast.10, bf16[256,128]{1,0:T(8,128)(2,1)S(1)} %collective-permute-done.7.rim_ref, ...), custom_call_target="tpu_custom_call" | custom-call | flops 603979776 | bytes 3522560 | tf_op jit(solution)/shard_map/pallas_call | solution.py:49
  36.6 0.1 collective-permute-start.13
  36.7 0.1 add_convert_fusion
  36.8 1.8 %collective-permute-start.11 = (bf16[864,256]{1,0:T(8,128)(2,1)S(1)}, bf16[864,256]{1,0:T(8,128)(2,1)S(1)}, u32[]{:S(2)}, u32[]{:S(2)}) collective-permute-start(bf16[864,256]{1,0:T(8,128)(2,1)S(1)} %add_convert_fusion), channel_id=1, source_target_pairs={{0,16},{8,24},{16,0},{24,8},{1,17},{9,25},{17,1},{25,9},{2,18},{10... | collective-permute-start | bytes 1327112 | tf_op jit(solution)/shard_map/ppermute | solution.py:443
  38.5 0.2 collective-permute-start.12
  38.8 1.0 %collective-permute-start.14 = (bf16[432,128]{1,0:T(8,128)(2,1)S(1)}, bf16[432,128]{1,0:T(8,128)(2,1)S(1)}, u32[]{:S(2)}, u32[]{:S(2)}) collective-permute-start(bf16[432,128]{1,0:T(8,128)(2,1)S(1)} %add_convert_fusion.1), channel_id=1, source_target_pairs={{0,16},{8,24},{16,0},{24,8},{1,17},{9,25},{17,1},{25,9},{2,18},{10... | collective-permute-start | bytes 331784 | tf_op jit(solution)/shard_map/ppermute | solution.py:443
  39.8 0.1 collective-permute-done.12.refs_4_
  39.9 11.9 %collective-permute-done.14.refs_5_ = bf16[432,128]{1,0:T(8,128)(2,1)S(1)} collective-permute-done((bf16[432,128]{1,0:T(8,128)(2,1)S(1)}, bf16[432,128]{1,0:T(8,128)(2,1)S(1)}, u32[]{:S(2)}, u32[]{:S(2)}) %collective-permute-start.14) | collective-permute-done | bytes 110624 | tf_op jit(solution)/shard_map/ppermute | solution.py:443
  51.8 0.9 %shard_map.82 = (bf16[272,128]{1,0:T(8,128)(2,1)S(1)}, bf16[272,128]{1,0:T(8,128)(2,1)S(1)}, bf16[272,128]{1,0:T(8,128)(2,1)S(1)}, bf16[272,128]{1,0:T(8,128)(2,...) custom-call(s32[8]{0:T(128)S(1)} %iota_xor_fusion.order, ...), custom_call_target="tpu_custom_call" | custom-call | bytes 2215936 | tf_op jit(solution)/shard_map/pallas_call | solution.py:49
  52.7 2.7 %collective-permute-start.15 = (bf16[272,128]{1,0:T(8,128)(2,1)S(1)}, bf16[272,128]{1,0:T(8,128)(2,1)S(1)}, u32[]{:S(2)}, u32[]{:S(2)}) collective-permute-start(bf16[272,128]{1,0:T(8,128)(2,1)S(1)} %get-tuple-element.51), channel_id=1, source_target_pairs={{0,1},{1,0},{2,3},{3,2},{4,5},{5,4},{6,7},{7,6},{8,9},{9,8},{10,11... | collective-permute-start | bytes 208904 | tf_op jit(solution)/shard_map/ppermute | solution.py:443
  55.4 1.6 %collective-permute-start.16 = (bf16[272,128]{1,0:T(8,128)(2,1)S(1)}, bf16[272,128]{1,0:T(8,128)(2,1)S(1)}, u32[]{:S(2)}, u32[]{:S(2)}) collective-permute-start(bf16[272,128]{1,0:T(8,128)(2,1)S(1)} %get-tuple-element.52), channel_id=1, source_target_pairs={{0,2},{1,3},{2,0},{3,1},{4,6},{5,7},{6,4},{7,5},{8,10},{9,11},{10,... | collective-permute-start | bytes 208904 | tf_op jit(solution)/shard_map/ppermute | solution.py:443
  57.0 2.6 %collective-permute-start.18 = (bf16[272,128]{1,0:T(8,128)(2,1)S(1)}, bf16[272,128]{1,0:T(8,128)(2,1)S(1)}, u32[]{:S(2)}, u32[]{:S(2)}) collective-permute-start(bf16[272,128]{1,0:T(8,128)(2,1)S(1)} %get-tuple-element.54), channel_id=1, source_target_pairs={{0,4},{1,5},{2,6},{3,7},{4,0},{5,1},{6,2},{7,3},{8,12},{9,13},{10,... | collective-permute-start | bytes 208904 | tf_op jit(solution)/shard_map/ppermute | solution.py:443
  59.6 1.7 %collective-permute-start.19 = (bf16[272,128]{1,0:T(8,128)(2,1)S(1)}, bf16[272,128]{1,0:T(8,128)(2,1)S(1)}, u32[]{:S(2)}, u32[]{:S(2)}) collective-permute-start(bf16[272,128]{1,0:T(8,128)(2,1)S(1)} %get-tuple-element.55), channel_id=1, source_target_pairs={{0,5},{1,4},{2,7},{3,6},{4,1},{5,0},{6,3},{7,2},{8,13},{9,12},{10,... | collective-permute-start | bytes 208904 | tf_op jit(solution)/shard_map/ppermute | solution.py:443
  61.3 2.0 %collective-permute-start.20 = (bf16[272,128]{1,0:T(8,128)(2,1)S(1)}, bf16[272,128]{1,0:T(8,128)(2,1)S(1)}, u32[]{:S(2)}, u32[]{:S(2)}) collective-permute-start(bf16[272,128]{1,0:T(8,128)(2,1)S(1)} %get-tuple-element.56), channel_id=1, source_target_pairs={{0,6},{1,7},{2,4},{3,5},{4,2},{5,3},{6,0},{7,1},{8,14},{9,15},{10,... | collective-permute-start | bytes 208904 | tf_op jit(solution)/shard_map/ppermute | solution.py:443
  63.3 1.5 %collective-permute-start.21 = (bf16[272,128]{1,0:T(8,128)(2,1)S(1)}, bf16[272,128]{1,0:T(8,128)(2,1)S(1)}, u32[]{:S(2)}, u32[]{:S(2)}) collective-permute-start(bf16[272,128]{1,0:T(8,128)(2,1)S(1)} %get-tuple-element.57), channel_id=1, source_target_pairs={{0,7},{1,6},{2,5},{3,4},{4,3},{5,2},{6,1},{7,0},{8,15},{9,14},{10,... | collective-permute-start | bytes 208904 | tf_op jit(solution)/shard_map/ppermute | solution.py:443
  64.8 2.7 %shard_map.80 = (bf16[32,2048]{1,0:T(8,128)(2,1)S(1)}, f32[32,2048]{1,0:T(8,128)S(1)}, bf16[8,32,2048]{2,1,0:T(8,128)(2,1)}) custom-call(s32[4]{0:T(128)S(1)} %fusion.offsets, bf16[1024,128]{1,0:T(8,128)(2,1)S(1)} %get-tuple-element.38.delta_ref, bf16[432,128]{1,0:T(8,128)(2,1)S(1)} %copy-done.4, bf16[432,128]{1,0:T(8,128)(2,1)S(1)} %collective-permute-done.1.w1, ...), custom_call_target="tpu_custom_call" | custom-call | flops 603979776 | bytes 2146304 | tf_op jit(solution)/shard_map/pallas_call | solution.py:49
  67.5 1.3 %collective-permute-start.8 = (bf16[32,2048]{1,0:T(8,128)(2,1)S(1)}, bf16[32,2048]{1,0:T(8,128)(2,1)S(1)}, u32[]{:S(2)}, u32[]{:S(2)}) collective-permute-start(bf16[32,2048]{1,0:T(8,128)(2,1)S(1)} %get-tuple-element.41), channel_id=1, source_target_pairs={{1,0},{2,1},{3,2},{4,3},{5,4},{6,5},{7,6},{9,8},{10,9},{11,10},{12... | collective-permute-start | bytes 393224 | tf_op jit(solution)/shard_map/ppermute | solution.py:449
  68.8 2.5 %collective-permute-done.19 = bf16[272,128]{1,0:T(8,128)(2,1)S(1)} collective-permute-done((bf16[272,128]{1,0:T(8,128)(2,1)S(1)}, bf16[272,128]{1,0:T(8,128)(2,1)S(1)}, u32[]{:S(2)}, u32[]{:S(2)}) %collective-permute-start.19) | collective-permute-done | bytes 69664 | tf_op jit(solution)/shard_map/ppermute | solution.py:443
  71.2 0.1 add_convert_fusion.2.refs_0_
  71.3 2.7 %collective-permute-start.28 = (bf16[272,128]{1,0:T(8,128)(2,1)S(1)}, bf16[272,128]{1,0:T(8,128)(2,1)S(1)}, u32[]{:S(2)}, u32[]{:S(2)}) collective-permute-start(bf16[272,128]{1,0:T(8,128)(2,1)S(1)} %add_convert_fusion.2.refs_0_), channel_id=1, source_target_pairs={{0,7},{1,6},{2,5},{3,4},{4,3},{5,2},{6,1},{7,0},{8,15},{9,14},{10,... | collective-permute-start | bytes 208904 | tf_op jit(solution)/shard_map/ppermute | solution.py:443
  74.0 1.0 %collective-permute-start.27 = (bf16[272,128]{1,0:T(8,128)(2,1)S(1)}, bf16[272,128]{1,0:T(8,128)(2,1)S(1)}, u32[]{:S(2)}, u32[]{:S(2)}) collective-permute-start(bf16[272,128]{1,0:T(8,128)(2,1)S(1)} %add_convert_fusion.2.refs_0_), channel_id=1, source_target_pairs={{0,6},{1,7},{2,4},{3,5},{4,2},{5,3},{6,0},{7,1},{8,14},{9,15},{10,... | collective-permute-start | bytes 208904 | tf_op jit(solution)/shard_map/ppermute | solution.py:443
  75.0 2.6 %collective-permute-start.26 = (bf16[272,128]{1,0:T(8,128)(2,1)S(1)}, bf16[272,128]{1,0:T(8,128)(2,1)S(1)}, u32[]{:S(2)}, u32[]{:S(2)}) collective-permute-start(bf16[272,128]{1,0:T(8,128)(2,1)S(1)} %add_convert_fusion.2.refs_0_), channel_id=1, source_target_pairs={{0,5},{1,4},{2,7},{3,6},{4,1},{5,0},{6,3},{7,2},{8,13},{9,12},{10,... | collective-permute-start | bytes 208904 | tf_op jit(solution)/shard_map/ppermute | solution.py:443
  77.6 1.4 %collective-permute-start.25 = (bf16[272,128]{1,0:T(8,128)(2,1)S(1)}, bf16[272,128]{1,0:T(8,128)(2,1)S(1)}, u32[]{:S(2)}, u32[]{:S(2)}) collective-permute-start(bf16[272,128]{1,0:T(8,128)(2,1)S(1)} %add_convert_fusion.2.refs_0_), channel_id=1, source_target_pairs={{0,4},{1,5},{2,6},{3,7},{4,0},{5,1},{6,2},{7,3},{8,12},{9,13},{10,... | collective-permute-start | bytes 208904 | tf_op jit(solution)/shard_map/ppermute | solution.py:443
  79.0 1.5 %collective-permute-start.24 = (bf16[272,128]{1,0:T(8,128)(2,1)S(1)}, bf16[272,128]{1,0:T(8,128)(2,1)S(1)}, u32[]{:S(2)}, u32[]{:S(2)}) collective-permute-start(bf16[272,128]{1,0:T(8,128)(2,1)S(1)} %add_convert_fusion.2.refs_0_), channel_id=1, source_target_pairs={{0,3},{1,2},{2,1},{3,0},{4,7},{5,6},{6,5},{7,4},{8,11},{9,10},{10,... | collective-permute-start | bytes 208904 | tf_op jit(solution)/shard_map/ppermute | solution.py:443
  80.5 3.2 %collective-permute-start.23 = (bf16[272,128]{1,0:T(8,128)(2,1)S(1)}, bf16[272,128]{1,0:T(8,128)(2,1)S(1)}, u32[]{:S(2)}, u32[]{:S(2)}) collective-permute-start(bf16[272,128]{1,0:T(8,128)(2,1)S(1)} %add_convert_fusion.2.refs_0_), channel_id=1, source_target_pairs={{0,2},{1,3},{2,0},{3,1},{4,6},{5,7},{6,4},{7,5},{8,10},{9,11},{10,... | collective-permute-start | bytes 208904 | tf_op jit(solution)/shard_map/ppermute | solution.py:443
  83.7 1.1 %collective-permute-start.22 = (bf16[272,128]{1,0:T(8,128)(2,1)S(1)}, bf16[272,128]{1,0:T(8,128)(2,1)S(1)}, u32[]{:S(2)}, u32[]{:S(2)}) collective-permute-start(bf16[272,128]{1,0:T(8,128)(2,1)S(1)} %add_convert_fusion.2.refs_0_), channel_id=1, source_target_pairs={{0,1},{1,0},{2,3},{3,2},{4,5},{5,4},{6,7},{7,6},{8,9},{9,8},{10,11... | collective-permute-start | bytes 208904 | tf_op jit(solution)/shard_map/ppermute | solution.py:443
  84.8 1.7 %shard_map.81 = bf16[8,32,2048]{2,1,0:T(8,128)(2,1)} custom-call(bf16[8,32,2048]{2,1,0:T(8,128)(2,1)} %get-tuple-element.39.whole_ref, f32[32,2048]{1,0:T(8,128)} %copy-done.2, bf16[32,2048]{1,0:T(8,128)(2,1)} %copy-done.5), custom_call_target="tpu_custom_call", output_to_operand_aliasing={{}: (0, {})} | custom-call | bytes 524288 | tf_op jit(solution)/shard_map/pallas_call | solution.py:391
  86.4 1.0 %collective-permute-done.25.refs_4_ = bf16[272,128]{1,0:T(8,128)(2,1)S(1)} collective-permute-done((bf16[272,128]{1,0:T(8,128)(2,1)S(1)}, bf16[272,128]{1,0:T(8,128)(2,1)S(1)}, u32[]{:S(2)}, u32[]{:S(2)}) %collective-permute-start.25) | collective-permute-done | bytes 69664 | tf_op jit(solution)/shard_map/ppermute | solution.py:443
  87.5 0.6 collective-permute-done.23.refs_2_
  88.1 1.7 %shard_map.83 = (f32[432,128]{1,0:T(8,128)}, f32[864,256]{1,0:T(8,128)}) custom-call(s32[8]{0:T(128)S(1)} %iota_xor_fusion.order, bf16[272,128]{1,0:T(8,128)(2,1)S(1)} %add_convert_fusion.2.refs_0_, bf16[272,128]{1,0:T(8,128)(2,1)S(1)} %collective-permute-done.22.refs_1_, bf16[272,128]{1,0:T(8,128)(2,1)S(1)} %collective-permute-done.23.refs_2_, ...), custom_call_target="tpu_custom_call" | custom-call | bytes 1662976 | tf_op jit(solution)/shard_map/pallas_call | solution.py:49
  (40 shorter events, 0.2 us)
Async XLA Ops:
  0.6 20.4 %copy-start.4 = (bf16[432,128]{1,0:T(8,128)(2,1)S(1)}, bf16[432,128]{1,0:T(8,128)(2,1)}, u32[]{:S(2)}) copy-start(bf16[432,128]{1,0:T(8,128)(2,1)} %w0.7) | copy-start | bytes 331780
  0.6 13.4 %collective-permute-start.5 = (bf16[864,256]{1,0:T(8,128)(2,1)}, bf16[864,256]{1,0:T(8,128)(2,1)S(1)}, u32[]{:S(2)}, u32[]{:S(2)}) collective-permute-start(bf16[864,256]{1,0:T(8,128)(2,1)} %w0.6), channel_id=1, source_target_pairs={{0,16},{8,24},{16,0},{24,8},{1,17},{9,25},{17,1},{25,9},{2,18},{10... | collective-permute-start | bytes 1327112 | tf_op jit(solution)/shard_map/ppermute | solution.py:443
  4.7 16.4 %collective-permute-start = (bf16[3,32,2048]{2,1,0:T(8,128)(2,1)S(1)}, bf16[3,32,2048]{2,1,0:T(8,128)(2,1)S(1)}, u32[]{:S(2)}, u32[]{:S(2)}) collective-permute-start(bf16[3,32,2048]{2,1,0:T(8,128)(2,1)S(1)} %slice_bitcast_fusion), channel_id=1, source_target_pairs={{0,1},{1,2},{2,3},{3,4},{4,5},{5,6},{6,7},{8,9},{9,10},{10,11},{11... | collective-permute-start | bytes 1179656 | tf_op jit(solution)/shard_map/ppermute | solution.py:449
  8.1 15.7 %collective-permute-start.4 = (bf16[864,256]{1,0:T(8,128)(2,1)}, bf16[864,256]{1,0:T(8,128)(2,1)S(1)}, u32[]{:S(2)}, u32[]{:S(2)}) collective-permute-start(bf16[864,256]{1,0:T(8,128)(2,1)} %w0.6), channel_id=1, source_target_pairs={{0,8},{8,0},{16,24},{24,16},{1,9},{9,1},{17,25},{25,17},{2,10},{10... | collective-permute-start | bytes 1327112 | tf_op jit(solution)/shard_map/ppermute | solution.py:443
  14.0 9.8 %collective-permute-start.6 = (bf16[864,256]{1,0:T(8,128)(2,1)S(1)}, bf16[864,256]{1,0:T(8,128)(2,1)S(1)}, u32[]{:S(2)}, u32[]{:S(2)}) collective-permute-start(bf16[864,256]{1,0:T(8,128)(2,1)S(1)} %collective-permute-done.5.w2), channel_id=1, source_target_pairs={{0,8},{8,0},{16,24},{24,16},{1,9},{9,1},{17,25},{25,17},{2,10},{10... | collective-permute-start | bytes 1327112 | tf_op jit(solution)/shard_map/ppermute | solution.py:443
  14.0 5.7 %collective-permute-start.2 = (bf16[432,128]{1,0:T(8,128)(2,1)}, bf16[432,128]{1,0:T(8,128)(2,1)S(1)}, u32[]{:S(2)}, u32[]{:S(2)}) collective-permute-start(bf16[432,128]{1,0:T(8,128)(2,1)} %w0.7), channel_id=1, source_target_pairs={{0,16},{8,24},{16,0},{24,8},{1,17},{9,25},{17,1},{25,9},{2,18},{10... | collective-permute-start | bytes 331784 | tf_op jit(solution)/shard_map/ppermute | solution.py:443
  15.8 4.0 %collective-permute-start.1 = (bf16[432,128]{1,0:T(8,128)(2,1)}, bf16[432,128]{1,0:T(8,128)(2,1)S(1)}, u32[]{:S(2)}, u32[]{:S(2)}) collective-permute-start(bf16[432,128]{1,0:T(8,128)(2,1)} %w0.7), channel_id=1, source_target_pairs={{0,8},{8,0},{16,24},{24,16},{1,9},{9,1},{17,25},{25,17},{2,10},{10... | collective-permute-start | bytes 331784 | tf_op jit(solution)/shard_map/ppermute | solution.py:443
  16.0 1.2 %copy-start = (bf16[1,8,32,2048]{3,2,1,0:T(8,128)(2,1)S(1)}, bf16[1,8,32,2048]{3,2,1,0:T(8,128)(2,1)}, u32[]{:S(2)}) copy-start(bf16[1,8,32,2048]{3,2,1,0:T(8,128)(2,1)} %param.4) | copy-start | bytes 3145732
  17.6 6.3 %copy-start.1 = (bf16[864,256]{1,0:T(8,128)(2,1)S(1)}, bf16[864,256]{1,0:T(8,128)(2,1)}, u32[]{:S(2)}) copy-start(bf16[864,256]{1,0:T(8,128)(2,1)} %w0.6) | copy-start | bytes 1327108
  17.6 6.3 %copy-start.3 = (bf16[1,2,8,2048]{3,2,1,0:T(8,128)(2,1)S(1)}, bf16[1,2,8,2048]{3,2,1,0:T(8,128)(2,1)}, u32[]{:S(2)}) copy-start(bf16[1,2,8,2048]{3,2,1,0:T(8,128)(2,1)} %param.7) | copy-start | bytes 196612
  19.7 1.3 %collective-permute-start.3 = (bf16[432,128]{1,0:T(8,128)(2,1)S(1)}, bf16[432,128]{1,0:T(8,128)(2,1)S(1)}, u32[]{:S(2)}, u32[]{:S(2)}) collective-permute-start(bf16[432,128]{1,0:T(8,128)(2,1)S(1)} %collective-permute-done.2.w2), channel_id=1, source_target_pairs={{0,8},{8,0},{16,24},{24,16},{1,9},{9,1},{17,25},{25,17},{2,10},{10... | collective-permute-start | bytes 331784 | tf_op jit(solution)/shard_map/ppermute | solution.py:443
  26.8 9.8 %collective-permute-start.10 = (bf16[864,256]{1,0:T(8,128)(2,1)S(1)}, bf16[864,256]{1,0:T(8,128)(2,1)S(1)}, u32[]{:S(2)}, u32[]{:S(2)}) collective-permute-start(bf16[864,256]{1,0:T(8,128)(2,1)S(1)} %get-tuple-element.45), channel_id=1, source_target_pairs={{0,8},{8,0},{16,24},{24,16},{1,9},{9,1},{17,25},{25,17},{2,10},{10... | collective-permute-start | bytes 1327112 | tf_op jit(solution)/shard_map/ppermute | solution.py:443
  28.4 6.3 %collective-permute-start.7 = (bf16[256,128]{1,0:T(8,128)(2,1)S(1)}, bf16[256,128]{1,0:T(8,128)(2,1)S(1)}, u32[]{:S(2)}, u32[]{:S(2)}) collective-permute-start(bf16[256,128]{1,0:T(8,128)(2,1)S(1)} %bitcast.13), channel_id=1, source_target_pairs={{1,0},{2,1},{3,2},{4,3},{5,4},{6,5},{7,6},{9,8},{10,9},{11,10},{12... | collective-permute-start | bytes 196616 | tf_op jit(solution)/shard_map/ppermute | solution.py:449
  29.7 22.1 %collective-permute-start.9 = (bf16[864,256]{1,0:T(8,128)(2,1)S(1)}, bf16[864,256]{1,0:T(8,128)(2,1)S(1)}, u32[]{:S(2)}, u32[]{:S(2)}) collective-permute-start(bf16[864,256]{1,0:T(8,128)(2,1)S(1)} %get-tuple-element.43), channel_id=1, source_target_pairs={{0,8},{8,0},{16,24},{24,16},{1,9},{9,1},{17,25},{25,17},{2,10},{10... | collective-permute-start | bytes 1327112 | tf_op jit(solution)/shard_map/ppermute | solution.py:443
  36.6 2.2 %collective-permute-start.13 = (bf16[432,128]{1,0:T(8,128)(2,1)S(1)}, bf16[432,128]{1,0:T(8,128)(2,1)S(1)}, u32[]{:S(2)}, u32[]{:S(2)}) collective-permute-start(bf16[432,128]{1,0:T(8,128)(2,1)S(1)} %get-tuple-element.49), channel_id=1, source_target_pairs={{0,8},{8,0},{16,24},{24,16},{1,9},{9,1},{17,25},{25,17},{2,10},{10... | collective-permute-start | bytes 331784 | tf_op jit(solution)/shard_map/ppermute | solution.py:443
  36.8 15.0 %collective-permute-start.11 = (bf16[864,256]{1,0:T(8,128)(2,1)S(1)}, bf16[864,256]{1,0:T(8,128)(2,1)S(1)}, u32[]{:S(2)}, u32[]{:S(2)}) collective-permute-start(bf16[864,256]{1,0:T(8,128)(2,1)S(1)} %add_convert_fusion), channel_id=1, source_target_pairs={{0,16},{8,24},{16,0},{24,8},{1,17},{9,25},{17,1},{25,9},{2,18},{10... | collective-permute-start | bytes 1327112 | tf_op jit(solution)/shard_map/ppermute | solution.py:443
  38.5 1.3 %collective-permute-start.12 = (bf16[432,128]{1,0:T(8,128)(2,1)S(1)}, bf16[432,128]{1,0:T(8,128)(2,1)S(1)}, u32[]{:S(2)}, u32[]{:S(2)}) collective-permute-start(bf16[432,128]{1,0:T(8,128)(2,1)S(1)} %get-tuple-element.47), channel_id=1, source_target_pairs={{0,8},{8,0},{16,24},{24,16},{1,9},{9,1},{17,25},{25,17},{2,10},{10... | collective-permute-start | bytes 331784 | tf_op jit(solution)/shard_map/ppermute | solution.py:443
  38.8 13.0 %collective-permute-start.14 = (bf16[432,128]{1,0:T(8,128)(2,1)S(1)}, bf16[432,128]{1,0:T(8,128)(2,1)S(1)}, u32[]{:S(2)}, u32[]{:S(2)}) collective-permute-start(bf16[432,128]{1,0:T(8,128)(2,1)S(1)} %add_convert_fusion.1), channel_id=1, source_target_pairs={{0,16},{8,24},{16,0},{24,8},{1,17},{9,25},{17,1},{25,9},{2,18},{10... | collective-permute-start | bytes 331784 | tf_op jit(solution)/shard_map/ppermute | solution.py:443
  52.7 8.6 %collective-permute-start.15 = (bf16[272,128]{1,0:T(8,128)(2,1)S(1)}, bf16[272,128]{1,0:T(8,128)(2,1)S(1)}, u32[]{:S(2)}, u32[]{:S(2)}) collective-permute-start(bf16[272,128]{1,0:T(8,128)(2,1)S(1)} %get-tuple-element.51), channel_id=1, source_target_pairs={{0,1},{1,0},{2,3},{3,2},{4,5},{5,4},{6,7},{7,6},{8,9},{9,8},{10,11... | collective-permute-start | bytes 208904 | tf_op jit(solution)/shard_map/ppermute | solution.py:443
  55.4 7.9 %collective-permute-start.16 = (bf16[272,128]{1,0:T(8,128)(2,1)S(1)}, bf16[272,128]{1,0:T(8,128)(2,1)S(1)}, u32[]{:S(2)}, u32[]{:S(2)}) collective-permute-start(bf16[272,128]{1,0:T(8,128)(2,1)S(1)} %get-tuple-element.52), channel_id=1, source_target_pairs={{0,2},{1,3},{2,0},{3,1},{4,6},{5,7},{6,4},{7,5},{8,10},{9,11},{10,... | collective-permute-start | bytes 208904 | tf_op jit(solution)/shard_map/ppermute | solution.py:443
  57.0 10.5 %collective-permute-start.17 = (bf16[272,128]{1,0:T(8,128)(2,1)S(1)}, bf16[272,128]{1,0:T(8,128)(2,1)S(1)}, u32[]{:S(2)}, u32[]{:S(2)}) collective-permute-start(bf16[272,128]{1,0:T(8,128)(2,1)S(1)} %get-tuple-element.53), channel_id=1, source_target_pairs={{0,3},{1,2},{2,1},{3,0},{4,7},{5,6},{6,5},{7,4},{8,11},{9,10},{10,... | collective-permute-start | bytes 208904 | tf_op jit(solution)/shard_map/ppermute | solution.py:443
  57.0 11.7 %collective-permute-start.18 = (bf16[272,128]{1,0:T(8,128)(2,1)S(1)}, bf16[272,128]{1,0:T(8,128)(2,1)S(1)}, u32[]{:S(2)}, u32[]{:S(2)}) collective-permute-start(bf16[272,128]{1,0:T(8,128)(2,1)S(1)} %get-tuple-element.54), channel_id=1, source_target_pairs={{0,4},{1,5},{2,6},{3,7},{4,0},{5,1},{6,2},{7,3},{8,12},{9,13},{10,... | collective-permute-start | bytes 208904 | tf_op jit(solution)/shard_map/ppermute | solution.py:443
  59.6 11.7 %collective-permute-start.19 = (bf16[272,128]{1,0:T(8,128)(2,1)S(1)}, bf16[272,128]{1,0:T(8,128)(2,1)S(1)}, u32[]{:S(2)}, u32[]{:S(2)}) collective-permute-start(bf16[272,128]{1,0:T(8,128)(2,1)S(1)} %get-tuple-element.55), channel_id=1, source_target_pairs={{0,5},{1,4},{2,7},{3,6},{4,1},{5,0},{6,3},{7,2},{8,13},{9,12},{10,... | collective-permute-start | bytes 208904 | tf_op jit(solution)/shard_map/ppermute | solution.py:443
  61.3 9.9 %collective-permute-start.20 = (bf16[272,128]{1,0:T(8,128)(2,1)S(1)}, bf16[272,128]{1,0:T(8,128)(2,1)S(1)}, u32[]{:S(2)}, u32[]{:S(2)}) collective-permute-start(bf16[272,128]{1,0:T(8,128)(2,1)S(1)} %get-tuple-element.56), channel_id=1, source_target_pairs={{0,6},{1,7},{2,4},{3,5},{4,2},{5,3},{6,0},{7,1},{8,14},{9,15},{10,... | collective-permute-start | bytes 208904 | tf_op jit(solution)/shard_map/ppermute | solution.py:443
  63.3 7.9 %collective-permute-start.21 = (bf16[272,128]{1,0:T(8,128)(2,1)S(1)}, bf16[272,128]{1,0:T(8,128)(2,1)S(1)}, u32[]{:S(2)}, u32[]{:S(2)}) collective-permute-start(bf16[272,128]{1,0:T(8,128)(2,1)S(1)} %get-tuple-element.57), channel_id=1, source_target_pairs={{0,7},{1,6},{2,5},{3,4},{4,3},{5,2},{6,1},{7,0},{8,15},{9,14},{10,... | collective-permute-start | bytes 208904 | tf_op jit(solution)/shard_map/ppermute | solution.py:443
  67.4 16.3 %copy-start.2 = (f32[32,2048]{1,0:T(8,128)}, f32[32,2048]{1,0:T(8,128)S(1)}, u32[]{:S(2)}) copy-start(f32[32,2048]{1,0:T(8,128)S(1)} %get-tuple-element.40.last_ref) | copy-start | bytes 786436
  67.5 11.6 %collective-permute-start.8 = (bf16[32,2048]{1,0:T(8,128)(2,1)S(1)}, bf16[32,2048]{1,0:T(8,128)(2,1)S(1)}, u32[]{:S(2)}, u32[]{:S(2)}) collective-permute-start(bf16[32,2048]{1,0:T(8,128)(2,1)S(1)} %get-tuple-element.41), channel_id=1, source_target_pairs={{1,0},{2,1},{3,2},{4,3},{5,4},{6,5},{7,6},{9,8},{10,9},{11,10},{12... | collective-permute-start | bytes 393224 | tf_op jit(solution)/shard_map/ppermute | solution.py:449
  71.3 9.2 %collective-permute-start.28 = (bf16[272,128]{1,0:T(8,128)(2,1)S(1)}, bf16[272,128]{1,0:T(8,128)(2,1)S(1)}, u32[]{:S(2)}, u32[]{:S(2)}) collective-permute-start(bf16[272,128]{1,0:T(8,128)(2,1)S(1)} %add_convert_fusion.2.refs_0_), channel_id=1, source_target_pairs={{0,7},{1,6},{2,5},{3,4},{4,3},{5,2},{6,1},{7,0},{8,15},{9,14},{10,... | collective-permute-start | bytes 208904 | tf_op jit(solution)/shard_map/ppermute | solution.py:443
  74.0 9.7 %collective-permute-start.27 = (bf16[272,128]{1,0:T(8,128)(2,1)S(1)}, bf16[272,128]{1,0:T(8,128)(2,1)S(1)}, u32[]{:S(2)}, u32[]{:S(2)}) collective-permute-start(bf16[272,128]{1,0:T(8,128)(2,1)S(1)} %add_convert_fusion.2.refs_0_), channel_id=1, source_target_pairs={{0,6},{1,7},{2,4},{3,5},{4,2},{5,3},{6,0},{7,1},{8,14},{9,15},{10,... | collective-permute-start | bytes 208904 | tf_op jit(solution)/shard_map/ppermute | solution.py:443
  75.0 11.4 %collective-permute-start.26 = (bf16[272,128]{1,0:T(8,128)(2,1)S(1)}, bf16[272,128]{1,0:T(8,128)(2,1)S(1)}, u32[]{:S(2)}, u32[]{:S(2)}) collective-permute-start(bf16[272,128]{1,0:T(8,128)(2,1)S(1)} %add_convert_fusion.2.refs_0_), channel_id=1, source_target_pairs={{0,5},{1,4},{2,7},{3,6},{4,1},{5,0},{6,3},{7,2},{8,13},{9,12},{10,... | collective-permute-start | bytes 208904 | tf_op jit(solution)/shard_map/ppermute | solution.py:443
  77.6 9.8 %collective-permute-start.25 = (bf16[272,128]{1,0:T(8,128)(2,1)S(1)}, bf16[272,128]{1,0:T(8,128)(2,1)S(1)}, u32[]{:S(2)}, u32[]{:S(2)}) collective-permute-start(bf16[272,128]{1,0:T(8,128)(2,1)S(1)} %add_convert_fusion.2.refs_0_), channel_id=1, source_target_pairs={{0,4},{1,5},{2,6},{3,7},{4,0},{5,1},{6,2},{7,3},{8,12},{9,13},{10,... | collective-permute-start | bytes 208904 | tf_op jit(solution)/shard_map/ppermute | solution.py:443
  79.0 5.7 %copy-start.5 = (bf16[32,2048]{1,0:T(8,128)(2,1)}, bf16[32,2048]{1,0:T(8,128)(2,1)S(1)}, u32[]{:S(2)}) copy-start(bf16[32,2048]{1,0:T(8,128)(2,1)S(1)} %collective-permute-done.8.rim_ref) | copy-start | bytes 393220
  79.0 8.4 %collective-permute-start.24 = (bf16[272,128]{1,0:T(8,128)(2,1)S(1)}, bf16[272,128]{1,0:T(8,128)(2,1)S(1)}, u32[]{:S(2)}, u32[]{:S(2)}) collective-permute-start(bf16[272,128]{1,0:T(8,128)(2,1)S(1)} %add_convert_fusion.2.refs_0_), channel_id=1, source_target_pairs={{0,3},{1,2},{2,1},{3,0},{4,7},{5,6},{6,5},{7,4},{8,11},{9,10},{10,... | collective-permute-start | bytes 208904 | tf_op jit(solution)/shard_map/ppermute | solution.py:443
  80.5 7.6 %collective-permute-start.23 = (bf16[272,128]{1,0:T(8,128)(2,1)S(1)}, bf16[272,128]{1,0:T(8,128)(2,1)S(1)}, u32[]{:S(2)}, u32[]{:S(2)}) collective-permute-start(bf16[272,128]{1,0:T(8,128)(2,1)S(1)} %add_convert_fusion.2.refs_0_), channel_id=1, source_target_pairs={{0,2},{1,3},{2,0},{3,1},{4,6},{5,7},{6,4},{7,5},{8,10},{9,11},{10,... | collective-permute-start | bytes 208904 | tf_op jit(solution)/shard_map/ppermute | solution.py:443
  83.7 4.4 %collective-permute-start.22 = (bf16[272,128]{1,0:T(8,128)(2,1)S(1)}, bf16[272,128]{1,0:T(8,128)(2,1)S(1)}, u32[]{:S(2)}, u32[]{:S(2)}) collective-permute-start(bf16[272,128]{1,0:T(8,128)(2,1)S(1)} %add_convert_fusion.2.refs_0_), channel_id=1, source_target_pairs={{0,1},{1,0},{2,3},{3,2},{4,5},{5,4},{6,7},{7,6},{8,9},{9,8},{10,11... | collective-permute-start | bytes 208904 | tf_op jit(solution)/shard_map/ppermute | solution.py:443
where the time goes:
time: 90 us; the launch traced here: 89.8 us
  starting transfers between devices  40.1 us (45%)
  waiting for transfers between devices  30 us (33%)
  Pallas kernels  16.3 us (18%)
  local copies, waits for them, and re-layouts  2.28 us (3%)
    ppermute x26, starting transfers between devices, swap(): return lax.ppermute(value, axis, [(i, i ^ bits) for i in range(size)])  34.1 us
    ppermute x26, waiting for transfers between devices, swap(): return lax.ppermute(value, axis, [(i, i ^ bits) for i in range(size)])  25.4 us
    pallas_call x8, Pallas kernels, call(): pl.pallas_call(kernel, out_shape=out_shape, in_specs=specs, out_specs=jax...  14.6 us
    ppermute x3, starting transfers between devices, shifted(): return lax.ppermute(value, axis, pairs)  6.02 us
    ppermute x3, waiting for transfers between devices, shifted(): return lax.ppermute(value, axis, pairs)  4.55 us
  transfers between devices with their start and end apart: 29, of which 9 were waited for; matrix products, arithmetic and copies ran while one was open for 1% of the time, Pallas kernels for 12%

commit v1 on v0

v1 whole, which is shorter than its diff:
```python
import functools

import jax
import jax.numpy as jnp
from jax import lax
from jax.experimental import pallas as pl
from jax.experimental.pallas import tpu as pltpu
from jax.sharding import PartitionSpec as P

LEAK_SLOPE = 0.2
F32 = jnp.float32
BF16 = jnp.bfloat16
VMEM_LIMIT = 48 * 1024 * 1024


def activate(values):
    small = jnp.exp(-jnp.abs(values))
    return LEAK_SLOPE * values + (1.0 - LEAK_SLOPE) * (
        jnp.maximum(values, 0.0) + jnp.log(1.0 + small)
    )


def activate_slope(values):
    small = jnp.exp(-jnp.abs(values))
    inverse = 1.0 / (1.0 + small)
    return LEAK_SLOPE + (1.0 - LEAK_SLOPE) * jnp.where(
        values >= 0.0, inverse, small * inverse
    )


def block_row(rows, width):
    return lax.broadcasted_iota(jnp.int32, (rows, width), 0) % 8


def from_before(block):
    moved = pltpu.roll(block, 1, 0)
    return jnp.where(block_row(*block.shape) == 0, 0.0, moved)


def from_after(block):
    moved = pltpu.roll(block, block.shape[0] - 1, 0)
    return jnp.where(block_row(*block.shape) == 7, 0.0, moved)


def call(kernel, out_shape, scratch, *operands, smem=(), micros=1.0):
    nbytes = sum(a.size * a.dtype.itemsize for a in (*operands, *jax.tree.leaves(out_shape)))
    specs = [pl.BlockSpec(memory_space=pltpu.SMEM)] * len(smem)
    specs += [pl.BlockSpec(memory_space=pltpu.VMEM)] * len(operands)
    return pl.pallas_call(
        kernel,
        out_shape=out_shape,
        in_specs=specs,
        out_specs=jax.tree.map(lambda _: pl.BlockSpec(memory_space=pltpu.VMEM), out_shape),
        scratch_shapes=scratch,
        compiler_params=pltpu.CompilerParams(vmem_limit_bytes=VMEM_LIMIT),
        cost_estimate=pl.CostEstimate(
            flops=int(micros * 1.15e9), bytes_accessed=nbytes, transcendentals=0
        ),
    )(*smem, *operands)


def sds(shape, dtype):
    return jax.ShapeDtypeStruct(shape, dtype)


def sort_kernel(planes, in_ref, out_ref, wide):
    pairs = wide.shape[0]
    for plane in range(planes):
        for pair in range(pairs):
            wide[pair] = in_ref[plane, :, pair * 128 : (pair + 1) * 128].astype(F32)
        classes = [
            wide[:, pl.ds(r, 8, stride=4), :].reshape(pairs * 8, 128) for r in range(4)
        ]
        before = from_before(classes[3])
        for tap, (even, odd) in enumerate(
            ((before, classes[1]), (classes[0], classes[2]), (classes[1], classes[3]))
        ):
            both = jnp.concatenate(
                [even.reshape(pairs, 1, 8, 128), odd.reshape(pairs, 1, 8, 128)], axis=1
            )
            out_ref[plane, tap] = both.reshape(pairs * 16, 128).astype(BF16)


def sorted_planes(volume):
    planes, rows, width = volume.shape
    pairs = width // 128
    return call(
        functools.partial(sort_kernel, planes),
        sds((planes, 3, pairs * 16, 128), BF16),
        [pltpu.VMEM((pairs, rows, 128), F32)],
        volume,
    )


def put_rows(dst, pieces, offsets):
    rows = pieces[0].shape[0]
    for index, piece in enumerate(pieces):
        dst[pl.ds(pl.multiple_of(offsets[index], 16), rows), :] = piece[...]


def gather_taps(columns, sorted_ref, halo_ref, first, count, base):
    rows = sorted_ref.shape[2]
    for cell in range(count):
        at = base + cell * rows
        for a in range(3):
            plane = 2 * (first + cell) - 1 + a
            for e in range(3):
                source = halo_ref.at[0, e] if plane < 0 else sorted_ref.at[plane, e]
                left = (a * 3 + e) * 256
                columns[at : at + 16, left : left + 128] = jnp.zeros((16, 128), BF16)
                columns[at + 16 : at + rows, left : left + 128] = source[0 : rows - 16, :]
                columns[at : at + rows, left + 128 : left + 256] = source[...]


def pad_first(whole, padded):
    for tap in range(9):
        padded[tap * 256 : tap * 256 + 64, :] = jnp.zeros((64, 128), BF16)
        padded[tap * 256 + 64 : (tap + 1) * 256, :] = whole[tap * 192 : (tap + 1) * 192, :]


def take_windows(read, dst, out, a, half):
    for e in range(3):
        for f in range(3):
            block = read(0 if f == 1 else 1, 0 if e == 1 else 1)
            if e == 0:
                block = from_before(block)
            if f == 0:
                block = jnp.concatenate(
                    [jnp.zeros((8, 128), F32), block[: half * 8 - 8]], axis=0
                )
            left = ((a * 3 + e) * 3 + f) * 128
            dst[out * half * 8 : (out + 1) * half * 8, left : left + 128] = block.astype(BF16)


def forward_upper_kernel(
    offsets, sorted_ref, w0, w1, w2, w3, slope_ref, hidden_ref, last_ref, columns, whole, padded
):
    cells = sorted_ref.shape[0] // 2
    put_rows(whole, (w0, w1, w2, w3), offsets)
    pad_first(whole, padded)
    gather_taps(columns, sorted_ref, None, 1, cells - 1, 0)
    linear = jnp.dot(columns[...], padded[...], preferred_element_type=F32)
    hidden = activate(linear)
    hidden_ref[...] = hidden.reshape(hidden_ref.shape)
    last_ref[...] = hidden[hidden.shape[0] - last_ref.shape[0] :].astype(BF16)
    slope_ref[...] = activate_slope(linear)


def forward_upper(sorted_volume, shards, offsets):
    planes, _, rows, _ = sorted_volume.shape
    cells = planes // 2
    shard = shards[0].shape[0]
    some = (cells - 1) * rows
    return call(
        forward_upper_kernel,
        (
            sds((some, 128), F32),
            sds((cells - 1, rows // 32, 2, 2, 8, 128), F32),
            sds((rows, 128), BF16),
        ),
        [
            pltpu.VMEM((some, 9 * 256), BF16),
            pltpu.VMEM((4 * shard, 128), BF16),
            pltpu.VMEM((9 * 256, 128), BF16),
        ],
        sorted_volume, *shards,
        smem=(offsets,),
        micros=2.5,
    )


def forward_lower_kernel(
    offsets, sorted_ref, halo_ref, hidden_ref, below_ref, w0, w1, w2, w3,
    slope_ref, windows_ref, sorted_halo, wide, columns, whole, padded, lowest, below,
):
    rows = sorted_ref.shape[2]
    cells = sorted_ref.shape[0] // 2
    half = rows // 32
    sort_kernel(1, halo_ref, sorted_halo, wide)
    put_rows(whole, (w0, w1, w2, w3), offsets)
    pad_first(whole, padded)
    gather_taps(columns, sorted_ref, sorted_halo, 0, 1, 0)
    linear = jnp.dot(columns[...], padded[...], preferred_element_type=F32)
    slope_ref[...] = activate_slope(linear)
    lowest[...] = activate(linear).reshape(lowest.shape)
    below[...] = below_ref[...].astype(F32).reshape(below.shape)
    for out in range(cells // 2):
        for a in range(3):
            plane = 2 * out - 1 + a
            source = (below, lowest)[plane + 1] if plane < 1 else hidden_ref.at[plane - 1]

            def read(column, row):
                return source[:, column, row].reshape(half * 8, 128)

            take_windows(read, windows_ref, out, a, half)


def forward_lower(sorted_volume, halo, hidden, below, shards, offsets):
    planes, _, rows, _ = sorted_volume.shape
    cells = planes // 2
    shard = shards[0].shape[0]
    return call(
        forward_lower_kernel,
        (sds((rows, 128), F32), sds((cells * rows // 8, 27 * 128), BF16)),
        [
            pltpu.VMEM((1, 3, rows, 128), BF16),
            pltpu.VMEM((rows // 16, halo.shape[1], 128), F32),
            pltpu.VMEM((rows, 9 * 256), BF16),
            pltpu.VMEM((4 * shard, 128), BF16),
            pltpu.VMEM((9 * 256, 128), BF16),
            pltpu.VMEM(hidden.shape[1:], F32),
            pltpu.VMEM(hidden.shape[1:], F32),
        ],
        sorted_volume, halo, hidden, below, *shards,
        smem=(offsets,),
        micros=1.5,
    )


def put_pieces(flat, outs, slots, order):
    for index, out in enumerate(outs):
        count, size, _ = out.shape
        for place in range(count):
            row = pl.multiple_of(order[place] * size, 16)
            out[place] = flat[slots[index], pl.ds(row, size), :]


def forward_second_kernel(
    offsets, slots, order, windows_ref, cot_ref, w0, w1, w2, w3,
    act_ref, delta_ref, lowest_ref, g0, g1, g2, g3, whole, flat,
):
    put_rows(whole, (w0, w1, w2, w3), offsets)
    linear = jnp.dot(windows_ref[...], whole[...], preferred_element_type=F32)
    outs, _, width = cot_ref.shape
    features = linear.shape[1]
    count = width // features
    acted = activate(linear)
    slope = activate_slope(linear)
    deltas = []
    for out in range(outs):
        base = out * count * 8
        act_ref[out] = jnp.concatenate(
            [acted[base + q * 8 : base + (q + 1) * 8] for q in range(count)], axis=1
        ).astype(BF16)
        cot = cot_ref[out].astype(F32)
        deltas.append(
            jnp.concatenate(
                [cot[:, q * features : (q + 1) * features] for q in range(count)], axis=0
            )
        )
    delta = (jnp.concatenate(deltas, axis=0) * slope).astype(BF16)
    delta_ref[...] = delta
    lowest_ref[...] = delta[: count * 8]
    total = lax.dot_general(
        windows_ref[...], delta, (((0,), (0,)), ((), ())), preferred_element_type=F32
    ).astype(BF16)
    rows = w0.shape[0]
    lanes = features // 128
    for shard in range(4):
        for lane in range(lanes):
            flat[shard, lane * rows : (lane + 1) * rows, :] = total[
                shard * rows : (shard + 1) * rows, lane * 128 : (lane + 1) * 128
            ]
        rest = flat.shape[1] - lanes * rows
        if rest:
            flat[shard, lanes * rows :, :] = jnp.zeros((rest, 128), BF16)
    put_pieces(flat, (g0, g1, g2, g3), slots, order)


def forward_second(windows, cot, shards, offsets, slots, order, places, size):
    rows, features = shards[0].shape
    piece = sds((places, size, 128), BF16)
    return call(
        forward_second_kernel,
        (
            sds(cot.shape, BF16),
            sds((windows.shape[0], features), BF16),
            sds((windows.shape[0] // cot.shape[0], features), BF16),
            piece, piece, piece, piece,
        ),
        [
            pltpu.VMEM((4 * rows, features), BF16),
            pltpu.VMEM((4, places * size, 128), BF16),
        ],
        windows, cot, *shards,
        smem=(offsets, slots, order),
        micros=3.0,
    )


def back_second_kernel(
    offsets, slots, order, delta_ref, upper_ref, w0, w1, w2, w3,
    slope_low_ref, slope_ref, sorted_ref, halo_ref,
    out_ref, lowest_ref, g0, g1, g2, g3,
    whole, product, above, sorted_halo, wide, columns, flat,
):
    rows = sorted_ref.shape[2]
    cells = sorted_ref.shape[0] // 2
    half = rows // 32
    size = half * 8
    put_rows(whole, (w0, w1, w2, w3), offsets)
    product[...] = lax.dot_general(
        delta_ref[...], whole[...], (((1,), (1,)), ((), ())), preferred_element_type=F32
    )
    above[...] = lax.dot_general(
        upper_ref[...], whole[: 9 * 128, :], (((1,), (1,)), ((), ())), preferred_element_type=F32
    )
    sort_kernel(1, halo_ref, sorted_halo, wide)
    gather_taps(columns, sorted_ref, sorted_halo, 0, cells, 0)

    def term(out, a, e, f):
        left = ((a * 3 + e) * 3 + f) * 128
        if out == cells // 2:
            block = above[:, left : left + 128]
        else:
            block = product[out * size : (out + 1) * size, left : left + 128]
        if f == 0:
            block = jnp.concatenate([block[8:], jnp.zeros((8, 128), F32)], axis=0)
        if e == 0:
            block = from_after(block)
        return block.reshape(half, 8, 128)

    for plane in range(cells):
        taps = [
            (out, a) for out in range(cells // 2 + 1) for a in range(3) if 2 * out - 1 + a == plane
        ]
        sums = [
            sum(
                term(out, a, e, f)
                for out, a in taps
                for e in ((0, 2) if row else (1,))
                for f in ((0, 2) if column else (1,))
            ).reshape(half, 1, 8, 128)
            for column in range(2)
            for row in range(2)
        ]
        spread = jnp.concatenate(sums, axis=1).reshape(rows, 128)
        slope = slope_low_ref[...] if plane == 0 else slope_ref[(plane - 1) * rows : plane * rows, :]
        delta = (spread * slope).astype(BF16)
        out_ref[plane * rows : (plane + 1) * rows, :] = delta
        if plane == 0:
            lowest_ref[...] = delta
    flipped = jnp.transpose(out_ref[...].astype(F32)).astype(BF16)
    tally = jnp.dot(flipped, columns[...], preferred_element_type=F32)
    shard_rows = 9 * 192 // 4
    for tap in range(9):
        turned = jnp.transpose(tally[:, tap * 256 : (tap + 1) * 256])[64:].astype(BF16)
        at = tap * 192
        while at < (tap + 1) * 192:
            shard = at // shard_rows
            to = min((tap + 1) * 192, (shard + 1) * shard_rows)
            flat[shard, at - shard * shard_rows : to - shard * shard_rows, :] = turned[
                at - tap * 192 : to - tap * 192
            ]
            at = to
    rest = flat.shape[1] - shard_rows
    if rest:
        flat[:, shard_rows:, :] = jnp.zeros((4, rest, 128), BF16)
    put_pieces(flat, (g0, g1, g2, g3), slots, order)


def back_second(
    delta, upper, shards, slopes, sorted_volume, halo, offsets, slots, order, places, size
):
    rows, features = shards[0].shape
    planes, _, width, _ = sorted_volume.shape
    cells = planes // 2
    piece = sds((places, size, 128), BF16)
    return call(
        back_second_kernel,
        (sds((cells * width, 128), BF16), sds((width, 128), BF16), piece, piece, piece, piece),
        [
            pltpu.VMEM((4 * rows, features), BF16),
            pltpu.VMEM((delta.shape[0], 4 * rows), F32),
            pltpu.VMEM((upper.shape[0], 9 * 128), F32),
            pltpu.VMEM((1, 3, width, 128), BF16),
            pltpu.VMEM((width // 16, halo.shape[1], 128), F32),
            pltpu.VMEM((cells * width, 9 * 256), BF16),
            pltpu.VMEM((4, places * size, 128), BF16),
        ],
        delta, upper, *shards, *slopes, sorted_volume, halo,
        smem=(offsets, slots, order),
        micros=3.5,
    )


def back_input_kernel(
    offsets, delta_ref, upper_ref, w0, w1, w2, w3, out_ref, whole, turned, pairs, product, wide
):
    put_rows(whole, (w0, w1, w2, w3), offsets)
    for tap in range(9):
        top = tap * 128
        turned[top : top + 128, 0:128] = whole[tap * 192 + 64 : (tap + 1) * 192, :]
        turned[top : top + 64, 128:256] = jnp.zeros((64, 128), BF16)
        turned[top + 64 : top + 128, 128:256] = whole[tap * 192 : tap * 192 + 64, :]
    planes = out_ref.shape[0]
    cells = planes // 2
    rows = upper_ref.shape[0]
    groups = rows // 16
    for cell in range(cells + 1):
        at = cell * rows
        source = upper_ref if cell == cells else delta_ref.at[at : at + rows]
        pairs[at : at + rows, 0:128] = source[...]
        pairs[at : at + rows - 16, 128:256] = source[16:rows, :]
        pairs[at + rows - 16 : at + rows, 128:256] = jnp.zeros((16, 128), BF16)
    product[...] = lax.dot_general(
        pairs[...], turned[...], (((1,), (1,)), ((), ())), preferred_element_type=F32
    ).reshape(product.shape)

    def part(cell, a, e, parity):
        left = (a * 3 + e) * 128
        return product[cell * groups : (cell + 1) * groups, parity, :, left : left + 128]

    def after(block):
        flat = block.reshape(groups * 8, 128)
        return from_after(flat).reshape(groups, 8, 128)

    for plane in range(planes):
        taps = [(o, a) for o in range(cells + 1) for a in range(3) if 2 * o - 1 + a == plane]
        wide[:, pl.ds(0, 8, stride=4), :] = sum(part(o, a, 1, 0) for o, a in taps)
        wide[:, pl.ds(1, 8, stride=4), :] = sum(
            part(o, a, 2, 0) + part(o, a, 0, 1) for o, a in taps
        )
        wide[:, pl.ds(2, 8, stride=4), :] = sum(part(o, a, 1, 1) for o, a in taps)
        wide[:, pl.ds(3, 8, stride=4), :] = sum(part(o, a, 2, 1) for o, a in taps) + after(
            sum(part(o, a, 0, 0) for o, a in taps)
        )
        for group in range(groups):
            lanes = slice(group * 128, (group + 1) * 128)
            out_ref[plane, :, lanes] = wide[group].astype(BF16)


def back_input(delta, upper, shards, offsets, shape):
    planes, side, width = shape
    shard = shards[0].shape[0]
    rows = delta.shape[0] + upper.shape[0]
    return call(
        back_input_kernel,
        sds(shape, BF16),
        [
            pltpu.VMEM((4 * shard, 128), BF16),
            pltpu.VMEM((9 * 128, 256), BF16),
            pltpu.VMEM((rows, 256), BF16),
            pltpu.VMEM((rows // 16, 2, 8, 9 * 128), F32),
            pltpu.VMEM((width // 128, side, 128), F32),
        ],
        delta, upper, *shards,
        smem=(offsets,),
        micros=3.0,
    )


def unpack_kernel(scale_first, scale_second, order, *refs):
    *chunks, first_ref, second_ref, flat_first, flat_second = refs
    high = len(chunks)
    places = 2 * high
    small = flat_first.shape[0] // places
    big = flat_second.shape[0] // (2 * places)
    for index, chunk in enumerate(chunks):
        for low in range(2):
            place = order[low * high + index]
            for part in range(2):
                row = pl.multiple_of((part * places + place) * big, 16)
                flat_second[pl.ds(row, big), :] = chunk[low, part * big : (part + 1) * big, :]
            row = pl.multiple_of(place * small, 16)
            flat_first[pl.ds(row, small), :] = chunk[low, 2 * big :, :]
    rows, features = second_ref.shape
    for lane in range(features // 128):
        second_ref[:, lane * 128 : (lane + 1) * 128] = (
            flat_second[lane * rows : (lane + 1) * rows, :].astype(F32) * scale_second
        )
    first_ref[...] = flat_first[: first_ref.shape[0], :].astype(F32) * scale_first


def added(*pieces):
    return sum(piece.astype(F32) for piece in pieces).astype(BF16)


def swap(value, axis, bits):
    size = lax.axis_size(axis)
    return lax.ppermute(value, axis, [(i, i ^ bits) for i in range(size)])


def shifted(value, axis, by):
    size = lax.axis_size(axis)
    pairs = [(i, i + by) for i in range(size) if 0 <= i + by < size]
    return lax.ppermute(value, axis, pairs)


def local(volume, weight_first, weight_second, cotangent):
    samples, planes, side, width = volume.shape
    data = lax.axis_index("dp")
    place = lax.axis_index("space")
    spaces = lax.axis_size("space")
    high = spaces // 2
    small, big = weight_first.shape[0], weight_second.shape[0]
    slots = jnp.arange(4, dtype=jnp.int32) ^ data
    offsets_first = slots * small
    offsets_second = slots * big
    steps = jnp.arange(spaces, dtype=jnp.int32)
    order = place ^ (2 * (steps % high) + steps // high)
    order_second = jnp.concatenate([order, spaces + order])
    lanes = weight_second.shape[1] // 128
    size_first = -(-small // (16 * spaces)) * 16
    size_second = -(-lanes * big // (32 * spaces)) * 16

    inputs = volume.reshape(planes, side, width)
    first_x = swap(weight_first, "dp", 2)
    first_core = swap(weight_first, "dp", 1)
    second_x = swap(weight_second, "dp", 2)
    second_core = swap(weight_second, "dp", 1)
    halo = shifted(inputs[planes - 1 :], "space", 1)
    first_far = swap(first_x, "dp", 1)
    shards_first = (weight_first, first_core, first_x, first_far)

    sorted_volume = sorted_planes(inputs)
    slope, hidden, last_hidden = forward_upper(sorted_volume, shards_first, offsets_first)
    hidden_halo = shifted(last_hidden, "space", 1)
    second_x, hidden = lax.optimization_barrier((second_x, hidden))
    slope_low, windows = forward_lower(
        sorted_volume, halo, hidden, hidden_halo, shards_first, offsets_first
    )
    second_far = swap(second_x, "dp", 1)
    shards_second = (weight_second, second_core, second_x, second_far)
    cot = cotangent.reshape(cotangent.shape[1:])
    activations, delta_second, lowest_second, *second = forward_second(
        windows, cot, shards_second, offsets_second, slots, order_second,
        2 * spaces, size_second,
    )
    far = swap(second[3], "dp", 1).reshape(2, 2, high, size_second, 128)
    near = swap(second[1], "dp", 1).reshape(2, 2, high, size_second, 128)
    own = second[0].reshape(2, 2, high, size_second, 128)
    there = second[2].reshape(2, 2, high, size_second, 128)
    upper_second = shifted(lowest_second, "space", -1)
    send_a = added(there[0], far[0])
    send_b = jnp.stack([added(own[1, 1], near[1, 1]), added(there[1, 1], far[1, 1])])
    got_a = swap(send_a, "dp", 2)
    got_b = swap(send_b, "space", 1)
    upper_second, _, _ = lax.optimization_barrier((upper_second, send_a, send_b))

    delta_first, lowest_first, *first = back_second(
        delta_second, upper_second, shards_second, (slope_low, slope), sorted_volume, halo,
        offsets_second, slots, order, spaces, size_first,
    )
    upper_first = shifted(lowest_first, "space", -1)
    far_first = swap(first[3], "dp", 1).reshape(2, high, size_first, 128)
    near_first = swap(first[1], "dp", 1).reshape(2, high, size_first, 128)
    own_first = first[0].reshape(2, high, size_first, 128)
    there_first = first[2].reshape(2, high, size_first, 128)

    send_y = jnp.concatenate(
        [added(own[0, 1], near[0, 1], got_a[1]), added(own_first[1], near_first[1])], axis=1
    )
    send_x = jnp.concatenate(
        [added(there[1, 0], far[1, 0], got_b[1]), added(there_first[0], far_first[0])], axis=1
    )
    got_y = swap(send_y, "space", 1)
    got_x = swap(send_x, "dp", 2)
    pairs = []
    for d in range(4):
        for s in range(spaces):
            pairs.append((d * spaces + s, (d ^ 2) * spaces + (s ^ 1)))
    got_xy = lax.ppermute(added(there_first[1], far_first[1]), ("dp", "space"), pairs)
    held = jnp.concatenate(
        [
            added(own[0, 0], near[0, 0], got_a[0], got_y[:, :size_second]),
            added(own[1, 0], near[1, 0], got_b[0], got_x[:, :size_second]),
            added(
                own_first[0], near_first[0], got_y[:, size_second:], got_x[:, size_second:], got_xy
            ),
        ],
        axis=1,
    )
    held, upper_first = lax.optimization_barrier((held, upper_first))
    mine = added(held[0], *(swap(held[k], "space", 2 * k) for k in range(1, high)))
    both = jnp.stack([mine, swap(mine, "space", 1)])
    chunks = [both] + [swap(both, "space", 2 * k) for k in range(1, high)]

    gradient = back_input(delta_first, upper_first, shards_first, offsets_first, inputs.shape)

    cells_first = samples * lax.axis_size("dp") * (planes // 2) * spaces * (side // 2) ** 2
    cells_second = cells_first // 8
    first_gradient, second_gradient = call(
        functools.partial(unpack_kernel, float(cells_first) ** -0.5, float(cells_second) ** -0.5),
        (sds(weight_first.shape, F32), sds(weight_second.shape, F32)),
        [
            pltpu.VMEM((spaces * size_first, 128), BF16),
            pltpu.VMEM((2 * spaces * size_second, 128), BF16),
        ],
        *chunks,
        smem=(order,),
    )
    return (
        activations.reshape(cotangent.shape),
        gradient.reshape(volume.shape),
        first_gradient,
        second_gradient,
    )


def solution(mesh):
    return jax.shard_map(
        local,
        mesh=mesh,
        in_specs=(
            P("dp", "space", None, None),
            P("dp", None),
            P("dp", None),
            P("dp", "space", None, None),
        ),
        out_specs=(
            P("dp", "space", None, None),
            P("dp", "space", None, None),
            P("dp", None),
            P("dp", None),
        ),
        check_vma=False,
    )
```

time: 90 us -> 84.7 us (0.941)
  starting transfers between devices: 40.1 us -> 35.3 us
  Pallas kernels: 16.3 us -> 13.7 us
  waiting for transfers between devices: 30 us -> 31.8 us
    ppermute x26 -> x21, starting transfers between devices: 34.1 us -> 22.5 us  [swap(): return lax.ppermute(value, axis, [(i, i ^ bits) for i in range(size)])]
    ppermute x3 -> x4, starting transfers between devices: 6.02 us -> 10 us  [shifted(): return lax.ppermute(value, axis, pairs)]
    ppermute x0 -> x1, starting transfers between devices: none -> 2.68 us  [local(): lax.ppermute(added(there_first[1], far_first[1]), ('dp', 'space'), pairs)]
    ppermute x3 -> x4, waiting for transfers between devices: 4.55 us -> 6.45 us  [shifted(): return lax.ppermute(value, axis, pairs)]
    pallas_call x1 -> x0, Pallas kernels: 1.66 us -> none  [close_input(): pl.pallas_call(close_kernel, grid=(1,), out_shape=sds(whole.shape, BF16),...]
    ppermute x26 -> x21, waiting for transfers between devices: 25.4 us -> 24.4 us  [swap(): return lax.ppermute(value, axis, [(i, i ^ bits) for i in range(size)])]
    pallas_call x8 -> x7, Pallas kernels: 14.6 us -> 13.7 us  [call(): pl.pallas_call(kernel, out_shape=out_shape, in_specs=specs, out_specs=jax...]
  transfers between devices with their start and end apart: 29 -> 26, of which waited for: 9 -> 15; matrix products, arithmetic and copies ran while one was open for 1% -> 2% of each run, Pallas kernels for 12% -> 7%
where the time goes in v1:
time: 84.7 us; the launch traced here: 84.5 us
  starting transfers between devices  35.3 us (42%)
  waiting for transfers between devices  31.8 us (38%)
  Pallas kernels  13.7 us (16%)
  local copies, waits for them, and re-layouts  2.16 us (3%)
  between operations  0.86 us (1%)
    ppermute x21, waiting for transfers between devices, swap(): return lax.ppermute(value, axis, [(i, i ^ bits) for i in range(size)])  24.4 us
    ppermute x21, starting transfers between devices, swap(): return lax.ppermute(value, axis, [(i, i ^ bits) for i in range(size)])  22.5 us
    pallas_call x7, Pallas kernels, call(): pl.pallas_call(kernel, out_shape=out_shape, in_specs=specs, out_specs=jax...  13.7 us
    ppermute x4, starting transfers between devices, shifted(): return lax.ppermute(value, axis, pairs)  10 us
    ppermute x4, waiting for transfers between devices, shifted(): return lax.ppermute(value, axis, pairs)  6.45 us
    ppermute x1, starting transfers between devices, local(): lax.ppermute(added(there_first[1], far_first[1]), ('dp', 'space'), pairs)  2.68 us
  transfers between devices with their start and end apart: 26, of which 15 were waited for; matrix products, arithmetic and copies ran while one was open for 2% of the time, Pallas kernels for 7%

profile of v1, /device:TPU:0, one launch (start us, length us, event | category | flops | bytes accessed | tf_op | source)
XLA Modules:
  0.0 84.5 jit_solution(1109633813970112057)
XLA Ops:
  0.6 0.5 collective-permute-start.2
  1.1 2.6 %collective-permute-start.3 = (bf16[432,128]{1,0:T(8,128)(2,1)}, bf16[432,128]{1,0:T(8,128)(2,1)S(1)}, u32[]{:S(2)}, u32[]{:S(2)}) collective-permute-start(bf16[432,128]{1,0:T(8,128)(2,1)} %w0.9), channel_id=1, source_target_pairs={{0,16},{8,24},{16,0},{24,8},{1,17},{9,25},{17,1},{25,9},{2,18},{10... | collective-permute-start | bytes 331784 | tf_op jit(solution)/shard_map/ppermute | solution.py:481
  3.7 0.1 collective-permute-start.1
  3.8 0.1 collective-permute-start.6
  3.9 0.9 %slice_bitcast_fusion = bf16[1,32,2048]{2,1,0:T(8,128)(2,1)S(1)} fusion(bf16[1,8,32,2048]{3,2,1,0:T(8,128)(2,1)} %param.4), kind=kLoop, calls=%fused_computation.26 | loop fusion | bytes 262144 | tf_op jit(solution)/shard_map/slice | solution.py:512
  4.8 3.8 %collective-permute-start = (bf16[1,32,2048]{2,1,0:T(8,128)(2,1)S(1)}, bf16[1,32,2048]{2,1,0:T(8,128)(2,1)S(1)}, u32[]{:S(2)}, u32[]{:S(2)}) collective-permute-start(bf16[1,32,2048]{2,1,0:T(8,128)(2,1)S(1)} %slice_bitcast_fusion), channel_id=1, source_target_pairs={{0,1},{1,2},{2,3},{3,4},{4,5},{5,6},{6,7},{8,9},{9,10},{10,11},{11... | collective-permute-start | bytes 393224 | tf_op jit(solution)/shard_map/ppermute | solution.py:487
  8.6 1.2 %copy-done = bf16[1,8,32,2048]{3,2,1,0:T(8,128)(2,1)S(1)} copy-done((bf16[1,8,32,2048]{3,2,1,0:T(8,128)(2,1)S(1)}, bf16[1,8,32,2048]{3,2,1,0:T(8,128)(2,1)}, u32[]{:S(2)}) %copy-start) | copy-done | bytes 1048600
  9.8 0.3 shard_map.75.sorted_ref
  10.2 0.3 collective-permute-start.4
  10.5 1.1 %collective-permute-done.4.w3 = bf16[432,128]{1,0:T(8,128)(2,1)S(1)} collective-permute-done((bf16[432,128]{1,0:T(8,128)(2,1)S(1)}, bf16[432,128]{1,0:T(8,128)(2,1)S(1)}, u32[]{:S(2)}, u32[]{:S(2)}) %collective-permute-start.4) | collective-permute-done | bytes 110624 | tf_op jit(solution)/shard_map/ppermute | solution.py:481
  11.6 1.8 %shard_map.76 = (f32[768,128]{1,0:T(8,128)S(1)}, f32[3,8,2,2,8,128]{5,4,3,2,1,0:T(8,128)S(1)}, bf16[256,128]{1,0:T(8,128)(2,1)S(1)}) custom-call(s32[4]{0:T(128)S(1)} %broadcast_multiply_fusion.offsets, bf16[8,3,256,128]{3,2,1,0:T(8,128)(2,1)S(1)} %shard_map.75.sorted_ref, bf16[432,128]{1,0:T(8,128)(2,1)S(1)} %copy-done.2, ...), custom_call_target="tpu_custom_call" | custom-call | flops 2875000064 | bytes 2867200 | tf_op jit(solution)/shard_map/pallas_call | solution.py:49
  13.4 3.6 %collective-permute-done.1.w2 = bf16[864,256]{1,0:T(8,128)(2,1)S(1)} collective-permute-done((bf16[864,256]{1,0:T(8,128)(2,1)}, bf16[864,256]{1,0:T(8,128)(2,1)S(1)}, u32[]{:S(2)}, u32[]{:S(2)}) %collective-permute-start.1) | collective-permute-done | bytes 442400 | tf_op jit(solution)/shard_map/ppermute | solution.py:481
  17.1 3.7 %collective-permute-start.5 = (bf16[256,128]{1,0:T(8,128)(2,1)S(1)}, bf16[256,128]{1,0:T(8,128)(2,1)S(1)}, u32[]{:S(2)}, u32[]{:S(2)}) collective-permute-start(bf16[256,128]{1,0:T(8,128)(2,1)S(1)} %get-tuple-element.31), channel_id=1, source_target_pairs={{0,1},{1,2},{2,3},{3,4},{4,5},{5,6},{6,7},{8,9},{9,10},{10,11},{11... | collective-permute-start | bytes 196616 | tf_op jit(solution)/shard_map/ppermute | solution.py:487
  20.8 0.1 pad_add_fusion.order
  20.9 1.9 %collective-permute-done.5.below_ref = bf16[256,128]{1,0:T(8,128)(2,1)S(1)} collective-permute-done((bf16[256,128]{1,0:T(8,128)(2,1)S(1)}, bf16[256,128]{1,0:T(8,128)(2,1)S(1)}, u32[]{:S(2)}, u32[]{:S(2)}) %collective-permute-start.5) | collective-permute-done | bytes 65568 | tf_op jit(solution)/shard_map/ppermute | solution.py:487
  22.8 1.3 %shard_map.77 = (f32[256,128]{1,0:T(8,128)S(1)}, bf16[128,3456]{1,0:T(8,128)(2,1)S(1)}) custom-call(s32[4]{0:T(128)S(1)} %broadcast_multiply_fusion.offsets, bf16[8,3,256,128]{3,2,1,0:T(8,128)(2,1)S(1)} %shard_map.75.sorted_ref, bf16[1,32,2048]{2,1,0:T(8,128)(2,1)S(1)} %collective-permute-done.halo_ref, ...), custom_call_target="tpu_custom_call" | custom-call | flops 1724999936 | bytes 3620864 | tf_op jit(solution)/shard_map/pallas_call | solution.py:49
  24.1 3.0 %shard_map.78 = (bf16[2,8,2048]{2,1,0:T(8,128)(2,1)}, bf16[128,256]{1,0:T(8,128)(2,1)S(1)}, bf16[64,256]{1,0:T(8,128)(2,1)S(1)}, bf16[16,112,128]{2,1,0:T(8,128)...) custom-call(s32[4]{0:T(128)S(1)} %get-tuple-element.62.offsets, ...), custom_call_target="tpu_custom_call" | custom-call | flops 3449999872 | bytes 4718592 | tf_op jit(solution)/shard_map/pallas_call | solution.py:49
  27.1 0.5 collective-permute-start.10
  27.6 1.3 %collective-permute-start.8 = (bf16[64,256]{1,0:T(8,128)(2,1)S(1)}, bf16[64,256]{1,0:T(8,128)(2,1)S(1)}, u32[]{:S(2)}, u32[]{:S(2)}) collective-permute-start(bf16[64,256]{1,0:T(8,128)(2,1)S(1)} %get-tuple-element.36), channel_id=1, source_target_pairs={{1,0},{2,1},{3,2},{4,3},{5,4},{6,5},{7,6},{9,8},{10,9},{11,10},{12... | collective-permute-start | bytes 98312 | tf_op jit(solution)/shard_map/ppermute | solution.py:487
  28.9 0.6 collective-permute-done.10
  29.7 4.2 %collective-permute-done.8.upper_ref = bf16[64,256]{1,0:T(8,128)(2,1)S(1)} collective-permute-done((bf16[64,256]{1,0:T(8,128)(2,1)S(1)}, bf16[64,256]{1,0:T(8,128)(2,1)S(1)}, u32[]{:S(2)}, u32[]{:S(2)}) %collective-permute-start.8) | collective-permute-done | bytes 32800 | tf_op jit(solution)/shard_map/ppermute | solution.py:487
  33.8 2.9 %shard_map.79 = (bf16[1024,128]{1,0:T(8,128)(2,1)S(1)}, bf16[256,128]{1,0:T(8,128)(2,1)S(1)}, bf16[8,64,128]{2,1,0:T(8,128)(2,1)S(1)}, bf16[8,64,128]{2,1,0:T(8,...) custom-call(s32[4]{0:T(128)S(1)} %get-tuple-element.62.offsets, ...), custom_call_target="tpu_custom_call" | custom-call | flops 4024999936 | bytes 4947968 | tf_op jit(solution)/shard_map/pallas_call | solution.py:49
  36.7 0.1 collective-permute-start.15
  36.8 3.0 %collective-permute-start.14 = (bf16[2,4,112,128]{3,2,1,0:T(8,128)(2,1)S(1)}, bf16[2,4,112,128]{3,2,1,0:T(8,128)(2,1)S(1)}, u32[]{:S(2)}, u32[]{:S(2)}) collective-permute-start(bf16[2,4,112,128]{3,2,1,0:T(8,128)(2,1)S(1)} %pad_maximum_fusion.1), channel_id=1, source_target_pairs={{0,1},{1,0},{2,3},{3,2},{4,5},{5,4},{6,7},{7,6},{8,9},{9,8},{10,11... | collective-permute-start | bytes 688136 | tf_op jit(solution)/shard_map/ppermute | solution.py:481
  39.8 1.5 %collective-permute-start.11 = (bf16[2,4,112,128]{3,2,1,0:T(8,128)(2,1)S(1)}, bf16[2,4,112,128]{3,2,1,0:T(8,128)(2,1)S(1)}, u32[]{:S(2)}, u32[]{:S(2)}) collective-permute-start(bf16[2,4,112,128]{3,2,1,0:T(8,128)(2,1)S(1)} %bitcast.67), channel_id=1, source_target_pairs={{0,16},{8,24},{16,0},{24,8},{1,17},{9,25},{17,1},{25,9},{2,18},{10... | collective-permute-start | bytes 688136 | tf_op jit(solution)/shard_map/ppermute | solution.py:481
  41.3 1.3 %collective-permute-done.12 = bf16[8,64,128]{2,1,0:T(8,128)(2,1)S(1)} collective-permute-done((bf16[8,64,128]{2,1,0:T(8,128)(2,1)S(1)}, bf16[8,64,128]{2,1,0:T(8,128)(2,1)S(1)}, u32[]{:S(2)}, u32[]{:S(2)}) %collective-permute-start.12) | collective-permute-done | bytes 131104 | tf_op jit(solution)/shard_map/ppermute | solution.py:481
  42.7 3.3 %collective-permute-done.14 = bf16[2,4,112,128]{3,2,1,0:T(8,128)(2,1)S(1)} collective-permute-done((bf16[2,4,112,128]{3,2,1,0:T(8,128)(2,1)S(1)}, bf16[2,4,112,128]{3,2,1,0:T(8,128)(2,1)S(1)}, u32[]{:S(2)}, u32[]{:S(2)}) %collective-permute-start.14) | collective-permute-done | bytes 229408 | tf_op jit(solution)/shard_map/ppermute | solution.py:481
  46.1 1.6 %collective-permute-start.16 = (bf16[4,176,128]{2,1,0:T(8,128)(2,1)S(1)}, bf16[4,176,128]{2,1,0:T(8,128)(2,1)S(1)}, u32[]{:S(2)}, u32[]{:S(2)}) collective-permute-start(bf16[4,176,128]{2,1,0:T(8,128)(2,1)S(1)} %pad_maximum_fusion.3), channel_id=1, source_target_pairs={{0,16},{8,24},{16,0},{24,8},{1,17},{9,25},{17,1},{25,9},{2,18},{10... | collective-permute-start | bytes 540680 | tf_op jit(solution)/shard_map/ppermute | solution.py:481
  47.7 1.8 %collective-permute-start.13 = (bf16[4,176,128]{2,1,0:T(8,128)(2,1)S(1)}, bf16[4,176,128]{2,1,0:T(8,128)(2,1)S(1)}, u32[]{:S(2)}, u32[]{:S(2)}) collective-permute-start(bf16[4,176,128]{2,1,0:T(8,128)(2,1)S(1)} %pad_maximum_fusion.2), channel_id=1, source_target_pairs={{0,1},{1,0},{2,3},{3,2},{4,5},{5,4},{6,7},{7,6},{8,9},{9,8},{10,11... | collective-permute-start | bytes 540680 | tf_op jit(solution)/shard_map/ppermute | solution.py:481
  49.5 1.3 %collective-permute-start.18 = (bf16[256,128]{1,0:T(8,128)(2,1)S(1)}, bf16[256,128]{1,0:T(8,128)(2,1)S(1)}, u32[]{:S(2)}, u32[]{:S(2)}) collective-permute-start(bf16[256,128]{1,0:T(8,128)(2,1)S(1)} %get-tuple-element.49), channel_id=1, source_target_pairs={{1,0},{2,1},{3,2},{4,3},{5,4},{6,5},{7,6},{9,8},{10,9},{11,10},{12... | collective-permute-start | bytes 196616 | tf_op jit(solution)/shard_map/ppermute | solution.py:487
  50.8 2.7 %collective-permute-start.17 = (bf16[4,64,128]{2,1,0:T(8,128)(2,1)S(1)}, bf16[4,64,128]{2,1,0:T(8,128)(2,1)S(1)}, u32[]{:S(2)}, u32[]{:S(2)}) collective-permute-start(bf16[4,64,128]{2,1,0:T(8,128)(2,1)S(1)} %get-tuple-element.60), channel_id=1, source_target_pairs={{0,17},{1,16},{2,19},{3,18},{4,21},{5,20},{6,23},{7,22},{8,25},{9,... | collective-permute-start | bytes 196616 | tf_op jit(solution)/shard_map/ppermute | solution.py:563
  53.5 1.6 %collective-permute-done.13 = bf16[4,176,128]{2,1,0:T(8,128)(2,1)S(1)} collective-permute-done((bf16[4,176,128]{2,1,0:T(8,128)(2,1)S(1)}, bf16[4,176,128]{2,1,0:T(8,128)(2,1)S(1)}, u32[]{:S(2)}, u32[]{:S(2)}) %collective-permute-start.13) | collective-permute-done | bytes 180256 | tf_op jit(solution)/shard_map/ppermute | solution.py:481
  55.1 0.1 fusion.5
  55.2 0.9 %collective-permute-done.17 = bf16[4,64,128]{2,1,0:T(8,128)(2,1)S(1)} collective-permute-done((bf16[4,64,128]{2,1,0:T(8,128)(2,1)S(1)}, bf16[4,64,128]{2,1,0:T(8,128)(2,1)S(1)}, u32[]{:S(2)}, u32[]{:S(2)}) %collective-permute-start.17) | collective-permute-done | bytes 65568 | tf_op jit(solution)/shard_map/ppermute | solution.py:563
  56.2 0.4 collective-permute-done.18.upper_ref
  56.6 4.2 %collective-permute-start.21 = (bf16[288,128]{1,0:T(8,128)(2,1)S(1)}, bf16[288,128]{1,0:T(8,128)(2,1)S(1)}, u32[]{:S(2)}, u32[]{:S(2)}) collective-permute-start(bf16[288,128]{1,0:T(8,128)(2,1)S(1)} %get-tuple-element.57), channel_id=1, source_target_pairs={{0,6},{1,7},{2,4},{3,5},{4,2},{5,3},{6,0},{7,1},{8,14},{9,15},{10,... | collective-permute-start | bytes 221192 | tf_op jit(solution)/shard_map/ppermute | solution.py:481
  60.8 0.6 collective-permute-start.19
  61.5 1.9 %collective-permute-done.21 = bf16[288,128]{1,0:T(8,128)(2,1)S(1)} collective-permute-done((bf16[288,128]{1,0:T(8,128)(2,1)S(1)}, bf16[288,128]{1,0:T(8,128)(2,1)S(1)}, u32[]{:S(2)}, u32[]{:S(2)}) %collective-permute-start.21) | collective-permute-done | bytes 73760 | tf_op jit(solution)/shard_map/ppermute | solution.py:481
  63.4 2.7 %collective-permute-done.20 = bf16[288,128]{1,0:T(8,128)(2,1)S(1)} collective-permute-done((bf16[288,128]{1,0:T(8,128)(2,1)S(1)}, bf16[288,128]{1,0:T(8,128)(2,1)S(1)}, u32[]{:S(2)}, u32[]{:S(2)}) %collective-permute-start.20) | collective-permute-done | bytes 73760 | tf_op jit(solution)/shard_map/ppermute | solution.py:481
  66.1 1.2 %collective-permute-start.22 = (bf16[288,128]{1,0:T(8,128)(2,1)S(1)}, bf16[288,128]{1,0:T(8,128)(2,1)S(1)}, u32[]{:S(2)}, u32[]{:S(2)}) collective-permute-start(bf16[288,128]{1,0:T(8,128)(2,1)S(1)} %fusion.8), channel_id=1, source_target_pairs={{0,1},{1,0},{2,3},{3,2},{4,5},{5,4},{6,7},{7,6},{8,9},{9,8},{10,11... | collective-permute-start | bytes 221192 | tf_op jit(solution)/shard_map/ppermute | solution.py:481
  67.4 3.2 %collective-permute-done.22 = bf16[288,128]{1,0:T(8,128)(2,1)S(1)} collective-permute-done((bf16[288,128]{1,0:T(8,128)(2,1)S(1)}, bf16[288,128]{1,0:T(8,128)(2,1)S(1)}, u32[]{:S(2)}, u32[]{:S(2)}) %collective-permute-start.22) | collective-permute-done | bytes 73760 | tf_op jit(solution)/shard_map/ppermute | solution.py:481
  70.6 0.8 collective-permute-start.23
  71.4 1.8 %collective-permute-start.24 = (bf16[2,288,128]{2,1,0:T(8,128)(2,1)S(1)}, bf16[2,288,128]{2,1,0:T(8,128)(2,1)S(1)}, u32[]{:S(2)}, u32[]{:S(2)}) collective-permute-start(bf16[2,288,128]{2,1,0:T(8,128)(2,1)S(1)} %pad_maximum_fusion.4.refs_0_), channel_id=1, source_target_pairs={{0,4},{1,5},{2,6},{3,7},{4,0},{5,1},{6,2},{7,3},{8,12},{9,13},{10,... | collective-permute-start | bytes 442376 | tf_op jit(solution)/shard_map/ppermute | solution.py:481
  73.2 1.9 %collective-permute-start.25 = (bf16[2,288,128]{2,1,0:T(8,128)(2,1)S(1)}, bf16[2,288,128]{2,1,0:T(8,128)(2,1)S(1)}, u32[]{:S(2)}, u32[]{:S(2)}) collective-permute-start(bf16[2,288,128]{2,1,0:T(8,128)(2,1)S(1)} %pad_maximum_fusion.4.refs_0_), channel_id=1, source_target_pairs={{0,6},{1,7},{2,4},{3,5},{4,2},{5,3},{6,0},{7,1},{8,14},{9,15},{10,... | collective-permute-start | bytes 442376 | tf_op jit(solution)/shard_map/ppermute | solution.py:481
  75.0 2.8 %shard_map.80 = bf16[8,32,2048]{2,1,0:T(8,128)(2,1)} custom-call(s32[4]{0:T(128)S(1)} %broadcast_multiply_fusion.offsets, bf16[1024,128]{1,0:T(8,128)(2,1)S(1)} %get-tuple-element.44.delta_ref, bf16[256,128]{1,0:T(8,128)(2,1)S(1)} %collective-permute-done.18.upper_ref, bf16[432,128]{1,0:T(8,128)(2,1)S(1)} %copy-done.2, ...), custom_call_target="tpu_custom_call" | custom-call | flops 3449999872 | bytes 1818624 | tf_op jit(solution)/shard_map/pallas_call | solution.py:49
  77.8 0.8 collective-permute-done.23.refs_1_
  78.5 4.3 %collective-permute-done.24.refs_2_ = bf16[2,288,128]{2,1,0:T(8,128)(2,1)S(1)} collective-permute-done((bf16[2,288,128]{2,1,0:T(8,128)(2,1)S(1)}, bf16[2,288,128]{2,1,0:T(8,128)(2,1)S(1)}, u32[]{:S(2)}, u32[]{:S(2)}) %collective-permute-start.24) | collective-permute-done | bytes 147488 | tf_op jit(solution)/shard_map/ppermute | solution.py:481
  82.8 1.7 %shard_map.81 = (f32[432,128]{1,0:T(8,128)}, f32[864,256]{1,0:T(8,128)}) custom-call(s32[8]{0:T(128)S(1)} %get-tuple-element.63.order, bf16[2,288,128]{2,1,0:T(8,128)(2,1)S(1)} %pad_maximum_fusion.4.refs_0_, bf16[2,288,128]{2,1,0:T(8,128)(2,1)S(1)} %collective-permute-done.23.refs_1_, bf16[2,288,128]{2,1,0:T(8,128)(2,1)S(1)} %collective-permute-done.24.refs_2_, ...), custom_call_target="tpu_custom_call" | custom-call | flops 1150000000 | bytes 1695744 | tf_op jit(solution)/shard_map/pallas_call | solution.py:49
  (40 shorter events, 0.6 us)
Async XLA Ops:
  0.6 9.9 %collective-permute-start.2 = (bf16[432,128]{1,0:T(8,128)(2,1)}, bf16[432,128]{1,0:T(8,128)(2,1)S(1)}, u32[]{:S(2)}, u32[]{:S(2)}) collective-permute-start(bf16[432,128]{1,0:T(8,128)(2,1)} %w0.9), channel_id=1, source_target_pairs={{0,8},{8,0},{16,24},{24,16},{1,9},{9,1},{17,25},{25,17},{2,10},{10... | collective-permute-start | bytes 331784 | tf_op jit(solution)/shard_map/ppermute | solution.py:481
  1.1 9.1 %collective-permute-start.3 = (bf16[432,128]{1,0:T(8,128)(2,1)}, bf16[432,128]{1,0:T(8,128)(2,1)S(1)}, u32[]{:S(2)}, u32[]{:S(2)}) collective-permute-start(bf16[432,128]{1,0:T(8,128)(2,1)} %w0.9), channel_id=1, source_target_pairs={{0,16},{8,24},{16,0},{24,8},{1,17},{9,25},{17,1},{25,9},{2,18},{10... | collective-permute-start | bytes 331784 | tf_op jit(solution)/shard_map/ppermute | solution.py:481
  3.7 13.3 %collective-permute-start.1 = (bf16[864,256]{1,0:T(8,128)(2,1)}, bf16[864,256]{1,0:T(8,128)(2,1)S(1)}, u32[]{:S(2)}, u32[]{:S(2)}) collective-permute-start(bf16[864,256]{1,0:T(8,128)(2,1)} %w0.8), channel_id=1, source_target_pairs={{0,16},{8,24},{16,0},{24,8},{1,17},{9,25},{17,1},{25,9},{2,18},{10... | collective-permute-start | bytes 1327112 | tf_op jit(solution)/shard_map/ppermute | solution.py:481
  3.8 20.2 %collective-permute-start.6 = (bf16[864,256]{1,0:T(8,128)(2,1)}, bf16[864,256]{1,0:T(8,128)(2,1)S(1)}, u32[]{:S(2)}, u32[]{:S(2)}) collective-permute-start(bf16[864,256]{1,0:T(8,128)(2,1)} %w0.8), channel_id=1, source_target_pairs={{0,8},{8,0},{16,24},{24,16},{1,9},{9,1},{17,25},{25,17},{2,10},{10... | collective-permute-start | bytes 1327112 | tf_op jit(solution)/shard_map/ppermute | solution.py:481
  4.8 16.0 %collective-permute-start = (bf16[1,32,2048]{2,1,0:T(8,128)(2,1)S(1)}, bf16[1,32,2048]{2,1,0:T(8,128)(2,1)S(1)}, u32[]{:S(2)}, u32[]{:S(2)}) collective-permute-start(bf16[1,32,2048]{2,1,0:T(8,128)(2,1)S(1)} %slice_bitcast_fusion), channel_id=1, source_target_pairs={{0,1},{1,2},{2,3},{3,4},{4,5},{5,6},{6,7},{8,9},{9,10},{10,11},{11... | collective-permute-start | bytes 393224 | tf_op jit(solution)/shard_map/ppermute | solution.py:487
  8.6 1.2 %copy-start = (bf16[1,8,32,2048]{3,2,1,0:T(8,128)(2,1)S(1)}, bf16[1,8,32,2048]{3,2,1,0:T(8,128)(2,1)}, u32[]{:S(2)}) copy-start(bf16[1,8,32,2048]{3,2,1,0:T(8,128)(2,1)} %param.4) | copy-start | bytes 3145732
  9.8 1.8 %copy-start.2 = (bf16[432,128]{1,0:T(8,128)(2,1)S(1)}, bf16[432,128]{1,0:T(8,128)(2,1)}, u32[]{:S(2)}) copy-start(bf16[432,128]{1,0:T(8,128)(2,1)} %w0.9) | copy-start | bytes 331780
  10.2 1.4 %collective-permute-start.4 = (bf16[432,128]{1,0:T(8,128)(2,1)S(1)}, bf16[432,128]{1,0:T(8,128)(2,1)S(1)}, u32[]{:S(2)}, u32[]{:S(2)}) collective-permute-start(bf16[432,128]{1,0:T(8,128)(2,1)S(1)} %collective-permute-done.3.w2), channel_id=1, source_target_pairs={{0,8},{8,0},{16,24},{24,16},{1,9},{9,1},{17,25},{25,17},{2,10},{10... | collective-permute-start | bytes 331784 | tf_op jit(solution)/shard_map/ppermute | solution.py:481
  17.1 7.0 %collective-permute-start.7 = (bf16[864,256]{1,0:T(8,128)(2,1)S(1)}, bf16[864,256]{1,0:T(8,128)(2,1)S(1)}, u32[]{:S(2)}, u32[]{:S(2)}) collective-permute-start(bf16[864,256]{1,0:T(8,128)(2,1)S(1)} %collective-permute-done.1.w2), channel_id=1, source_target_pairs={{0,8},{8,0},{16,24},{24,16},{1,9},{9,1},{17,25},{25,17},{2,10},{10... | collective-permute-start | bytes 1327112 | tf_op jit(solution)/shard_map/ppermute | solution.py:481
  17.1 5.7 %collective-permute-start.5 = (bf16[256,128]{1,0:T(8,128)(2,1)S(1)}, bf16[256,128]{1,0:T(8,128)(2,1)S(1)}, u32[]{:S(2)}, u32[]{:S(2)}) collective-permute-start(bf16[256,128]{1,0:T(8,128)(2,1)S(1)} %get-tuple-element.31), channel_id=1, source_target_pairs={{0,1},{1,2},{2,3},{3,4},{4,5},{5,6},{6,7},{8,9},{9,10},{10,11},{11... | collective-permute-start | bytes 196616 | tf_op jit(solution)/shard_map/ppermute | solution.py:487
  20.8 3.2 %copy-start.1 = (bf16[864,256]{1,0:T(8,128)(2,1)S(1)}, bf16[864,256]{1,0:T(8,128)(2,1)}, u32[]{:S(2)}) copy-start(bf16[864,256]{1,0:T(8,128)(2,1)} %w0.8) | copy-start | bytes 1327108
  20.9 3.2 %copy-start.3 = (bf16[1,2,8,2048]{3,2,1,0:T(8,128)(2,1)S(1)}, bf16[1,2,8,2048]{3,2,1,0:T(8,128)(2,1)}, u32[]{:S(2)}) copy-start(bf16[1,2,8,2048]{3,2,1,0:T(8,128)(2,1)} %param.7) | copy-start | bytes 196612
  27.1 1.8 %collective-permute-start.9 = (bf16[16,112,128]{2,1,0:T(8,128)(2,1)S(1)}, bf16[16,112,128]{2,1,0:T(8,128)(2,1)S(1)}, u32[]{:S(2)}, u32[]{:S(2)}) collective-permute-start(bf16[16,112,128]{2,1,0:T(8,128)(2,1)S(1)} %get-tuple-element.38), channel_id=1, source_target_pairs={{0,8},{8,0},{16,24},{24,16},{1,9},{9,1},{17,25},{25,17},{2,10},{10... | collective-permute-start | bytes 1376264 | tf_op jit(solution)/shard_map/ppermute | solution.py:481
  27.1 2.5 %collective-permute-start.10 = (bf16[16,112,128]{2,1,0:T(8,128)(2,1)S(1)}, bf16[16,112,128]{2,1,0:T(8,128)(2,1)S(1)}, u32[]{:S(2)}, u32[]{:S(2)}) collective-permute-start(bf16[16,112,128]{2,1,0:T(8,128)(2,1)S(1)} %get-tuple-element.40), channel_id=1, source_target_pairs={{0,8},{8,0},{16,24},{24,16},{1,9},{9,1},{17,25},{25,17},{2,10},{10... | collective-permute-start | bytes 1376264 | tf_op jit(solution)/shard_map/ppermute | solution.py:481
  27.6 6.3 %collective-permute-start.8 = (bf16[64,256]{1,0:T(8,128)(2,1)S(1)}, bf16[64,256]{1,0:T(8,128)(2,1)S(1)}, u32[]{:S(2)}, u32[]{:S(2)}) collective-permute-start(bf16[64,256]{1,0:T(8,128)(2,1)S(1)} %get-tuple-element.36), channel_id=1, source_target_pairs={{1,0},{2,1},{3,2},{4,3},{5,4},{6,5},{7,6},{9,8},{10,9},{11,10},{12... | collective-permute-start | bytes 98312 | tf_op jit(solution)/shard_map/ppermute | solution.py:487
  36.7 4.5 %collective-permute-start.15 = (bf16[8,64,128]{2,1,0:T(8,128)(2,1)S(1)}, bf16[8,64,128]{2,1,0:T(8,128)(2,1)S(1)}, u32[]{:S(2)}, u32[]{:S(2)}) collective-permute-start(bf16[8,64,128]{2,1,0:T(8,128)(2,1)S(1)} %get-tuple-element.48), channel_id=1, source_target_pairs={{0,8},{8,0},{16,24},{24,16},{1,9},{9,1},{17,25},{25,17},{2,10},{10... | collective-permute-start | bytes 393224 | tf_op jit(solution)/shard_map/ppermute | solution.py:481
  36.8 9.2 %collective-permute-start.14 = (bf16[2,4,112,128]{3,2,1,0:T(8,128)(2,1)S(1)}, bf16[2,4,112,128]{3,2,1,0:T(8,128)(2,1)S(1)}, u32[]{:S(2)}, u32[]{:S(2)}) collective-permute-start(bf16[2,4,112,128]{3,2,1,0:T(8,128)(2,1)S(1)} %pad_maximum_fusion.1), channel_id=1, source_target_pairs={{0,1},{1,0},{2,3},{3,2},{4,5},{5,4},{6,7},{7,6},{8,9},{9,8},{10,11... | collective-permute-start | bytes 688136 | tf_op jit(solution)/shard_map/ppermute | solution.py:481
  39.8 7.8 %collective-permute-start.11 = (bf16[2,4,112,128]{3,2,1,0:T(8,128)(2,1)S(1)}, bf16[2,4,112,128]{3,2,1,0:T(8,128)(2,1)S(1)}, u32[]{:S(2)}, u32[]{:S(2)}) collective-permute-start(bf16[2,4,112,128]{3,2,1,0:T(8,128)(2,1)S(1)} %bitcast.67), channel_id=1, source_target_pairs={{0,16},{8,24},{16,0},{24,8},{1,17},{9,25},{17,1},{25,9},{2,18},{10... | collective-permute-start | bytes 688136 | tf_op jit(solution)/shard_map/ppermute | solution.py:481
  41.3 1.3 %collective-permute-start.12 = (bf16[8,64,128]{2,1,0:T(8,128)(2,1)S(1)}, bf16[8,64,128]{2,1,0:T(8,128)(2,1)S(1)}, u32[]{:S(2)}, u32[]{:S(2)}) collective-permute-start(bf16[8,64,128]{2,1,0:T(8,128)(2,1)S(1)} %get-tuple-element.46), channel_id=1, source_target_pairs={{0,8},{8,0},{16,24},{24,16},{1,9},{9,1},{17,25},{25,17},{2,10},{10... | collective-permute-start | bytes 393224 | tf_op jit(solution)/shard_map/ppermute | solution.py:481
  46.1 7.4 %collective-permute-start.16 = (bf16[4,176,128]{2,1,0:T(8,128)(2,1)S(1)}, bf16[4,176,128]{2,1,0:T(8,128)(2,1)S(1)}, u32[]{:S(2)}, u32[]{:S(2)}) collective-permute-start(bf16[4,176,128]{2,1,0:T(8,128)(2,1)S(1)} %pad_maximum_fusion.3), channel_id=1, source_target_pairs={{0,16},{8,24},{16,0},{24,8},{1,17},{9,25},{17,1},{25,9},{2,18},{10... | collective-permute-start | bytes 540680 | tf_op jit(solution)/shard_map/ppermute | solution.py:481
  47.7 7.4 %collective-permute-start.13 = (bf16[4,176,128]{2,1,0:T(8,128)(2,1)S(1)}, bf16[4,176,128]{2,1,0:T(8,128)(2,1)S(1)}, u32[]{:S(2)}, u32[]{:S(2)}) collective-permute-start(bf16[4,176,128]{2,1,0:T(8,128)(2,1)S(1)} %pad_maximum_fusion.2), channel_id=1, source_target_pairs={{0,1},{1,0},{2,3},{3,2},{4,5},{5,4},{6,7},{7,6},{8,9},{9,8},{10,11... | collective-permute-start | bytes 540680 | tf_op jit(solution)/shard_map/ppermute | solution.py:481
  49.5 7.1 %collective-permute-start.18 = (bf16[256,128]{1,0:T(8,128)(2,1)S(1)}, bf16[256,128]{1,0:T(8,128)(2,1)S(1)}, u32[]{:S(2)}, u32[]{:S(2)}) collective-permute-start(bf16[256,128]{1,0:T(8,128)(2,1)S(1)} %get-tuple-element.49), channel_id=1, source_target_pairs={{1,0},{2,1},{3,2},{4,3},{5,4},{6,5},{7,6},{9,8},{10,9},{11,10},{12... | collective-permute-start | bytes 196616 | tf_op jit(solution)/shard_map/ppermute | solution.py:487
  50.8 5.3 %collective-permute-start.17 = (bf16[4,64,128]{2,1,0:T(8,128)(2,1)S(1)}, bf16[4,64,128]{2,1,0:T(8,128)(2,1)S(1)}, u32[]{:S(2)}, u32[]{:S(2)}) collective-permute-start(bf16[4,64,128]{2,1,0:T(8,128)(2,1)S(1)} %get-tuple-element.60), channel_id=1, source_target_pairs={{0,17},{1,16},{2,19},{3,18},{4,21},{5,20},{6,23},{7,22},{8,25},{9,... | collective-permute-start | bytes 196616 | tf_op jit(solution)/shard_map/ppermute | solution.py:563
  56.6 6.8 %collective-permute-start.21 = (bf16[288,128]{1,0:T(8,128)(2,1)S(1)}, bf16[288,128]{1,0:T(8,128)(2,1)S(1)}, u32[]{:S(2)}, u32[]{:S(2)}) collective-permute-start(bf16[288,128]{1,0:T(8,128)(2,1)S(1)} %get-tuple-element.57), channel_id=1, source_target_pairs={{0,6},{1,7},{2,4},{3,5},{4,2},{5,3},{6,0},{7,1},{8,14},{9,15},{10,... | collective-permute-start | bytes 221192 | tf_op jit(solution)/shard_map/ppermute | solution.py:481
  60.8 5.3 %collective-permute-start.20 = (bf16[288,128]{1,0:T(8,128)(2,1)S(1)}, bf16[288,128]{1,0:T(8,128)(2,1)S(1)}, u32[]{:S(2)}, u32[]{:S(2)}) collective-permute-start(bf16[288,128]{1,0:T(8,128)(2,1)S(1)} %get-tuple-element.58), channel_id=1, source_target_pairs={{0,4},{1,5},{2,6},{3,7},{4,0},{5,1},{6,2},{7,3},{8,12},{9,13},{10,... | collective-permute-start | bytes 221192 | tf_op jit(solution)/shard_map/ppermute | solution.py:481
  60.8 5.3 %collective-permute-start.19 = (bf16[288,128]{1,0:T(8,128)(2,1)S(1)}, bf16[288,128]{1,0:T(8,128)(2,1)S(1)}, u32[]{:S(2)}, u32[]{:S(2)}) collective-permute-start(bf16[288,128]{1,0:T(8,128)(2,1)S(1)} %get-tuple-element.56), channel_id=1, source_target_pairs={{0,2},{1,3},{2,0},{3,1},{4,6},{5,7},{6,4},{7,5},{8,10},{9,11},{10,... | collective-permute-start | bytes 221192 | tf_op jit(solution)/shard_map/ppermute | solution.py:481
  66.1 4.4 %collective-permute-start.22 = (bf16[288,128]{1,0:T(8,128)(2,1)S(1)}, bf16[288,128]{1,0:T(8,128)(2,1)S(1)}, u32[]{:S(2)}, u32[]{:S(2)}) collective-permute-start(bf16[288,128]{1,0:T(8,128)(2,1)S(1)} %fusion.8), channel_id=1, source_target_pairs={{0,1},{1,0},{2,3},{3,2},{4,5},{5,4},{6,7},{7,6},{8,9},{9,8},{10,11... | collective-permute-start | bytes 221192 | tf_op jit(solution)/shard_map/ppermute | solution.py:481
  70.6 8.0 %collective-permute-start.23 = (bf16[2,288,128]{2,1,0:T(8,128)(2,1)S(1)}, bf16[2,288,128]{2,1,0:T(8,128)(2,1)S(1)}, u32[]{:S(2)}, u32[]{:S(2)}) collective-permute-start(bf16[2,288,128]{2,1,0:T(8,128)(2,1)S(1)} %pad_maximum_fusion.4.refs_0_), channel_id=1, source_target_pairs={{0,2},{1,3},{2,0},{3,1},{4,6},{5,7},{6,4},{7,5},{8,10},{9,11},{10,... | collective-permute-start | bytes 442376 | tf_op jit(solution)/shard_map/ppermute | solution.py:481
  71.4 11.4 %collective-permute-start.24 = (bf16[2,288,128]{2,1,0:T(8,128)(2,1)S(1)}, bf16[2,288,128]{2,1,0:T(8,128)(2,1)S(1)}, u32[]{:S(2)}, u32[]{:S(2)}) collective-permute-start(bf16[2,288,128]{2,1,0:T(8,128)(2,1)S(1)} %pad_maximum_fusion.4.refs_0_), channel_id=1, source_target_pairs={{0,4},{1,5},{2,6},{3,7},{4,0},{5,1},{6,2},{7,3},{8,12},{9,13},{10,... | collective-permute-start | bytes 442376 | tf_op jit(solution)/shard_map/ppermute | solution.py:481
  73.2 9.7 %collective-permute-start.25 = (bf16[2,288,128]{2,1,0:T(8,128)(2,1)S(1)}, bf16[2,288,128]{2,1,0:T(8,128)(2,1)S(1)}, u32[]{:S(2)}, u32[]{:S(2)}) collective-permute-start(bf16[2,288,128]{2,1,0:T(8,128)(2,1)S(1)} %pad_maximum_fusion.4.refs_0_), channel_id=1, source_target_pairs={{0,6},{1,7},{2,4},{3,5},{4,2},{5,3},{6,0},{7,1},{8,14},{9,15},{10,... | collective-permute-start | bytes 442376 | tf_op jit(solution)/shard_map/ppermute | solution.py:481

commit v2 on v1

--- a/solution.py
+++ b/solution.py
@@ -105,7 +105,9 @@
         for a in range(3):
             plane = 2 * (first + cell) - 1 + a
             for e in range(3):
-                source = halo_ref.at[0, e] if plane < 0 else sorted_ref.at[plane, e]
+                source = (
+                    halo_ref.at[halo_ref.shape[0] + plane, e] if plane < 0 else sorted_ref.at[plane, e]
+                )
                 left = (a * 3 + e) * 256
                 columns[at : at + 16, left : left + 128] = jnp.zeros((16, 128), BF16)
                 columns[at + 16 : at + rows, left : left + 128] = source[0 : rows - 16, :]
@@ -133,7 +135,7 @@
 
 
 def forward_upper_kernel(
-    offsets, sorted_ref, w0, w1, w2, w3, slope_ref, hidden_ref, last_ref, columns, whole, padded
+    offsets, sorted_ref, w0, w1, w2, w3, slope_ref, hidden_ref, columns, whole, padded
 ):
     cells = sorted_ref.shape[0] // 2
     put_rows(whole, (w0, w1, w2, w3), offsets)
@@ -142,7 +144,6 @@
     linear = jnp.dot(columns[...], padded[...], preferred_element_type=F32)
     hidden = activate(linear)
     hidden_ref[...] = hidden.reshape(hidden_ref.shape)
-    last_ref[...] = hidden[hidden.shape[0] - last_ref.shape[0] :].astype(BF16)
     slope_ref[...] = activate_slope(linear)
 
 
@@ -156,7 +157,6 @@
         (
             sds((some, 128), F32),
             sds((cells - 1, rows // 32, 2, 2, 8, 128), F32),
-            sds((rows, 128), BF16),
         ),
         [
             pltpu.VMEM((some, 9 * 256), BF16),
@@ -170,24 +170,24 @@
 
 
 def forward_lower_kernel(
-    offsets, sorted_ref, halo_ref, hidden_ref, below_ref, w0, w1, w2, w3,
-    slope_ref, windows_ref, sorted_halo, wide, columns, whole, padded, lowest, below,
+    offsets, alive, sorted_ref, halo_ref, hidden_ref, w0, w1, w2, w3,
+    slope_ref, windows_ref, sorted_halo, wide, columns, whole, padded, lowest,
 ):
     rows = sorted_ref.shape[2]
     cells = sorted_ref.shape[0] // 2
     half = rows // 32
-    sort_kernel(1, halo_ref, sorted_halo, wide)
+    sort_kernel(halo_ref.shape[0], halo_ref, sorted_halo, wide)
     put_rows(whole, (w0, w1, w2, w3), offsets)
     pad_first(whole, padded)
-    gather_taps(columns, sorted_ref, sorted_halo, 0, 1, 0)
+    gather_taps(columns, sorted_ref, sorted_halo, -1, 2, 0)
     linear = jnp.dot(columns[...], padded[...], preferred_element_type=F32)
     slope_ref[...] = activate_slope(linear)
     lowest[...] = activate(linear).reshape(lowest.shape)
-    below[...] = below_ref[...].astype(F32).reshape(below.shape)
+    lowest[0] = lowest[0] * alive[0]
     for out in range(cells // 2):
         for a in range(3):
             plane = 2 * out - 1 + a
-            source = (below, lowest)[plane + 1] if plane < 1 else hidden_ref.at[plane - 1]
+            source = lowest.at[plane + 1] if plane < 1 else hidden_ref.at[plane - 1]
 
             def read(column, row):
                 return source[:, column, row].reshape(half * 8, 128)
@@ -195,25 +195,27 @@
             take_windows(read, windows_ref, out, a, half)
 
 
-def forward_lower(sorted_volume, halo, hidden, below, shards, offsets):
+def forward_lower(sorted_volume, halo, hidden, shards, offsets, alive):
     planes, _, rows, _ = sorted_volume.shape
     cells = planes // 2
     shard = shards[0].shape[0]
     return call(
         forward_lower_kernel,
-        (sds((rows, 128), F32), sds((cells * rows // 8, 27 * 128), BF16)),
+        (
+            sds((2 * rows, 128), F32),
+            sds((cells * rows // 8, 27 * 128), BF16),
+            sds((halo.shape[0], 3, rows, 128), BF16),
+        ),
         [
-            pltpu.VMEM((1, 3, rows, 128), BF16),
             pltpu.VMEM((rows // 16, halo.shape[1], 128), F32),
-            pltpu.VMEM((rows, 9 * 256), BF16),
+            pltpu.VMEM((2 * rows, 9 * 256), BF16),
             pltpu.VMEM((4 * shard, 128), BF16),
             pltpu.VMEM((9 * 256, 128), BF16),
-            pltpu.VMEM(hidden.shape[1:], F32),
-            pltpu.VMEM(hidden.shape[1:], F32),
+            pltpu.VMEM((2, *hidden.shape[1:]), F32),
         ],
-        sorted_volume, halo, hidden, below, *shards,
-        smem=(offsets,),
-        micros=1.5,
+        sorted_volume, halo, hidden, *shards,
+        smem=(offsets, alive),
+        micros=2.0,
     )
 
 
@@ -227,7 +229,7 @@
 
 def forward_second_kernel(
     offsets, slots, order, windows_ref, cot_ref, w0, w1, w2, w3,
-    act_ref, delta_ref, lowest_ref, g0, g1, g2, g3, whole, flat,
+    act_ref, delta_ref, g0, g1, g2, g3, whole, flat,
 ):
     put_rows(whole, (w0, w1, w2, w3), offsets)
     linear = jnp.dot(windows_ref[...], whole[...], preferred_element_type=F32)
@@ -250,7 +252,6 @@
         )
     delta = (jnp.concatenate(deltas, axis=0) * slope).astype(BF16)
     delta_ref[...] = delta
-    lowest_ref[...] = delta[: count * 8]
     total = lax.dot_general(
         windows_ref[...], delta, (((0,), (0,)), ((), ())), preferred_element_type=F32
     ).astype(BF16)
@@ -275,7 +276,6 @@
         (
             sds(cot.shape, BF16),
             sds((windows.shape[0], features), BF16),
-            sds((windows.shape[0] // cot.shape[0], features), BF16),
             piece, piece, piece, piece,
         ),
         [
@@ -289,10 +289,10 @@
 
 
 def back_second_kernel(
-    offsets, slots, order, delta_ref, upper_ref, w0, w1, w2, w3,
+    offsets, slots, order, delta_ref, w0, w1, w2, w3,
     slope_low_ref, slope_ref, sorted_ref, halo_ref,
-    out_ref, lowest_ref, g0, g1, g2, g3,
-    whole, product, above, sorted_halo, wide, columns, flat,
+    low_ref, last_ref, down_ref, g0, g1, g2, g3,
+    whole, product, columns, deltas, flat,
 ):
     rows = sorted_ref.shape[2]
     cells = sorted_ref.shape[0] // 2
@@ -302,27 +302,20 @@
     product[...] = lax.dot_general(
         delta_ref[...], whole[...], (((1,), (1,)), ((), ())), preferred_element_type=F32
     )
-    above[...] = lax.dot_general(
-        upper_ref[...], whole[: 9 * 128, :], (((1,), (1,)), ((), ())), preferred_element_type=F32
-    )
-    sort_kernel(1, halo_ref, sorted_halo, wide)
-    gather_taps(columns, sorted_ref, sorted_halo, 0, cells, 0)
+    gather_taps(columns, sorted_ref, halo_ref, -1, cells + 1, 0)
 
     def term(out, a, e, f):
         left = ((a * 3 + e) * 3 + f) * 128
-        if out == cells // 2:
-            block = above[:, left : left + 128]
-        else:
-            block = product[out * size : (out + 1) * size, left : left + 128]
+        block = product[out * size : (out + 1) * size, left : left + 128]
         if f == 0:
             block = jnp.concatenate([block[8:], jnp.zeros((8, 128), F32)], axis=0)
         if e == 0:
             block = from_after(block)
         return block.reshape(half, 8, 128)
 
-    for plane in range(cells):
+    for plane in range(-1, cells):
         taps = [
-            (out, a) for out in range(cells // 2 + 1) for a in range(3) if 2 * out - 1 + a == plane
+            (out, a) for out in range(cells // 2) for a in range(3) if 2 * out - 1 + a == plane
         ]
         sums = [
             sum(
@@ -335,12 +328,21 @@
             for row in range(2)
         ]
         spread = jnp.concatenate(sums, axis=1).reshape(rows, 128)
-        slope = slope_low_ref[...] if plane == 0 else slope_ref[(plane - 1) * rows : plane * rows, :]
+        if plane < 1:
+            slope = slope_low_ref[(plane + 1) * rows : (plane + 2) * rows, :]
+        else:
+            slope = slope_ref[(plane - 1) * rows : plane * rows, :]
         delta = (spread * slope).astype(BF16)
-        out_ref[plane * rows : (plane + 1) * rows, :] = delta
+        deltas[(plane + 1) * rows : (plane + 2) * rows, :] = delta
+        if plane < 0:
+            down_ref[:rows, :] = spread.astype(BF16)
         if plane == 0:
-            lowest_ref[...] = delta
-    flipped = jnp.transpose(out_ref[...].astype(F32)).astype(BF16)
+            down_ref[rows:, :] = delta
+        if plane == cells - 1:
+            last_ref[...] = spread
+        elif plane >= 0:
+            low_ref[plane * rows : (plane + 1) * rows, :] = delta
+    flipped = jnp.transpose(deltas[...].astype(F32)).astype(BF16)
     tally = jnp.dot(flipped, columns[...], preferred_element_type=F32)
     shard_rows = 9 * 192 // 4
     for tap in range(9):
@@ -359,33 +361,35 @@
     put_pieces(flat, (g0, g1, g2, g3), slots, order)
 
 
-def back_second(
-    delta, upper, shards, slopes, sorted_volume, halo, offsets, slots, order, places, size
-):
+def back_second(delta, shards, slopes, sorted_volume, halo, offsets, slots, order, places, size):
     rows, features = shards[0].shape
     planes, _, width, _ = sorted_volume.shape
     cells = planes // 2
     piece = sds((places, size, 128), BF16)
     return call(
         back_second_kernel,
-        (sds((cells * width, 128), BF16), sds((width, 128), BF16), piece, piece, piece, piece),
+        (
+            sds(((cells - 1) * width, 128), BF16),
+            sds((width, 128), F32),
+            sds((2 * width, 128), BF16),
+            piece, piece, piece, piece,
+        ),
         [
             pltpu.VMEM((4 * rows, features), BF16),
             pltpu.VMEM((delta.shape[0], 4 * rows), F32),
-            pltpu.VMEM((upper.shape[0], 9 * 128), F32),
-            pltpu.VMEM((1, 3, width, 128), BF16),
-            pltpu.VMEM((width // 16, halo.shape[1], 128), F32),
-            pltpu.VMEM((cells * width, 9 * 256), BF16),
+            pltpu.VMEM(((cells + 1) * width, 9 * 256), BF16),
+            pltpu.VMEM(((cells + 1) * width, 128), BF16),
             pltpu.VMEM((4, places * size, 128), BF16),
         ],
-        delta, upper, *shards, *slopes, sorted_volume, halo,
+        delta, *shards, *slopes, sorted_volume, halo,
         smem=(offsets, slots, order),
         micros=3.5,
     )
 
 
 def back_input_kernel(
-    offsets, delta_ref, upper_ref, w0, w1, w2, w3, out_ref, whole, turned, pairs, product, wide
+    offsets, low_ref, last_ref, slope_ref, upper_ref, w0, w1, w2, w3,
+    out_ref, whole, turned, pairs, product, wide, last,
 ):
     put_rows(whole, (w0, w1, w2, w3), offsets)
     for tap in range(9):
@@ -395,11 +399,17 @@
         turned[top + 64 : top + 128, 128:256] = whole[tap * 192 : tap * 192 + 64, :]
     planes = out_ref.shape[0]
     cells = planes // 2
-    rows = upper_ref.shape[0]
+    rows = last_ref.shape[0]
     groups = rows // 16
+    last[...] = (
+        (last_ref[...] + upper_ref[:rows, :].astype(F32)) * slope_ref[(cells - 2) * rows :, :]
+    ).astype(BF16)
     for cell in range(cells + 1):
         at = cell * rows
-        source = upper_ref if cell == cells else delta_ref.at[at : at + rows]
+        if cell < cells - 1:
+            source = low_ref.at[at : at + rows]
+        else:
+            source = last if cell == cells - 1 else upper_ref.at[rows : 2 * rows]
         pairs[at : at + rows, 0:128] = source[...]
         pairs[at : at + rows - 16, 128:256] = source[16:rows, :]
         pairs[at + rows - 16 : at + rows, 128:256] = jnp.zeros((16, 128), BF16)
@@ -430,10 +440,10 @@
             out_ref[plane, :, lanes] = wide[group].astype(BF16)
 
 
-def back_input(delta, upper, shards, offsets, shape):
+def back_input(low, last, slope, upper, shards, offsets, shape):
     planes, side, width = shape
     shard = shards[0].shape[0]
-    rows = delta.shape[0] + upper.shape[0]
+    rows = low.shape[0] + upper.shape[0]
     return call(
         back_input_kernel,
         sds(shape, BF16),
@@ -443,8 +453,9 @@
             pltpu.VMEM((rows, 256), BF16),
             pltpu.VMEM((rows // 16, 2, 8, 9 * 128), F32),
             pltpu.VMEM((width // 128, side, 128), F32),
+            pltpu.VMEM(last.shape, BF16),
         ],
-        delta, upper, *shards,
+        low, last, slope, upper, *shards,
         smem=(offsets,),
         micros=3.0,
     )
@@ -453,17 +464,16 @@
 def unpack_kernel(scale_first, scale_second, order, *refs):
     *chunks, first_ref, second_ref, flat_first, flat_second = refs
     high = len(chunks)
-    places = 2 * high
-    small = flat_first.shape[0] // places
-    big = flat_second.shape[0] // (2 * places)
+    small = flat_first.shape[0] // (4 * high)
+    big = flat_second.shape[0] // (4 * high)
     for index, chunk in enumerate(chunks):
         for low in range(2):
-            place = order[low * high + index]
             for part in range(2):
-                row = pl.multiple_of((part * places + place) * big, 16)
-                flat_second[pl.ds(row, big), :] = chunk[low, part * big : (part + 1) * big, :]
-            row = pl.multiple_of(place * small, 16)
-            flat_first[pl.ds(row, small), :] = chunk[low, 2 * big :, :]
+                place = order[(part * 2 + low) * high + index]
+                row = pl.multiple_of(place * big, 16)
+                flat_second[pl.ds(row, big), :] = chunk[low, part, :big, :]
+                row = pl.multiple_of(place * small, 16)
+                flat_first[pl.ds(row, small), :] = chunk[low, part, big:, :]
     rows, features = second_ref.shape
     for lane in range(features // 128):
         second_ref[:, lane * 128 : (lane + 1) * 128] = (
@@ -472,8 +482,12 @@
     first_ref[...] = flat_first[: first_ref.shape[0], :].astype(F32) * scale_first
 
 
+def wide_sum(*pieces):
+    return sum(piece.astype(F32) for piece in pieces)
+
+
 def added(*pieces):
-    return sum(piece.astype(F32) for piece in pieces).astype(BF16)
+    return wide_sum(*pieces).astype(BF16)
 
 
 def swap(value, axis, bits):
@@ -497,11 +511,12 @@
     slots = jnp.arange(4, dtype=jnp.int32) ^ data
     offsets_first = slots * small
     offsets_second = slots * big
+    alive = (place > 0).astype(F32).reshape(1)
     steps = jnp.arange(spaces, dtype=jnp.int32)
     order = place ^ (2 * (steps % high) + steps // high)
-    order_second = jnp.concatenate([order, spaces + order])
+    order = jnp.concatenate([order, spaces + order])
     lanes = weight_second.shape[1] // 128
-    size_first = -(-small // (16 * spaces)) * 16
+    size_first = -(-small // (32 * spaces)) * 16
     size_second = -(-lanes * big // (32 * spaces)) * 16
 
     inputs = volume.reshape(planes, side, width)
@@ -509,74 +524,66 @@
     first_core = swap(weight_first, "dp", 1)
     second_x = swap(weight_second, "dp", 2)
     second_core = swap(weight_second, "dp", 1)
-    halo = shifted(inputs[planes - 1 :], "space", 1)
+    halo = shifted(inputs[planes - 3 :], "space", 1)
     first_far = swap(first_x, "dp", 1)
     shards_first = (weight_first, first_core, first_x, first_far)
 
     sorted_volume = sorted_planes(inputs)
-    slope, hidden, last_hidden = forward_upper(sorted_volume, shards_first, offsets_first)
-    hidden_halo = shifted(last_hidden, "space", 1)
+    slope, hidden = forward_upper(sorted_volume, shards_first, offsets_first)
     second_x, hidden = lax.optimization_barrier((second_x, hidden))
-    slope_low, windows = forward_lower(
-        sorted_volume, halo, hidden, hidden_halo, shards_first, offsets_first
-    )
     second_far = swap(second_x, "dp", 1)
     shards_second = (weight_second, second_core, second_x, second_far)
+    slope_low, windows, sorted_halo = forward_lower(
+        sorted_volume, halo, hidden, shards_first, offsets_first, alive
+    )
     cot = cotangent.reshape(cotangent.shape[1:])
-    activations, delta_second, lowest_second, *second = forward_second(
-        windows, cot, shards_second, offsets_second, slots, order_second,
-        2 * spaces, size_second,
-    )
-    far = swap(second[3], "dp", 1).reshape(2, 2, high, size_second, 128)
-    near = swap(second[1], "dp", 1).reshape(2, 2, high, size_second, 128)
-    own = second[0].reshape(2, 2, high, size_second, 128)
-    there = second[2].reshape(2, 2, high, size_second, 128)
-    upper_second = shifted(lowest_second, "space", -1)
-    send_a = added(there[0], far[0])
-    send_b = jnp.stack([added(own[1, 1], near[1, 1]), added(there[1, 1], far[1, 1])])
-    got_a = swap(send_a, "dp", 2)
-    got_b = swap(send_b, "space", 1)
-    upper_second, _, _ = lax.optimization_barrier((upper_second, send_a, send_b))
-
-    delta_first, lowest_first, *first = back_second(
-        delta_second, upper_second, shards_second, (slope_low, slope), sorted_volume, halo,
-        offsets_second, slots, order, spaces, size_first,
-    )
-    upper_first = shifted(lowest_first, "space", -1)
-    far_first = swap(first[3], "dp", 1).reshape(2, high, size_first, 128)
-    near_first = swap(first[1], "dp", 1).reshape(2, high, size_first, 128)
-    own_first = first[0].reshape(2, high, size_first, 128)
-    there_first = first[2].reshape(2, high, size_first, 128)
-
-    send_y = jnp.concatenate(
-        [added(own[0, 1], near[0, 1], got_a[1]), added(own_first[1], near_first[1])], axis=1
-    )
-    send_x = jnp.concatenate(
-        [added(there[1, 0], far[1, 0], got_b[1]), added(there_first[0], far_first[0])], axis=1
-    )
+    activations, delta_second, *second = forward_second(
+        windows, cot, shards_second, offsets_second, slots, order, 2 * spaces, size_second,
+    )
+    low, last, down, *first = back_second(
+        delta_second, shards_second, (slope_low, slope), sorted_volume, sorted_halo,
+        offsets_second, slots, order, 2 * spaces, size_first,
+    )
+    upper = shifted(down, "space", -1)
+    def pieces(value):
+        return value.reshape(2, 2, high, -1, 128)
+
+    def joined(at, *terms):
+        return jnp.concatenate(
+            [
+                wide_sum(*(second[at] for second, _ in terms)),
+                wide_sum(*(first[at] for _, first in terms)),
+            ],
+            axis=-2,
+        )
+
+    second_far, second_near = swap(second[3], "dp", 1), swap(second[1], "dp", 1)
+    first, second_far, second_near = lax.optimization_barrier((first, second_far, second_near))
+    far = pieces(second_far), pieces(swap(first[3], "dp", 1))
+    near = pieces(second_near), pieces(swap(first[1], "dp", 1))
+    own = pieces(second[0]), pieces(first[0])
+    there = pieces(second[2]), pieces(first[2])
+    got_a = swap(joined(0, there, far).astype(BF16), "dp", 2)
+    got_b = swap(
+        jnp.stack([joined((1, 1), own, near), joined((1, 1), there, far)]).astype(BF16), "space", 1
+    )
+    send_y = added(joined((0, 1), own, near), got_a[1])
+    send_x = added(joined((1, 0), there, far), got_b[1])
     got_y = swap(send_y, "space", 1)
     got_x = swap(send_x, "dp", 2)
-    pairs = []
-    for d in range(4):
-        for s in range(spaces):
-            pairs.append((d * spaces + s, (d ^ 2) * spaces + (s ^ 1)))
-    got_xy = lax.ppermute(added(there_first[1], far_first[1]), ("dp", "space"), pairs)
-    held = jnp.concatenate(
+    held = jnp.stack(
         [
-            added(own[0, 0], near[0, 0], got_a[0], got_y[:, :size_second]),
-            added(own[1, 0], near[1, 0], got_b[0], got_x[:, :size_second]),
-            added(
-                own_first[0], near_first[0], got_y[:, size_second:], got_x[:, size_second:], got_xy
-            ),
+            added(joined((0, 0), own, near), got_a[0], got_y),
+            added(joined((1, 0), own, near), got_b[0], got_x),
         ],
         axis=1,
     )
-    held, upper_first = lax.optimization_barrier((held, upper_first))
+    held, upper = lax.optimization_barrier((held, upper))
     mine = added(held[0], *(swap(held[k], "space", 2 * k) for k in range(1, high)))
     both = jnp.stack([mine, swap(mine, "space", 1)])
     chunks = [both] + [swap(both, "space", 2 * k) for k in range(1, high)]
 
-    gradient = back_input(delta_first, upper_first, shards_first, offsets_first, inputs.shape)
+    gradient = back_input(low, last, slope, upper, shards_first, offsets_first, inputs.shape)
 
     cells_first = samples * lax.axis_size("dp") * (planes // 2) * spaces * (side // 2) ** 2
     cells_second = cells_first // 8
@@ -584,7 +591,7 @@
         functools.partial(unpack_kernel, float(cells_first) ** -0.5, float(cells_second) ** -0.5),
         (sds(weight_first.shape, F32), sds(weight_second.shape, F32)),
         [
-            pltpu.VMEM((spaces * size_first, 128), BF16),
+            pltpu.VMEM((2 * spaces * size_first, 128), BF16),
             pltpu.VMEM((2 * spaces * size_second, 128), BF16),
         ],
         *chunks,

time: 84.7 us -> 77.8 us (0.919)
  starting transfers between devices: 35.3 us -> 27.8 us
  waiting for transfers between devices: 31.8 us -> 30 us
  local copies, waits for them, and re-layouts: 2.16 us -> 3.68 us
    ppermute x4 -> x2, waiting for transfers between devices: 6.45 us -> 0.85 us  [shifted(): return lax.ppermute(value, axis, pairs)]
    ppermute x4 -> x2, starting transfers between devices: 10 us -> 5.18 us  [shifted(): return lax.ppermute(value, axis, pairs)]
    ppermute x21, waiting for transfers between devices: 24.4 us -> 29.2 us  [swap(): return lax.ppermute(value, axis, [(i, i ^ bits) for i in range(size)])]
    ppermute x1 -> x0, starting transfers between devices: 2.68 us -> none  [local(): lax.ppermute(added(there_first[1], far_first[1]), ('dp', 'space'), pairs)]
    unnamed x8 -> x14, local copies, waits for them, and re-layouts: 1.23 us -> 2.65 us
    ppermute x1 -> x0, waiting for transfers between devices: 0.9 us -> none  [local(): lax.ppermute(added(there_first[1], far_first[1]), ('dp', 'space'), pairs)]
  transfers between devices with their start and end apart: 26 -> 23, of which waited for: 15 -> 14; matrix products, arithmetic and copies ran while one was open for 2% -> 2% of each run, Pallas kernels for 7% -> 12%
where the time goes in v2:
time: 77.8 us; the launch traced here: 77.5 us
  waiting for transfers between devices  30 us (39%)
  starting transfers between devices  27.8 us (36%)
  Pallas kernels  14.3 us (18%)
  local copies, waits for them, and re-layouts  3.68 us (5%)
  between operations  0.94 us (1%)
    ppermute x21, waiting for transfers between devices, swap(): return lax.ppermute(value, axis, [(i, i ^ bits) for i in range(size)])  29.2 us
    ppermute x21, starting transfers between devices, swap(): return lax.ppermute(value, axis, [(i, i ^ bits) for i in range(size)])  22.7 us
    pallas_call x7, Pallas kernels, call(): pl.pallas_call(kernel, out_shape=out_shape, in_specs=specs, out_specs=jax...  14.3 us
    ppermute x2, starting transfers between devices, shifted(): return lax.ppermute(value, axis, pairs)  5.18 us
    unnamed x14, local copies, waits for them, and re-layouts  2.65 us
  transfers between devices with their start and end apart: 23, of which 14 were waited for; matrix products, arithmetic and copies ran while one was open for 2% of the time, Pallas kernels for 12%

profile of v2, /device:TPU:0, one launch (start us, length us, event | category | flops | bytes accessed | tf_op | source)
XLA Modules:
  0.0 77.5 jit_solution(14652043639257302829)
XLA Ops:
  0.6 3.0 %collective-permute-start.3 = (bf16[432,128]{1,0:T(8,128)(2,1)}, bf16[432,128]{1,0:T(8,128)(2,1)S(1)}, u32[]{:S(2)}, u32[]{:S(2)}) collective-permute-start(bf16[432,128]{1,0:T(8,128)(2,1)} %w0.9), channel_id=1, source_target_pairs={{0,16},{8,24},{16,0},{24,8},{1,17},{9,25},{17,1},{25,9},{2,18},{10... | collective-permute-start | bytes 331784 | tf_op jit(solution)/shard_map/ppermute | solution.py:495
  3.6 0.5 collective-permute-start.5
  4.1 0.1 collective-permute-start.1
  4.2 1.0 %slice_bitcast_fusion = bf16[3,32,2048]{2,1,0:T(8,128)(2,1)S(1)} fusion(bf16[1,8,32,2048]{3,2,1,0:T(8,128)(2,1)} %param.4), kind=kLoop, calls=%fused_computation.1 | loop fusion | bytes 786432 | tf_op jit(solution)/shard_map/slice | solution.py:527
  5.2 3.9 %collective-permute-start = (bf16[3,32,2048]{2,1,0:T(8,128)(2,1)S(1)}, bf16[3,32,2048]{2,1,0:T(8,128)(2,1)S(1)}, u32[]{:S(2)}, u32[]{:S(2)}) collective-permute-start(bf16[3,32,2048]{2,1,0:T(8,128)(2,1)S(1)} %slice_bitcast_fusion), channel_id=1, source_target_pairs={{0,1},{1,2},{2,3},{3,4},{4,5},{5,6},{6,7},{8,9},{9,10},{10,11},{11... | collective-permute-start | bytes 1179656 | tf_op jit(solution)/shard_map/ppermute | solution.py:501
  9.2 1.2 %copy-done = bf16[1,8,32,2048]{3,2,1,0:T(8,128)(2,1)S(1)} copy-done((bf16[1,8,32,2048]{3,2,1,0:T(8,128)(2,1)S(1)}, bf16[1,8,32,2048]{3,2,1,0:T(8,128)(2,1)}, u32[]{:S(2)}) %copy-start) | copy-done | bytes 1048600
  10.4 0.3 shard_map.75.sorted_ref
  10.8 0.1 collective-permute-start.4
  10.9 1.3 %collective-permute-done.4.w3 = bf16[432,128]{1,0:T(8,128)(2,1)S(1)} collective-permute-done((bf16[432,128]{1,0:T(8,128)(2,1)S(1)}, bf16[432,128]{1,0:T(8,128)(2,1)S(1)}, u32[]{:S(2)}, u32[]{:S(2)}) %collective-permute-start.4) | collective-permute-done | bytes 110624 | tf_op jit(solution)/shard_map/ppermute | solution.py:495
  12.2 1.8 %shard_map.76 = (f32[768,128]{1,0:T(8,128)S(1)}, f32[3,8,2,2,8,128]{5,4,3,2,1,0:T(8,128)S(1)}) custom-call(s32[4]{0:T(128)S(1)} %broadcast_multiply_fusion.offsets, bf16[8,3,256,128]{3,2,1,0:T(8,128)(2,1)S(1)} %shard_map.75.sorted_ref, bf16[432,128]{1,0:T(8,128)(2,1)S(1)} %copy-done.2, bf16[432,128]{1,0:T(8,128)(2,1)S(1)} %collective-permute-done.2.w1, ...), custom_call_target="tpu_custom_call" | custom-call | flops 2875000064 | bytes 2801664 | tf_op jit(solution)/shard_map/pallas_call | solution.py:49
  14.0 2.4 %collective-permute-done.1.w2 = bf16[864,256]{1,0:T(8,128)(2,1)S(1)} collective-permute-done((bf16[864,256]{1,0:T(8,128)(2,1)}, bf16[864,256]{1,0:T(8,128)(2,1)S(1)}, u32[]{:S(2)}, u32[]{:S(2)}) %collective-permute-start.1) | collective-permute-done | bytes 442400 | tf_op jit(solution)/shard_map/ppermute | solution.py:495
  16.4 0.1 pad_add_fusion.order
  16.5 0.8 %collective-permute-done.halo_ref = bf16[3,32,2048]{2,1,0:T(8,128)(2,1)S(1)} collective-permute-done((bf16[3,32,2048]{2,1,0:T(8,128)(2,1)S(1)}, bf16[3,32,2048]{2,1,0:T(8,128)(2,1)S(1)}, u32[]{:S(2)}, u32[]{:S(2)}) %collective-permute-start) | collective-permute-done | bytes 393248 | tf_op jit(solution)/shard_map/ppermute | solution.py:501
  17.4 1.4 %copy-done.5 = bf16[8,3,256,128]{3,2,1,0:T(8,128)(2,1)S(1)} copy-done((bf16[8,3,256,128]{3,2,1,0:T(8,128)(2,1)S(1)}, bf16[8,3,256,128]{3,2,1,0:T(8,128)(2,1)}, u32[]{:S(2)}) %copy-start.5) | copy-done | bytes 1572888
  18.8 1.7 %shard_map.77 = (f32[512,128]{1,0:T(8,128)S(1)}, bf16[128,3456]{1,0:T(8,128)(2,1)S(1)}, bf16[3,3,256,128]{3,2,1,0:T(8,128)(2,1)S(1)}) custom-call(s32[4]{0:T(128)S(1)} %broadcast_multiply_fusion.offsets, f32[1]{0:T(128)} %bitcast.alive, bf16[8,3,256,128]{3,2,1,0:T(8,128)(2,1)S(1)} %copy-done.5, bf16[3,32,2048]{2,1,0:T(8,128)(2,1)S(1)} %collective-permute-done.halo_ref, ...), custom_call_target="tpu_custom_call" | custom-call | flops 2300000000 | bytes 4538368 | tf_op jit(solution)/shard_map/pallas_call | solution.py:49
  20.6 3.0 %shard_map.78 = (bf16[2,8,2048]{2,1,0:T(8,128)(2,1)}, bf16[128,256]{1,0:T(8,128)(2,1)S(1)}, bf16[16,112,128]{2,1,0:T(8,128)(2,1)S(1)}, bf16[16,112,128]{2,1,0:T(...) custom-call(s32[4]{0:T(128)S(1)} %get-tuple-element.80.offsets, ...), custom_call_target="tpu_custom_call" | custom-call | flops 3449999872 | bytes 4685824 | tf_op jit(solution)/shard_map/pallas_call | solution.py:49
  23.5 0.5 collective-permute-start.8
  24.1 3.0 %shard_map.79 = (bf16[768,128]{1,0:T(8,128)(2,1)S(1)}, f32[256,128]{1,0:T(8,128)S(1)}, bf16[512,128]{1,0:T(8,128)(2,1)S(1)}, bf16[16,32,128]{2,1,0:T(8,128)(2,1)...) custom-call(s32[4]{0:T(128)S(1)} %get-tuple-element.80.offsets, ...), custom_call_target="tpu_custom_call" | custom-call | flops 4024999936 | bytes 5636096 | tf_op jit(solution)/shard_map/pallas_call | solution.py:49
  27.1 0.1 collective-permute-start.9
  27.2 0.5 collective-permute-start.10
  27.7 0.1 add_bitcast_fusion.3
  27.8 0.1 add_convert_fusion
  27.8 0.1 fusion.12
  27.9 0.8 %collective-permute-done.10 = bf16[16,32,128]{2,1,0:T(8,128)(2,1)S(1)} collective-permute-done((bf16[16,32,128]{2,1,0:T(8,128)(2,1)S(1)}, bf16[16,32,128]{2,1,0:T(8,128)(2,1)S(1)}, u32[]{:S(2)}, u32[]{:S(2)}) %collective-permute-start.10) | collective-permute-done | bytes 131104 | tf_op jit(solution)/shard_map/ppermute | solution.py:495
  28.7 1.6 %collective-permute-start.11 = (bf16[2,4,144,128]{3,2,1,0:T(8,128)(2,1)S(1)}, bf16[2,4,144,128]{3,2,1,0:T(8,128)(2,1)S(1)}, u32[]{:S(2)}, u32[]{:S(2)}) collective-permute-start(bf16[2,4,144,128]{3,2,1,0:T(8,128)(2,1)S(1)} %pad_maximum_fusion), channel_id=1, source_target_pairs={{0,16},{8,24},{16,0},{24,8},{1,17},{9,25},{17,1},{25,9},{2,18},{10... | collective-permute-start | bytes 884744 | tf_op jit(solution)/shard_map/ppermute | solution.py:495
  30.4 2.5 %collective-permute-start.13 = (bf16[2,4,144,128]{3,2,1,0:T(8,128)(2,1)S(1)}, bf16[2,4,144,128]{3,2,1,0:T(8,128)(2,1)S(1)}, u32[]{:S(2)}, u32[]{:S(2)}) collective-permute-start(bf16[2,4,144,128]{3,2,1,0:T(8,128)(2,1)S(1)} %pad_maximum_fusion.1), channel_id=1, source_target_pairs={{0,1},{1,0},{2,3},{3,2},{4,5},{5,4},{6,7},{7,6},{8,9},{9,8},{10,11... | collective-permute-start | bytes 884744 | tf_op jit(solution)/shard_map/ppermute | solution.py:495
  33.0 1.3 %collective-permute-start.15 = (bf16[512,128]{1,0:T(8,128)(2,1)S(1)}, bf16[512,128]{1,0:T(8,128)(2,1)S(1)}, u32[]{:S(2)}, u32[]{:S(2)}) collective-permute-start(bf16[512,128]{1,0:T(8,128)(2,1)S(1)} %get-tuple-element.59), channel_id=1, source_target_pairs={{1,0},{2,1},{3,2},{4,3},{5,4},{6,5},{7,6},{9,8},{10,9},{11,10},{12... | collective-permute-start | bytes 393224 | tf_op jit(solution)/shard_map/ppermute | solution.py:501
  34.3 3.8 %collective-permute-done.11 = bf16[2,4,144,128]{3,2,1,0:T(8,128)(2,1)S(1)} collective-permute-done((bf16[2,4,144,128]{3,2,1,0:T(8,128)(2,1)S(1)}, bf16[2,4,144,128]{3,2,1,0:T(8,128)(2,1)S(1)}, u32[]{:S(2)}, u32[]{:S(2)}) %collective-permute-start.11) | collective-permute-done | bytes 294944 | tf_op jit(solution)/shard_map/ppermute | solution.py:495
  38.1 2.5 %collective-permute-start.12 = (bf16[4,144,128]{2,1,0:T(8,128)(2,1)S(1)}, bf16[4,144,128]{2,1,0:T(8,128)(2,1)S(1)}, u32[]{:S(2)}, u32[]{:S(2)}) collective-permute-start(bf16[4,144,128]{2,1,0:T(8,128)(2,1)S(1)} %fusion.2), channel_id=1, source_target_pairs={{0,1},{1,0},{2,3},{3,2},{4,5},{5,4},{6,7},{7,6},{8,9},{9,8},{10,11... | collective-permute-start | bytes 442376 | tf_op jit(solution)/shard_map/ppermute | solution.py:495
  40.6 2.6 %collective-permute-done.13 = bf16[2,4,144,128]{3,2,1,0:T(8,128)(2,1)S(1)} collective-permute-done((bf16[2,4,144,128]{3,2,1,0:T(8,128)(2,1)S(1)}, bf16[2,4,144,128]{3,2,1,0:T(8,128)(2,1)S(1)}, u32[]{:S(2)}, u32[]{:S(2)}) %collective-permute-start.13) | collective-permute-done | bytes 294944 | tf_op jit(solution)/shard_map/ppermute | solution.py:495
  43.2 0.6 collective-permute-start.14
  43.8 2.4 %collective-permute-done.12 = bf16[4,144,128]{2,1,0:T(8,128)(2,1)S(1)} collective-permute-done((bf16[4,144,128]{2,1,0:T(8,128)(2,1)S(1)}, bf16[4,144,128]{2,1,0:T(8,128)(2,1)S(1)}, u32[]{:S(2)}, u32[]{:S(2)}) %collective-permute-start.12) | collective-permute-done | bytes 147488 | tf_op jit(solution)/shard_map/ppermute | solution.py:495
  46.2 0.1 fusion.7
  46.2 2.2 %collective-permute-done.14 = bf16[4,144,128]{2,1,0:T(8,128)(2,1)S(1)} collective-permute-done((bf16[4,144,128]{2,1,0:T(8,128)(2,1)S(1)}, bf16[4,144,128]{2,1,0:T(8,128)(2,1)S(1)}, u32[]{:S(2)}, u32[]{:S(2)}) %collective-permute-start.14) | collective-permute-done | bytes 147488 | tf_op jit(solution)/shard_map/ppermute | solution.py:495
  48.4 0.1 fusion.6
  48.6 1.6 %collective-permute-start.16 = (bf16[2,144,128]{2,1,0:T(8,128)(2,1)S(1)}, bf16[2,144,128]{2,1,0:T(8,128)(2,1)S(1)}, u32[]{:S(2)}, u32[]{:S(2)}) collective-permute-start(bf16[2,144,128]{2,1,0:T(8,128)(2,1)S(1)} %get-tuple-element.70), channel_id=1, source_target_pairs={{0,2},{1,3},{2,0},{3,1},{4,6},{5,7},{6,4},{7,5},{8,10},{9,11},{10,... | collective-permute-start | bytes 221192 | tf_op jit(solution)/shard_map/ppermute | solution.py:495
  50.2 2.5 %collective-permute-start.18 = (bf16[2,144,128]{2,1,0:T(8,128)(2,1)S(1)}, bf16[2,144,128]{2,1,0:T(8,128)(2,1)S(1)}, u32[]{:S(2)}, u32[]{:S(2)}) collective-permute-start(bf16[2,144,128]{2,1,0:T(8,128)(2,1)S(1)} %get-tuple-element.71), channel_id=1, source_target_pairs={{0,6},{1,7},{2,4},{3,5},{4,2},{5,3},{6,0},{7,1},{8,14},{9,15},{10,... | collective-permute-start | bytes 221192 | tf_op jit(solution)/shard_map/ppermute | solution.py:495
  52.7 1.1 %collective-permute-done.16 = bf16[2,144,128]{2,1,0:T(8,128)(2,1)S(1)} collective-permute-done((bf16[2,144,128]{2,1,0:T(8,128)(2,1)S(1)}, bf16[2,144,128]{2,1,0:T(8,128)(2,1)S(1)}, u32[]{:S(2)}, u32[]{:S(2)}) %collective-permute-start.16) | collective-permute-done | bytes 73760 | tf_op jit(solution)/shard_map/ppermute | solution.py:495
  53.8 2.6 %collective-permute-done.18 = bf16[2,144,128]{2,1,0:T(8,128)(2,1)S(1)} collective-permute-done((bf16[2,144,128]{2,1,0:T(8,128)(2,1)S(1)}, bf16[2,144,128]{2,1,0:T(8,128)(2,1)S(1)}, u32[]{:S(2)}, u32[]{:S(2)}) %collective-permute-start.18) | collective-permute-done | bytes 73760 | tf_op jit(solution)/shard_map/ppermute | solution.py:495
  56.4 2.0 %collective-permute-done.17 = bf16[2,144,128]{2,1,0:T(8,128)(2,1)S(1)} collective-permute-done((bf16[2,144,128]{2,1,0:T(8,128)(2,1)S(1)}, bf16[2,144,128]{2,1,0:T(8,128)(2,1)S(1)}, u32[]{:S(2)}, u32[]{:S(2)}) %collective-permute-start.17) | collective-permute-done | bytes 73760 | tf_op jit(solution)/shard_map/ppermute | solution.py:495
  58.4 2.1 %collective-permute-start.19 = (bf16[2,144,128]{2,1,0:T(8,128)(2,1)S(1)}, bf16[2,144,128]{2,1,0:T(8,128)(2,1)S(1)}, u32[]{:S(2)}, u32[]{:S(2)}) collective-permute-start(bf16[2,144,128]{2,1,0:T(8,128)(2,1)S(1)} %fusion.10), channel_id=1, source_target_pairs={{0,1},{1,0},{2,3},{3,2},{4,5},{5,4},{6,7},{7,6},{8,9},{9,8},{10,11... | collective-permute-start | bytes 221192 | tf_op jit(solution)/shard_map/ppermute | solution.py:495
  60.5 2.3 %collective-permute-done.19 = bf16[2,144,128]{2,1,0:T(8,128)(2,1)S(1)} collective-permute-done((bf16[2,144,128]{2,1,0:T(8,128)(2,1)S(1)}, bf16[2,144,128]{2,1,0:T(8,128)(2,1)S(1)}, u32[]{:S(2)}, u32[]{:S(2)}) %collective-permute-start.19) | collective-permute-done | bytes 73760 | tf_op jit(solution)/shard_map/ppermute | solution.py:495
  62.9 2.5 %collective-permute-start.22 = (bf16[2,2,144,128]{3,2,1,0:T(8,128)(2,1)S(1)}, bf16[2,2,144,128]{3,2,1,0:T(8,128)(2,1)S(1)}, u32[]{:S(2)}, u32[]{:S(2)}) collective-permute-start(bf16[2,2,144,128]{3,2,1,0:T(8,128)(2,1)S(1)} %pad_maximum_fusion.3.refs_0_), channel_id=1, source_target_pairs={{0,6},{1,7},{2,4},{3,5},{4,2},{5,3},{6,0},{7,1},{8,14},{9,15},{10,... | collective-permute-start | bytes 442376 | tf_op jit(solution)/shard_map/ppermute | solution.py:495
  65.4 1.9 %collective-permute-start.20 = (bf16[2,2,144,128]{3,2,1,0:T(8,128)(2,1)S(1)}, bf16[2,2,144,128]{3,2,1,0:T(8,128)(2,1)S(1)}, u32[]{:S(2)}, u32[]{:S(2)}) collective-permute-start(bf16[2,2,144,128]{3,2,1,0:T(8,128)(2,1)S(1)} %pad_maximum_fusion.3.refs_0_), channel_id=1, source_target_pairs={{0,2},{1,3},{2,0},{3,1},{4,6},{5,7},{6,4},{7,5},{8,10},{9,11},{10,... | collective-permute-start | bytes 442376 | tf_op jit(solution)/shard_map/ppermute | solution.py:495
  67.3 2.8 %shard_map.80 = bf16[8,32,2048]{2,1,0:T(8,128)(2,1)} custom-call(s32[4]{0:T(128)S(1)} %broadcast_multiply_fusion.offsets, bf16[768,128]{1,0:T(8,128)(2,1)S(1)} %get-tuple-element.43.low_ref, f32[256,128]{1,0:T(8,128)S(1)} %get-tuple-element.44.last_ref, f32[768,128]{1,0:T(8,128)S(1)} %get-tuple-element.41.slope_ref, ...), custom_call_target="tpu_custom_call" | custom-call | flops 3449999872 | bytes 2342912 | tf_op jit(solution)/shard_map/pallas_call | solution.py:49
  70.1 1.4 %collective-permute-done.22.refs_3_ = bf16[2,2,144,128]{3,2,1,0:T(8,128)(2,1)S(1)} collective-permute-done((bf16[2,2,144,128]{3,2,1,0:T(8,128)(2,1)S(1)}, bf16[2,2,144,128]{3,2,1,0:T(8,128)(2,1)S(1)}, u32[]{:S(2)}, u32[]{:S(2)}) %collective-permute-start.22) | collective-permute-done | bytes 147488 | tf_op jit(solution)/shard_map/ppermute | solution.py:495
  71.5 4.3 %collective-permute-done.21.refs_2_ = bf16[2,2,144,128]{3,2,1,0:T(8,128)(2,1)S(1)} collective-permute-done((bf16[2,2,144,128]{3,2,1,0:T(8,128)(2,1)S(1)}, bf16[2,2,144,128]{3,2,1,0:T(8,128)(2,1)S(1)}, u32[]{:S(2)}, u32[]{:S(2)}) %collective-permute-start.21) | collective-permute-done | bytes 147488 | tf_op jit(solution)/shard_map/ppermute | solution.py:495
  75.8 1.7 %shard_map.81 = (f32[432,128]{1,0:T(8,128)}, f32[864,256]{1,0:T(8,128)}) custom-call(s32[16]{0:T(128)S(1)} %pad_add_fusion.order, bf16[2,2,144,128]{3,2,1,0:T(8,128)(2,1)S(1)} %pad_maximum_fusion.3.refs_0_, bf16[2,2,144,128]{3,2,1,0:T(8,128)(2,1)S(1)} %collective-permute-done.20.refs_1_, bf16[2,2,144,128]{3,2,1,0:T(8,128)(2,1)S(1)} %collective-permute-done.21.refs_2_, ...), custom_call_target="tpu_custom_call" | custom-call | flops 1150000000 | bytes 1695744 | tf_op jit(solution)/shard_map/pallas_call | solution.py:49
  (42 shorter events, 0.4 us)
Async XLA Ops:
  0.6 10.1 %collective-permute-start.3 = (bf16[432,128]{1,0:T(8,128)(2,1)}, bf16[432,128]{1,0:T(8,128)(2,1)S(1)}, u32[]{:S(2)}, u32[]{:S(2)}) collective-permute-start(bf16[432,128]{1,0:T(8,128)(2,1)} %w0.9), channel_id=1, source_target_pairs={{0,16},{8,24},{16,0},{24,8},{1,17},{9,25},{17,1},{25,9},{2,18},{10... | collective-permute-start | bytes 331784 | tf_op jit(solution)/shard_map/ppermute | solution.py:495
  3.6 7.2 %collective-permute-start.2 = (bf16[432,128]{1,0:T(8,128)(2,1)}, bf16[432,128]{1,0:T(8,128)(2,1)S(1)}, u32[]{:S(2)}, u32[]{:S(2)}) collective-permute-start(bf16[432,128]{1,0:T(8,128)(2,1)} %w0.9), channel_id=1, source_target_pairs={{0,8},{8,0},{16,24},{24,16},{1,9},{9,1},{17,25},{25,17},{2,10},{10... | collective-permute-start | bytes 331784 | tf_op jit(solution)/shard_map/ppermute | solution.py:495
  3.6 16.9 %collective-permute-start.5 = (bf16[864,256]{1,0:T(8,128)(2,1)}, bf16[864,256]{1,0:T(8,128)(2,1)S(1)}, u32[]{:S(2)}, u32[]{:S(2)}) collective-permute-start(bf16[864,256]{1,0:T(8,128)(2,1)} %w0.8), channel_id=1, source_target_pairs={{0,8},{8,0},{16,24},{24,16},{1,9},{9,1},{17,25},{25,17},{2,10},{10... | collective-permute-start | bytes 1327112 | tf_op jit(solution)/shard_map/ppermute | solution.py:495
  4.1 12.3 %collective-permute-start.1 = (bf16[864,256]{1,0:T(8,128)(2,1)}, bf16[864,256]{1,0:T(8,128)(2,1)S(1)}, u32[]{:S(2)}, u32[]{:S(2)}) collective-permute-start(bf16[864,256]{1,0:T(8,128)(2,1)} %w0.8), channel_id=1, source_target_pairs={{0,16},{8,24},{16,0},{24,8},{1,17},{9,25},{17,1},{25,9},{2,18},{10... | collective-permute-start | bytes 1327112 | tf_op jit(solution)/shard_map/ppermute | solution.py:495
  5.2 12.1 %collective-permute-start = (bf16[3,32,2048]{2,1,0:T(8,128)(2,1)S(1)}, bf16[3,32,2048]{2,1,0:T(8,128)(2,1)S(1)}, u32[]{:S(2)}, u32[]{:S(2)}) collective-permute-start(bf16[3,32,2048]{2,1,0:T(8,128)(2,1)S(1)} %slice_bitcast_fusion), channel_id=1, source_target_pairs={{0,1},{1,2},{2,3},{3,4},{4,5},{5,6},{6,7},{8,9},{9,10},{10,11},{11... | collective-permute-start | bytes 1179656 | tf_op jit(solution)/shard_map/ppermute | solution.py:501
  9.2 1.2 %copy-start = (bf16[1,8,32,2048]{3,2,1,0:T(8,128)(2,1)S(1)}, bf16[1,8,32,2048]{3,2,1,0:T(8,128)(2,1)}, u32[]{:S(2)}) copy-start(bf16[1,8,32,2048]{3,2,1,0:T(8,128)(2,1)} %param.4) | copy-start | bytes 3145732
  10.4 1.8 %copy-start.2 = (bf16[432,128]{1,0:T(8,128)(2,1)S(1)}, bf16[432,128]{1,0:T(8,128)(2,1)}, u32[]{:S(2)}) copy-start(bf16[432,128]{1,0:T(8,128)(2,1)} %w0.9) | copy-start | bytes 331780
  10.7 3.2 %copy-start.4 = (bf16[8,3,256,128]{3,2,1,0:T(8,128)(2,1)}, bf16[8,3,256,128]{3,2,1,0:T(8,128)(2,1)S(1)}, u32[]{:S(2)}) copy-start(bf16[8,3,256,128]{3,2,1,0:T(8,128)(2,1)S(1)} %shard_map.75.sorted_ref) | copy-start | bytes 4718596
  10.8 1.4 %collective-permute-start.4 = (bf16[432,128]{1,0:T(8,128)(2,1)S(1)}, bf16[432,128]{1,0:T(8,128)(2,1)S(1)}, u32[]{:S(2)}, u32[]{:S(2)}) collective-permute-start(bf16[432,128]{1,0:T(8,128)(2,1)S(1)} %collective-permute-done.3.w2), channel_id=1, source_target_pairs={{0,8},{8,0},{16,24},{24,16},{1,9},{9,1},{17,25},{25,17},{2,10},{10... | collective-permute-start | bytes 331784 | tf_op jit(solution)/shard_map/ppermute | solution.py:495
  16.4 4.1 %collective-permute-start.6 = (bf16[864,256]{1,0:T(8,128)(2,1)S(1)}, bf16[864,256]{1,0:T(8,128)(2,1)S(1)}, u32[]{:S(2)}, u32[]{:S(2)}) collective-permute-start(bf16[864,256]{1,0:T(8,128)(2,1)S(1)} %collective-permute-done.1.w2), channel_id=1, source_target_pairs={{0,8},{8,0},{16,24},{24,16},{1,9},{9,1},{17,25},{25,17},{2,10},{10... | collective-permute-start | bytes 1327112 | tf_op jit(solution)/shard_map/ppermute | solution.py:495
  17.4 1.4 %copy-start.5 = (bf16[8,3,256,128]{3,2,1,0:T(8,128)(2,1)S(1)}, bf16[8,3,256,128]{3,2,1,0:T(8,128)(2,1)}, u32[]{:S(2)}) copy-start(bf16[8,3,256,128]{3,2,1,0:T(8,128)(2,1)} %copy-done.4) | copy-start | bytes 4718596
  18.8 1.7 %copy-start.1 = (bf16[864,256]{1,0:T(8,128)(2,1)S(1)}, bf16[864,256]{1,0:T(8,128)(2,1)}, u32[]{:S(2)}) copy-start(bf16[864,256]{1,0:T(8,128)(2,1)} %w0.8) | copy-start | bytes 1327108
  18.8 1.8 %copy-start.3 = (bf16[1,2,8,2048]{3,2,1,0:T(8,128)(2,1)S(1)}, bf16[1,2,8,2048]{3,2,1,0:T(8,128)(2,1)}, u32[]{:S(2)}) copy-start(bf16[1,2,8,2048]{3,2,1,0:T(8,128)(2,1)} %param.7) | copy-start | bytes 196612
  20.6 3.5 %copy-start.6 = (bf16[8,3,256,128]{3,2,1,0:T(8,128)(2,1)S(1)}, bf16[8,3,256,128]{3,2,1,0:T(8,128)(2,1)}, u32[]{:S(2)}) copy-start(bf16[8,3,256,128]{3,2,1,0:T(8,128)(2,1)} %copy-done.4) | copy-start | bytes 4718596
  23.5 3.5 %collective-permute-start.7 = (bf16[16,112,128]{2,1,0:T(8,128)(2,1)S(1)}, bf16[16,112,128]{2,1,0:T(8,128)(2,1)S(1)}, u32[]{:S(2)}, u32[]{:S(2)}) collective-permute-start(bf16[16,112,128]{2,1,0:T(8,128)(2,1)S(1)} %get-tuple-element.50), channel_id=1, source_target_pairs={{0,8},{8,0},{16,24},{24,16},{1,9},{9,1},{17,25},{25,17},{2,10},{10... | collective-permute-start | bytes 1376264 | tf_op jit(solution)/shard_map/ppermute | solution.py:495
  23.5 3.5 %collective-permute-start.8 = (bf16[16,112,128]{2,1,0:T(8,128)(2,1)S(1)}, bf16[16,112,128]{2,1,0:T(8,128)(2,1)S(1)}, u32[]{:S(2)}, u32[]{:S(2)}) collective-permute-start(bf16[16,112,128]{2,1,0:T(8,128)(2,1)S(1)} %get-tuple-element.51), channel_id=1, source_target_pairs={{0,8},{8,0},{16,24},{24,16},{1,9},{9,1},{17,25},{25,17},{2,10},{10... | collective-permute-start | bytes 1376264 | tf_op jit(solution)/shard_map/ppermute | solution.py:495
  27.1 3.2 %collective-permute-start.9 = (bf16[16,32,128]{2,1,0:T(8,128)(2,1)S(1)}, bf16[16,32,128]{2,1,0:T(8,128)(2,1)S(1)}, u32[]{:S(2)}, u32[]{:S(2)}) collective-permute-start(bf16[16,32,128]{2,1,0:T(8,128)(2,1)S(1)} %get-tuple-element.54), channel_id=1, source_target_pairs={{0,8},{8,0},{16,24},{24,16},{1,9},{9,1},{17,25},{25,17},{2,10},{10... | collective-permute-start | bytes 393224 | tf_op jit(solution)/shard_map/ppermute | solution.py:495
  27.2 1.5 %collective-permute-start.10 = (bf16[16,32,128]{2,1,0:T(8,128)(2,1)S(1)}, bf16[16,32,128]{2,1,0:T(8,128)(2,1)S(1)}, u32[]{:S(2)}, u32[]{:S(2)}) collective-permute-start(bf16[16,32,128]{2,1,0:T(8,128)(2,1)S(1)} %get-tuple-element.58), channel_id=1, source_target_pairs={{0,8},{8,0},{16,24},{24,16},{1,9},{9,1},{17,25},{25,17},{2,10},{10... | collective-permute-start | bytes 393224 | tf_op jit(solution)/shard_map/ppermute | solution.py:495
  28.7 9.3 %collective-permute-start.11 = (bf16[2,4,144,128]{3,2,1,0:T(8,128)(2,1)S(1)}, bf16[2,4,144,128]{3,2,1,0:T(8,128)(2,1)S(1)}, u32[]{:S(2)}, u32[]{:S(2)}) collective-permute-start(bf16[2,4,144,128]{3,2,1,0:T(8,128)(2,1)S(1)} %pad_maximum_fusion), channel_id=1, source_target_pairs={{0,16},{8,24},{16,0},{24,8},{1,17},{9,25},{17,1},{25,9},{2,18},{10... | collective-permute-start | bytes 884744 | tf_op jit(solution)/shard_map/ppermute | solution.py:495
  30.4 12.7 %collective-permute-start.13 = (bf16[2,4,144,128]{3,2,1,0:T(8,128)(2,1)S(1)}, bf16[2,4,144,128]{3,2,1,0:T(8,128)(2,1)S(1)}, u32[]{:S(2)}, u32[]{:S(2)}) collective-permute-start(bf16[2,4,144,128]{3,2,1,0:T(8,128)(2,1)S(1)} %pad_maximum_fusion.1), channel_id=1, source_target_pairs={{0,1},{1,0},{2,3},{3,2},{4,5},{5,4},{6,7},{7,6},{8,9},{9,8},{10,11... | collective-permute-start | bytes 884744 | tf_op jit(solution)/shard_map/ppermute | solution.py:495
  33.0 15.5 %collective-permute-start.15 = (bf16[512,128]{1,0:T(8,128)(2,1)S(1)}, bf16[512,128]{1,0:T(8,128)(2,1)S(1)}, u32[]{:S(2)}, u32[]{:S(2)}) collective-permute-start(bf16[512,128]{1,0:T(8,128)(2,1)S(1)} %get-tuple-element.59), channel_id=1, source_target_pairs={{1,0},{2,1},{3,2},{4,3},{5,4},{6,5},{7,6},{9,8},{10,9},{11,10},{12... | collective-permute-start | bytes 393224 | tf_op jit(solution)/shard_map/ppermute | solution.py:501
  38.1 8.1 %collective-permute-start.12 = (bf16[4,144,128]{2,1,0:T(8,128)(2,1)S(1)}, bf16[4,144,128]{2,1,0:T(8,128)(2,1)S(1)}, u32[]{:S(2)}, u32[]{:S(2)}) collective-permute-start(bf16[4,144,128]{2,1,0:T(8,128)(2,1)S(1)} %fusion.2), channel_id=1, source_target_pairs={{0,1},{1,0},{2,3},{3,2},{4,5},{5,4},{6,7},{7,6},{8,9},{9,8},{10,11... | collective-permute-start | bytes 442376 | tf_op jit(solution)/shard_map/ppermute | solution.py:495
  43.2 5.2 %collective-permute-start.14 = (bf16[4,144,128]{2,1,0:T(8,128)(2,1)S(1)}, bf16[4,144,128]{2,1,0:T(8,128)(2,1)S(1)}, u32[]{:S(2)}, u32[]{:S(2)}) collective-permute-start(bf16[4,144,128]{2,1,0:T(8,128)(2,1)S(1)} %fusion.5), channel_id=1, source_target_pairs={{0,16},{8,24},{16,0},{24,8},{1,17},{9,25},{17,1},{25,9},{2,18},{10... | collective-permute-start | bytes 442376 | tf_op jit(solution)/shard_map/ppermute | solution.py:495
  48.6 5.2 %collective-permute-start.16 = (bf16[2,144,128]{2,1,0:T(8,128)(2,1)S(1)}, bf16[2,144,128]{2,1,0:T(8,128)(2,1)S(1)}, u32[]{:S(2)}, u32[]{:S(2)}) collective-permute-start(bf16[2,144,128]{2,1,0:T(8,128)(2,1)S(1)} %get-tuple-element.70), channel_id=1, source_target_pairs={{0,2},{1,3},{2,0},{3,1},{4,6},{5,7},{6,4},{7,5},{8,10},{9,11},{10,... | collective-permute-start | bytes 221192 | tf_op jit(solution)/shard_map/ppermute | solution.py:495
  50.2 6.2 %collective-permute-start.18 = (bf16[2,144,128]{2,1,0:T(8,128)(2,1)S(1)}, bf16[2,144,128]{2,1,0:T(8,128)(2,1)S(1)}, u32[]{:S(2)}, u32[]{:S(2)}) collective-permute-start(bf16[2,144,128]{2,1,0:T(8,128)(2,1)S(1)} %get-tuple-element.71), channel_id=1, source_target_pairs={{0,6},{1,7},{2,4},{3,5},{4,2},{5,3},{6,0},{7,1},{8,14},{9,15},{10,... | collective-permute-start | bytes 221192 | tf_op jit(solution)/shard_map/ppermute | solution.py:495
  52.7 5.7 %collective-permute-start.17 = (bf16[2,144,128]{2,1,0:T(8,128)(2,1)S(1)}, bf16[2,144,128]{2,1,0:T(8,128)(2,1)S(1)}, u32[]{:S(2)}, u32[]{:S(2)}) collective-permute-start(bf16[2,144,128]{2,1,0:T(8,128)(2,1)S(1)} %get-tuple-element.72), channel_id=1, source_target_pairs={{0,4},{1,5},{2,6},{3,7},{4,0},{5,1},{6,2},{7,3},{8,12},{9,13},{10,... | collective-permute-start | bytes 221192 | tf_op jit(solution)/shard_map/ppermute | solution.py:495
  58.4 4.4 %collective-permute-start.19 = (bf16[2,144,128]{2,1,0:T(8,128)(2,1)S(1)}, bf16[2,144,128]{2,1,0:T(8,128)(2,1)S(1)}, u32[]{:S(2)}, u32[]{:S(2)}) collective-permute-start(bf16[2,144,128]{2,1,0:T(8,128)(2,1)S(1)} %fusion.10), channel_id=1, source_target_pairs={{0,1},{1,0},{2,3},{3,2},{4,5},{5,4},{6,7},{7,6},{8,9},{9,8},{10,11... | collective-permute-start | bytes 221192 | tf_op jit(solution)/shard_map/ppermute | solution.py:495
  62.9 8.6 %collective-permute-start.22 = (bf16[2,2,144,128]{3,2,1,0:T(8,128)(2,1)S(1)}, bf16[2,2,144,128]{3,2,1,0:T(8,128)(2,1)S(1)}, u32[]{:S(2)}, u32[]{:S(2)}) collective-permute-start(bf16[2,2,144,128]{3,2,1,0:T(8,128)(2,1)S(1)} %pad_maximum_fusion.3.refs_0_), channel_id=1, source_target_pairs={{0,6},{1,7},{2,4},{3,5},{4,2},{5,3},{6,0},{7,1},{8,14},{9,15},{10,... | collective-permute-start | bytes 442376 | tf_op jit(solution)/shard_map/ppermute | solution.py:495
  65.4 10.4 %collective-permute-start.21 = (bf16[2,2,144,128]{3,2,1,0:T(8,128)(2,1)S(1)}, bf16[2,2,144,128]{3,2,1,0:T(8,128)(2,1)S(1)}, u32[]{:S(2)}, u32[]{:S(2)}) collective-permute-start(bf16[2,2,144,128]{3,2,1,0:T(8,128)(2,1)S(1)} %pad_maximum_fusion.3.refs_0_), channel_id=1, source_target_pairs={{0,4},{1,5},{2,6},{3,7},{4,0},{5,1},{6,2},{7,3},{8,12},{9,13},{10,... | collective-permute-start | bytes 442376 | tf_op jit(solution)/shard_map/ppermute | solution.py:495
  65.4 10.4 %collective-permute-start.20 = (bf16[2,2,144,128]{3,2,1,0:T(8,128)(2,1)S(1)}, bf16[2,2,144,128]{3,2,1,0:T(8,128)(2,1)S(1)}, u32[]{:S(2)}, u32[]{:S(2)}) collective-permute-start(bf16[2,2,144,128]{3,2,1,0:T(8,128)(2,1)S(1)} %pad_maximum_fusion.3.refs_0_), channel_id=1, source_target_pairs={{0,2},{1,3},{2,0},{3,1},{4,6},{5,7},{6,4},{7,5},{8,10},{9,11},{10,... | collective-permute-start | bytes 442376 | tf_op jit(solution)/shard_map/ppermute | solution.py:495

commit v3 on v2

--- a/solution.py
+++ b/solution.py
@@ -10,7 +10,7 @@
 LEAK_SLOPE = 0.2
 F32 = jnp.float32
 BF16 = jnp.bfloat16
-VMEM_LIMIT = 48 * 1024 * 1024
+VMEM_LIMIT = 24 * 1024 * 1024
 
 
 def activate(values):
@@ -98,20 +98,23 @@
         dst[pl.ds(pl.multiple_of(offsets[index], 16), rows), :] = piece[...]
 
 
-def gather_taps(columns, sorted_ref, halo_ref, first, count, base):
+def put_tap(columns, at, left, source):
+    rows = source.shape[0]
+    columns[at : at + 16, left : left + 128] = jnp.zeros((16, 128), BF16)
+    columns[at + 16 : at + rows, left : left + 128] = source[0 : rows - 16, :]
+    columns[at : at + rows, left + 128 : left + 256] = source[...]
+
+
+def gather_taps(columns, sorted_ref, halo_ref, first, count):
     rows = sorted_ref.shape[2]
     for cell in range(count):
-        at = base + cell * rows
         for a in range(3):
             plane = 2 * (first + cell) - 1 + a
             for e in range(3):
                 source = (
                     halo_ref.at[halo_ref.shape[0] + plane, e] if plane < 0 else sorted_ref.at[plane, e]
                 )
-                left = (a * 3 + e) * 256
-                columns[at : at + 16, left : left + 128] = jnp.zeros((16, 128), BF16)
-                columns[at + 16 : at + rows, left : left + 128] = source[0 : rows - 16, :]
-                columns[at : at + rows, left + 128 : left + 256] = source[...]
+                put_tap(columns, cell * rows, (a * 3 + e) * 256, source)
 
 
 def pad_first(whole, padded):
@@ -135,16 +138,20 @@
 
 
 def forward_upper_kernel(
-    offsets, sorted_ref, w0, w1, w2, w3, slope_ref, hidden_ref, columns, whole, padded
+    offsets, sorted_ref, w0, w1, w2, w3,
+    slope_ref, hidden_ref, partial_ref, padded_ref, columns, some, whole,
 ):
     cells = sorted_ref.shape[0] // 2
     put_rows(whole, (w0, w1, w2, w3), offsets)
-    pad_first(whole, padded)
-    gather_taps(columns, sorted_ref, None, 1, cells - 1, 0)
-    linear = jnp.dot(columns[...], padded[...], preferred_element_type=F32)
-    hidden = activate(linear)
-    hidden_ref[...] = hidden.reshape(hidden_ref.shape)
+    pad_first(whole, padded_ref)
+    gather_taps(columns, sorted_ref, None, 1, cells - 1)
+    linear = jnp.dot(columns[...], padded_ref[...], preferred_element_type=F32)
+    hidden_ref[...] = activate(linear).reshape(hidden_ref.shape)
     slope_ref[...] = activate_slope(linear)
+    for a in range(1, 3):
+        for e in range(3):
+            put_tap(some, 0, ((a - 1) * 3 + e) * 256, sorted_ref.at[a - 1, e])
+    partial_ref[...] = jnp.dot(some[...], padded_ref[3 * 256 :, :], preferred_element_type=F32)
 
 
 def forward_upper(sorted_volume, shards, offsets):
@@ -157,11 +164,13 @@
         (
             sds((some, 128), F32),
             sds((cells - 1, rows // 32, 2, 2, 8, 128), F32),
+            sds((rows, 128), F32),
+            sds((9 * 256, 128), BF16),
         ),
         [
             pltpu.VMEM((some, 9 * 256), BF16),
+            pltpu.VMEM((rows, 6 * 256), BF16),
             pltpu.VMEM((4 * shard, 128), BF16),
-            pltpu.VMEM((9 * 256, 128), BF16),
         ],
         sorted_volume, *shards,
         smem=(offsets,),
@@ -170,20 +179,25 @@
 
 
 def forward_lower_kernel(
-    offsets, alive, sorted_ref, halo_ref, hidden_ref, w0, w1, w2, w3,
-    slope_ref, windows_ref, sorted_halo, wide, columns, whole, padded, lowest,
+    alive, halo_ref, hidden_ref, partial_ref, padded_ref,
+    slope_ref, windows_ref, sorted_ref, wide, columns, some, lowest,
 ):
-    rows = sorted_ref.shape[2]
-    cells = sorted_ref.shape[0] // 2
+    rows = partial_ref.shape[0]
+    cells = hidden_ref.shape[0] + 1
     half = rows // 32
-    sort_kernel(halo_ref.shape[0], halo_ref, sorted_halo, wide)
-    put_rows(whole, (w0, w1, w2, w3), offsets)
-    pad_first(whole, padded)
-    gather_taps(columns, sorted_ref, sorted_halo, -1, 2, 0)
-    linear = jnp.dot(columns[...], padded[...], preferred_element_type=F32)
-    slope_ref[...] = activate_slope(linear)
-    lowest[...] = activate(linear).reshape(lowest.shape)
-    lowest[0] = lowest[0] * alive[0]
+    sort_kernel(halo_ref.shape[0], halo_ref, sorted_ref, wide)
+    for e in range(3):
+        for a in range(3):
+            put_tap(columns, 0, (a * 3 + e) * 256, sorted_ref.at[a, e])
+        put_tap(some, 0, e * 256, sorted_ref.at[2, e])
+    below = jnp.dot(columns[...], padded_ref[...], preferred_element_type=F32)
+    here = partial_ref[...] + jnp.dot(
+        some[...], padded_ref[: 3 * 256, :], preferred_element_type=F32
+    )
+    slope_ref[:rows, :] = activate_slope(below)
+    slope_ref[rows:, :] = activate_slope(here)
+    lowest[0] = (activate(below) * alive[0]).reshape(lowest.shape[1:])
+    lowest[1] = activate(here).reshape(lowest.shape[1:])
     for out in range(cells // 2):
         for a in range(3):
             plane = 2 * out - 1 + a
@@ -195,10 +209,9 @@
             take_windows(read, windows_ref, out, a, half)
 
 
-def forward_lower(sorted_volume, halo, hidden, shards, offsets, alive):
-    planes, _, rows, _ = sorted_volume.shape
-    cells = planes // 2
-    shard = shards[0].shape[0]
+def forward_lower(halo, hidden, partial, padded, alive):
+    rows = partial.shape[0]
+    cells = hidden.shape[0] + 1
     return call(
         forward_lower_kernel,
         (
@@ -208,14 +221,13 @@
         ),
         [
             pltpu.VMEM((rows // 16, halo.shape[1], 128), F32),
-            pltpu.VMEM((2 * rows, 9 * 256), BF16),
-            pltpu.VMEM((4 * shard, 128), BF16),
-            pltpu.VMEM((9 * 256, 128), BF16),
+            pltpu.VMEM((rows, 9 * 256), BF16),
+            pltpu.VMEM((rows, 3 * 256), BF16),
             pltpu.VMEM((2, *hidden.shape[1:]), F32),
         ],
-        sorted_volume, halo, hidden, *shards,
-        smem=(offsets, alive),
-        micros=2.0,
+        halo, hidden, partial, padded,
+        smem=(alive,),
+        micros=1.5,
     )
 
 
@@ -302,7 +314,7 @@
     product[...] = lax.dot_general(
         delta_ref[...], whole[...], (((1,), (1,)), ((), ())), preferred_element_type=F32
     )
-    gather_taps(columns, sorted_ref, halo_ref, -1, cells + 1, 0)
+    gather_taps(columns, sorted_ref, halo_ref, -1, cells + 1)
 
     def term(out, a, e, f):
         left = ((a * 3 + e) * 3 + f) * 128
@@ -462,18 +474,16 @@
 
 
 def unpack_kernel(scale_first, scale_second, order, *refs):
-    *chunks, first_ref, second_ref, flat_first, flat_second = refs
+    *chunks, other, first_ref, second_ref, flat_first, flat_second = refs
     high = len(chunks)
-    small = flat_first.shape[0] // (4 * high)
-    big = flat_second.shape[0] // (4 * high)
-    for index, chunk in enumerate(chunks):
-        for low in range(2):
-            for part in range(2):
-                place = order[(part * 2 + low) * high + index]
-                row = pl.multiple_of(place * big, 16)
-                flat_second[pl.ds(row, big), :] = chunk[low, part, :big, :]
-                row = pl.multiple_of(place * small, 16)
-                flat_first[pl.ds(row, small), :] = chunk[low, part, big:, :]
+    small = flat_first.shape[0] // (2 * high)
+    big = flat_second.shape[0] // (2 * high)
+    for low in range(2):
+        for index in range(high):
+            chunk = other.at[index] if low else chunks[index]
+            place = order[low * high + index]
+            flat_second[pl.ds(pl.multiple_of(place * big, 16), big), :] = chunk[:big, :]
+            flat_first[pl.ds(pl.multiple_of(place * small, 16), small), :] = chunk[big:, :]
     rows, features = second_ref.shape
     for lane in range(features // 128):
         second_ref[:, lane * 128 : (lane + 1) * 128] = (
@@ -514,10 +524,9 @@
     alive = (place > 0).astype(F32).reshape(1)
     steps = jnp.arange(spaces, dtype=jnp.int32)
     order = place ^ (2 * (steps % high) + steps // high)
-    order = jnp.concatenate([order, spaces + order])
     lanes = weight_second.shape[1] // 128
-    size_first = -(-small // (32 * spaces)) * 16
-    size_second = -(-lanes * big // (32 * spaces)) * 16
+    size_first = -(-small // (16 * spaces)) * 16
+    size_second = -(-lanes * big // (16 * spaces)) * 16
 
     inputs = volume.reshape(planes, side, width)
     first_x = swap(weight_first, "dp", 2)
@@ -529,24 +538,22 @@
     shards_first = (weight_first, first_core, first_x, first_far)
 
     sorted_volume = sorted_planes(inputs)
-    slope, hidden = forward_upper(sorted_volume, shards_first, offsets_first)
+    slope, hidden, partial, padded = forward_upper(sorted_volume, shards_first, offsets_first)
     second_x, hidden = lax.optimization_barrier((second_x, hidden))
     second_far = swap(second_x, "dp", 1)
     shards_second = (weight_second, second_core, second_x, second_far)
-    slope_low, windows, sorted_halo = forward_lower(
-        sorted_volume, halo, hidden, shards_first, offsets_first, alive
-    )
+    slope_low, windows, sorted_halo = forward_lower(halo, hidden, partial, padded, alive)
     cot = cotangent.reshape(cotangent.shape[1:])
     activations, delta_second, *second = forward_second(
-        windows, cot, shards_second, offsets_second, slots, order, 2 * spaces, size_second,
+        windows, cot, shards_second, offsets_second, slots, order, spaces, size_second,
     )
     low, last, down, *first = back_second(
         delta_second, shards_second, (slope_low, slope), sorted_volume, sorted_halo,
-        offsets_second, slots, order, 2 * spaces, size_first,
+        offsets_second, slots, order, spaces, size_first,
     )
     upper = shifted(down, "space", -1)
     def pieces(value):
-        return value.reshape(2, 2, high, -1, 128)
+        return value.reshape(2, high, -1, 128)
 
     def joined(at, *terms):
         return jnp.concatenate(
@@ -563,25 +570,17 @@
     near = pieces(second_near), pieces(swap(first[1], "dp", 1))
     own = pieces(second[0]), pieces(first[0])
     there = pieces(second[2]), pieces(first[2])
-    got_a = swap(joined(0, there, far).astype(BF16), "dp", 2)
-    got_b = swap(
-        jnp.stack([joined((1, 1), own, near), joined((1, 1), there, far)]).astype(BF16), "space", 1
-    )
-    send_y = added(joined((0, 1), own, near), got_a[1])
-    send_x = added(joined((1, 0), there, far), got_b[1])
-    got_y = swap(send_y, "space", 1)
-    got_x = swap(send_x, "dp", 2)
-    held = jnp.stack(
-        [
-            added(joined((0, 0), own, near), got_a[0], got_y),
-            added(joined((1, 0), own, near), got_b[0], got_x),
-        ],
-        axis=1,
-    )
+    both = [
+        (d * spaces + s, (d ^ 2) * spaces + (s ^ 1)) for d in range(4) for s in range(spaces)
+    ]
+    got_xy = lax.ppermute(joined(1, there, far).astype(BF16), ("dp", "space"), both)
+    got_x = swap(joined(0, there, far).astype(BF16), "dp", 2)
+    got_y = swap(joined(1, own, near).astype(BF16), "space", 1)
+    held = added(joined(0, own, near), got_x, got_y, got_xy)
     held, upper = lax.optimization_barrier((held, upper))
     mine = added(held[0], *(swap(held[k], "space", 2 * k) for k in range(1, high)))
-    both = jnp.stack([mine, swap(mine, "space", 1)])
-    chunks = [both] + [swap(both, "space", 2 * k) for k in range(1, high)]
+    chunks = [mine] + [swap(mine, "space", 2 * k) for k in range(1, high)]
+    chunks.append(swap(jnp.stack(chunks), "space", 1))
 
     gradient = back_input(low, last, slope, upper, shards_first, offsets_first, inputs.shape)
 
@@ -591,8 +590,8 @@
         functools.partial(unpack_kernel, float(cells_first) ** -0.5, float(cells_second) ** -0.5),
         (sds(weight_first.shape, F32), sds(weight_second.shape, F32)),
         [
-            pltpu.VMEM((2 * spaces * size_first, 128), BF16),
-            pltpu.VMEM((2 * spaces * size_second, 128), BF16),
+            pltpu.VMEM((spaces * size_first, 128), BF16),
+            pltpu.VMEM((spaces * size_second, 128), BF16),
         ],
         *chunks,
         smem=(order,),

time: 77.8 us -> 80.1 us (1.030)
  waiting for transfers between devices: 30 us -> 36.3 us
  starting transfers between devices: 27.8 us -> 24.5 us
    ppermute x21 -> x19, starting transfers between devices: 22.7 us -> 15.9 us  [swap(): return lax.ppermute(value, axis, [(i, i ^ bits) for i in range(size)])]
    ppermute x0 -> x1, waiting for transfers between devices: none -> 5.71 us  [local(): lax.ppermute(joined(1, there, far).astype(BF16), ('dp', 'space'), both)]
    ppermute x0 -> x1, starting transfers between devices: none -> 3.37 us  [local(): lax.ppermute(joined(1, there, far).astype(BF16), ('dp', 'space'), both)]
    ppermute x2, waiting for transfers between devices: 0.85 us -> 2.58 us  [shifted(): return lax.ppermute(value, axis, pairs)]
    ppermute x21 -> x19, waiting for transfers between devices: 29.2 us -> 28 us  [swap(): return lax.ppermute(value, axis, [(i, i ^ bits) for i in range(size)])]
    unnamed x14 -> x16, local copies, waits for them, and re-layouts: 2.65 us -> 2.1 us
  transfers between devices with their start and end apart: 23 -> 22, of which waited for: 14 -> 13; matrix products, arithmetic and copies ran while one was open for 2% -> 3% of each run, Pallas kernels for 12% -> 11%
where the time goes in v3:
time: 80.1 us; the launch traced here: 79.9 us
  waiting for transfers between devices  36.3 us (45%)
  starting transfers between devices  24.5 us (31%)
  Pallas kernels  13.7 us (17%)
  local copies, waits for them, and re-layouts  3.88 us (5%)
  between operations  0.86 us (1%)
    ppermute x19, waiting for transfers between devices, swap(): return lax.ppermute(value, axis, [(i, i ^ bits) for i in range(size)])  28 us
    ppermute x19, starting transfers between devices, swap(): return lax.ppermute(value, axis, [(i, i ^ bits) for i in range(size)])  15.9 us
    pallas_call x7, Pallas kernels, call(): pl.pallas_call(kernel, out_shape=out_shape, in_specs=specs, out_specs=jax...  13.7 us
    ppermute x1, waiting for transfers between devices, local(): lax.ppermute(joined(1, there, far).astype(BF16), ('dp', 'space'), both)  5.71 us
    ppermute x2, starting transfers between devices, shifted(): return lax.ppermute(value, axis, pairs)  5.17 us
    ppermute x1, starting transfers between devices, local(): lax.ppermute(joined(1, there, far).astype(BF16), ('dp', 'space'), both)  3.37 us
    ppermute x2, waiting for transfers between devices, shifted(): return lax.ppermute(value, axis, pairs)  2.58 us
    unnamed x16, local copies, waits for them, and re-layouts  2.1 us
  transfers between devices with their start and end apart: 22, of which 13 were waited for; matrix products, arithmetic and copies ran while one was open for 3% of the time, Pallas kernels for 11%

profile of v3, /device:TPU:0, one launch (start us, length us, event | category | flops | bytes accessed | tf_op | source)
XLA Modules:
  0.0 79.9 jit_solution(9726666105284540904)
XLA Ops:
  0.6 3.0 %collective-permute-start.3 = (bf16[432,128]{1,0:T(8,128)(2,1)}, bf16[432,128]{1,0:T(8,128)(2,1)S(1)}, u32[]{:S(2)}, u32[]{:S(2)}) collective-permute-start(bf16[432,128]{1,0:T(8,128)(2,1)} %w0.7), channel_id=1, source_target_pairs={{0,16},{8,24},{16,0},{24,8},{1,17},{9,25},{17,1},{25,9},{2,18},{10... | collective-permute-start | bytes 331784 | tf_op jit(solution)/shard_map/ppermute | solution.py:505
  3.6 0.5 collective-permute-start.5
  4.1 0.1 collective-permute-start.1
  4.2 1.8 %slice_bitcast_fusion = bf16[3,32,2048]{2,1,0:T(8,128)(2,1)} fusion(bf16[1,8,32,2048]{3,2,1,0:T(8,128)(2,1)} %param.4), kind=kLoop, calls=%fused_computation.8 | loop fusion | bytes 786432 | tf_op jit(solution)/shard_map/slice | solution.py:536
  6.0 3.9 %collective-permute-start = (bf16[3,32,2048]{2,1,0:T(8,128)(2,1)}, bf16[3,32,2048]{2,1,0:T(8,128)(2,1)S(1)}, u32[]{:S(2)}, u32[]{:S(2)}) collective-permute-start(bf16[3,32,2048]{2,1,0:T(8,128)(2,1)} %slice_bitcast_fusion), channel_id=1, source_target_pairs={{0,1},{1,2},{2,3},{3,4},{4,5},{5,6},{6,7},{8,9},{9,10},{10,11},{11... | collective-permute-start | bytes 1179656 | tf_op jit(solution)/shard_map/ppermute | solution.py:511
  9.9 0.0 copy-start
  9.9 1.2 %copy-done = bf16[1,8,32,2048]{3,2,1,0:T(8,128)(2,1)S(1)} copy-done((bf16[1,8,32,2048]{3,2,1,0:T(8,128)(2,1)S(1)}, bf16[1,8,32,2048]{3,2,1,0:T(8,128)(2,1)}, u32[]{:S(2)}) %copy-start) | copy-done | bytes 1048600
  11.1 0.3 shard_map.75.sorted_ref
  11.5 0.1 collective-permute-start.4
  11.6 0.0 collective-permute-done.2.w1
  11.6 1.3 %collective-permute-done.4.w3 = bf16[432,128]{1,0:T(8,128)(2,1)S(1)} collective-permute-done((bf16[432,128]{1,0:T(8,128)(2,1)S(1)}, bf16[432,128]{1,0:T(8,128)(2,1)S(1)}, u32[]{:S(2)}, u32[]{:S(2)}) %collective-permute-start.4) | collective-permute-done | bytes 110624 | tf_op jit(solution)/shard_map/ppermute | solution.py:505
  12.9 2.1 %shard_map.76 = (f32[768,128]{1,0:T(8,128)S(1)}, f32[3,8,2,2,8,128]{5,4,3,2,1,0:T(8,128)S(1)}, f32[256,128]{1,0:T(8,128)S(1)}, bf16[2304,128]{1,0:T(8,128)(2,1)S(1)}) custom-call(s32[4]{0:T(128)S(1)} %broadcast_multiply_fusion.offsets, bf16[8,3,256,128]{3,2,1,0:T(8,128)(2,1)S(1)} %shard_map.75.sorted_ref, bf16[432,128]{1,0:T(8,128)(2,1)S(1)} %copy-done.2, ...), custom_call_target="tpu_custom_call" | custom-call | flops 2875000064 | bytes 3522560 | tf_op jit(solution)/shard_map/pallas_call | solution.py:49
  15.0 0.0 copy-start.6
  15.0 0.7 copy-done.6
  15.7 0.7 collective-permute-done.1.w2
  16.5 2.0 %collective-permute-done.halo_ref = bf16[3,32,2048]{2,1,0:T(8,128)(2,1)S(1)} collective-permute-done((bf16[3,32,2048]{2,1,0:T(8,128)(2,1)}, bf16[3,32,2048]{2,1,0:T(8,128)(2,1)S(1)}, u32[]{:S(2)}, u32[]{:S(2)}) %collective-permute-start) | collective-permute-done | bytes 393248 | tf_op jit(solution)/shard_map/ppermute | solution.py:511
  18.4 0.9 %shard_map.77 = (f32[512,128]{1,0:T(8,128)S(1)}, bf16[128,3456]{1,0:T(8,128)(2,1)S(1)}, bf16[3,3,256,128]{3,2,1,0:T(8,128)(2,1)S(1)}) custom-call(f32[1]{0:T(128)} %bitcast.alive, bf16[3,32,2048]{2,1,0:T(8,128)(2,1)S(1)} %collective-permute-done.halo_ref, f32[3,8,2,2,8,128]{5,4,3,2,1,0:T(8,128)S(1)} %get-tuple-element.37.hidden_ref, ...), custom_call_target="tpu_custom_call" | custom-call | flops 1724999936 | bytes 3244032 | tf_op jit(solution)/shard_map/pallas_call | solution.py:49
  19.3 0.1 copy-done.1
  19.4 3.0 %shard_map.78 = (bf16[2,8,2048]{2,1,0:T(8,128)(2,1)}, bf16[128,256]{1,0:T(8,128)(2,1)S(1)}, bf16[8,224,128]{2,1,0:T(8,128)(2,1)S(1)}, bf16[8,224,128]{2,1,0:T(8,...) custom-call(s32[4]{0:T(128)S(1)} %get-tuple-element.80.offsets, ...), custom_call_target="tpu_custom_call" | custom-call | flops 3449999872 | bytes 4685824 | tf_op jit(solution)/shard_map/pallas_call | solution.py:49
  22.4 0.5 collective-permute-start.8
  22.9 3.0 %shard_map.79 = (bf16[768,128]{1,0:T(8,128)(2,1)S(1)}, f32[256,128]{1,0:T(8,128)S(1)}, bf16[512,128]{1,0:T(8,128)(2,1)S(1)}, bf16[8,64,128]{2,1,0:T(8,128)(2,1)S...) custom-call(s32[4]{0:T(128)S(1)} %get-tuple-element.80.offsets, ...), custom_call_target="tpu_custom_call" | custom-call | flops 4024999936 | bytes 5636096 | tf_op jit(solution)/shard_map/pallas_call | solution.py:49
  25.9 0.1 collective-permute-start.9
  26.0 0.5 collective-permute-start.10
  26.5 0.2 add_convert_fusion.1
  26.7 0.1 add_convert_fusion.2
  26.8 0.7 collective-permute-done.10
  27.6 3.4 %collective-permute-start.13 = (bf16[4,288,128]{2,1,0:T(8,128)(2,1)S(1)}, bf16[4,288,128]{2,1,0:T(8,128)(2,1)S(1)}, u32[]{:S(2)}, u32[]{:S(2)}) collective-permute-start(bf16[4,288,128]{2,1,0:T(8,128)(2,1)S(1)} %pad_maximum_fusion.2), channel_id=1, source_target_pairs={{0,17},{1,16},{2,19},{3,18},{4,21},{5,20},{6,23},{7,22},{8,25},{9,... | collective-permute-start | bytes 884744 | tf_op jit(solution)/shard_map/ppermute | solution.py:576
  31.0 0.6 collective-permute-start.11
  31.7 0.1 collective-permute-start.12
  31.8 1.3 %collective-permute-start.14 = (bf16[512,128]{1,0:T(8,128)(2,1)S(1)}, bf16[512,128]{1,0:T(8,128)(2,1)S(1)}, u32[]{:S(2)}, u32[]{:S(2)}) collective-permute-start(bf16[512,128]{1,0:T(8,128)(2,1)S(1)} %get-tuple-element.63), channel_id=1, source_target_pairs={{1,0},{2,1},{3,2},{4,3},{5,4},{6,5},{7,6},{9,8},{10,9},{11,10},{12... | collective-permute-start | bytes 393224 | tf_op jit(solution)/shard_map/ppermute | solution.py:511
  33.1 5.7 %collective-permute-done.13 = bf16[4,288,128]{2,1,0:T(8,128)(2,1)S(1)} collective-permute-done((bf16[4,288,128]{2,1,0:T(8,128)(2,1)S(1)}, bf16[4,288,128]{2,1,0:T(8,128)(2,1)S(1)}, u32[]{:S(2)}, u32[]{:S(2)}) %collective-permute-start.13) | collective-permute-done | bytes 294944 | tf_op jit(solution)/shard_map/ppermute | solution.py:576
  38.8 6.4 %collective-permute-done.11 = bf16[4,288,128]{2,1,0:T(8,128)(2,1)S(1)} collective-permute-done((bf16[4,288,128]{2,1,0:T(8,128)(2,1)S(1)}, bf16[4,288,128]{2,1,0:T(8,128)(2,1)S(1)}, u32[]{:S(2)}, u32[]{:S(2)}) %collective-permute-start.11) | collective-permute-done | bytes 294944 | tf_op jit(solution)/shard_map/ppermute | solution.py:505
  45.1 1.7 %collective-permute-done.12 = bf16[4,288,128]{2,1,0:T(8,128)(2,1)S(1)} collective-permute-done((bf16[4,288,128]{2,1,0:T(8,128)(2,1)S(1)}, bf16[4,288,128]{2,1,0:T(8,128)(2,1)S(1)}, u32[]{:S(2)}, u32[]{:S(2)}) %collective-permute-start.12) | collective-permute-done | bytes 294944 | tf_op jit(solution)/shard_map/ppermute | solution.py:505
  46.8 0.1 fusion.2
  47.0 0.6 collective-permute-done.14.upper_ref
  47.6 2.7 %collective-permute-start.15 = (bf16[288,128]{1,0:T(8,128)(2,1)S(1)}, bf16[288,128]{1,0:T(8,128)(2,1)S(1)}, u32[]{:S(2)}, u32[]{:S(2)}) collective-permute-start(bf16[288,128]{1,0:T(8,128)(2,1)S(1)} %get-tuple-element.72), channel_id=1, source_target_pairs={{0,2},{1,3},{2,0},{3,1},{4,6},{5,7},{6,4},{7,5},{8,10},{9,11},{10,... | collective-permute-start | bytes 221192 | tf_op jit(solution)/shard_map/ppermute | solution.py:505
  50.3 2.5 %collective-permute-start.17 = (bf16[288,128]{1,0:T(8,128)(2,1)S(1)}, bf16[288,128]{1,0:T(8,128)(2,1)S(1)}, u32[]{:S(2)}, u32[]{:S(2)}) collective-permute-start(bf16[288,128]{1,0:T(8,128)(2,1)S(1)} %get-tuple-element.73), channel_id=1, source_target_pairs={{0,6},{1,7},{2,4},{3,5},{4,2},{5,3},{6,0},{7,1},{8,14},{9,15},{10,... | collective-permute-start | bytes 221192 | tf_op jit(solution)/shard_map/ppermute | solution.py:505
  52.8 0.1 collective-permute-start.16
  52.9 4.6 %collective-permute-done.17 = bf16[288,128]{1,0:T(8,128)(2,1)S(1)} collective-permute-done((bf16[288,128]{1,0:T(8,128)(2,1)S(1)}, bf16[288,128]{1,0:T(8,128)(2,1)S(1)}, u32[]{:S(2)}, u32[]{:S(2)}) %collective-permute-start.17) | collective-permute-done | bytes 73760 | tf_op jit(solution)/shard_map/ppermute | solution.py:505
  57.5 2.5 %collective-permute-done.16 = bf16[288,128]{1,0:T(8,128)(2,1)S(1)} collective-permute-done((bf16[288,128]{1,0:T(8,128)(2,1)S(1)}, bf16[288,128]{1,0:T(8,128)(2,1)S(1)}, u32[]{:S(2)}, u32[]{:S(2)}) %collective-permute-start.16) | collective-permute-done | bytes 73760 | tf_op jit(solution)/shard_map/ppermute | solution.py:505
  60.0 2.5 %collective-permute-start.20 = (bf16[288,128]{1,0:T(8,128)(2,1)S(1)}, bf16[288,128]{1,0:T(8,128)(2,1)S(1)}, u32[]{:S(2)}, u32[]{:S(2)}) collective-permute-start(bf16[288,128]{1,0:T(8,128)(2,1)S(1)} %fusion.5.refs_0_), channel_id=1, source_target_pairs={{0,6},{1,7},{2,4},{3,5},{4,2},{5,3},{6,0},{7,1},{8,14},{9,15},{10,... | collective-permute-start | bytes 221192 | tf_op jit(solution)/shard_map/ppermute | solution.py:505
  62.6 1.9 %collective-permute-start.18 = (bf16[288,128]{1,0:T(8,128)(2,1)S(1)}, bf16[288,128]{1,0:T(8,128)(2,1)S(1)}, u32[]{:S(2)}, u32[]{:S(2)}) collective-permute-start(bf16[288,128]{1,0:T(8,128)(2,1)S(1)} %fusion.5.refs_0_), channel_id=1, source_target_pairs={{0,2},{1,3},{2,0},{3,1},{4,6},{5,7},{6,4},{7,5},{8,10},{9,11},{10,... | collective-permute-start | bytes 221192 | tf_op jit(solution)/shard_map/ppermute | solution.py:505
  64.5 2.6 %collective-permute-done.20.refs_3_ = bf16[288,128]{1,0:T(8,128)(2,1)S(1)} collective-permute-done((bf16[288,128]{1,0:T(8,128)(2,1)S(1)}, bf16[288,128]{1,0:T(8,128)(2,1)S(1)}, u32[]{:S(2)}, u32[]{:S(2)}) %collective-permute-start.20) | collective-permute-done | bytes 73760 | tf_op jit(solution)/shard_map/ppermute | solution.py:505
  67.1 2.1 %collective-permute-done.19.refs_2_ = bf16[288,128]{1,0:T(8,128)(2,1)S(1)} collective-permute-done((bf16[288,128]{1,0:T(8,128)(2,1)S(1)}, bf16[288,128]{1,0:T(8,128)(2,1)S(1)}, u32[]{:S(2)}, u32[]{:S(2)}) %collective-permute-start.19) | collective-permute-done | bytes 73760 | tf_op jit(solution)/shard_map/ppermute | solution.py:505
  69.3 0.7 collective-permute-start.21
  70.0 2.8 %shard_map.80 = bf16[8,32,2048]{2,1,0:T(8,128)(2,1)} custom-call(s32[4]{0:T(128)S(1)} %broadcast_multiply_fusion.offsets, bf16[768,128]{1,0:T(8,128)(2,1)S(1)} %get-tuple-element.47.low_ref, f32[256,128]{1,0:T(8,128)S(1)} %get-tuple-element.48.last_ref, f32[768,128]{1,0:T(8,128)S(1)} %copy-done.7, bf16[512,128]{1,0:T(8,128)(2,1)S(1)} %collective-permute-done.14.upper_ref, ...), custom_call_target="tpu_custom_call" | custom-call | flops 3449999872 | bytes 2342912 | tf_op jit(solution)/shard_map/pallas_call | solution.py:49
  72.8 5.4 %collective-permute-done.21.refs_4_ = bf16[4,288,128]{2,1,0:T(8,128)(2,1)S(1)} collective-permute-done((bf16[4,288,128]{2,1,0:T(8,128)(2,1)S(1)}, bf16[4,288,128]{2,1,0:T(8,128)(2,1)S(1)}, u32[]{:S(2)}, u32[]{:S(2)}) %collective-permute-start.21) | collective-permute-done | bytes 294944 | tf_op jit(solution)/shard_map/ppermute | solution.py:505
  78.2 1.7 %shard_map.81 = (f32[432,128]{1,0:T(8,128)}, f32[864,256]{1,0:T(8,128)}) custom-call(s32[8]{0:T(128)S(1)} %fusion.8.order, bf16[288,128]{1,0:T(8,128)(2,1)S(1)} %fusion.5.refs_0_, bf16[288,128]{1,0:T(8,128)(2,1)S(1)} %collective-permute-done.18.refs_1_, bf16[288,128]{1,0:T(8,128)(2,1)S(1)} %collective-permute-done.19.refs_2_, ...), custom_call_target="tpu_custom_call" | custom-call | flops 1150000000 | bytes 1695744 | tf_op jit(solution)/shard_map/pallas_call | solution.py:49
  (34 shorter events, 0.3 us)
Async XLA Ops:
  0.6 10.9 %collective-permute-start.3 = (bf16[432,128]{1,0:T(8,128)(2,1)}, bf16[432,128]{1,0:T(8,128)(2,1)S(1)}, u32[]{:S(2)}, u32[]{:S(2)}) collective-permute-start(bf16[432,128]{1,0:T(8,128)(2,1)} %w0.7), channel_id=1, source_target_pairs={{0,16},{8,24},{16,0},{24,8},{1,17},{9,25},{17,1},{25,9},{2,18},{10... | collective-permute-start | bytes 331784 | tf_op jit(solution)/shard_map/ppermute | solution.py:505
  3.6 8.0 %collective-permute-start.2 = (bf16[432,128]{1,0:T(8,128)(2,1)}, bf16[432,128]{1,0:T(8,128)(2,1)S(1)}, u32[]{:S(2)}, u32[]{:S(2)}) collective-permute-start(bf16[432,128]{1,0:T(8,128)(2,1)} %w0.7), channel_id=1, source_target_pairs={{0,8},{8,0},{16,24},{24,16},{1,9},{9,1},{17,25},{25,17},{2,10},{10... | collective-permute-start | bytes 331784 | tf_op jit(solution)/shard_map/ppermute | solution.py:505
  3.6 15.7 %collective-permute-start.5 = (bf16[864,256]{1,0:T(8,128)(2,1)}, bf16[864,256]{1,0:T(8,128)(2,1)S(1)}, u32[]{:S(2)}, u32[]{:S(2)}) collective-permute-start(bf16[864,256]{1,0:T(8,128)(2,1)} %w0.6), channel_id=1, source_target_pairs={{0,8},{8,0},{16,24},{24,16},{1,9},{9,1},{17,25},{25,17},{2,10},{10... | collective-permute-start | bytes 1327112 | tf_op jit(solution)/shard_map/ppermute | solution.py:505
  4.1 12.3 %collective-permute-start.1 = (bf16[864,256]{1,0:T(8,128)(2,1)}, bf16[864,256]{1,0:T(8,128)(2,1)S(1)}, u32[]{:S(2)}, u32[]{:S(2)}) collective-permute-start(bf16[864,256]{1,0:T(8,128)(2,1)} %w0.6), channel_id=1, source_target_pairs={{0,16},{8,24},{16,0},{24,8},{1,17},{9,25},{17,1},{25,9},{2,18},{10... | collective-permute-start | bytes 1327112 | tf_op jit(solution)/shard_map/ppermute | solution.py:505
  6.0 12.4 %collective-permute-start = (bf16[3,32,2048]{2,1,0:T(8,128)(2,1)}, bf16[3,32,2048]{2,1,0:T(8,128)(2,1)S(1)}, u32[]{:S(2)}, u32[]{:S(2)}) collective-permute-start(bf16[3,32,2048]{2,1,0:T(8,128)(2,1)} %slice_bitcast_fusion), channel_id=1, source_target_pairs={{0,1},{1,2},{2,3},{3,4},{4,5},{5,6},{6,7},{8,9},{9,10},{10,11},{11... | collective-permute-start | bytes 1179656 | tf_op jit(solution)/shard_map/ppermute | solution.py:511
  9.9 1.2 %copy-start = (bf16[1,8,32,2048]{3,2,1,0:T(8,128)(2,1)S(1)}, bf16[1,8,32,2048]{3,2,1,0:T(8,128)(2,1)}, u32[]{:S(2)}) copy-start(bf16[1,8,32,2048]{3,2,1,0:T(8,128)(2,1)} %param.4) | copy-start | bytes 3145732
  11.1 1.8 %copy-start.2 = (bf16[432,128]{1,0:T(8,128)(2,1)S(1)}, bf16[432,128]{1,0:T(8,128)(2,1)}, u32[]{:S(2)}) copy-start(bf16[432,128]{1,0:T(8,128)(2,1)} %w0.7) | copy-start | bytes 331780
  11.5 3.5 %copy-start.4 = (bf16[8,3,256,128]{3,2,1,0:T(8,128)(2,1)}, bf16[8,3,256,128]{3,2,1,0:T(8,128)(2,1)S(1)}, u32[]{:S(2)}) copy-start(bf16[8,3,256,128]{3,2,1,0:T(8,128)(2,1)S(1)} %shard_map.75.sorted_ref) | copy-start | bytes 4718596
  11.5 1.4 %collective-permute-start.4 = (bf16[432,128]{1,0:T(8,128)(2,1)S(1)}, bf16[432,128]{1,0:T(8,128)(2,1)S(1)}, u32[]{:S(2)}, u32[]{:S(2)}) collective-permute-start(bf16[432,128]{1,0:T(8,128)(2,1)S(1)} %collective-permute-done.3.w2), channel_id=1, source_target_pairs={{0,8},{8,0},{16,24},{24,16},{1,9},{9,1},{17,25},{25,17},{2,10},{10... | collective-permute-start | bytes 331784 | tf_op jit(solution)/shard_map/ppermute | solution.py:505
  15.0 0.7 copy-start.6
  16.4 2.9 %collective-permute-start.6 = (bf16[864,256]{1,0:T(8,128)(2,1)S(1)}, bf16[864,256]{1,0:T(8,128)(2,1)S(1)}, u32[]{:S(2)}, u32[]{:S(2)}) collective-permute-start(bf16[864,256]{1,0:T(8,128)(2,1)S(1)} %collective-permute-done.1.w2), channel_id=1, source_target_pairs={{0,8},{8,0},{16,24},{24,16},{1,9},{9,1},{17,25},{25,17},{2,10},{10... | collective-permute-start | bytes 1327112 | tf_op jit(solution)/shard_map/ppermute | solution.py:505
  18.4 1.0 %copy-start.1 = (bf16[864,256]{1,0:T(8,128)(2,1)S(1)}, bf16[864,256]{1,0:T(8,128)(2,1)}, u32[]{:S(2)}) copy-start(bf16[864,256]{1,0:T(8,128)(2,1)} %w0.6) | copy-start | bytes 1327108
  18.4 1.0 %copy-start.3 = (bf16[1,2,8,2048]{3,2,1,0:T(8,128)(2,1)S(1)}, bf16[1,2,8,2048]{3,2,1,0:T(8,128)(2,1)}, u32[]{:S(2)}) copy-start(bf16[1,2,8,2048]{3,2,1,0:T(8,128)(2,1)} %param.7) | copy-start | bytes 196612
  19.4 3.5 %copy-start.5 = (bf16[8,3,256,128]{3,2,1,0:T(8,128)(2,1)S(1)}, bf16[8,3,256,128]{3,2,1,0:T(8,128)(2,1)}, u32[]{:S(2)}) copy-start(bf16[8,3,256,128]{3,2,1,0:T(8,128)(2,1)} %copy-done.4) | copy-start | bytes 4718596
  19.4 3.5 %copy-start.7 = (f32[768,128]{1,0:T(8,128)S(1)}, f32[768,128]{1,0:T(8,128)}, u32[]{:S(2)}) copy-start(f32[768,128]{1,0:T(8,128)} %copy-done.6) | copy-start | bytes 1179652
  22.4 3.5 %collective-permute-start.7 = (bf16[8,224,128]{2,1,0:T(8,128)(2,1)S(1)}, bf16[8,224,128]{2,1,0:T(8,128)(2,1)S(1)}, u32[]{:S(2)}, u32[]{:S(2)}) collective-permute-start(bf16[8,224,128]{2,1,0:T(8,128)(2,1)S(1)} %get-tuple-element.54), channel_id=1, source_target_pairs={{0,8},{8,0},{16,24},{24,16},{1,9},{9,1},{17,25},{25,17},{2,10},{10... | collective-permute-start | bytes 1376264 | tf_op jit(solution)/shard_map/ppermute | solution.py:505
  22.4 3.5 %collective-permute-start.8 = (bf16[8,224,128]{2,1,0:T(8,128)(2,1)S(1)}, bf16[8,224,128]{2,1,0:T(8,128)(2,1)S(1)}, u32[]{:S(2)}, u32[]{:S(2)}) collective-permute-start(bf16[8,224,128]{2,1,0:T(8,128)(2,1)S(1)} %get-tuple-element.55), channel_id=1, source_target_pairs={{0,8},{8,0},{16,24},{24,16},{1,9},{9,1},{17,25},{25,17},{2,10},{10... | collective-permute-start | bytes 1376264 | tf_op jit(solution)/shard_map/ppermute | solution.py:505
  25.9 5.7 %collective-permute-start.9 = (bf16[8,64,128]{2,1,0:T(8,128)(2,1)S(1)}, bf16[8,64,128]{2,1,0:T(8,128)(2,1)S(1)}, u32[]{:S(2)}, u32[]{:S(2)}) collective-permute-start(bf16[8,64,128]{2,1,0:T(8,128)(2,1)S(1)} %get-tuple-element.58), channel_id=1, source_target_pairs={{0,8},{8,0},{16,24},{24,16},{1,9},{9,1},{17,25},{25,17},{2,10},{10... | collective-permute-start | bytes 393224 | tf_op jit(solution)/shard_map/ppermute | solution.py:505
  26.0 1.5 %collective-permute-start.10 = (bf16[8,64,128]{2,1,0:T(8,128)(2,1)S(1)}, bf16[8,64,128]{2,1,0:T(8,128)(2,1)S(1)}, u32[]{:S(2)}, u32[]{:S(2)}) collective-permute-start(bf16[8,64,128]{2,1,0:T(8,128)(2,1)S(1)} %get-tuple-element.62), channel_id=1, source_target_pairs={{0,8},{8,0},{16,24},{24,16},{1,9},{9,1},{17,25},{25,17},{2,10},{10... | collective-permute-start | bytes 393224 | tf_op jit(solution)/shard_map/ppermute | solution.py:505
  27.6 11.2 %collective-permute-start.13 = (bf16[4,288,128]{2,1,0:T(8,128)(2,1)S(1)}, bf16[4,288,128]{2,1,0:T(8,128)(2,1)S(1)}, u32[]{:S(2)}, u32[]{:S(2)}) collective-permute-start(bf16[4,288,128]{2,1,0:T(8,128)(2,1)S(1)} %pad_maximum_fusion.2), channel_id=1, source_target_pairs={{0,17},{1,16},{2,19},{3,18},{4,21},{5,20},{6,23},{7,22},{8,25},{9,... | collective-permute-start | bytes 884744 | tf_op jit(solution)/shard_map/ppermute | solution.py:576
  31.0 14.1 %collective-permute-start.11 = (bf16[4,288,128]{2,1,0:T(8,128)(2,1)S(1)}, bf16[4,288,128]{2,1,0:T(8,128)(2,1)S(1)}, u32[]{:S(2)}, u32[]{:S(2)}) collective-permute-start(bf16[4,288,128]{2,1,0:T(8,128)(2,1)S(1)} %pad_maximum_fusion), channel_id=1, source_target_pairs={{0,16},{8,24},{16,0},{24,8},{1,17},{9,25},{17,1},{25,9},{2,18},{10... | collective-permute-start | bytes 884744 | tf_op jit(solution)/shard_map/ppermute | solution.py:505
  31.7 15.2 %collective-permute-start.12 = (bf16[4,288,128]{2,1,0:T(8,128)(2,1)S(1)}, bf16[4,288,128]{2,1,0:T(8,128)(2,1)S(1)}, u32[]{:S(2)}, u32[]{:S(2)}) collective-permute-start(bf16[4,288,128]{2,1,0:T(8,128)(2,1)S(1)} %pad_maximum_fusion.1), channel_id=1, source_target_pairs={{0,1},{1,0},{2,3},{3,2},{4,5},{5,4},{6,7},{7,6},{8,9},{9,8},{10,11... | collective-permute-start | bytes 884744 | tf_op jit(solution)/shard_map/ppermute | solution.py:505
  31.8 15.8 %collective-permute-start.14 = (bf16[512,128]{1,0:T(8,128)(2,1)S(1)}, bf16[512,128]{1,0:T(8,128)(2,1)S(1)}, u32[]{:S(2)}, u32[]{:S(2)}) collective-permute-start(bf16[512,128]{1,0:T(8,128)(2,1)S(1)} %get-tuple-element.63), channel_id=1, source_target_pairs={{1,0},{2,1},{3,2},{4,3},{5,4},{6,5},{7,6},{9,8},{10,9},{11,10},{12... | collective-permute-start | bytes 393224 | tf_op jit(solution)/shard_map/ppermute | solution.py:511
  47.6 5.3 %collective-permute-start.15 = (bf16[288,128]{1,0:T(8,128)(2,1)S(1)}, bf16[288,128]{1,0:T(8,128)(2,1)S(1)}, u32[]{:S(2)}, u32[]{:S(2)}) collective-permute-start(bf16[288,128]{1,0:T(8,128)(2,1)S(1)} %get-tuple-element.72), channel_id=1, source_target_pairs={{0,2},{1,3},{2,0},{3,1},{4,6},{5,7},{6,4},{7,5},{8,10},{9,11},{10,... | collective-permute-start | bytes 221192 | tf_op jit(solution)/shard_map/ppermute | solution.py:505
  50.3 7.1 %collective-permute-start.17 = (bf16[288,128]{1,0:T(8,128)(2,1)S(1)}, bf16[288,128]{1,0:T(8,128)(2,1)S(1)}, u32[]{:S(2)}, u32[]{:S(2)}) collective-permute-start(bf16[288,128]{1,0:T(8,128)(2,1)S(1)} %get-tuple-element.73), channel_id=1, source_target_pairs={{0,6},{1,7},{2,4},{3,5},{4,2},{5,3},{6,0},{7,1},{8,14},{9,15},{10,... | collective-permute-start | bytes 221192 | tf_op jit(solution)/shard_map/ppermute | solution.py:505
  52.8 7.2 %collective-permute-start.16 = (bf16[288,128]{1,0:T(8,128)(2,1)S(1)}, bf16[288,128]{1,0:T(8,128)(2,1)S(1)}, u32[]{:S(2)}, u32[]{:S(2)}) collective-permute-start(bf16[288,128]{1,0:T(8,128)(2,1)S(1)} %get-tuple-element.74), channel_id=1, source_target_pairs={{0,4},{1,5},{2,6},{3,7},{4,0},{5,1},{6,2},{7,3},{8,12},{9,13},{10,... | collective-permute-start | bytes 221192 | tf_op jit(solution)/shard_map/ppermute | solution.py:505
  60.0 7.1 %collective-permute-start.20 = (bf16[288,128]{1,0:T(8,128)(2,1)S(1)}, bf16[288,128]{1,0:T(8,128)(2,1)S(1)}, u32[]{:S(2)}, u32[]{:S(2)}) collective-permute-start(bf16[288,128]{1,0:T(8,128)(2,1)S(1)} %fusion.5.refs_0_), channel_id=1, source_target_pairs={{0,6},{1,7},{2,4},{3,5},{4,2},{5,3},{6,0},{7,1},{8,14},{9,15},{10,... | collective-permute-start | bytes 221192 | tf_op jit(solution)/shard_map/ppermute | solution.py:505
  62.6 6.7 %collective-permute-start.19 = (bf16[288,128]{1,0:T(8,128)(2,1)S(1)}, bf16[288,128]{1,0:T(8,128)(2,1)S(1)}, u32[]{:S(2)}, u32[]{:S(2)}) collective-permute-start(bf16[288,128]{1,0:T(8,128)(2,1)S(1)} %fusion.5.refs_0_), channel_id=1, source_target_pairs={{0,4},{1,5},{2,6},{3,7},{4,0},{5,1},{6,2},{7,3},{8,12},{9,13},{10,... | collective-permute-start | bytes 221192 | tf_op jit(solution)/shard_map/ppermute | solution.py:505
  62.6 6.7 %collective-permute-start.18 = (bf16[288,128]{1,0:T(8,128)(2,1)S(1)}, bf16[288,128]{1,0:T(8,128)(2,1)S(1)}, u32[]{:S(2)}, u32[]{:S(2)}) collective-permute-start(bf16[288,128]{1,0:T(8,128)(2,1)S(1)} %fusion.5.refs_0_), channel_id=1, source_target_pairs={{0,2},{1,3},{2,0},{3,1},{4,6},{5,7},{6,4},{7,5},{8,10},{9,11},{10,... | collective-permute-start | bytes 221192 | tf_op jit(solution)/shard_map/ppermute | solution.py:505
  69.3 8.9 %collective-permute-start.21 = (bf16[4,288,128]{2,1,0:T(8,128)(2,1)S(1)}, bf16[4,288,128]{2,1,0:T(8,128)(2,1)S(1)}, u32[]{:S(2)}, u32[]{:S(2)}) collective-permute-start(bf16[4,288,128]{2,1,0:T(8,128)(2,1)S(1)} %pad_maximum_fusion.3), channel_id=1, source_target_pairs={{0,1},{1,0},{2,3},{3,2},{4,5},{5,4},{6,7},{7,6},{8,9},{9,8},{10,11... | collective-permute-start | bytes 884744 | tf_op jit(solution)/shard_map/ppermute | solution.py:505

commit v4 on v3

--- a/solution.py
+++ b/solution.py
@@ -179,8 +179,8 @@
 
 
 def forward_lower_kernel(
-    alive, halo_ref, hidden_ref, partial_ref, padded_ref,
-    slope_ref, windows_ref, sorted_ref, wide, columns, some, lowest,
+    alive, side, halo_ref, hidden_ref, partial_ref, padded_ref,
+    slope_ref, windows_ref, sorted_ref, here_ref, there_ref, wide, columns, some, lowest, planes,
 ):
     rows = partial_ref.shape[0]
     cells = hidden_ref.shape[0] + 1
@@ -198,6 +198,11 @@
     slope_ref[rows:, :] = activate_slope(here)
     lowest[0] = (activate(below) * alive[0]).reshape(lowest.shape[1:])
     lowest[1] = activate(here).reshape(lowest.shape[1:])
+    for plane in range(cells + 1):
+        source = lowest.at[plane] if plane < 2 else hidden_ref.at[plane - 2]
+        planes[plane] = source[...].reshape(rows, 128).astype(BF16)
+    here_ref[...] = planes[pl.ds(side[0], cells)]
+    there_ref[...] = planes[pl.ds(1 - side[0], cells)]
     for out in range(cells // 2):
         for a in range(3):
             plane = 2 * out - 1 + a
@@ -209,7 +214,7 @@
             take_windows(read, windows_ref, out, a, half)
 
 
-def forward_lower(halo, hidden, partial, padded, alive):
+def forward_lower(halo, hidden, partial, padded, alive, side):
     rows = partial.shape[0]
     cells = hidden.shape[0] + 1
     return call(
@@ -218,15 +223,18 @@
             sds((2 * rows, 128), F32),
             sds((cells * rows // 8, 27 * 128), BF16),
             sds((halo.shape[0], 3, rows, 128), BF16),
+            sds((cells, rows, 128), BF16),
+            sds((cells, rows, 128), BF16),
         ),
         [
             pltpu.VMEM((rows // 16, halo.shape[1], 128), F32),
             pltpu.VMEM((rows, 9 * 256), BF16),
             pltpu.VMEM((rows, 3 * 256), BF16),
             pltpu.VMEM((2, *hidden.shape[1:]), F32),
+            pltpu.VMEM((cells + 1, rows, 128), BF16),
         ],
         halo, hidden, partial, padded,
-        smem=(alive,),
+        smem=(alive, side),
         micros=1.5,
     )
 
@@ -240,8 +248,7 @@
 
 
 def forward_second_kernel(
-    offsets, slots, order, windows_ref, cot_ref, w0, w1, w2, w3,
-    act_ref, delta_ref, g0, g1, g2, g3, whole, flat,
+    offsets, windows_ref, cot_ref, w0, w1, w2, w3, act_ref, delta_ref, whole
 ):
     put_rows(whole, (w0, w1, w2, w3), offsets)
     linear = jnp.dot(windows_ref[...], whole[...], preferred_element_type=F32)
@@ -262,41 +269,91 @@
                 [cot[:, q * features : (q + 1) * features] for q in range(count)], axis=0
             )
         )
-    delta = (jnp.concatenate(deltas, axis=0) * slope).astype(BF16)
-    delta_ref[...] = delta
-    total = lax.dot_general(
-        windows_ref[...], delta, (((0,), (0,)), ((), ())), preferred_element_type=F32
-    ).astype(BF16)
-    rows = w0.shape[0]
-    lanes = features // 128
-    for shard in range(4):
-        for lane in range(lanes):
-            flat[shard, lane * rows : (lane + 1) * rows, :] = total[
-                shard * rows : (shard + 1) * rows, lane * 128 : (lane + 1) * 128
-            ]
-        rest = flat.shape[1] - lanes * rows
-        if rest:
-            flat[shard, lanes * rows :, :] = jnp.zeros((rest, 128), BF16)
-    put_pieces(flat, (g0, g1, g2, g3), slots, order)
-
-
-def forward_second(windows, cot, shards, offsets, slots, order, places, size):
+    delta_ref[...] = (jnp.concatenate(deltas, axis=0) * slope).astype(BF16)
+
+
+def forward_second(windows, cot, shards, offsets):
     rows, features = shards[0].shape
-    piece = sds((places, size, 128), BF16)
     return call(
         forward_second_kernel,
-        (
-            sds(cot.shape, BF16),
-            sds((windows.shape[0], features), BF16),
-            piece, piece, piece, piece,
-        ),
+        (sds(cot.shape, BF16), sds((windows.shape[0], features), BF16)),
+        [pltpu.VMEM((4 * rows, features), BF16)],
+        windows, cot, *shards,
+        smem=(offsets,),
+        micros=1.5,
+    )
+
+
+def second_rows_kernel(
+    data, table, order, h0, h1, h2, h3, d0, d1, d2, d3,
+    out_ref, wide, windows, deltas, product, flat,
+):
+    cells, rows, _ = h0.shape
+    half = rows // 32
+    outs = cells // 2
+    size = half * 8
+    for sample, (hidden, delta) in enumerate(((h0, d0), (h1, d1), (h2, d2), (h3, d3))):
+        wide[sample * cells : (sample + 1) * cells] = (
+            hidden[...].astype(F32).reshape(cells, half, 2, 2, 8, 128)
+        )
+        deltas[sample * outs * size : (sample + 1) * outs * size, :] = delta[...]
+    for tap in range(windows.shape[1] // 128):
+        e, f = table[data[0], 8 + tap], table[data[0], 16 + tap]
+        row = jnp.where(e == 1, 0, 1)
+        column = jnp.where(f == 1, 0, 1)
+        for sample in range(4):
+            for out in range(outs):
+                plane = sample * cells + 2 * out + table[data[0], tap]
+                block = wide[plane, :, column, row].reshape(size, 128)
+                block = jnp.where(e == 0, from_before(block), block)
+                later = jnp.concatenate([jnp.zeros((8, 128), F32), block[: size - 8]], axis=0)
+                block = jnp.where(f == 0, later, block)
+                at = (sample * outs + out) * size
+                windows[at : at + size, tap * 128 : (tap + 1) * 128] = block.astype(BF16)
+    product[...] = lax.dot_general(
+        windows[...], deltas[...], (((0,), (0,)), ((), ())), preferred_element_type=F32
+    ).astype(BF16)
+    lanes = product.shape[1] // 128
+    count, piece, _ = out_ref.shape
+    shard = 27 * 128 // 4
+    for lane in range(lanes):
+        flat[lane * shard : (lane + 1) * shard, :] = product[
+            pl.ds(pl.multiple_of(table[data[0], 24], 16), shard), lane * 128 : (lane + 1) * 128
+        ]
+    rest = flat.shape[0] - lanes * shard
+    if rest:
+        flat[lanes * shard :, :] = jnp.zeros((rest, 128), BF16)
+    for place in range(count):
+        out_ref[place] = flat[pl.ds(pl.multiple_of(order[place] * piece, 16), piece), :]
+
+
+def second_rows(hiddens, deltas, data, order, places, size):
+    cells, rows, _ = hiddens[0].shape
+    cellrows, features = deltas[0].shape
+    taps = 8
+    table = []
+    for shard in range(4):
+        start = shard * 27 // 4
+        at = [min(start + tap, 26) for tap in range(taps)]
+        table.append(
+            [tap // 9 - shard // 2 for tap in at]
+            + [tap // 3 % 3 for tap in at]
+            + [tap % 3 for tap in at]
+            + [shard * (27 * 128 // 4) - start * 128]
+        )
+    return call(
+        second_rows_kernel,
+        sds((places, size, 128), BF16),
         [
-            pltpu.VMEM((4 * rows, features), BF16),
-            pltpu.VMEM((4, places * size, 128), BF16),
+            pltpu.VMEM((4 * cells, rows // 32, 2, 2, 8, 128), F32),
+            pltpu.VMEM((4 * cellrows, taps * 128), BF16),
+            pltpu.VMEM((4 * cellrows, features), BF16),
+            pltpu.VMEM((taps * 128, features), BF16),
+            pltpu.VMEM((places * size, 128), BF16),
         ],
-        windows, cot, *shards,
-        smem=(offsets, slots, order),
-        micros=3.0,
+        *hiddens, *deltas,
+        smem=(data.reshape(1), jnp.array(table, jnp.int32), order),
+        micros=2.0,
     )
 
 
@@ -522,6 +579,7 @@
     offsets_first = slots * small
     offsets_second = slots * big
     alive = (place > 0).astype(F32).reshape(1)
+    x_side = lax.shift_right_logical(data, 1)
     steps = jnp.arange(spaces, dtype=jnp.int32)
     order = place ^ (2 * (steps % high) + steps // high)
     lanes = weight_second.shape[1] // 128
@@ -542,41 +600,45 @@
     second_x, hidden = lax.optimization_barrier((second_x, hidden))
     second_far = swap(second_x, "dp", 1)
     shards_second = (weight_second, second_core, second_x, second_far)
-    slope_low, windows, sorted_halo = forward_lower(halo, hidden, partial, padded, alive)
+    slope_low, windows, sorted_halo, hidden_here, hidden_there = forward_lower(
+        halo, hidden, partial, padded, alive, x_side.reshape(1)
+    )
     cot = cotangent.reshape(cotangent.shape[1:])
-    activations, delta_second, *second = forward_second(
-        windows, cot, shards_second, offsets_second, slots, order, spaces, size_second,
-    )
+    activations, delta_second = forward_second(windows, cot, shards_second, offsets_second)
+    hidden_x = swap(hidden_there, "dp", 2)
+    delta_x = swap(delta_second, "dp", 2)
+    hidden_core = swap(hidden_here, "dp", 1)
+    delta_core = swap(delta_second, "dp", 1)
     low, last, down, *first = back_second(
         delta_second, shards_second, (slope_low, slope), sorted_volume, sorted_halo,
         offsets_second, slots, order, spaces, size_first,
     )
+    first, delta_x, hidden_x, delta_core, hidden_core = lax.optimization_barrier(
+        (first, delta_x, hidden_x, delta_core, hidden_core)
+    )
+    hiddens = (hidden_here, hidden_core, hidden_x, swap(hidden_x, "dp", 1))
+    deltas = (delta_second, delta_core, delta_x, swap(delta_x, "dp", 1))
+    second = second_rows(hiddens, deltas, data, order, spaces, size_second)
     upper = shifted(down, "space", -1)
     def pieces(value):
         return value.reshape(2, high, -1, 128)
 
-    def joined(at, *terms):
-        return jnp.concatenate(
-            [
-                wide_sum(*(second[at] for second, _ in terms)),
-                wide_sum(*(first[at] for _, first in terms)),
-            ],
-            axis=-2,
-        )
-
-    second_far, second_near = swap(second[3], "dp", 1), swap(second[1], "dp", 1)
-    first, second_far, second_near = lax.optimization_barrier((first, second_far, second_near))
-    far = pieces(second_far), pieces(swap(first[3], "dp", 1))
-    near = pieces(second_near), pieces(swap(first[1], "dp", 1))
-    own = pieces(second[0]), pieces(first[0])
-    there = pieces(second[2]), pieces(first[2])
+    second = pieces(second)
+    far, near = pieces(swap(first[3], "dp", 1)), pieces(swap(first[1], "dp", 1))
+    own, there = pieces(first[0]), pieces(first[2])
     both = [
         (d * spaces + s, (d ^ 2) * spaces + (s ^ 1)) for d in range(4) for s in range(spaces)
     ]
-    got_xy = lax.ppermute(joined(1, there, far).astype(BF16), ("dp", "space"), both)
-    got_x = swap(joined(0, there, far).astype(BF16), "dp", 2)
-    got_y = swap(joined(1, own, near).astype(BF16), "space", 1)
-    held = added(joined(0, own, near), got_x, got_y, got_xy)
+    got_xy = lax.ppermute(added(there[1], far[1]), ("dp", "space"), both)
+    got_x = swap(added(there[0], far[0]), "dp", 2)
+    got_y = swap(jnp.concatenate([second[1], added(own[1], near[1])], axis=1), "space", 1)
+    held = jnp.concatenate(
+        [
+            added(second[0], got_y[:, :size_second]),
+            added(own[0], near[0], got_x, got_xy, got_y[:, size_second:]),
+        ],
+        axis=1,
+    )
     held, upper = lax.optimization_barrier((held, upper))
     mine = added(held[0], *(swap(held[k], "space", 2 * k) for k in range(1, high)))
     chunks = [mine] + [swap(mine, "space", 2 * k) for k in range(1, high)]

time: 80.1 us -> 76.9 us (0.960)
  waiting for transfers between devices: 36.3 us -> 28.3 us
  starting transfers between devices: 24.5 us -> 28.8 us
    ppermute x1, waiting for transfers between devices: 5.71 us -> 0.01 us  [local(): got_xy = lax.ppermute(added(there[1], far[1]), ('dp', 'space'), both)]
    ppermute x19 -> x23, starting transfers between devices: 15.9 us -> 21.3 us  [swap(): return lax.ppermute(value, axis, [(i, i ^ bits) for i in range(size)])]
    ppermute x19 -> x23, waiting for transfers between devices: 28 us -> 25.5 us  [swap(): return lax.ppermute(value, axis, [(i, i ^ bits) for i in range(size)])]
    pallas_call x7 -> x8, Pallas kernels: 13.7 us -> 14.4 us  [call(): pl.pallas_call(kernel, out_shape=out_shape, in_specs=specs, out_specs=jax...]
    unnamed x16 -> x18, local copies, waits for them, and re-layouts: 2.1 us -> 1.99 us
  transfers between devices with their start and end apart: 22 -> 26, of which waited for: 13 -> 14; matrix products, arithmetic and copies ran while one was open for 3% -> 3% of each run, Pallas kernels for 11% -> 17%
where the time goes in v4:
time: 76.9 us; the launch traced here: 76.6 us
  starting transfers between devices  28.8 us (37%)
  waiting for transfers between devices  28.3 us (37%)
  Pallas kernels  14.4 us (19%)
  local copies, waits for them, and re-layouts  3.79 us (5%)
  between operations  0.91 us (1%)
    ppermute x23, waiting for transfers between devices, swap(): return lax.ppermute(value, axis, [(i, i ^ bits) for i in range(size)])  25.5 us
    ppermute x23, starting transfers between devices, swap(): return lax.ppermute(value, axis, [(i, i ^ bits) for i in range(size)])  21.3 us
    pallas_call x8, Pallas kernels, call(): pl.pallas_call(kernel, out_shape=out_shape, in_specs=specs, out_specs=jax...  14.4 us
    ppermute x2, starting transfers between devices, shifted(): return lax.ppermute(value, axis, pairs)  4.97 us
    ppermute x2, waiting for transfers between devices, shifted(): return lax.ppermute(value, axis, pairs)  2.82 us
    ppermute x1, starting transfers between devices, local(): got_xy = lax.ppermute(added(there[1], far[1]), ('dp', 'space'), both)  2.62 us
    unnamed x18, local copies, waits for them, and re-layouts  1.99 us
    slice x1, local copies, waits for them, and re-layouts, local(): halo = shifted(inputs[planes - 3:], 'space', 1)  1.77 us
  transfers between devices with their start and end apart: 26, of which 14 were waited for; matrix products, arithmetic and copies ran while one was open for 3% of the time, Pallas kernels for 17%

profile of v4, /device:TPU:0, one launch (start us, length us, event | category | flops | bytes accessed | tf_op | source)
XLA Modules:
  0.0 76.6 jit_solution(15454029468241540997)
XLA Ops:
  0.6 3.0 %collective-permute-start.3 = (bf16[432,128]{1,0:T(8,128)(2,1)}, bf16[432,128]{1,0:T(8,128)(2,1)S(1)}, u32[]{:S(2)}, u32[]{:S(2)}) collective-permute-start(bf16[432,128]{1,0:T(8,128)(2,1)} %w0.7), channel_id=1, source_target_pairs={{0,16},{8,24},{16,0},{24,8},{1,17},{9,25},{17,1},{25,9},{2,18},{10... | collective-permute-start | bytes 331784 | tf_op jit(solution)/shard_map/ppermute | solution.py:562
  3.6 0.2 collective-permute-start.1
  3.8 0.4 collective-permute-start.5
  4.1 1.8 %slice_bitcast_fusion = bf16[3,32,2048]{2,1,0:T(8,128)(2,1)} fusion(bf16[1,8,32,2048]{3,2,1,0:T(8,128)(2,1)} %param.5), kind=kLoop, calls=%fused_computation.1 | loop fusion | bytes 786432 | tf_op jit(solution)/shard_map/slice | solution.py:594
  5.9 3.7 %collective-permute-start = (bf16[3,32,2048]{2,1,0:T(8,128)(2,1)}, bf16[3,32,2048]{2,1,0:T(8,128)(2,1)S(1)}, u32[]{:S(2)}, u32[]{:S(2)}) collective-permute-start(bf16[3,32,2048]{2,1,0:T(8,128)(2,1)} %slice_bitcast_fusion), channel_id=1, source_target_pairs={{0,1},{1,2},{2,3},{3,4},{4,5},{5,6},{6,7},{8,9},{9,10},{10,11},{11... | collective-permute-start | bytes 1179656 | tf_op jit(solution)/shard_map/ppermute | solution.py:568
  9.6 1.2 %copy-done = bf16[1,8,32,2048]{3,2,1,0:T(8,128)(2,1)S(1)} copy-done((bf16[1,8,32,2048]{3,2,1,0:T(8,128)(2,1)S(1)}, bf16[1,8,32,2048]{3,2,1,0:T(8,128)(2,1)}, u32[]{:S(2)}) %copy-start) | copy-done | bytes 1048600
  10.8 0.3 shard_map.84.sorted_ref
  11.2 0.1 collective-permute-start.4
  11.3 1.3 %collective-permute-done.4.w3 = bf16[432,128]{1,0:T(8,128)(2,1)S(1)} collective-permute-done((bf16[432,128]{1,0:T(8,128)(2,1)S(1)}, bf16[432,128]{1,0:T(8,128)(2,1)S(1)}, u32[]{:S(2)}, u32[]{:S(2)}) %collective-permute-start.4) | collective-permute-done | bytes 110624 | tf_op jit(solution)/shard_map/ppermute | solution.py:562
  12.6 2.1 %shard_map.85 = (f32[768,128]{1,0:T(8,128)S(1)}, f32[3,8,2,2,8,128]{5,4,3,2,1,0:T(8,128)S(1)}, f32[256,128]{1,0:T(8,128)S(1)}, bf16[2304,128]{1,0:T(8,128)(2,1)S(1)}) custom-call(s32[4]{0:T(128)S(1)} %broadcast_multiply_fusion.offsets, bf16[8,3,256,128]{3,2,1,0:T(8,128)(2,1)S(1)} %shard_map.84.sorted_ref, bf16[432,128]{1,0:T(8,128)(2,1)S(1)} %copy-done.2, ...), custom_call_target="tpu_custom_call" | custom-call | flops 2875000064 | bytes 3522560 | tf_op jit(solution)/shard_map/pallas_call | solution.py:49
  14.7 0.7 copy-done.7
  15.5 1.0 %collective-permute-done.1.w2 = bf16[864,256]{1,0:T(8,128)(2,1)S(1)} collective-permute-done((bf16[864,256]{1,0:T(8,128)(2,1)}, bf16[864,256]{1,0:T(8,128)(2,1)S(1)}, u32[]{:S(2)}, u32[]{:S(2)}) %collective-permute-start.1) | collective-permute-done | bytes 442400 | tf_op jit(solution)/shard_map/ppermute | solution.py:562
  16.5 2.3 %collective-permute-done.halo_ref = bf16[3,32,2048]{2,1,0:T(8,128)(2,1)S(1)} collective-permute-done((bf16[3,32,2048]{2,1,0:T(8,128)(2,1)}, bf16[3,32,2048]{2,1,0:T(8,128)(2,1)S(1)}, u32[]{:S(2)}, u32[]{:S(2)}) %collective-permute-start) | collective-permute-done | bytes 393248 | tf_op jit(solution)/shard_map/ppermute | solution.py:568
  18.7 0.9 %shard_map.86 = (f32[512,128]{1,0:T(8,128)S(1)}, bf16[128,3456]{1,0:T(8,128)(2,1)S(1)}, bf16[3,3,256,128]{3,2,1,0:T(8,128)(2,1)S(1)}, bf16[4,256,128]{2,1,0:T(8,128)(2,1)S(1)}, bf16[4,256,128]{2,1,0:T(8,128)(2,1)S(1)}) custom-call(f32[1]{0:T(128)} %bitcast.alive, s32[1]{0:T(128)} %bitcast.1.side, bf16[3,32,2048]{2,1,0:T(8,128)(2,1)S(1)} %collective-permute-done.halo_ref, ...), custom_call_target="tpu_custom_call" | custom-call | flops 1724999936 | bytes 3768320 | tf_op jit(solution)/shard_map/pallas_call | solution.py:49
  19.6 0.1 collective-permute-start.10
  19.7 1.6 %collective-permute-start.8 = (bf16[4,256,128]{2,1,0:T(8,128)(2,1)S(1)}, bf16[4,256,128]{2,1,0:T(8,128)(2,1)S(1)}, u32[]{:S(2)}, u32[]{:S(2)}) collective-permute-start(bf16[4,256,128]{2,1,0:T(8,128)(2,1)S(1)} %get-tuple-element.54), channel_id=1, source_target_pairs={{0,16},{8,24},{16,0},{24,8},{1,17},{9,25},{17,1},{25,9},{2,18},{10... | collective-permute-start | bytes 786440 | tf_op jit(solution)/shard_map/ppermute | solution.py:562
  21.3 1.8 %shard_map.87 = (bf16[2,8,2048]{2,1,0:T(8,128)(2,1)}, bf16[128,256]{1,0:T(8,128)(2,1)S(1)}) custom-call(s32[4]{0:T(128)S(1)} %get-tuple-element.74.offsets, bf16[128,3456]{1,0:T(8,128)(2,1)S(1)} %get-tuple-element.40.windows_ref, bf16[2,8,2048]{2,1,0:T(8,128)(2,1)S(1)} %bitcast.27, bf16[864,256]{1,0:T(8,128)(2,1)S(1)} %copy-done.1, ...), custom_call_target="tpu_custom_call" | custom-call | flops 1724999936 | bytes 2850816 | tf_op jit(solution)/shard_map/pallas_call | solution.py:49
  23.1 0.5 collective-permute-start.7
  23.7 0.0 copy-start.4
  23.7 3.0 %shard_map.88 = (bf16[768,128]{1,0:T(8,128)(2,1)S(1)}, f32[256,128]{1,0:T(8,128)S(1)}, bf16[512,128]{1,0:T(8,128)(2,1)S(1)}, bf16[8,64,128]{2,1,0:T(8,128)(2,1)S...) custom-call(s32[4]{0:T(128)S(1)} %get-tuple-element.74.offsets, ...), custom_call_target="tpu_custom_call" | custom-call | flops 4024999936 | bytes 5636096 | tf_op jit(solution)/shard_map/pallas_call | solution.py:49
  26.7 2.2 %collective-permute-done.8.h2 = bf16[4,256,128]{2,1,0:T(8,128)(2,1)S(1)} collective-permute-done((bf16[4,256,128]{2,1,0:T(8,128)(2,1)S(1)}, bf16[4,256,128]{2,1,0:T(8,128)(2,1)S(1)}, u32[]{:S(2)}, u32[]{:S(2)}) %collective-permute-start.8) | collective-permute-done | bytes 262176 | tf_op jit(solution)/shard_map/ppermute | solution.py:562
  28.9 1.0 %collective-permute-done.7.d2 = bf16[128,256]{1,0:T(8,128)(2,1)S(1)} collective-permute-done((bf16[128,256]{1,0:T(8,128)(2,1)S(1)}, bf16[128,256]{1,0:T(8,128)(2,1)S(1)}, u32[]{:S(2)}, u32[]{:S(2)}) %collective-permute-start.7) | collective-permute-done | bytes 65568 | tf_op jit(solution)/shard_map/ppermute | solution.py:562
  29.9 0.5 collective-permute-start.11
  30.4 0.5 collective-permute-start.15
  30.9 0.3 collective-permute-done.13
  31.2 0.4 collective-permute-done.12.d3
  31.7 1.8 %shard_map.89 = bf16[8,224,128]{2,1,0:T(8,128)(2,1)S(1)} custom-call(s32[1]{0:T(128)} %bitcast.6.data, s32[4,25]{1,0:T(4,128)S(1)} %copy-done.4, s32[8]{0:T(128)S(1)} %fusion.5.order, bf16[4,256,128]{2,1,0:T(8,128)(2,1)S(1)} %get-tuple-element.49.h0, bf16[4,256,128]{2,1,0:T(8,128)(2,1)S(1)} %collective-permute-done.10.h1, ...), custom_call_target="tpu_custom_call" | custom-call | flops 2300000000 | bytes 1769472 | tf_op jit(solution)/shard_map/pallas_call | solution.py:49
  33.5 2.4 %collective-permute-start.14 = (bf16[4,288,128]{2,1,0:T(8,128)(2,1)S(1)}, bf16[4,288,128]{2,1,0:T(8,128)(2,1)S(1)}, u32[]{:S(2)}, u32[]{:S(2)}) collective-permute-start(bf16[4,288,128]{2,1,0:T(8,128)(2,1)S(1)} %pad_maximum_fusion), channel_id=1, source_target_pairs={{0,1},{1,0},{2,3},{3,2},{4,5},{5,4},{6,7},{7,6},{8,9},{9,8},{10,11... | collective-permute-start | bytes 884744 | tf_op jit(solution)/shard_map/ppermute | solution.py:562
  36.0 1.3 %collective-permute-start.18 = (bf16[512,128]{1,0:T(8,128)(2,1)S(1)}, bf16[512,128]{1,0:T(8,128)(2,1)S(1)}, u32[]{:S(2)}, u32[]{:S(2)}) collective-permute-start(bf16[512,128]{1,0:T(8,128)(2,1)S(1)} %get-tuple-element.63), channel_id=1, source_target_pairs={{1,0},{2,1},{3,2},{4,3},{5,4},{6,5},{7,6},{9,8},{10,9},{11,10},{12... | collective-permute-start | bytes 393224 | tf_op jit(solution)/shard_map/ppermute | solution.py:568
  37.3 1.6 %collective-permute-start.16 = (bf16[4,64,128]{2,1,0:T(8,128)(2,1)S(1)}, bf16[4,64,128]{2,1,0:T(8,128)(2,1)S(1)}, u32[]{:S(2)}, u32[]{:S(2)}) collective-permute-start(bf16[4,64,128]{2,1,0:T(8,128)(2,1)S(1)} %get-tuple-element.71), channel_id=1, source_target_pairs={{0,16},{8,24},{16,0},{24,8},{1,17},{9,25},{17,1},{25,9},{2,18},{10... | collective-permute-start | bytes 196616 | tf_op jit(solution)/shard_map/ppermute | solution.py:562
  38.9 2.6 %collective-permute-start.17 = (bf16[4,64,128]{2,1,0:T(8,128)(2,1)S(1)}, bf16[4,64,128]{2,1,0:T(8,128)(2,1)S(1)}, u32[]{:S(2)}, u32[]{:S(2)}) collective-permute-start(bf16[4,64,128]{2,1,0:T(8,128)(2,1)S(1)} %get-tuple-element.72), channel_id=1, source_target_pairs={{0,17},{1,16},{2,19},{3,18},{4,21},{5,20},{6,23},{7,22},{8,25},{9,... | collective-permute-start | bytes 196616 | tf_op jit(solution)/shard_map/ppermute | solution.py:632
  41.5 5.4 %collective-permute-done.14 = bf16[4,288,128]{2,1,0:T(8,128)(2,1)S(1)} collective-permute-done((bf16[4,288,128]{2,1,0:T(8,128)(2,1)S(1)}, bf16[4,288,128]{2,1,0:T(8,128)(2,1)S(1)}, u32[]{:S(2)}, u32[]{:S(2)}) %collective-permute-start.14) | collective-permute-done | bytes 294944 | tf_op jit(solution)/shard_map/ppermute | solution.py:562
  47.0 0.1 add_convert_fusion
  47.0 0.1 add_convert_fusion.1
  47.1 0.6 collective-permute-done.18.upper_ref
  47.7 2.8 %collective-permute-start.19 = (bf16[288,128]{1,0:T(8,128)(2,1)S(1)}, bf16[288,128]{1,0:T(8,128)(2,1)S(1)}, u32[]{:S(2)}, u32[]{:S(2)}) collective-permute-start(bf16[288,128]{1,0:T(8,128)(2,1)S(1)} %get-tuple-element.68), channel_id=1, source_target_pairs={{0,2},{1,3},{2,0},{3,1},{4,6},{5,7},{6,4},{7,5},{8,10},{9,11},{10,... | collective-permute-start | bytes 221192 | tf_op jit(solution)/shard_map/ppermute | solution.py:562
  50.5 2.6 %collective-permute-start.20 = (bf16[288,128]{1,0:T(8,128)(2,1)S(1)}, bf16[288,128]{1,0:T(8,128)(2,1)S(1)}, u32[]{:S(2)}, u32[]{:S(2)}) collective-permute-start(bf16[288,128]{1,0:T(8,128)(2,1)S(1)} %get-tuple-element.70), channel_id=1, source_target_pairs={{0,4},{1,5},{2,6},{3,7},{4,0},{5,1},{6,2},{7,3},{8,12},{9,13},{10,... | collective-permute-start | bytes 221192 | tf_op jit(solution)/shard_map/ppermute | solution.py:562
  53.1 4.9 %collective-permute-done.20 = bf16[288,128]{1,0:T(8,128)(2,1)S(1)} collective-permute-done((bf16[288,128]{1,0:T(8,128)(2,1)S(1)}, bf16[288,128]{1,0:T(8,128)(2,1)S(1)}, u32[]{:S(2)}, u32[]{:S(2)}) %collective-permute-start.20) | collective-permute-done | bytes 73760 | tf_op jit(solution)/shard_map/ppermute | solution.py:562
  57.9 1.4 %collective-permute-done.21 = bf16[288,128]{1,0:T(8,128)(2,1)S(1)} collective-permute-done((bf16[288,128]{1,0:T(8,128)(2,1)S(1)}, bf16[288,128]{1,0:T(8,128)(2,1)S(1)}, u32[]{:S(2)}, u32[]{:S(2)}) %collective-permute-start.21) | collective-permute-done | bytes 73760 | tf_op jit(solution)/shard_map/ppermute | solution.py:562
  59.4 0.8 %collective-permute-start.22 = (bf16[288,128]{1,0:T(8,128)(2,1)S(1)}, bf16[288,128]{1,0:T(8,128)(2,1)S(1)}, u32[]{:S(2)}, u32[]{:S(2)}) collective-permute-start(bf16[288,128]{1,0:T(8,128)(2,1)S(1)} %fusion.2.refs_0_), channel_id=1, source_target_pairs={{0,2},{1,3},{2,0},{3,1},{4,6},{5,7},{6,4},{7,5},{8,10},{9,11},{10,... | collective-permute-start | bytes 221192 | tf_op jit(solution)/shard_map/ppermute | solution.py:562
  60.2 1.7 %collective-permute-start.23 = (bf16[288,128]{1,0:T(8,128)(2,1)S(1)}, bf16[288,128]{1,0:T(8,128)(2,1)S(1)}, u32[]{:S(2)}, u32[]{:S(2)}) collective-permute-start(bf16[288,128]{1,0:T(8,128)(2,1)S(1)} %fusion.2.refs_0_), channel_id=1, source_target_pairs={{0,4},{1,5},{2,6},{3,7},{4,0},{5,1},{6,2},{7,3},{8,12},{9,13},{10,... | collective-permute-start | bytes 221192 | tf_op jit(solution)/shard_map/ppermute | solution.py:562
  61.9 1.9 %collective-permute-start.24 = (bf16[288,128]{1,0:T(8,128)(2,1)S(1)}, bf16[288,128]{1,0:T(8,128)(2,1)S(1)}, u32[]{:S(2)}, u32[]{:S(2)}) collective-permute-start(bf16[288,128]{1,0:T(8,128)(2,1)S(1)} %fusion.2.refs_0_), channel_id=1, source_target_pairs={{0,6},{1,7},{2,4},{3,5},{4,2},{5,3},{6,0},{7,1},{8,14},{9,15},{10,... | collective-permute-start | bytes 221192 | tf_op jit(solution)/shard_map/ppermute | solution.py:562
  63.8 2.8 %collective-permute-done.23.refs_2_ = bf16[288,128]{1,0:T(8,128)(2,1)S(1)} collective-permute-done((bf16[288,128]{1,0:T(8,128)(2,1)S(1)}, bf16[288,128]{1,0:T(8,128)(2,1)S(1)}, u32[]{:S(2)}, u32[]{:S(2)}) %collective-permute-start.23) | collective-permute-done | bytes 73760 | tf_op jit(solution)/shard_map/ppermute | solution.py:562
  66.6 1.5 %collective-permute-done.24.refs_3_ = bf16[288,128]{1,0:T(8,128)(2,1)S(1)} collective-permute-done((bf16[288,128]{1,0:T(8,128)(2,1)S(1)}, bf16[288,128]{1,0:T(8,128)(2,1)S(1)}, u32[]{:S(2)}, u32[]{:S(2)}) %collective-permute-start.24) | collective-permute-done | bytes 73760 | tf_op jit(solution)/shard_map/ppermute | solution.py:562
  68.2 0.7 collective-permute-start.25
  68.9 2.8 %shard_map.90 = bf16[8,32,2048]{2,1,0:T(8,128)(2,1)} custom-call(s32[4]{0:T(128)S(1)} %broadcast_multiply_fusion.offsets, bf16[768,128]{1,0:T(8,128)(2,1)S(1)} %get-tuple-element.47.low_ref, f32[256,128]{1,0:T(8,128)S(1)} %get-tuple-element.48.last_ref, f32[768,128]{1,0:T(8,128)S(1)} %copy-done.8, bf16[512,128]{1,0:T(8,128)(2,1)S(1)} %collective-permute-done.18.upper_ref, ...), custom_call_target="tpu_custom_call" | custom-call | flops 3449999872 | bytes 2342912 | tf_op jit(solution)/shard_map/pallas_call | solution.py:49
  71.6 3.3 %collective-permute-done.25.refs_4_ = bf16[4,288,128]{2,1,0:T(8,128)(2,1)S(1)} collective-permute-done((bf16[4,288,128]{2,1,0:T(8,128)(2,1)S(1)}, bf16[4,288,128]{2,1,0:T(8,128)(2,1)S(1)}, u32[]{:S(2)}, u32[]{:S(2)}) %collective-permute-start.25) | collective-permute-done | bytes 294944 | tf_op jit(solution)/shard_map/ppermute | solution.py:562
  75.0 1.7 %shard_map.91 = (f32[432,128]{1,0:T(8,128)}, f32[864,256]{1,0:T(8,128)}) custom-call(s32[8]{0:T(128)S(1)} %fusion.5.order, bf16[288,128]{1,0:T(8,128)(2,1)S(1)} %fusion.2.refs_0_, bf16[288,128]{1,0:T(8,128)(2,1)S(1)} %collective-permute-done.22.refs_1_, bf16[288,128]{1,0:T(8,128)(2,1)S(1)} %collective-permute-done.23.refs_2_, ...), custom_call_target="tpu_custom_call" | custom-call | flops 1150000000 | bytes 1695744 | tf_op jit(solution)/shard_map/pallas_call | solution.py:49
  (44 shorter events, 0.3 us)
Async XLA Ops:
  0.6 10.6 %collective-permute-start.3 = (bf16[432,128]{1,0:T(8,128)(2,1)}, bf16[432,128]{1,0:T(8,128)(2,1)S(1)}, u32[]{:S(2)}, u32[]{:S(2)}) collective-permute-start(bf16[432,128]{1,0:T(8,128)(2,1)} %w0.7), channel_id=1, source_target_pairs={{0,16},{8,24},{16,0},{24,8},{1,17},{9,25},{17,1},{25,9},{2,18},{10... | collective-permute-start | bytes 331784 | tf_op jit(solution)/shard_map/ppermute | solution.py:562
  3.6 7.7 %collective-permute-start.2 = (bf16[432,128]{1,0:T(8,128)(2,1)}, bf16[432,128]{1,0:T(8,128)(2,1)S(1)}, u32[]{:S(2)}, u32[]{:S(2)}) collective-permute-start(bf16[432,128]{1,0:T(8,128)(2,1)} %w0.7), channel_id=1, source_target_pairs={{0,8},{8,0},{16,24},{24,16},{1,9},{9,1},{17,25},{25,17},{2,10},{10... | collective-permute-start | bytes 331784 | tf_op jit(solution)/shard_map/ppermute | solution.py:562
  3.6 12.8 %collective-permute-start.1 = (bf16[864,256]{1,0:T(8,128)(2,1)}, bf16[864,256]{1,0:T(8,128)(2,1)S(1)}, u32[]{:S(2)}, u32[]{:S(2)}) collective-permute-start(bf16[864,256]{1,0:T(8,128)(2,1)} %w0.6), channel_id=1, source_target_pairs={{0,16},{8,24},{16,0},{24,8},{1,17},{9,25},{17,1},{25,9},{2,18},{10... | collective-permute-start | bytes 1327112 | tf_op jit(solution)/shard_map/ppermute | solution.py:562
  3.8 17.5 %collective-permute-start.5 = (bf16[864,256]{1,0:T(8,128)(2,1)}, bf16[864,256]{1,0:T(8,128)(2,1)S(1)}, u32[]{:S(2)}, u32[]{:S(2)}) collective-permute-start(bf16[864,256]{1,0:T(8,128)(2,1)} %w0.6), channel_id=1, source_target_pairs={{0,8},{8,0},{16,24},{24,16},{1,9},{9,1},{17,25},{25,17},{2,10},{10... | collective-permute-start | bytes 1327112 | tf_op jit(solution)/shard_map/ppermute | solution.py:562
  5.9 12.8 %collective-permute-start = (bf16[3,32,2048]{2,1,0:T(8,128)(2,1)}, bf16[3,32,2048]{2,1,0:T(8,128)(2,1)S(1)}, u32[]{:S(2)}, u32[]{:S(2)}) collective-permute-start(bf16[3,32,2048]{2,1,0:T(8,128)(2,1)} %slice_bitcast_fusion), channel_id=1, source_target_pairs={{0,1},{1,2},{2,3},{3,4},{4,5},{5,6},{6,7},{8,9},{9,10},{10,11},{11... | collective-permute-start | bytes 1179656 | tf_op jit(solution)/shard_map/ppermute | solution.py:568
  9.6 1.2 %copy-start = (bf16[1,8,32,2048]{3,2,1,0:T(8,128)(2,1)S(1)}, bf16[1,8,32,2048]{3,2,1,0:T(8,128)(2,1)}, u32[]{:S(2)}) copy-start(bf16[1,8,32,2048]{3,2,1,0:T(8,128)(2,1)} %param.5) | copy-start | bytes 3145732
  10.8 1.8 %copy-start.2 = (bf16[432,128]{1,0:T(8,128)(2,1)S(1)}, bf16[432,128]{1,0:T(8,128)(2,1)}, u32[]{:S(2)}) copy-start(bf16[432,128]{1,0:T(8,128)(2,1)} %w0.7) | copy-start | bytes 331780
  11.2 3.5 %copy-start.5 = (bf16[8,3,256,128]{3,2,1,0:T(8,128)(2,1)}, bf16[8,3,256,128]{3,2,1,0:T(8,128)(2,1)S(1)}, u32[]{:S(2)}) copy-start(bf16[8,3,256,128]{3,2,1,0:T(8,128)(2,1)S(1)} %shard_map.84.sorted_ref) | copy-start | bytes 4718596
  11.2 1.4 %collective-permute-start.4 = (bf16[432,128]{1,0:T(8,128)(2,1)S(1)}, bf16[432,128]{1,0:T(8,128)(2,1)S(1)}, u32[]{:S(2)}, u32[]{:S(2)}) collective-permute-start(bf16[432,128]{1,0:T(8,128)(2,1)S(1)} %collective-permute-done.3.w2), channel_id=1, source_target_pairs={{0,8},{8,0},{16,24},{24,16},{1,9},{9,1},{17,25},{25,17},{2,10},{10... | collective-permute-start | bytes 331784 | tf_op jit(solution)/shard_map/ppermute | solution.py:562
  14.7 0.7 copy-start.7
  16.4 4.9 %collective-permute-start.6 = (bf16[864,256]{1,0:T(8,128)(2,1)S(1)}, bf16[864,256]{1,0:T(8,128)(2,1)S(1)}, u32[]{:S(2)}, u32[]{:S(2)}) collective-permute-start(bf16[864,256]{1,0:T(8,128)(2,1)S(1)} %collective-permute-done.1.w2), channel_id=1, source_target_pairs={{0,8},{8,0},{16,24},{24,16},{1,9},{9,1},{17,25},{25,17},{2,10},{10... | collective-permute-start | bytes 1327112 | tf_op jit(solution)/shard_map/ppermute | solution.py:562
  18.7 2.6 %copy-start.1 = (bf16[864,256]{1,0:T(8,128)(2,1)S(1)}, bf16[864,256]{1,0:T(8,128)(2,1)}, u32[]{:S(2)}) copy-start(bf16[864,256]{1,0:T(8,128)(2,1)} %w0.6) | copy-start | bytes 1327108
  18.7 2.6 %copy-start.3 = (bf16[1,2,8,2048]{3,2,1,0:T(8,128)(2,1)S(1)}, bf16[1,2,8,2048]{3,2,1,0:T(8,128)(2,1)}, u32[]{:S(2)}) copy-start(bf16[1,2,8,2048]{3,2,1,0:T(8,128)(2,1)} %param.8) | copy-start | bytes 196612
  19.6 7.1 %collective-permute-start.10 = (bf16[4,256,128]{2,1,0:T(8,128)(2,1)S(1)}, bf16[4,256,128]{2,1,0:T(8,128)(2,1)S(1)}, u32[]{:S(2)}, u32[]{:S(2)}) collective-permute-start(bf16[4,256,128]{2,1,0:T(8,128)(2,1)S(1)} %get-tuple-element.49.h0), channel_id=1, source_target_pairs={{0,8},{8,0},{16,24},{24,16},{1,9},{9,1},{17,25},{25,17},{2,10},{10... | collective-permute-start | bytes 786440 | tf_op jit(solution)/shard_map/ppermute | solution.py:562
  19.7 9.2 %collective-permute-start.8 = (bf16[4,256,128]{2,1,0:T(8,128)(2,1)S(1)}, bf16[4,256,128]{2,1,0:T(8,128)(2,1)S(1)}, u32[]{:S(2)}, u32[]{:S(2)}) collective-permute-start(bf16[4,256,128]{2,1,0:T(8,128)(2,1)S(1)} %get-tuple-element.54), channel_id=1, source_target_pairs={{0,16},{8,24},{16,0},{24,8},{1,17},{9,25},{17,1},{25,9},{2,18},{10... | collective-permute-start | bytes 786440 | tf_op jit(solution)/shard_map/ppermute | solution.py:562
  21.3 2.4 %copy-start.6 = (bf16[8,3,256,128]{3,2,1,0:T(8,128)(2,1)S(1)}, bf16[8,3,256,128]{3,2,1,0:T(8,128)(2,1)}, u32[]{:S(2)}) copy-start(bf16[8,3,256,128]{3,2,1,0:T(8,128)(2,1)} %copy-done.5) | copy-start | bytes 4718596
  21.3 2.4 %copy-start.8 = (f32[768,128]{1,0:T(8,128)S(1)}, f32[768,128]{1,0:T(8,128)}, u32[]{:S(2)}) copy-start(f32[768,128]{1,0:T(8,128)} %copy-done.7) | copy-start | bytes 1179652
  23.1 6.7 %collective-permute-start.7 = (bf16[128,256]{1,0:T(8,128)(2,1)S(1)}, bf16[128,256]{1,0:T(8,128)(2,1)S(1)}, u32[]{:S(2)}, u32[]{:S(2)}) collective-permute-start(bf16[128,256]{1,0:T(8,128)(2,1)S(1)} %get-tuple-element.43.delta_ref.d0), channel_id=1, source_target_pairs={{0,16},{8,24},{16,0},{24,8},{1,17},{9,25},{17,1},{25,9},{2,18},{10... | collective-permute-start | bytes 196616 | tf_op jit(solution)/shard_map/ppermute | solution.py:562
  23.7 6.2 %collective-permute-start.9 = (bf16[128,256]{1,0:T(8,128)(2,1)S(1)}, bf16[128,256]{1,0:T(8,128)(2,1)S(1)}, u32[]{:S(2)}, u32[]{:S(2)}) collective-permute-start(bf16[128,256]{1,0:T(8,128)(2,1)S(1)} %get-tuple-element.43.delta_ref.d0), channel_id=1, source_target_pairs={{0,8},{8,0},{16,24},{24,16},{1,9},{9,1},{17,25},{25,17},{2,10},{10... | collective-permute-start | bytes 196616 | tf_op jit(solution)/shard_map/ppermute | solution.py:562
  23.7 8.0 %copy-start.4 = (s32[4,25]{1,0:T(4,128)S(1)}, s32[4,25]{1,0:T(4,128)}, u32[]{:S(2)}) copy-start(s32[4,25]{1,0:T(4,128)} %constant.48.clone.table) | copy-start | bytes 1204
  29.8 1.3 %collective-permute-start.13 = (bf16[8,64,128]{2,1,0:T(8,128)(2,1)S(1)}, bf16[8,64,128]{2,1,0:T(8,128)(2,1)S(1)}, u32[]{:S(2)}, u32[]{:S(2)}) collective-permute-start(bf16[8,64,128]{2,1,0:T(8,128)(2,1)S(1)} %get-tuple-element.60), channel_id=1, source_target_pairs={{0,8},{8,0},{16,24},{24,16},{1,9},{9,1},{17,25},{25,17},{2,10},{10... | collective-permute-start | bytes 393224 | tf_op jit(solution)/shard_map/ppermute | solution.py:562
  29.9 1.8 %collective-permute-start.11 = (bf16[4,256,128]{2,1,0:T(8,128)(2,1)S(1)}, bf16[4,256,128]{2,1,0:T(8,128)(2,1)S(1)}, u32[]{:S(2)}, u32[]{:S(2)}) collective-permute-start(bf16[4,256,128]{2,1,0:T(8,128)(2,1)S(1)} %collective-permute-done.8.h2), channel_id=1, source_target_pairs={{0,8},{8,0},{16,24},{24,16},{1,9},{9,1},{17,25},{25,17},{2,10},{10... | collective-permute-start | bytes 786440 | tf_op jit(solution)/shard_map/ppermute | solution.py:562
  30.4 1.3 %collective-permute-start.12 = (bf16[128,256]{1,0:T(8,128)(2,1)S(1)}, bf16[128,256]{1,0:T(8,128)(2,1)S(1)}, u32[]{:S(2)}, u32[]{:S(2)}) collective-permute-start(bf16[128,256]{1,0:T(8,128)(2,1)S(1)} %collective-permute-done.7.d2), channel_id=1, source_target_pairs={{0,8},{8,0},{16,24},{24,16},{1,9},{9,1},{17,25},{25,17},{2,10},{10... | collective-permute-start | bytes 196616 | tf_op jit(solution)/shard_map/ppermute | solution.py:562
  30.4 6.9 %collective-permute-start.15 = (bf16[8,64,128]{2,1,0:T(8,128)(2,1)S(1)}, bf16[8,64,128]{2,1,0:T(8,128)(2,1)S(1)}, u32[]{:S(2)}, u32[]{:S(2)}) collective-permute-start(bf16[8,64,128]{2,1,0:T(8,128)(2,1)S(1)} %get-tuple-element.62), channel_id=1, source_target_pairs={{0,8},{8,0},{16,24},{24,16},{1,9},{9,1},{17,25},{25,17},{2,10},{10... | collective-permute-start | bytes 393224 | tf_op jit(solution)/shard_map/ppermute | solution.py:562
  33.5 13.4 %collective-permute-start.14 = (bf16[4,288,128]{2,1,0:T(8,128)(2,1)S(1)}, bf16[4,288,128]{2,1,0:T(8,128)(2,1)S(1)}, u32[]{:S(2)}, u32[]{:S(2)}) collective-permute-start(bf16[4,288,128]{2,1,0:T(8,128)(2,1)S(1)} %pad_maximum_fusion), channel_id=1, source_target_pairs={{0,1},{1,0},{2,3},{3,2},{4,5},{5,4},{6,7},{7,6},{8,9},{9,8},{10,11... | collective-permute-start | bytes 884744 | tf_op jit(solution)/shard_map/ppermute | solution.py:562
  36.0 11.7 %collective-permute-start.18 = (bf16[512,128]{1,0:T(8,128)(2,1)S(1)}, bf16[512,128]{1,0:T(8,128)(2,1)S(1)}, u32[]{:S(2)}, u32[]{:S(2)}) collective-permute-start(bf16[512,128]{1,0:T(8,128)(2,1)S(1)} %get-tuple-element.63), channel_id=1, source_target_pairs={{1,0},{2,1},{3,2},{4,3},{5,4},{6,5},{7,6},{9,8},{10,9},{11,10},{12... | collective-permute-start | bytes 393224 | tf_op jit(solution)/shard_map/ppermute | solution.py:568
  37.3 9.7 %collective-permute-start.16 = (bf16[4,64,128]{2,1,0:T(8,128)(2,1)S(1)}, bf16[4,64,128]{2,1,0:T(8,128)(2,1)S(1)}, u32[]{:S(2)}, u32[]{:S(2)}) collective-permute-start(bf16[4,64,128]{2,1,0:T(8,128)(2,1)S(1)} %get-tuple-element.71), channel_id=1, source_target_pairs={{0,16},{8,24},{16,0},{24,8},{1,17},{9,25},{17,1},{25,9},{2,18},{10... | collective-permute-start | bytes 196616 | tf_op jit(solution)/shard_map/ppermute | solution.py:562
  38.9 8.1 %collective-permute-start.17 = (bf16[4,64,128]{2,1,0:T(8,128)(2,1)S(1)}, bf16[4,64,128]{2,1,0:T(8,128)(2,1)S(1)}, u32[]{:S(2)}, u32[]{:S(2)}) collective-permute-start(bf16[4,64,128]{2,1,0:T(8,128)(2,1)S(1)} %get-tuple-element.72), channel_id=1, source_target_pairs={{0,17},{1,16},{2,19},{3,18},{4,21},{5,20},{6,23},{7,22},{8,25},{9,... | collective-permute-start | bytes 196616 | tf_op jit(solution)/shard_map/ppermute | solution.py:632
  47.7 5.4 %collective-permute-start.19 = (bf16[288,128]{1,0:T(8,128)(2,1)S(1)}, bf16[288,128]{1,0:T(8,128)(2,1)S(1)}, u32[]{:S(2)}, u32[]{:S(2)}) collective-permute-start(bf16[288,128]{1,0:T(8,128)(2,1)S(1)} %get-tuple-element.68), channel_id=1, source_target_pairs={{0,2},{1,3},{2,0},{3,1},{4,6},{5,7},{6,4},{7,5},{8,10},{9,11},{10,... | collective-permute-start | bytes 221192 | tf_op jit(solution)/shard_map/ppermute | solution.py:562
  50.5 7.5 %collective-permute-start.20 = (bf16[288,128]{1,0:T(8,128)(2,1)S(1)}, bf16[288,128]{1,0:T(8,128)(2,1)S(1)}, u32[]{:S(2)}, u32[]{:S(2)}) collective-permute-start(bf16[288,128]{1,0:T(8,128)(2,1)S(1)} %get-tuple-element.70), channel_id=1, source_target_pairs={{0,4},{1,5},{2,6},{3,7},{4,0},{5,1},{6,2},{7,3},{8,12},{9,13},{10,... | collective-permute-start | bytes 221192 | tf_op jit(solution)/shard_map/ppermute | solution.py:562
  53.1 6.3 %collective-permute-start.21 = (bf16[288,128]{1,0:T(8,128)(2,1)S(1)}, bf16[288,128]{1,0:T(8,128)(2,1)S(1)}, u32[]{:S(2)}, u32[]{:S(2)}) collective-permute-start(bf16[288,128]{1,0:T(8,128)(2,1)S(1)} %get-tuple-element.69), channel_id=1, source_target_pairs={{0,6},{1,7},{2,4},{3,5},{4,2},{5,3},{6,0},{7,1},{8,14},{9,15},{10,... | collective-permute-start | bytes 221192 | tf_op jit(solution)/shard_map/ppermute | solution.py:562
  59.4 4.5 %collective-permute-start.22 = (bf16[288,128]{1,0:T(8,128)(2,1)S(1)}, bf16[288,128]{1,0:T(8,128)(2,1)S(1)}, u32[]{:S(2)}, u32[]{:S(2)}) collective-permute-start(bf16[288,128]{1,0:T(8,128)(2,1)S(1)} %fusion.2.refs_0_), channel_id=1, source_target_pairs={{0,2},{1,3},{2,0},{3,1},{4,6},{5,7},{6,4},{7,5},{8,10},{9,11},{10,... | collective-permute-start | bytes 221192 | tf_op jit(solution)/shard_map/ppermute | solution.py:562
  60.2 6.4 %collective-permute-start.23 = (bf16[288,128]{1,0:T(8,128)(2,1)S(1)}, bf16[288,128]{1,0:T(8,128)(2,1)S(1)}, u32[]{:S(2)}, u32[]{:S(2)}) collective-permute-start(bf16[288,128]{1,0:T(8,128)(2,1)S(1)} %fusion.2.refs_0_), channel_id=1, source_target_pairs={{0,4},{1,5},{2,6},{3,7},{4,0},{5,1},{6,2},{7,3},{8,12},{9,13},{10,... | collective-permute-start | bytes 221192 | tf_op jit(solution)/shard_map/ppermute | solution.py:562
  61.9 6.3 %collective-permute-start.24 = (bf16[288,128]{1,0:T(8,128)(2,1)S(1)}, bf16[288,128]{1,0:T(8,128)(2,1)S(1)}, u32[]{:S(2)}, u32[]{:S(2)}) collective-permute-start(bf16[288,128]{1,0:T(8,128)(2,1)S(1)} %fusion.2.refs_0_), channel_id=1, source_target_pairs={{0,6},{1,7},{2,4},{3,5},{4,2},{5,3},{6,0},{7,1},{8,14},{9,15},{10,... | collective-permute-start | bytes 221192 | tf_op jit(solution)/shard_map/ppermute | solution.py:562
  68.2 6.8 %collective-permute-start.25 = (bf16[4,288,128]{2,1,0:T(8,128)(2,1)S(1)}, bf16[4,288,128]{2,1,0:T(8,128)(2,1)S(1)}, u32[]{:S(2)}, u32[]{:S(2)}) collective-permute-start(bf16[4,288,128]{2,1,0:T(8,128)(2,1)S(1)} %pad_maximum_fusion.2), channel_id=1, source_target_pairs={{0,1},{1,0},{2,3},{3,2},{4,5},{5,4},{6,7},{7,6},{8,9},{9,8},{10,11... | collective-permute-start | bytes 884744 | tf_op jit(solution)/shard_map/ppermute | solution.py:562

commit v5 on v4

--- a/solution.py
+++ b/solution.py
@@ -81,6 +81,29 @@
             out_ref[plane, tap] = both.reshape(pairs * 16, 128).astype(BF16)
 
 
+def last_planes_kernel(volume_ref, out_ref, sem):
+    count = out_ref.shape[0]
+    copy = pltpu.make_async_copy(
+        volume_ref.at[pl.ds(volume_ref.shape[0] - count, count)], out_ref, sem
+    )
+    copy.start()
+    copy.wait()
+
+
+def last_planes(volume, count):
+    shape = (count, *volume.shape[1:])
+    return pl.pallas_call(
+        last_planes_kernel,
+        out_shape=sds(shape, BF16),
+        in_specs=[pl.BlockSpec(memory_space=pltpu.HBM)],
+        out_specs=pl.BlockSpec(memory_space=pltpu.HBM),
+        scratch_shapes=[pltpu.SemaphoreType.DMA],
+        cost_estimate=pl.CostEstimate(
+            flops=0, bytes_accessed=4 * shape[0] * shape[1] * shape[2], transcendentals=0
+        ),
+    )(volume)
+
+
 def sorted_planes(volume):
     planes, rows, width = volume.shape
     pairs = width // 128
@@ -139,14 +162,17 @@
 
 def forward_upper_kernel(
     offsets, sorted_ref, w0, w1, w2, w3,
-    slope_ref, hidden_ref, partial_ref, padded_ref, columns, some, whole,
+    slope_ref, hidden_ref, middle_ref, partial_ref, padded_ref, columns, some, whole,
 ):
     cells = sorted_ref.shape[0] // 2
     put_rows(whole, (w0, w1, w2, w3), offsets)
     pad_first(whole, padded_ref)
     gather_taps(columns, sorted_ref, None, 1, cells - 1)
     linear = jnp.dot(columns[...], padded_ref[...], preferred_element_type=F32)
-    hidden_ref[...] = activate(linear).reshape(hidden_ref.shape)
+    hidden = activate(linear)
+    hidden_ref[...] = hidden.reshape(hidden_ref.shape)
+    count = middle_ref.shape[0] * middle_ref.shape[1]
+    middle_ref[...] = hidden[:count].reshape(middle_ref.shape).astype(BF16)
     slope_ref[...] = activate_slope(linear)
     for a in range(1, 3):
         for e in range(3):
@@ -164,6 +190,7 @@
         (
             sds((some, 128), F32),
             sds((cells - 1, rows // 32, 2, 2, 8, 128), F32),
+            sds((cells - 2, rows, 128), BF16),
             sds((rows, 128), F32),
             sds((9 * 256, 128), BF16),
         ),
@@ -198,11 +225,12 @@
     slope_ref[rows:, :] = activate_slope(here)
     lowest[0] = (activate(below) * alive[0]).reshape(lowest.shape[1:])
     lowest[1] = activate(here).reshape(lowest.shape[1:])
-    for plane in range(cells + 1):
-        source = lowest.at[plane] if plane < 2 else hidden_ref.at[plane - 2]
-        planes[plane] = source[...].reshape(rows, 128).astype(BF16)
-    here_ref[...] = planes[pl.ds(side[0], cells)]
-    there_ref[...] = planes[pl.ds(1 - side[0], cells)]
+    planes[0] = lowest[0].reshape(rows, 128).astype(BF16)
+    planes[1] = lowest[1].reshape(rows, 128).astype(BF16)
+    planes[2] = planes[1]
+    planes[3] = hidden_ref[cells - 2].reshape(rows, 128).astype(BF16)
+    here_ref[...] = planes[pl.ds(2 * side[0], 2)]
+    there_ref[...] = planes[pl.ds(2 - 2 * side[0], 2)]
     for out in range(cells // 2):
         for a in range(3):
             plane = 2 * out - 1 + a
@@ -223,15 +251,15 @@
             sds((2 * rows, 128), F32),
             sds((cells * rows // 8, 27 * 128), BF16),
             sds((halo.shape[0], 3, rows, 128), BF16),
-            sds((cells, rows, 128), BF16),
-            sds((cells, rows, 128), BF16),
+            sds((2, rows, 128), BF16),
+            sds((2, rows, 128), BF16),
         ),
         [
             pltpu.VMEM((rows // 16, halo.shape[1], 128), F32),
             pltpu.VMEM((rows, 9 * 256), BF16),
             pltpu.VMEM((rows, 3 * 256), BF16),
             pltpu.VMEM((2, *hidden.shape[1:]), F32),
-            pltpu.VMEM((cells + 1, rows, 128), BF16),
+            pltpu.VMEM((4, rows, 128), BF16),
         ],
         halo, hidden, partial, padded,
         smem=(alive, side),
@@ -285,25 +313,30 @@
 
 
 def second_rows_kernel(
-    data, table, order, h0, h1, h2, h3, d0, d1, d2, d3,
+    data, table, order, e0, e1, e2, e3, m0, m1, m2, m3, d0, d1, d2, d3,
     out_ref, wide, windows, deltas, product, flat,
 ):
-    cells, rows, _ = h0.shape
+    edges, rows, _ = e0.shape
+    cells = edges + m0.shape[0]
     half = rows // 32
     outs = cells // 2
     size = half * 8
-    for sample, (hidden, delta) in enumerate(((h0, d0), (h1, d1), (h2, d2), (h3, d3))):
-        wide[sample * cells : (sample + 1) * cells] = (
-            hidden[...].astype(F32).reshape(cells, half, 2, 2, 8, 128)
+    taps = windows.shape[1] // 128
+    samples = ((e0, m0, d0), (e1, m1, d1), (e2, m2, d2), (e3, m3, d3))
+    for sample, (edge, middle, delta) in enumerate(samples):
+        at = sample * cells
+        wide[at : at + edges] = edge[...].astype(F32).reshape(edges, half, 2, 2, 8, 128)
+        wide[at + edges : at + cells] = (
+            middle[...].astype(F32).reshape(cells - edges, half, 2, 2, 8, 128)
         )
         deltas[sample * outs * size : (sample + 1) * outs * size, :] = delta[...]
-    for tap in range(windows.shape[1] // 128):
-        e, f = table[data[0], 8 + tap], table[data[0], 16 + tap]
+    for tap in range(taps):
+        e, f = table[data[0], tap], table[data[0], taps + tap]
         row = jnp.where(e == 1, 0, 1)
         column = jnp.where(f == 1, 0, 1)
         for sample in range(4):
             for out in range(outs):
-                plane = sample * cells + 2 * out + table[data[0], tap]
+                plane = sample * cells + table[data[0], (2 + out) * taps + tap]
                 block = wide[plane, :, column, row].reshape(size, 128)
                 block = jnp.where(e == 0, from_before(block), block)
                 later = jnp.concatenate([jnp.zeros((8, 128), F32), block[: size - 8]], axis=0)
@@ -318,7 +351,7 @@
     shard = 27 * 128 // 4
     for lane in range(lanes):
         flat[lane * shard : (lane + 1) * shard, :] = product[
-            pl.ds(pl.multiple_of(table[data[0], 24], 16), shard), lane * 128 : (lane + 1) * 128
+            pl.ds(pl.multiple_of(table[data[0], (2 + outs) * taps], 16), shard), lane * 128 : (lane + 1) * 128
         ]
     rest = flat.shape[0] - lanes * shard
     if rest:
@@ -327,18 +360,20 @@
         out_ref[place] = flat[pl.ds(pl.multiple_of(order[place] * piece, 16), piece), :]
 
 
-def second_rows(hiddens, deltas, data, order, places, size):
-    cells, rows, _ = hiddens[0].shape
+def second_rows(edges, middles, deltas, data, order, places, size):
+    _, rows, _ = edges[0].shape
+    cells = edges[0].shape[0] + middles[0].shape[0]
     cellrows, features = deltas[0].shape
     taps = 8
     table = []
     for shard in range(4):
         start = shard * 27 // 4
         at = [min(start + tap, 26) for tap in range(taps)]
+        held = (-1, 0, *range(1, cells - 1)) if shard < 2 else (0, cells - 1, *range(1, cells - 1))
         table.append(
-            [tap // 9 - shard // 2 for tap in at]
-            + [tap // 3 % 3 for tap in at]
+            [tap // 3 % 3 for tap in at]
             + [tap % 3 for tap in at]
+            + [held.index(2 * out - 1 + tap // 9) for out in range(cells // 2) for tap in at]
             + [shard * (27 * 128 // 4) - start * 128]
         )
     return call(
@@ -351,7 +386,7 @@
             pltpu.VMEM((taps * 128, features), BF16),
             pltpu.VMEM((places * size, 128), BF16),
         ],
-        *hiddens, *deltas,
+        *edges, *middles, *deltas,
         smem=(data.reshape(1), jnp.array(table, jnp.int32), order),
         micros=2.0,
     )
@@ -587,59 +622,65 @@
     size_second = -(-lanes * big // (16 * spaces)) * 16
 
     inputs = volume.reshape(planes, side, width)
+    uppermost = last_planes(inputs, 3)
+    weight_first, uppermost = lax.optimization_barrier((weight_first, uppermost))
     first_x = swap(weight_first, "dp", 2)
     first_core = swap(weight_first, "dp", 1)
     second_x = swap(weight_second, "dp", 2)
     second_core = swap(weight_second, "dp", 1)
-    halo = shifted(inputs[planes - 3 :], "space", 1)
+    halo = shifted(uppermost, "space", 1)
     first_far = swap(first_x, "dp", 1)
     shards_first = (weight_first, first_core, first_x, first_far)
 
     sorted_volume = sorted_planes(inputs)
-    slope, hidden, partial, padded = forward_upper(sorted_volume, shards_first, offsets_first)
+    slope, hidden, middle, partial, padded = forward_upper(
+        sorted_volume, shards_first, offsets_first
+    )
+    middle_x, middle_core = swap(middle, "dp", 2), swap(middle, "dp", 1)
     second_x, hidden = lax.optimization_barrier((second_x, hidden))
     second_far = swap(second_x, "dp", 1)
     shards_second = (weight_second, second_core, second_x, second_far)
-    slope_low, windows, sorted_halo, hidden_here, hidden_there = forward_lower(
+    slope_low, windows, sorted_halo, edge, edge_there = forward_lower(
         halo, hidden, partial, padded, alive, x_side.reshape(1)
     )
     cot = cotangent.reshape(cotangent.shape[1:])
     activations, delta_second = forward_second(windows, cot, shards_second, offsets_second)
-    hidden_x = swap(hidden_there, "dp", 2)
-    delta_x = swap(delta_second, "dp", 2)
-    hidden_core = swap(hidden_here, "dp", 1)
-    delta_core = swap(delta_second, "dp", 1)
+    edge_x, edge_core = swap(edge_there, "dp", 2), swap(edge, "dp", 1)
+    delta_x, delta_core = swap(delta_second, "dp", 2), swap(delta_second, "dp", 1)
     low, last, down, *first = back_second(
         delta_second, shards_second, (slope_low, slope), sorted_volume, sorted_halo,
         offsets_second, slots, order, spaces, size_first,
     )
-    first, delta_x, hidden_x, delta_core, hidden_core = lax.optimization_barrier(
-        (first, delta_x, hidden_x, delta_core, hidden_core)
-    )
-    hiddens = (hidden_here, hidden_core, hidden_x, swap(hidden_x, "dp", 1))
-    deltas = (delta_second, delta_core, delta_x, swap(delta_x, "dp", 1))
-    second = second_rows(hiddens, deltas, data, order, spaces, size_second)
+    first, down, delta_x, edge_x, delta_core, edge_core, middle_x, middle_core = (
+        lax.optimization_barrier(
+            (first, down, delta_x, edge_x, delta_core, edge_core, middle_x, middle_core)
+        )
+    )
+    second = second_rows(
+        (edge, edge_core, edge_x, swap(edge_x, "dp", 1)),
+        (middle, middle_core, middle_x, swap(middle_x, "dp", 1)),
+        (delta_second, delta_core, delta_x, swap(delta_x, "dp", 1)),
+        data, order, spaces, size_second,
+    )
     upper = shifted(down, "space", -1)
+
     def pieces(value):
         return value.reshape(2, high, -1, 128)
 
-    second = pieces(second)
     far, near = pieces(swap(first[3], "dp", 1)), pieces(swap(first[1], "dp", 1))
     own, there = pieces(first[0]), pieces(first[2])
-    both = [
-        (d * spaces + s, (d ^ 2) * spaces + (s ^ 1)) for d in range(4) for s in range(spaces)
-    ]
-    got_xy = lax.ppermute(added(there[1], far[1]), ("dp", "space"), both)
-    got_x = swap(added(there[0], far[0]), "dp", 2)
-    got_y = swap(jnp.concatenate([second[1], added(own[1], near[1])], axis=1), "space", 1)
+    got_x = swap(added(there, far), "dp", 2)
+    second = pieces(second)
+    got_y = swap(
+        jnp.concatenate([second[1], added(own[1], near[1], got_x[1])], axis=1), "space", 1
+    )
     held = jnp.concatenate(
         [
             added(second[0], got_y[:, :size_second]),
-            added(own[0], near[0], got_x, got_xy, got_y[:, size_second:]),
+            added(own[0], near[0], got_x[0], got_y[:, size_second:]),
         ],
         axis=1,
     )
-    held, upper = lax.optimization_barrier((held, upper))
     mine = added(held[0], *(swap(held[k], "space", 2 * k) for k in range(1, high)))
     chunks = [mine] + [swap(mine, "space", 2 * k) for k in range(1, high)]
     chunks.append(swap(jnp.stack(chunks), "space", 1))

time: 76.9 us -> 83.6 us (1.087)
  Pallas kernels: 14.4 us -> 27.5 us
  waiting for transfers between devices: 28.3 us -> 25.1 us
  local copies, waits for them, and re-layouts: 3.79 us -> 2.01 us
  starting transfers between devices: 28.8 us -> 27.5 us
    pallas_call x0 -> x1, Pallas kernels: none -> 13 us  [last_planes(): pl.pallas_call(last_planes_kernel, out_shape=sds(shape, BF16), in_specs=[...]
    ppermute x23 -> x26, waiting for transfers between devices: 25.5 us -> 22.9 us  [swap(): return lax.ppermute(value, axis, [(i, i ^ bits) for i in range(size)])]
    ppermute x1 -> x0, starting transfers between devices: 2.62 us -> none  [local(): got_xy = lax.ppermute(added(there[1], far[1]), ('dp', 'space'), both)]
    slice x1 -> x0, local copies, waits for them, and re-layouts: 1.77 us -> none  [local(): halo = shifted(inputs[planes - 3:], 'space', 1)]
    ppermute x23 -> x26, starting transfers between devices: 21.3 us -> 22.5 us  [swap(): return lax.ppermute(value, axis, [(i, i ^ bits) for i in range(size)])]
  transfers between devices with their start and end apart: 26 -> 28, of which waited for: 14 -> 12; matrix products, arithmetic and copies ran while one was open for 3% -> 0% of each run, Pallas kernels for 17% -> 15%
where the time goes in v5:
time: 83.6 us; the launch traced here: 83.4 us
  Pallas kernels  27.5 us (33%)
  starting transfers between devices  27.5 us (33%)
  waiting for transfers between devices  25.1 us (30%)
  local copies, waits for them, and re-layouts  2.01 us (2%)
  between operations  0.94 us (1%)
    ppermute x26, waiting for transfers between devices, swap(): return lax.ppermute(value, axis, [(i, i ^ bits) for i in range(size)])  22.9 us
    ppermute x26, starting transfers between devices, swap(): return lax.ppermute(value, axis, [(i, i ^ bits) for i in range(size)])  22.5 us
    pallas_call x8, Pallas kernels, call(): pl.pallas_call(kernel, out_shape=out_shape, in_specs=specs, out_specs=jax...  14.5 us
    pallas_call x1, Pallas kernels, last_planes(): pl.pallas_call(last_planes_kernel, out_shape=sds(shape, BF16), in_specs=[...  13 us
    ppermute x2, starting transfers between devices, shifted(): return lax.ppermute(value, axis, pairs)  4.97 us
    ppermute x2, waiting for transfers between devices, shifted(): return lax.ppermute(value, axis, pairs)  2.25 us
    unnamed x18, local copies, waits for them, and re-layouts  1.99 us
  transfers between devices with their start and end apart: 28, of which 12 were waited for; matrix products, arithmetic and copies ran while one was open for 0% of the time, Pallas kernels for 15%

profile of v5, /device:TPU:0, one launch (start us, length us, event | category | flops | bytes accessed | tf_op | source)
XLA Modules:
  0.0 83.4 jit_solution(306755238752855860)
XLA Ops:
  0.6 13.0 %shard_map.84 = bf16[3,32,2048]{2,1,0:T(8,128)(2,1)} custom-call(bf16[8,32,2048]{2,1,0:T(8,128)(2,1)} %bitcast.33), custom_call_target="tpu_custom_call" | custom-call | bytes 786432 | tf_op jit(solution)/shard_map/pallas_call | solution.py:95
  13.7 3.0 %collective-permute-start.3 = (bf16[432,128]{1,0:T(8,128)(2,1)}, bf16[432,128]{1,0:T(8,128)(2,1)S(1)}, u32[]{:S(2)}, u32[]{:S(2)}) collective-permute-start(bf16[432,128]{1,0:T(8,128)(2,1)} %w0.5), channel_id=1, source_target_pairs={{0,16},{8,24},{16,0},{24,8},{1,17},{9,25},{17,1},{25,9},{2,18},{10... | collective-permute-start | bytes 331784 | tf_op jit(solution)/shard_map/ppermute | solution.py:597
  16.7 0.2 collective-permute-start.1
  16.8 0.4 collective-permute-start.5
  17.2 3.7 %collective-permute-start = (bf16[3,32,2048]{2,1,0:T(8,128)(2,1)}, bf16[3,32,2048]{2,1,0:T(8,128)(2,1)S(1)}, u32[]{:S(2)}, u32[]{:S(2)}) collective-permute-start(bf16[3,32,2048]{2,1,0:T(8,128)(2,1)} %shard_map.84), channel_id=1, source_target_pairs={{0,1},{1,2},{2,3},{3,4},{4,5},{5,6},{6,7},{8,9},{9,10},{10,11},{11... | collective-permute-start | bytes 1179656 | tf_op jit(solution)/shard_map/ppermute | solution.py:603
  20.9 1.2 %copy-done = bf16[1,8,32,2048]{3,2,1,0:T(8,128)(2,1)S(1)} copy-done((bf16[1,8,32,2048]{3,2,1,0:T(8,128)(2,1)S(1)}, bf16[1,8,32,2048]{3,2,1,0:T(8,128)(2,1)}, u32[]{:S(2)}) %copy-start) | copy-done | bytes 1048600
  22.1 0.3 shard_map.85.sorted_ref
  22.5 0.1 collective-permute-start.4
  22.6 1.3 %collective-permute-done.4.w3 = bf16[432,128]{1,0:T(8,128)(2,1)S(1)} collective-permute-done((bf16[432,128]{1,0:T(8,128)(2,1)S(1)}, bf16[432,128]{1,0:T(8,128)(2,1)S(1)}, u32[]{:S(2)}, u32[]{:S(2)}) %collective-permute-start.4) | collective-permute-done | bytes 110624 | tf_op jit(solution)/shard_map/ppermute | solution.py:597
  23.9 2.1 %shard_map.86 = (f32[768,128]{1,0:T(8,128)S(1)}, f32[3,8,2,2,8,128]{5,4,3,2,1,0:T(8,128)S(1)}, bf16[2,256,128]{2,1,0:T(8,128)(2,1)S(1)}, f32[256,128]{1,0:T(8,128)S(1)}, bf16[2304,128]{1,0:T(8,128)(2,1)S(1)}) custom-call(s32[4]{0:T(128)S(1)} %broadcast_multiply_fusion.offsets, bf16[8,3,256,128]{3,2,1,0:T(8,128)(2,1)S(1)} %shard_map.85.sorted_ref, ...), custom_call_target="tpu_custom_call" | custom-call | flops 2875000064 | bytes 3653632 | tf_op jit(solution)/shard_map/pallas_call | solution.py:49
  26.0 0.7 copy-done.7
  26.7 2.7 %collective-permute-done.1.w2 = bf16[864,256]{1,0:T(8,128)(2,1)S(1)} collective-permute-done((bf16[864,256]{1,0:T(8,128)(2,1)}, bf16[864,256]{1,0:T(8,128)(2,1)S(1)}, u32[]{:S(2)}, u32[]{:S(2)}) %collective-permute-start.1) | collective-permute-done | bytes 442400 | tf_op jit(solution)/shard_map/ppermute | solution.py:597
  29.5 1.8 %collective-permute-start.11 = (bf16[2,256,128]{2,1,0:T(8,128)(2,1)S(1)}, bf16[2,256,128]{2,1,0:T(8,128)(2,1)S(1)}, u32[]{:S(2)}, u32[]{:S(2)}) collective-permute-start(bf16[2,256,128]{2,1,0:T(8,128)(2,1)S(1)} %get-tuple-element.62.m0), channel_id=1, source_target_pairs={{0,16},{8,24},{16,0},{24,8},{1,17},{9,25},{17,1},{25,9},{2,18},{10... | collective-permute-start | bytes 393224 | tf_op jit(solution)/shard_map/ppermute | solution.py:597
  31.2 0.2 collective-permute-start.12
  31.5 0.9 %shard_map.87 = (f32[512,128]{1,0:T(8,128)S(1)}, bf16[128,3456]{1,0:T(8,128)(2,1)S(1)}, bf16[3,3,256,128]{3,2,1,0:T(8,128)(2,1)S(1)}, bf16[2,256,128]{2,1,0:T(8,128)(2,1)S(1)}, bf16[2,256,128]{2,1,0:T(8,128)(2,1)S(1)}) custom-call(f32[1]{0:T(128)} %bitcast.alive, s32[1]{0:T(128)} %bitcast.1.side, bf16[3,32,2048]{2,1,0:T(8,128)(2,1)S(1)} %collective-permute-done.halo_ref, ...), custom_call_target="tpu_custom_call" | custom-call | flops 1724999936 | bytes 3506176 | tf_op jit(solution)/shard_map/pallas_call | solution.py:49
  32.4 0.4 collective-permute-start.10
  32.8 0.3 collective-permute-start.8
  33.1 1.8 %shard_map.88 = (bf16[2,8,2048]{2,1,0:T(8,128)(2,1)}, bf16[128,256]{1,0:T(8,128)(2,1)S(1)}) custom-call(s32[4]{0:T(128)S(1)} %get-tuple-element.80.offsets, bf16[128,3456]{1,0:T(8,128)(2,1)S(1)} %get-tuple-element.46.windows_ref, bf16[2,8,2048]{2,1,0:T(8,128)(2,1)S(1)} %bitcast.39, bf16[864,256]{1,0:T(8,128)(2,1)S(1)} %copy-done.1, ...), custom_call_target="tpu_custom_call" | custom-call | flops 1724999936 | bytes 2850816 | tf_op jit(solution)/shard_map/pallas_call | solution.py:49
  34.9 1.7 %collective-permute-start.7 = (bf16[128,256]{1,0:T(8,128)(2,1)S(1)}, bf16[128,256]{1,0:T(8,128)(2,1)S(1)}, u32[]{:S(2)}, u32[]{:S(2)}) collective-permute-start(bf16[128,256]{1,0:T(8,128)(2,1)S(1)} %get-tuple-element.49.delta_ref.d0), channel_id=1, source_target_pairs={{0,16},{8,24},{16,0},{24,8},{1,17},{9,25},{17,1},{25,9},{2,18},{10... | collective-permute-start | bytes 196616 | tf_op jit(solution)/shard_map/ppermute | solution.py:597
  36.7 3.0 %shard_map.89 = (bf16[768,128]{1,0:T(8,128)(2,1)S(1)}, f32[256,128]{1,0:T(8,128)S(1)}, bf16[512,128]{1,0:T(8,128)(2,1)S(1)}, bf16[8,64,128]{2,1,0:T(8,128)(2,1)S...) custom-call(s32[4]{0:T(128)S(1)} %get-tuple-element.80.offsets, ...), custom_call_target="tpu_custom_call" | custom-call | flops 4024999936 | bytes 5636096 | tf_op jit(solution)/shard_map/pallas_call | solution.py:49
  39.7 0.1 collective-permute-done.7.d2
  39.8 0.5 collective-permute-start.18
  40.3 0.1 collective-permute-start.14
  40.4 0.4 collective-permute-start.15
  40.8 0.1 collective-permute-start.16
  40.9 0.4 collective-permute-start.17
  41.4 1.5 %collective-permute-start.19 = (bf16[2,4,64,128]{3,2,1,0:T(8,128)(2,1)S(1)}, bf16[2,4,64,128]{3,2,1,0:T(8,128)(2,1)S(1)}, u32[]{:S(2)}, u32[]{:S(2)}) collective-permute-start(bf16[2,4,64,128]{3,2,1,0:T(8,128)(2,1)S(1)} %bitcast.40), channel_id=1, source_target_pairs={{0,16},{8,24},{16,0},{24,8},{1,17},{9,25},{17,1},{25,9},{2,18},{10... | collective-permute-start | bytes 393224 | tf_op jit(solution)/shard_map/ppermute | solution.py:597
  42.8 1.8 %shard_map.91 = bf16[8,224,128]{2,1,0:T(8,128)(2,1)S(1)} custom-call(s32[1]{0:T(128)} %bitcast.6.data, s32[4,33]{1,0:T(4,128)S(1)} %copy-done.4, s32[8]{0:T(128)S(1)} %fusion.15.order, bf16[2,256,128]{2,1,0:T(8,128)(2,1)S(1)} %get-tuple-element.61.e0, bf16[2,256,128]{2,1,0:T(8,128)(2,1)S(1)} %collective-permute-done.10.e1, ...), custom_call_target="tpu_custom_call" | custom-call | flops 2300000000 | bytes 1769472 | tf_op jit(solution)/shard_map/pallas_call | solution.py:49
  44.7 2.4 %collective-permute-done.19 = bf16[2,4,64,128]{3,2,1,0:T(8,128)(2,1)S(1)} collective-permute-done((bf16[2,4,64,128]{3,2,1,0:T(8,128)(2,1)S(1)}, bf16[2,4,64,128]{3,2,1,0:T(8,128)(2,1)S(1)}, u32[]{:S(2)}, u32[]{:S(2)}) %collective-permute-start.19) | collective-permute-done | bytes 131104 | tf_op jit(solution)/shard_map/ppermute | solution.py:597
  47.2 1.6 %collective-permute-start.20 = (bf16[4,288,128]{2,1,0:T(8,128)(2,1)S(1)}, bf16[4,288,128]{2,1,0:T(8,128)(2,1)S(1)}, u32[]{:S(2)}, u32[]{:S(2)}) collective-permute-start(bf16[4,288,128]{2,1,0:T(8,128)(2,1)S(1)} %pad_maximum_fusion), channel_id=1, source_target_pairs={{0,1},{1,0},{2,3},{3,2},{4,5},{5,4},{6,7},{7,6},{8,9},{9,8},{10,11... | collective-permute-start | bytes 884744 | tf_op jit(solution)/shard_map/ppermute | solution.py:597
  48.8 6.9 %collective-permute-done.20 = bf16[4,288,128]{2,1,0:T(8,128)(2,1)S(1)} collective-permute-done((bf16[4,288,128]{2,1,0:T(8,128)(2,1)S(1)}, bf16[4,288,128]{2,1,0:T(8,128)(2,1)S(1)}, u32[]{:S(2)}, u32[]{:S(2)}) %collective-permute-start.20) | collective-permute-done | bytes 294944 | tf_op jit(solution)/shard_map/ppermute | solution.py:597
  55.7 0.1 add_convert_fusion
  55.8 1.8 %collective-permute-start.21 = (bf16[288,128]{1,0:T(8,128)(2,1)S(1)}, bf16[288,128]{1,0:T(8,128)(2,1)S(1)}, u32[]{:S(2)}, u32[]{:S(2)}) collective-permute-start(bf16[288,128]{1,0:T(8,128)(2,1)S(1)} %get-tuple-element.76), channel_id=1, source_target_pairs={{0,2},{1,3},{2,0},{3,1},{4,6},{5,7},{6,4},{7,5},{8,10},{9,11},{10,... | collective-permute-start | bytes 221192 | tf_op jit(solution)/shard_map/ppermute | solution.py:597
  57.7 2.6 %collective-permute-start.22 = (bf16[288,128]{1,0:T(8,128)(2,1)S(1)}, bf16[288,128]{1,0:T(8,128)(2,1)S(1)}, u32[]{:S(2)}, u32[]{:S(2)}) collective-permute-start(bf16[288,128]{1,0:T(8,128)(2,1)S(1)} %get-tuple-element.78), channel_id=1, source_target_pairs={{0,4},{1,5},{2,6},{3,7},{4,0},{5,1},{6,2},{7,3},{8,12},{9,13},{10,... | collective-permute-start | bytes 221192 | tf_op jit(solution)/shard_map/ppermute | solution.py:597
  60.3 0.5 collective-permute-done.21
  60.8 3.7 %collective-permute-done.22 = bf16[288,128]{1,0:T(8,128)(2,1)S(1)} collective-permute-done((bf16[288,128]{1,0:T(8,128)(2,1)S(1)}, bf16[288,128]{1,0:T(8,128)(2,1)S(1)}, u32[]{:S(2)}, u32[]{:S(2)}) %collective-permute-start.22) | collective-permute-done | bytes 73760 | tf_op jit(solution)/shard_map/ppermute | solution.py:597
  64.5 2.4 %collective-permute-done.23 = bf16[288,128]{1,0:T(8,128)(2,1)S(1)} collective-permute-done((bf16[288,128]{1,0:T(8,128)(2,1)S(1)}, bf16[288,128]{1,0:T(8,128)(2,1)S(1)}, u32[]{:S(2)}, u32[]{:S(2)}) %collective-permute-start.23) | collective-permute-done | bytes 73760 | tf_op jit(solution)/shard_map/ppermute | solution.py:597
  67.0 0.1 collective-permute-start.24
  67.1 1.2 %collective-permute-start.25 = (bf16[288,128]{1,0:T(8,128)(2,1)S(1)}, bf16[288,128]{1,0:T(8,128)(2,1)S(1)}, u32[]{:S(2)}, u32[]{:S(2)}) collective-permute-start(bf16[288,128]{1,0:T(8,128)(2,1)S(1)} %fusion.2.refs_0_), channel_id=1, source_target_pairs={{0,4},{1,5},{2,6},{3,7},{4,0},{5,1},{6,2},{7,3},{8,12},{9,13},{10,... | collective-permute-start | bytes 221192 | tf_op jit(solution)/shard_map/ppermute | solution.py:597
  68.2 3.2 %collective-permute-start.26 = (bf16[288,128]{1,0:T(8,128)(2,1)S(1)}, bf16[288,128]{1,0:T(8,128)(2,1)S(1)}, u32[]{:S(2)}, u32[]{:S(2)}) collective-permute-start(bf16[288,128]{1,0:T(8,128)(2,1)S(1)} %fusion.2.refs_0_), channel_id=1, source_target_pairs={{0,6},{1,7},{2,4},{3,5},{4,2},{5,3},{6,0},{7,1},{8,14},{9,15},{10,... | collective-permute-start | bytes 221192 | tf_op jit(solution)/shard_map/ppermute | solution.py:597
  71.4 1.3 %collective-permute-start.13 = (bf16[512,128]{1,0:T(8,128)(2,1)S(1)}, bf16[512,128]{1,0:T(8,128)(2,1)S(1)}, u32[]{:S(2)}, u32[]{:S(2)}) collective-permute-start(bf16[512,128]{1,0:T(8,128)(2,1)S(1)} %get-tuple-element.63), channel_id=1, source_target_pairs={{1,0},{2,1},{3,2},{4,3},{5,4},{6,5},{7,6},{9,8},{10,9},{11,10},{12... | collective-permute-start | bytes 393224 | tf_op jit(solution)/shard_map/ppermute | solution.py:603
  72.7 0.3 collective-permute-done.25.refs_2_
  73.0 1.9 %collective-permute-done.26.refs_3_ = bf16[288,128]{1,0:T(8,128)(2,1)S(1)} collective-permute-done((bf16[288,128]{1,0:T(8,128)(2,1)S(1)}, bf16[288,128]{1,0:T(8,128)(2,1)S(1)}, u32[]{:S(2)}, u32[]{:S(2)}) %collective-permute-start.26) | collective-permute-done | bytes 73760 | tf_op jit(solution)/shard_map/ppermute | solution.py:597
  74.9 1.1 %collective-permute-start.27 = (bf16[4,288,128]{2,1,0:T(8,128)(2,1)S(1)}, bf16[4,288,128]{2,1,0:T(8,128)(2,1)S(1)}, u32[]{:S(2)}, u32[]{:S(2)}) collective-permute-start(bf16[4,288,128]{2,1,0:T(8,128)(2,1)S(1)} %pad_maximum_fusion.1), channel_id=1, source_target_pairs={{0,1},{1,0},{2,3},{3,2},{4,5},{5,4},{6,7},{7,6},{8,9},{9,8},{10,11... | collective-permute-start | bytes 884744 | tf_op jit(solution)/shard_map/ppermute | solution.py:597
  76.0 2.3 %collective-permute-done.13.upper_ref = bf16[512,128]{1,0:T(8,128)(2,1)S(1)} collective-permute-done((bf16[512,128]{1,0:T(8,128)(2,1)S(1)}, bf16[512,128]{1,0:T(8,128)(2,1)S(1)}, u32[]{:S(2)}, u32[]{:S(2)}) %collective-permute-start.13) | collective-permute-done | bytes 131104 | tf_op jit(solution)/shard_map/ppermute | solution.py:603
  78.3 2.8 %shard_map.90 = bf16[8,32,2048]{2,1,0:T(8,128)(2,1)} custom-call(s32[4]{0:T(128)S(1)} %broadcast_multiply_fusion.offsets, bf16[768,128]{1,0:T(8,128)(2,1)S(1)} %get-tuple-element.53.low_ref, f32[256,128]{1,0:T(8,128)S(1)} %get-tuple-element.54.last_ref, f32[768,128]{1,0:T(8,128)S(1)} %copy-done.8, bf16[512,128]{1,0:T(8,128)(2,1)S(1)} %collective-permute-done.13.upper_ref, ...), custom_call_target="tpu_custom_call" | custom-call | flops 3449999872 | bytes 2342912 | tf_op jit(solution)/shard_map/pallas_call | solution.py:49
  81.1 0.6 collective-permute-done.27.refs_4_
  81.7 1.7 %shard_map.92 = (f32[432,128]{1,0:T(8,128)}, f32[864,256]{1,0:T(8,128)}) custom-call(s32[8]{0:T(128)S(1)} %fusion.15.order, bf16[288,128]{1,0:T(8,128)(2,1)S(1)} %fusion.2.refs_0_, bf16[288,128]{1,0:T(8,128)(2,1)S(1)} %collective-permute-done.24.refs_1_, bf16[288,128]{1,0:T(8,128)(2,1)S(1)} %collective-permute-done.25.refs_2_, ...), custom_call_target="tpu_custom_call" | custom-call | flops 1150000000 | bytes 1695744 | tf_op jit(solution)/shard_map/pallas_call | solution.py:49
  (47 shorter events, 0.4 us)
Async XLA Ops:
  13.7 8.8 %collective-permute-start.3 = (bf16[432,128]{1,0:T(8,128)(2,1)}, bf16[432,128]{1,0:T(8,128)(2,1)S(1)}, u32[]{:S(2)}, u32[]{:S(2)}) collective-permute-start(bf16[432,128]{1,0:T(8,128)(2,1)} %w0.5), channel_id=1, source_target_pairs={{0,16},{8,24},{16,0},{24,8},{1,17},{9,25},{17,1},{25,9},{2,18},{10... | collective-permute-start | bytes 331784 | tf_op jit(solution)/shard_map/ppermute | solution.py:597
  16.7 5.9 %collective-permute-start.2 = (bf16[432,128]{1,0:T(8,128)(2,1)}, bf16[432,128]{1,0:T(8,128)(2,1)S(1)}, u32[]{:S(2)}, u32[]{:S(2)}) collective-permute-start(bf16[432,128]{1,0:T(8,128)(2,1)} %w0.5), channel_id=1, source_target_pairs={{0,8},{8,0},{16,24},{24,16},{1,9},{9,1},{17,25},{25,17},{2,10},{10... | collective-permute-start | bytes 331784 | tf_op jit(solution)/shard_map/ppermute | solution.py:597
  16.7 12.8 %collective-permute-start.1 = (bf16[864,256]{1,0:T(8,128)(2,1)}, bf16[864,256]{1,0:T(8,128)(2,1)S(1)}, u32[]{:S(2)}, u32[]{:S(2)}) collective-permute-start(bf16[864,256]{1,0:T(8,128)(2,1)} %w0.4), channel_id=1, source_target_pairs={{0,16},{8,24},{16,0},{24,8},{1,17},{9,25},{17,1},{25,9},{2,18},{10... | collective-permute-start | bytes 1327112 | tf_op jit(solution)/shard_map/ppermute | solution.py:597
  16.8 15.9 %collective-permute-start.5 = (bf16[864,256]{1,0:T(8,128)(2,1)}, bf16[864,256]{1,0:T(8,128)(2,1)S(1)}, u32[]{:S(2)}, u32[]{:S(2)}) collective-permute-start(bf16[864,256]{1,0:T(8,128)(2,1)} %w0.4), channel_id=1, source_target_pairs={{0,8},{8,0},{16,24},{24,16},{1,9},{9,1},{17,25},{25,17},{2,10},{10... | collective-permute-start | bytes 1327112 | tf_op jit(solution)/shard_map/ppermute | solution.py:597
  17.2 14.3 %collective-permute-start = (bf16[3,32,2048]{2,1,0:T(8,128)(2,1)}, bf16[3,32,2048]{2,1,0:T(8,128)(2,1)S(1)}, u32[]{:S(2)}, u32[]{:S(2)}) collective-permute-start(bf16[3,32,2048]{2,1,0:T(8,128)(2,1)} %shard_map.84), channel_id=1, source_target_pairs={{0,1},{1,2},{2,3},{3,4},{4,5},{5,6},{6,7},{8,9},{9,10},{10,11},{11... | collective-permute-start | bytes 1179656 | tf_op jit(solution)/shard_map/ppermute | solution.py:603
  20.9 1.2 %copy-start = (bf16[1,8,32,2048]{3,2,1,0:T(8,128)(2,1)S(1)}, bf16[1,8,32,2048]{3,2,1,0:T(8,128)(2,1)}, u32[]{:S(2)}) copy-start(bf16[1,8,32,2048]{3,2,1,0:T(8,128)(2,1)} %param.5) | copy-start | bytes 3145732
  22.1 1.8 %copy-start.2 = (bf16[432,128]{1,0:T(8,128)(2,1)S(1)}, bf16[432,128]{1,0:T(8,128)(2,1)}, u32[]{:S(2)}) copy-start(bf16[432,128]{1,0:T(8,128)(2,1)} %w0.5) | copy-start | bytes 331780
  22.5 3.5 %copy-start.5 = (bf16[8,3,256,128]{3,2,1,0:T(8,128)(2,1)}, bf16[8,3,256,128]{3,2,1,0:T(8,128)(2,1)S(1)}, u32[]{:S(2)}) copy-start(bf16[8,3,256,128]{3,2,1,0:T(8,128)(2,1)S(1)} %shard_map.85.sorted_ref) | copy-start | bytes 4718596
  22.5 1.4 %collective-permute-start.4 = (bf16[432,128]{1,0:T(8,128)(2,1)S(1)}, bf16[432,128]{1,0:T(8,128)(2,1)S(1)}, u32[]{:S(2)}, u32[]{:S(2)}) collective-permute-start(bf16[432,128]{1,0:T(8,128)(2,1)S(1)} %collective-permute-done.3.w2), channel_id=1, source_target_pairs={{0,8},{8,0},{16,24},{24,16},{1,9},{9,1},{17,25},{25,17},{2,10},{10... | collective-permute-start | bytes 331784 | tf_op jit(solution)/shard_map/ppermute | solution.py:597
  26.0 0.7 copy-start.7
  29.5 3.6 %collective-permute-start.6 = (bf16[864,256]{1,0:T(8,128)(2,1)S(1)}, bf16[864,256]{1,0:T(8,128)(2,1)S(1)}, u32[]{:S(2)}, u32[]{:S(2)}) collective-permute-start(bf16[864,256]{1,0:T(8,128)(2,1)S(1)} %collective-permute-done.1.w2), channel_id=1, source_target_pairs={{0,8},{8,0},{16,24},{24,16},{1,9},{9,1},{17,25},{25,17},{2,10},{10... | collective-permute-start | bytes 1327112 | tf_op jit(solution)/shard_map/ppermute | solution.py:597
  29.5 7.2 %collective-permute-start.11 = (bf16[2,256,128]{2,1,0:T(8,128)(2,1)S(1)}, bf16[2,256,128]{2,1,0:T(8,128)(2,1)S(1)}, u32[]{:S(2)}, u32[]{:S(2)}) collective-permute-start(bf16[2,256,128]{2,1,0:T(8,128)(2,1)S(1)} %get-tuple-element.62.m0), channel_id=1, source_target_pairs={{0,16},{8,24},{16,0},{24,8},{1,17},{9,25},{17,1},{25,9},{2,18},{10... | collective-permute-start | bytes 393224 | tf_op jit(solution)/shard_map/ppermute | solution.py:597
  31.2 8.5 %collective-permute-start.12 = (bf16[2,256,128]{2,1,0:T(8,128)(2,1)S(1)}, bf16[2,256,128]{2,1,0:T(8,128)(2,1)S(1)}, u32[]{:S(2)}, u32[]{:S(2)}) collective-permute-start(bf16[2,256,128]{2,1,0:T(8,128)(2,1)S(1)} %get-tuple-element.62.m0), channel_id=1, source_target_pairs={{0,8},{8,0},{16,24},{24,16},{1,9},{9,1},{17,25},{25,17},{2,10},{10... | collective-permute-start | bytes 393224 | tf_op jit(solution)/shard_map/ppermute | solution.py:597
  31.5 1.6 %copy-start.1 = (bf16[864,256]{1,0:T(8,128)(2,1)S(1)}, bf16[864,256]{1,0:T(8,128)(2,1)}, u32[]{:S(2)}) copy-start(bf16[864,256]{1,0:T(8,128)(2,1)} %w0.4) | copy-start | bytes 1327108
  31.5 1.6 %copy-start.3 = (bf16[1,2,8,2048]{3,2,1,0:T(8,128)(2,1)S(1)}, bf16[1,2,8,2048]{3,2,1,0:T(8,128)(2,1)}, u32[]{:S(2)}) copy-start(bf16[1,2,8,2048]{3,2,1,0:T(8,128)(2,1)} %param.8) | copy-start | bytes 196612
  32.4 7.3 %collective-permute-start.10 = (bf16[2,256,128]{2,1,0:T(8,128)(2,1)S(1)}, bf16[2,256,128]{2,1,0:T(8,128)(2,1)S(1)}, u32[]{:S(2)}, u32[]{:S(2)}) collective-permute-start(bf16[2,256,128]{2,1,0:T(8,128)(2,1)S(1)} %get-tuple-element.61.e0), channel_id=1, source_target_pairs={{0,8},{8,0},{16,24},{24,16},{1,9},{9,1},{17,25},{25,17},{2,10},{10... | collective-permute-start | bytes 393224 | tf_op jit(solution)/shard_map/ppermute | solution.py:597
  32.8 7.0 %collective-permute-start.8 = (bf16[2,256,128]{2,1,0:T(8,128)(2,1)S(1)}, bf16[2,256,128]{2,1,0:T(8,128)(2,1)S(1)}, u32[]{:S(2)}, u32[]{:S(2)}) collective-permute-start(bf16[2,256,128]{2,1,0:T(8,128)(2,1)S(1)} %get-tuple-element.60), channel_id=1, source_target_pairs={{0,16},{8,24},{16,0},{24,8},{1,17},{9,25},{17,1},{25,9},{2,18},{10... | collective-permute-start | bytes 393224 | tf_op jit(solution)/shard_map/ppermute | solution.py:597
  33.1 3.5 %copy-start.6 = (bf16[8,3,256,128]{3,2,1,0:T(8,128)(2,1)S(1)}, bf16[8,3,256,128]{3,2,1,0:T(8,128)(2,1)}, u32[]{:S(2)}) copy-start(bf16[8,3,256,128]{3,2,1,0:T(8,128)(2,1)} %copy-done.5) | copy-start | bytes 4718596
  33.1 3.5 %copy-start.8 = (f32[768,128]{1,0:T(8,128)S(1)}, f32[768,128]{1,0:T(8,128)}, u32[]{:S(2)}) copy-start(f32[768,128]{1,0:T(8,128)} %copy-done.7) | copy-start | bytes 1179652
  34.9 4.8 %collective-permute-start.7 = (bf16[128,256]{1,0:T(8,128)(2,1)S(1)}, bf16[128,256]{1,0:T(8,128)(2,1)S(1)}, u32[]{:S(2)}, u32[]{:S(2)}) collective-permute-start(bf16[128,256]{1,0:T(8,128)(2,1)S(1)} %get-tuple-element.49.delta_ref.d0), channel_id=1, source_target_pairs={{0,16},{8,24},{16,0},{24,8},{1,17},{9,25},{17,1},{25,9},{2,18},{10... | collective-permute-start | bytes 196616 | tf_op jit(solution)/shard_map/ppermute | solution.py:597
  36.6 3.2 %collective-permute-start.9 = (bf16[128,256]{1,0:T(8,128)(2,1)S(1)}, bf16[128,256]{1,0:T(8,128)(2,1)S(1)}, u32[]{:S(2)}, u32[]{:S(2)}) collective-permute-start(bf16[128,256]{1,0:T(8,128)(2,1)S(1)} %get-tuple-element.49.delta_ref.d0), channel_id=1, source_target_pairs={{0,8},{8,0},{16,24},{24,16},{1,9},{9,1},{17,25},{25,17},{2,10},{10... | collective-permute-start | bytes 196616 | tf_op jit(solution)/shard_map/ppermute | solution.py:597
  36.7 6.2 %copy-start.4 = (s32[4,33]{1,0:T(4,128)S(1)}, s32[4,33]{1,0:T(4,128)}, u32[]{:S(2)}) copy-start(s32[4,33]{1,0:T(4,128)} %constant.48.clone.table) | copy-start | bytes 1588
  39.8 1.5 %collective-permute-start.18 = (bf16[8,64,128]{2,1,0:T(8,128)(2,1)S(1)}, bf16[8,64,128]{2,1,0:T(8,128)(2,1)S(1)}, u32[]{:S(2)}, u32[]{:S(2)}) collective-permute-start(bf16[8,64,128]{2,1,0:T(8,128)(2,1)S(1)} %get-tuple-element.73), channel_id=1, source_target_pairs={{0,8},{8,0},{16,24},{24,16},{1,9},{9,1},{17,25},{25,17},{2,10},{10... | collective-permute-start | bytes 393224 | tf_op jit(solution)/shard_map/ppermute | solution.py:597
  40.3 2.5 %collective-permute-start.14 = (bf16[2,256,128]{2,1,0:T(8,128)(2,1)S(1)}, bf16[2,256,128]{2,1,0:T(8,128)(2,1)S(1)}, u32[]{:S(2)}, u32[]{:S(2)}) collective-permute-start(bf16[2,256,128]{2,1,0:T(8,128)(2,1)S(1)} %collective-permute-done.8.e2), channel_id=1, source_target_pairs={{0,8},{8,0},{16,24},{24,16},{1,9},{9,1},{17,25},{25,17},{2,10},{10... | collective-permute-start | bytes 393224 | tf_op jit(solution)/shard_map/ppermute | solution.py:597
  40.4 2.5 %collective-permute-start.15 = (bf16[2,256,128]{2,1,0:T(8,128)(2,1)S(1)}, bf16[2,256,128]{2,1,0:T(8,128)(2,1)S(1)}, u32[]{:S(2)}, u32[]{:S(2)}) collective-permute-start(bf16[2,256,128]{2,1,0:T(8,128)(2,1)S(1)} %collective-permute-done.11.m2), channel_id=1, source_target_pairs={{0,8},{8,0},{16,24},{24,16},{1,9},{9,1},{17,25},{25,17},{2,10},{10... | collective-permute-start | bytes 393224 | tf_op jit(solution)/shard_map/ppermute | solution.py:597
  40.8 2.0 %collective-permute-start.16 = (bf16[128,256]{1,0:T(8,128)(2,1)S(1)}, bf16[128,256]{1,0:T(8,128)(2,1)S(1)}, u32[]{:S(2)}, u32[]{:S(2)}) collective-permute-start(bf16[128,256]{1,0:T(8,128)(2,1)S(1)} %collective-permute-done.7.d2), channel_id=1, source_target_pairs={{0,8},{8,0},{16,24},{24,16},{1,9},{9,1},{17,25},{25,17},{2,10},{10... | collective-permute-start | bytes 196616 | tf_op jit(solution)/shard_map/ppermute | solution.py:597
  40.9 3.8 %collective-permute-start.17 = (bf16[8,64,128]{2,1,0:T(8,128)(2,1)S(1)}, bf16[8,64,128]{2,1,0:T(8,128)(2,1)S(1)}, u32[]{:S(2)}, u32[]{:S(2)}) collective-permute-start(bf16[8,64,128]{2,1,0:T(8,128)(2,1)S(1)} %get-tuple-element.71), channel_id=1, source_target_pairs={{0,8},{8,0},{16,24},{24,16},{1,9},{9,1},{17,25},{25,17},{2,10},{10... | collective-permute-start | bytes 393224 | tf_op jit(solution)/shard_map/ppermute | solution.py:597
  41.4 5.8 %collective-permute-start.19 = (bf16[2,4,64,128]{3,2,1,0:T(8,128)(2,1)S(1)}, bf16[2,4,64,128]{3,2,1,0:T(8,128)(2,1)S(1)}, u32[]{:S(2)}, u32[]{:S(2)}) collective-permute-start(bf16[2,4,64,128]{3,2,1,0:T(8,128)(2,1)S(1)} %bitcast.40), channel_id=1, source_target_pairs={{0,16},{8,24},{16,0},{24,8},{1,17},{9,25},{17,1},{25,9},{2,18},{10... | collective-permute-start | bytes 393224 | tf_op jit(solution)/shard_map/ppermute | solution.py:597
  47.2 8.5 %collective-permute-start.20 = (bf16[4,288,128]{2,1,0:T(8,128)(2,1)S(1)}, bf16[4,288,128]{2,1,0:T(8,128)(2,1)S(1)}, u32[]{:S(2)}, u32[]{:S(2)}) collective-permute-start(bf16[4,288,128]{2,1,0:T(8,128)(2,1)S(1)} %pad_maximum_fusion), channel_id=1, source_target_pairs={{0,1},{1,0},{2,3},{3,2},{4,5},{5,4},{6,7},{7,6},{8,9},{9,8},{10,11... | collective-permute-start | bytes 884744 | tf_op jit(solution)/shard_map/ppermute | solution.py:597
  55.8 5.0 %collective-permute-start.21 = (bf16[288,128]{1,0:T(8,128)(2,1)S(1)}, bf16[288,128]{1,0:T(8,128)(2,1)S(1)}, u32[]{:S(2)}, u32[]{:S(2)}) collective-permute-start(bf16[288,128]{1,0:T(8,128)(2,1)S(1)} %get-tuple-element.76), channel_id=1, source_target_pairs={{0,2},{1,3},{2,0},{3,1},{4,6},{5,7},{6,4},{7,5},{8,10},{9,11},{10,... | collective-permute-start | bytes 221192 | tf_op jit(solution)/shard_map/ppermute | solution.py:597
  57.7 6.8 %collective-permute-start.22 = (bf16[288,128]{1,0:T(8,128)(2,1)S(1)}, bf16[288,128]{1,0:T(8,128)(2,1)S(1)}, u32[]{:S(2)}, u32[]{:S(2)}) collective-permute-start(bf16[288,128]{1,0:T(8,128)(2,1)S(1)} %get-tuple-element.78), channel_id=1, source_target_pairs={{0,4},{1,5},{2,6},{3,7},{4,0},{5,1},{6,2},{7,3},{8,12},{9,13},{10,... | collective-permute-start | bytes 221192 | tf_op jit(solution)/shard_map/ppermute | solution.py:597
  60.2 6.7 %collective-permute-start.23 = (bf16[288,128]{1,0:T(8,128)(2,1)S(1)}, bf16[288,128]{1,0:T(8,128)(2,1)S(1)}, u32[]{:S(2)}, u32[]{:S(2)}) collective-permute-start(bf16[288,128]{1,0:T(8,128)(2,1)S(1)} %get-tuple-element.77), channel_id=1, source_target_pairs={{0,6},{1,7},{2,4},{3,5},{4,2},{5,3},{6,0},{7,1},{8,14},{9,15},{10,... | collective-permute-start | bytes 221192 | tf_op jit(solution)/shard_map/ppermute | solution.py:597
  67.0 5.7 %collective-permute-start.24 = (bf16[288,128]{1,0:T(8,128)(2,1)S(1)}, bf16[288,128]{1,0:T(8,128)(2,1)S(1)}, u32[]{:S(2)}, u32[]{:S(2)}) collective-permute-start(bf16[288,128]{1,0:T(8,128)(2,1)S(1)} %fusion.2.refs_0_), channel_id=1, source_target_pairs={{0,2},{1,3},{2,0},{3,1},{4,6},{5,7},{6,4},{7,5},{8,10},{9,11},{10,... | collective-permute-start | bytes 221192 | tf_op jit(solution)/shard_map/ppermute | solution.py:597
  67.1 5.9 %collective-permute-start.25 = (bf16[288,128]{1,0:T(8,128)(2,1)S(1)}, bf16[288,128]{1,0:T(8,128)(2,1)S(1)}, u32[]{:S(2)}, u32[]{:S(2)}) collective-permute-start(bf16[288,128]{1,0:T(8,128)(2,1)S(1)} %fusion.2.refs_0_), channel_id=1, source_target_pairs={{0,4},{1,5},{2,6},{3,7},{4,0},{5,1},{6,2},{7,3},{8,12},{9,13},{10,... | collective-permute-start | bytes 221192 | tf_op jit(solution)/shard_map/ppermute | solution.py:597
  68.2 6.7 %collective-permute-start.26 = (bf16[288,128]{1,0:T(8,128)(2,1)S(1)}, bf16[288,128]{1,0:T(8,128)(2,1)S(1)}, u32[]{:S(2)}, u32[]{:S(2)}) collective-permute-start(bf16[288,128]{1,0:T(8,128)(2,1)S(1)} %fusion.2.refs_0_), channel_id=1, source_target_pairs={{0,6},{1,7},{2,4},{3,5},{4,2},{5,3},{6,0},{7,1},{8,14},{9,15},{10,... | collective-permute-start | bytes 221192 | tf_op jit(solution)/shard_map/ppermute | solution.py:597
  71.4 6.8 %collective-permute-start.13 = (bf16[512,128]{1,0:T(8,128)(2,1)S(1)}, bf16[512,128]{1,0:T(8,128)(2,1)S(1)}, u32[]{:S(2)}, u32[]{:S(2)}) collective-permute-start(bf16[512,128]{1,0:T(8,128)(2,1)S(1)} %get-tuple-element.63), channel_id=1, source_target_pairs={{1,0},{2,1},{3,2},{4,3},{5,4},{6,5},{7,6},{9,8},{10,9},{11,10},{12... | collective-permute-start | bytes 393224 | tf_op jit(solution)/shard_map/ppermute | solution.py:603
  74.9 6.8 %collective-permute-start.27 = (bf16[4,288,128]{2,1,0:T(8,128)(2,1)S(1)}, bf16[4,288,128]{2,1,0:T(8,128)(2,1)S(1)}, u32[]{:S(2)}, u32[]{:S(2)}) collective-permute-start(bf16[4,288,128]{2,1,0:T(8,128)(2,1)S(1)} %pad_maximum_fusion.1), channel_id=1, source_target_pairs={{0,1},{1,0},{2,3},{3,2},{4,5},{5,4},{6,7},{7,6},{8,9},{9,8},{10,11... | collective-permute-start | bytes 884744 | tf_op jit(solution)/shard_map/ppermute | solution.py:597

commit v6 on v5

--- a/solution.py
+++ b/solution.py
@@ -96,7 +96,7 @@
         last_planes_kernel,
         out_shape=sds(shape, BF16),
         in_specs=[pl.BlockSpec(memory_space=pltpu.HBM)],
-        out_specs=pl.BlockSpec(memory_space=pltpu.HBM),
+        out_specs=pl.BlockSpec(memory_space=pltpu.VMEM),
         scratch_shapes=[pltpu.SemaphoreType.DMA],
         cost_estimate=pl.CostEstimate(
             flops=0, bytes_accessed=4 * shape[0] * shape[1] * shape[2], transcendentals=0

time: 83.6 us -> 72.4 us (0.87)
  Pallas kernels: 27.5 us -> 16.2 us
    pallas_call x1, Pallas kernels: 13 us -> 1.75 us  [last_planes(): pl.pallas_call(last_planes_kernel, out_shape=sds(shape, BF16), in_specs=[...]
  transfers between devices with their start and end apart: 28 -> 28, of which waited for: 12 -> 12; matrix products, arithmetic and copies ran while one was open for 0% -> 0% of each run, Pallas kernels for 15% -> 18%
where the time goes in v6:
time: 72.4 us; the launch traced here: 72.1 us
  starting transfers between devices  27.5 us (38%)
  waiting for transfers between devices  25.2 us (35%)
  Pallas kernels  16.2 us (22%)
  local copies, waits for them, and re-layouts  2.01 us (3%)
  between operations  0.94 us (1%)
    ppermute x26, waiting for transfers between devices, swap(): return lax.ppermute(value, axis, [(i, i ^ bits) for i in range(size)])  22.9 us
    ppermute x26, starting transfers between devices, swap(): return lax.ppermute(value, axis, [(i, i ^ bits) for i in range(size)])  22.5 us
    pallas_call x8, Pallas kernels, call(): pl.pallas_call(kernel, out_shape=out_shape, in_specs=specs, out_specs=jax...  14.4 us
    ppermute x2, starting transfers between devices, shifted(): return lax.ppermute(value, axis, pairs)  4.97 us
    ppermute x2, waiting for transfers between devices, shifted(): return lax.ppermute(value, axis, pairs)  2.23 us
    unnamed x18, local copies, waits for them, and re-layouts  1.99 us
    pallas_call x1, Pallas kernels, last_planes(): pl.pallas_call(last_planes_kernel, out_shape=sds(shape, BF16), in_specs=[...  1.75 us
  transfers between devices with their start and end apart: 28, of which 12 were waited for; matrix products, arithmetic and copies ran while one was open for 0% of the time, Pallas kernels for 18%

profile of v6, /device:TPU:0, one launch (start us, length us, event | category | flops | bytes accessed | tf_op | source)
XLA Modules:
  0.0 72.1 jit_solution(6051148679057708285)
XLA Ops:
  0.6 1.8 %shard_map.84 = bf16[3,32,2048]{2,1,0:T(8,128)(2,1)} custom-call(bf16[8,32,2048]{2,1,0:T(8,128)(2,1)} %bitcast.33), custom_call_target="tpu_custom_call" | custom-call | bytes 786432 | tf_op jit(solution)/shard_map/pallas_call | solution.py:95
  2.4 3.0 %collective-permute-start.3 = (bf16[432,128]{1,0:T(8,128)(2,1)}, bf16[432,128]{1,0:T(8,128)(2,1)S(1)}, u32[]{:S(2)}, u32[]{:S(2)}) collective-permute-start(bf16[432,128]{1,0:T(8,128)(2,1)} %w0.5), channel_id=1, source_target_pairs={{0,16},{8,24},{16,0},{24,8},{1,17},{9,25},{17,1},{25,9},{2,18},{10... | collective-permute-start | bytes 331784 | tf_op jit(solution)/shard_map/ppermute | solution.py:597
  5.4 0.2 collective-permute-start.1
  5.6 0.4 collective-permute-start.5
  5.9 3.7 %collective-permute-start = (bf16[3,32,2048]{2,1,0:T(8,128)(2,1)}, bf16[3,32,2048]{2,1,0:T(8,128)(2,1)S(1)}, u32[]{:S(2)}, u32[]{:S(2)}) collective-permute-start(bf16[3,32,2048]{2,1,0:T(8,128)(2,1)} %shard_map.84), channel_id=1, source_target_pairs={{0,1},{1,2},{2,3},{3,4},{4,5},{5,6},{6,7},{8,9},{9,10},{10,11},{11... | collective-permute-start | bytes 1179656 | tf_op jit(solution)/shard_map/ppermute | solution.py:603
  9.6 1.2 %copy-done = bf16[1,8,32,2048]{3,2,1,0:T(8,128)(2,1)S(1)} copy-done((bf16[1,8,32,2048]{3,2,1,0:T(8,128)(2,1)S(1)}, bf16[1,8,32,2048]{3,2,1,0:T(8,128)(2,1)}, u32[]{:S(2)}) %copy-start) | copy-done | bytes 1048600
  10.8 0.3 shard_map.85.sorted_ref
  11.2 0.1 collective-permute-start.4
  11.3 1.3 %collective-permute-done.4.w3 = bf16[432,128]{1,0:T(8,128)(2,1)S(1)} collective-permute-done((bf16[432,128]{1,0:T(8,128)(2,1)S(1)}, bf16[432,128]{1,0:T(8,128)(2,1)S(1)}, u32[]{:S(2)}, u32[]{:S(2)}) %collective-permute-start.4) | collective-permute-done | bytes 110624 | tf_op jit(solution)/shard_map/ppermute | solution.py:597
  12.6 2.1 %shard_map.86 = (f32[768,128]{1,0:T(8,128)S(1)}, f32[3,8,2,2,8,128]{5,4,3,2,1,0:T(8,128)S(1)}, bf16[2,256,128]{2,1,0:T(8,128)(2,1)S(1)}, f32[256,128]{1,0:T(8,128)S(1)}, bf16[2304,128]{1,0:T(8,128)(2,1)S(1)}) custom-call(s32[4]{0:T(128)S(1)} %broadcast_multiply_fusion.offsets, bf16[8,3,256,128]{3,2,1,0:T(8,128)(2,1)S(1)} %shard_map.85.sorted_ref, ...), custom_call_target="tpu_custom_call" | custom-call | flops 2875000064 | bytes 3653632 | tf_op jit(solution)/shard_map/pallas_call | solution.py:49
  14.7 0.7 %copy-done.7 = f32[768,128]{1,0:T(8,128)} copy-done((f32[768,128]{1,0:T(8,128)}, f32[768,128]{1,0:T(8,128)S(1)}, u32[]{:S(2)}) %copy-start.7) | copy-done | bytes 393240
  15.5 2.7 %collective-permute-done.1.w2 = bf16[864,256]{1,0:T(8,128)(2,1)S(1)} collective-permute-done((bf16[864,256]{1,0:T(8,128)(2,1)}, bf16[864,256]{1,0:T(8,128)(2,1)S(1)}, u32[]{:S(2)}, u32[]{:S(2)}) %collective-permute-start.1) | collective-permute-done | bytes 442400 | tf_op jit(solution)/shard_map/ppermute | solution.py:597
  18.2 1.8 %collective-permute-start.11 = (bf16[2,256,128]{2,1,0:T(8,128)(2,1)S(1)}, bf16[2,256,128]{2,1,0:T(8,128)(2,1)S(1)}, u32[]{:S(2)}, u32[]{:S(2)}) collective-permute-start(bf16[2,256,128]{2,1,0:T(8,128)(2,1)S(1)} %get-tuple-element.62.m0), channel_id=1, source_target_pairs={{0,16},{8,24},{16,0},{24,8},{1,17},{9,25},{17,1},{25,9},{2,18},{10... | collective-permute-start | bytes 393224 | tf_op jit(solution)/shard_map/ppermute | solution.py:597
  20.0 0.2 collective-permute-start.12
  20.2 0.9 %shard_map.87 = (f32[512,128]{1,0:T(8,128)S(1)}, bf16[128,3456]{1,0:T(8,128)(2,1)S(1)}, bf16[3,3,256,128]{3,2,1,0:T(8,128)(2,1)S(1)}, bf16[2,256,128]{2,1,0:T(8,128)(2,1)S(1)}, bf16[2,256,128]{2,1,0:T(8,128)(2,1)S(1)}) custom-call(f32[1]{0:T(128)} %bitcast.alive, s32[1]{0:T(128)} %bitcast.1.side, bf16[3,32,2048]{2,1,0:T(8,128)(2,1)S(1)} %collective-permute-done.halo_ref, ...), custom_call_target="tpu_custom_call" | custom-call | flops 1724999936 | bytes 3506176 | tf_op jit(solution)/shard_map/pallas_call | solution.py:49
  21.1 0.4 collective-permute-start.10
  21.5 0.3 collective-permute-start.8
  21.9 1.8 %shard_map.88 = (bf16[2,8,2048]{2,1,0:T(8,128)(2,1)}, bf16[128,256]{1,0:T(8,128)(2,1)S(1)}) custom-call(s32[4]{0:T(128)S(1)} %get-tuple-element.80.offsets, bf16[128,3456]{1,0:T(8,128)(2,1)S(1)} %get-tuple-element.46.windows_ref, bf16[2,8,2048]{2,1,0:T(8,128)(2,1)S(1)} %bitcast.39, bf16[864,256]{1,0:T(8,128)(2,1)S(1)} %copy-done.1, ...), custom_call_target="tpu_custom_call" | custom-call | flops 1724999936 | bytes 2850816 | tf_op jit(solution)/shard_map/pallas_call | solution.py:49
  23.7 1.7 %collective-permute-start.7 = (bf16[128,256]{1,0:T(8,128)(2,1)S(1)}, bf16[128,256]{1,0:T(8,128)(2,1)S(1)}, u32[]{:S(2)}, u32[]{:S(2)}) collective-permute-start(bf16[128,256]{1,0:T(8,128)(2,1)S(1)} %get-tuple-element.49.delta_ref.d0), channel_id=1, source_target_pairs={{0,16},{8,24},{16,0},{24,8},{1,17},{9,25},{17,1},{25,9},{2,18},{10... | collective-permute-start | bytes 196616 | tf_op jit(solution)/shard_map/ppermute | solution.py:597
  25.4 3.0 %shard_map.89 = (bf16[768,128]{1,0:T(8,128)(2,1)S(1)}, f32[256,128]{1,0:T(8,128)S(1)}, bf16[512,128]{1,0:T(8,128)(2,1)S(1)}, bf16[8,64,128]{2,1,0:T(8,128)(2,1)S...) custom-call(s32[4]{0:T(128)S(1)} %get-tuple-element.80.offsets, ...), custom_call_target="tpu_custom_call" | custom-call | flops 4024999936 | bytes 5636096 | tf_op jit(solution)/shard_map/pallas_call | solution.py:49
  28.5 0.1 collective-permute-done.7.d2
  28.5 0.5 collective-permute-start.18
  29.0 0.1 collective-permute-start.14
  29.1 0.4 collective-permute-start.15
  29.5 0.1 collective-permute-start.16
  29.6 0.4 collective-permute-start.17
  30.1 1.5 %collective-permute-start.19 = (bf16[2,4,64,128]{3,2,1,0:T(8,128)(2,1)S(1)}, bf16[2,4,64,128]{3,2,1,0:T(8,128)(2,1)S(1)}, u32[]{:S(2)}, u32[]{:S(2)}) collective-permute-start(bf16[2,4,64,128]{3,2,1,0:T(8,128)(2,1)S(1)} %bitcast.40), channel_id=1, source_target_pairs={{0,16},{8,24},{16,0},{24,8},{1,17},{9,25},{17,1},{25,9},{2,18},{10... | collective-permute-start | bytes 393224 | tf_op jit(solution)/shard_map/ppermute | solution.py:597
  31.6 1.8 %shard_map.91 = bf16[8,224,128]{2,1,0:T(8,128)(2,1)S(1)} custom-call(s32[1]{0:T(128)} %bitcast.6.data, s32[4,33]{1,0:T(4,128)S(1)} %copy-done.4, s32[8]{0:T(128)S(1)} %fusion.15.order, bf16[2,256,128]{2,1,0:T(8,128)(2,1)S(1)} %get-tuple-element.61.e0, bf16[2,256,128]{2,1,0:T(8,128)(2,1)S(1)} %collective-permute-done.10.e1, ...), custom_call_target="tpu_custom_call" | custom-call | flops 2300000000 | bytes 1769472 | tf_op jit(solution)/shard_map/pallas_call | solution.py:49
  33.4 2.5 %collective-permute-done.19 = bf16[2,4,64,128]{3,2,1,0:T(8,128)(2,1)S(1)} collective-permute-done((bf16[2,4,64,128]{3,2,1,0:T(8,128)(2,1)S(1)}, bf16[2,4,64,128]{3,2,1,0:T(8,128)(2,1)S(1)}, u32[]{:S(2)}, u32[]{:S(2)}) %collective-permute-start.19) | collective-permute-done | bytes 131104 | tf_op jit(solution)/shard_map/ppermute | solution.py:597
  35.9 1.6 %collective-permute-start.20 = (bf16[4,288,128]{2,1,0:T(8,128)(2,1)S(1)}, bf16[4,288,128]{2,1,0:T(8,128)(2,1)S(1)}, u32[]{:S(2)}, u32[]{:S(2)}) collective-permute-start(bf16[4,288,128]{2,1,0:T(8,128)(2,1)S(1)} %pad_maximum_fusion), channel_id=1, source_target_pairs={{0,1},{1,0},{2,3},{3,2},{4,5},{5,4},{6,7},{7,6},{8,9},{9,8},{10,11... | collective-permute-start | bytes 884744 | tf_op jit(solution)/shard_map/ppermute | solution.py:597
  37.5 6.9 %collective-permute-done.20 = bf16[4,288,128]{2,1,0:T(8,128)(2,1)S(1)} collective-permute-done((bf16[4,288,128]{2,1,0:T(8,128)(2,1)S(1)}, bf16[4,288,128]{2,1,0:T(8,128)(2,1)S(1)}, u32[]{:S(2)}, u32[]{:S(2)}) %collective-permute-start.20) | collective-permute-done | bytes 294944 | tf_op jit(solution)/shard_map/ppermute | solution.py:597
  44.5 0.1 add_convert_fusion
  44.6 1.8 %collective-permute-start.21 = (bf16[288,128]{1,0:T(8,128)(2,1)S(1)}, bf16[288,128]{1,0:T(8,128)(2,1)S(1)}, u32[]{:S(2)}, u32[]{:S(2)}) collective-permute-start(bf16[288,128]{1,0:T(8,128)(2,1)S(1)} %get-tuple-element.76), channel_id=1, source_target_pairs={{0,2},{1,3},{2,0},{3,1},{4,6},{5,7},{6,4},{7,5},{8,10},{9,11},{10,... | collective-permute-start | bytes 221192 | tf_op jit(solution)/shard_map/ppermute | solution.py:597
  46.4 2.6 %collective-permute-start.22 = (bf16[288,128]{1,0:T(8,128)(2,1)S(1)}, bf16[288,128]{1,0:T(8,128)(2,1)S(1)}, u32[]{:S(2)}, u32[]{:S(2)}) collective-permute-start(bf16[288,128]{1,0:T(8,128)(2,1)S(1)} %get-tuple-element.78), channel_id=1, source_target_pairs={{0,4},{1,5},{2,6},{3,7},{4,0},{5,1},{6,2},{7,3},{8,12},{9,13},{10,... | collective-permute-start | bytes 221192 | tf_op jit(solution)/shard_map/ppermute | solution.py:597
  49.0 0.5 collective-permute-done.21
  49.5 3.7 %collective-permute-done.22 = bf16[288,128]{1,0:T(8,128)(2,1)S(1)} collective-permute-done((bf16[288,128]{1,0:T(8,128)(2,1)S(1)}, bf16[288,128]{1,0:T(8,128)(2,1)S(1)}, u32[]{:S(2)}, u32[]{:S(2)}) %collective-permute-start.22) | collective-permute-done | bytes 73760 | tf_op jit(solution)/shard_map/ppermute | solution.py:597
  53.2 2.4 %collective-permute-done.23 = bf16[288,128]{1,0:T(8,128)(2,1)S(1)} collective-permute-done((bf16[288,128]{1,0:T(8,128)(2,1)S(1)}, bf16[288,128]{1,0:T(8,128)(2,1)S(1)}, u32[]{:S(2)}, u32[]{:S(2)}) %collective-permute-start.23) | collective-permute-done | bytes 73760 | tf_op jit(solution)/shard_map/ppermute | solution.py:597
  55.7 0.1 collective-permute-start.24
  55.8 1.2 %collective-permute-start.25 = (bf16[288,128]{1,0:T(8,128)(2,1)S(1)}, bf16[288,128]{1,0:T(8,128)(2,1)S(1)}, u32[]{:S(2)}, u32[]{:S(2)}) collective-permute-start(bf16[288,128]{1,0:T(8,128)(2,1)S(1)} %fusion.2.refs_0_), channel_id=1, source_target_pairs={{0,4},{1,5},{2,6},{3,7},{4,0},{5,1},{6,2},{7,3},{8,12},{9,13},{10,... | collective-permute-start | bytes 221192 | tf_op jit(solution)/shard_map/ppermute | solution.py:597
  56.9 3.2 %collective-permute-start.26 = (bf16[288,128]{1,0:T(8,128)(2,1)S(1)}, bf16[288,128]{1,0:T(8,128)(2,1)S(1)}, u32[]{:S(2)}, u32[]{:S(2)}) collective-permute-start(bf16[288,128]{1,0:T(8,128)(2,1)S(1)} %fusion.2.refs_0_), channel_id=1, source_target_pairs={{0,6},{1,7},{2,4},{3,5},{4,2},{5,3},{6,0},{7,1},{8,14},{9,15},{10,... | collective-permute-start | bytes 221192 | tf_op jit(solution)/shard_map/ppermute | solution.py:597
  60.2 1.3 %collective-permute-start.13 = (bf16[512,128]{1,0:T(8,128)(2,1)S(1)}, bf16[512,128]{1,0:T(8,128)(2,1)S(1)}, u32[]{:S(2)}, u32[]{:S(2)}) collective-permute-start(bf16[512,128]{1,0:T(8,128)(2,1)S(1)} %get-tuple-element.63), channel_id=1, source_target_pairs={{1,0},{2,1},{3,2},{4,3},{5,4},{6,5},{7,6},{9,8},{10,9},{11,10},{12... | collective-permute-start | bytes 393224 | tf_op jit(solution)/shard_map/ppermute | solution.py:603
  61.5 0.2 collective-permute-done.25.refs_2_
  61.7 1.9 %collective-permute-done.26.refs_3_ = bf16[288,128]{1,0:T(8,128)(2,1)S(1)} collective-permute-done((bf16[288,128]{1,0:T(8,128)(2,1)S(1)}, bf16[288,128]{1,0:T(8,128)(2,1)S(1)}, u32[]{:S(2)}, u32[]{:S(2)}) %collective-permute-start.26) | collective-permute-done | bytes 73760 | tf_op jit(solution)/shard_map/ppermute | solution.py:597
  63.7 1.1 %collective-permute-start.27 = (bf16[4,288,128]{2,1,0:T(8,128)(2,1)S(1)}, bf16[4,288,128]{2,1,0:T(8,128)(2,1)S(1)}, u32[]{:S(2)}, u32[]{:S(2)}) collective-permute-start(bf16[4,288,128]{2,1,0:T(8,128)(2,1)S(1)} %pad_maximum_fusion.1), channel_id=1, source_target_pairs={{0,1},{1,0},{2,3},{3,2},{4,5},{5,4},{6,7},{7,6},{8,9},{9,8},{10,11... | collective-permute-start | bytes 884744 | tf_op jit(solution)/shard_map/ppermute | solution.py:597
  64.8 2.2 %collective-permute-done.13.upper_ref = bf16[512,128]{1,0:T(8,128)(2,1)S(1)} collective-permute-done((bf16[512,128]{1,0:T(8,128)(2,1)S(1)}, bf16[512,128]{1,0:T(8,128)(2,1)S(1)}, u32[]{:S(2)}, u32[]{:S(2)}) %collective-permute-start.13) | collective-permute-done | bytes 131104 | tf_op jit(solution)/shard_map/ppermute | solution.py:603
  67.0 2.8 %shard_map.90 = bf16[8,32,2048]{2,1,0:T(8,128)(2,1)} custom-call(s32[4]{0:T(128)S(1)} %broadcast_multiply_fusion.offsets, bf16[768,128]{1,0:T(8,128)(2,1)S(1)} %get-tuple-element.53.low_ref, f32[256,128]{1,0:T(8,128)S(1)} %get-tuple-element.54.last_ref, f32[768,128]{1,0:T(8,128)S(1)} %copy-done.8, bf16[512,128]{1,0:T(8,128)(2,1)S(1)} %collective-permute-done.13.upper_ref, ...), custom_call_target="tpu_custom_call" | custom-call | flops 3449999872 | bytes 2342912 | tf_op jit(solution)/shard_map/pallas_call | solution.py:49
  69.8 0.7 collective-permute-done.27.refs_4_
  70.5 1.7 %shard_map.92 = (f32[432,128]{1,0:T(8,128)}, f32[864,256]{1,0:T(8,128)}) custom-call(s32[8]{0:T(128)S(1)} %fusion.15.order, bf16[288,128]{1,0:T(8,128)(2,1)S(1)} %fusion.2.refs_0_, bf16[288,128]{1,0:T(8,128)(2,1)S(1)} %collective-permute-done.24.refs_1_, bf16[288,128]{1,0:T(8,128)(2,1)S(1)} %collective-permute-done.25.refs_2_, ...), custom_call_target="tpu_custom_call" | custom-call | flops 1150000000 | bytes 1695744 | tf_op jit(solution)/shard_map/pallas_call | solution.py:49
  (47 shorter events, 0.4 us)
Async XLA Ops:
  2.4 8.8 %collective-permute-start.3 = (bf16[432,128]{1,0:T(8,128)(2,1)}, bf16[432,128]{1,0:T(8,128)(2,1)S(1)}, u32[]{:S(2)}, u32[]{:S(2)}) collective-permute-start(bf16[432,128]{1,0:T(8,128)(2,1)} %w0.5), channel_id=1, source_target_pairs={{0,16},{8,24},{16,0},{24,8},{1,17},{9,25},{17,1},{25,9},{2,18},{10... | collective-permute-start | bytes 331784 | tf_op jit(solution)/shard_map/ppermute | solution.py:597
  5.4 5.9 %collective-permute-start.2 = (bf16[432,128]{1,0:T(8,128)(2,1)}, bf16[432,128]{1,0:T(8,128)(2,1)S(1)}, u32[]{:S(2)}, u32[]{:S(2)}) collective-permute-start(bf16[432,128]{1,0:T(8,128)(2,1)} %w0.5), channel_id=1, source_target_pairs={{0,8},{8,0},{16,24},{24,16},{1,9},{9,1},{17,25},{25,17},{2,10},{10... | collective-permute-start | bytes 331784 | tf_op jit(solution)/shard_map/ppermute | solution.py:597
  5.4 12.8 %collective-permute-start.1 = (bf16[864,256]{1,0:T(8,128)(2,1)}, bf16[864,256]{1,0:T(8,128)(2,1)S(1)}, u32[]{:S(2)}, u32[]{:S(2)}) collective-permute-start(bf16[864,256]{1,0:T(8,128)(2,1)} %w0.4), channel_id=1, source_target_pairs={{0,16},{8,24},{16,0},{24,8},{1,17},{9,25},{17,1},{25,9},{2,18},{10... | collective-permute-start | bytes 1327112 | tf_op jit(solution)/shard_map/ppermute | solution.py:597
  5.6 15.9 %collective-permute-start.5 = (bf16[864,256]{1,0:T(8,128)(2,1)}, bf16[864,256]{1,0:T(8,128)(2,1)S(1)}, u32[]{:S(2)}, u32[]{:S(2)}) collective-permute-start(bf16[864,256]{1,0:T(8,128)(2,1)} %w0.4), channel_id=1, source_target_pairs={{0,8},{8,0},{16,24},{24,16},{1,9},{9,1},{17,25},{25,17},{2,10},{10... | collective-permute-start | bytes 1327112 | tf_op jit(solution)/shard_map/ppermute | solution.py:597
  5.9 14.3 %collective-permute-start = (bf16[3,32,2048]{2,1,0:T(8,128)(2,1)}, bf16[3,32,2048]{2,1,0:T(8,128)(2,1)S(1)}, u32[]{:S(2)}, u32[]{:S(2)}) collective-permute-start(bf16[3,32,2048]{2,1,0:T(8,128)(2,1)} %shard_map.84), channel_id=1, source_target_pairs={{0,1},{1,2},{2,3},{3,4},{4,5},{5,6},{6,7},{8,9},{9,10},{10,11},{11... | collective-permute-start | bytes 1179656 | tf_op jit(solution)/shard_map/ppermute | solution.py:603
  9.6 1.2 %copy-start = (bf16[1,8,32,2048]{3,2,1,0:T(8,128)(2,1)S(1)}, bf16[1,8,32,2048]{3,2,1,0:T(8,128)(2,1)}, u32[]{:S(2)}) copy-start(bf16[1,8,32,2048]{3,2,1,0:T(8,128)(2,1)} %param.5) | copy-start | bytes 3145732
  10.8 1.8 %copy-start.2 = (bf16[432,128]{1,0:T(8,128)(2,1)S(1)}, bf16[432,128]{1,0:T(8,128)(2,1)}, u32[]{:S(2)}) copy-start(bf16[432,128]{1,0:T(8,128)(2,1)} %w0.5) | copy-start | bytes 331780
  11.2 3.5 %copy-start.5 = (bf16[8,3,256,128]{3,2,1,0:T(8,128)(2,1)}, bf16[8,3,256,128]{3,2,1,0:T(8,128)(2,1)S(1)}, u32[]{:S(2)}) copy-start(bf16[8,3,256,128]{3,2,1,0:T(8,128)(2,1)S(1)} %shard_map.85.sorted_ref) | copy-start | bytes 4718596
  11.2 1.4 %collective-permute-start.4 = (bf16[432,128]{1,0:T(8,128)(2,1)S(1)}, bf16[432,128]{1,0:T(8,128)(2,1)S(1)}, u32[]{:S(2)}, u32[]{:S(2)}) collective-permute-start(bf16[432,128]{1,0:T(8,128)(2,1)S(1)} %collective-permute-done.3.w2), channel_id=1, source_target_pairs={{0,8},{8,0},{16,24},{24,16},{1,9},{9,1},{17,25},{25,17},{2,10},{10... | collective-permute-start | bytes 331784 | tf_op jit(solution)/shard_map/ppermute | solution.py:597
  14.7 0.7 %copy-start.7 = (f32[768,128]{1,0:T(8,128)}, f32[768,128]{1,0:T(8,128)S(1)}, u32[]{:S(2)}) copy-start(f32[768,128]{1,0:T(8,128)S(1)} %get-tuple-element.51.slope_ref) | copy-start | bytes 1179652
  18.2 3.6 %collective-permute-start.6 = (bf16[864,256]{1,0:T(8,128)(2,1)S(1)}, bf16[864,256]{1,0:T(8,128)(2,1)S(1)}, u32[]{:S(2)}, u32[]{:S(2)}) collective-permute-start(bf16[864,256]{1,0:T(8,128)(2,1)S(1)} %collective-permute-done.1.w2), channel_id=1, source_target_pairs={{0,8},{8,0},{16,24},{24,16},{1,9},{9,1},{17,25},{25,17},{2,10},{10... | collective-permute-start | bytes 1327112 | tf_op jit(solution)/shard_map/ppermute | solution.py:597
  18.2 7.2 %collective-permute-start.11 = (bf16[2,256,128]{2,1,0:T(8,128)(2,1)S(1)}, bf16[2,256,128]{2,1,0:T(8,128)(2,1)S(1)}, u32[]{:S(2)}, u32[]{:S(2)}) collective-permute-start(bf16[2,256,128]{2,1,0:T(8,128)(2,1)S(1)} %get-tuple-element.62.m0), channel_id=1, source_target_pairs={{0,16},{8,24},{16,0},{24,8},{1,17},{9,25},{17,1},{25,9},{2,18},{10... | collective-permute-start | bytes 393224 | tf_op jit(solution)/shard_map/ppermute | solution.py:597
  20.0 8.5 %collective-permute-start.12 = (bf16[2,256,128]{2,1,0:T(8,128)(2,1)S(1)}, bf16[2,256,128]{2,1,0:T(8,128)(2,1)S(1)}, u32[]{:S(2)}, u32[]{:S(2)}) collective-permute-start(bf16[2,256,128]{2,1,0:T(8,128)(2,1)S(1)} %get-tuple-element.62.m0), channel_id=1, source_target_pairs={{0,8},{8,0},{16,24},{24,16},{1,9},{9,1},{17,25},{25,17},{2,10},{10... | collective-permute-start | bytes 393224 | tf_op jit(solution)/shard_map/ppermute | solution.py:597
  20.2 1.6 %copy-start.1 = (bf16[864,256]{1,0:T(8,128)(2,1)S(1)}, bf16[864,256]{1,0:T(8,128)(2,1)}, u32[]{:S(2)}) copy-start(bf16[864,256]{1,0:T(8,128)(2,1)} %w0.4) | copy-start | bytes 1327108
  20.2 1.6 %copy-start.3 = (bf16[1,2,8,2048]{3,2,1,0:T(8,128)(2,1)S(1)}, bf16[1,2,8,2048]{3,2,1,0:T(8,128)(2,1)}, u32[]{:S(2)}) copy-start(bf16[1,2,8,2048]{3,2,1,0:T(8,128)(2,1)} %param.8) | copy-start | bytes 196612
  21.1 7.3 %collective-permute-start.10 = (bf16[2,256,128]{2,1,0:T(8,128)(2,1)S(1)}, bf16[2,256,128]{2,1,0:T(8,128)(2,1)S(1)}, u32[]{:S(2)}, u32[]{:S(2)}) collective-permute-start(bf16[2,256,128]{2,1,0:T(8,128)(2,1)S(1)} %get-tuple-element.61.e0), channel_id=1, source_target_pairs={{0,8},{8,0},{16,24},{24,16},{1,9},{9,1},{17,25},{25,17},{2,10},{10... | collective-permute-start | bytes 393224 | tf_op jit(solution)/shard_map/ppermute | solution.py:597
  21.5 7.0 %collective-permute-start.8 = (bf16[2,256,128]{2,1,0:T(8,128)(2,1)S(1)}, bf16[2,256,128]{2,1,0:T(8,128)(2,1)S(1)}, u32[]{:S(2)}, u32[]{:S(2)}) collective-permute-start(bf16[2,256,128]{2,1,0:T(8,128)(2,1)S(1)} %get-tuple-element.60), channel_id=1, source_target_pairs={{0,16},{8,24},{16,0},{24,8},{1,17},{9,25},{17,1},{25,9},{2,18},{10... | collective-permute-start | bytes 393224 | tf_op jit(solution)/shard_map/ppermute | solution.py:597
  21.8 3.5 %copy-start.6 = (bf16[8,3,256,128]{3,2,1,0:T(8,128)(2,1)S(1)}, bf16[8,3,256,128]{3,2,1,0:T(8,128)(2,1)}, u32[]{:S(2)}) copy-start(bf16[8,3,256,128]{3,2,1,0:T(8,128)(2,1)} %copy-done.5) | copy-start | bytes 4718596
  21.8 3.5 %copy-start.8 = (f32[768,128]{1,0:T(8,128)S(1)}, f32[768,128]{1,0:T(8,128)}, u32[]{:S(2)}) copy-start(f32[768,128]{1,0:T(8,128)} %copy-done.7) | copy-start | bytes 1179652
  23.7 4.8 %collective-permute-start.7 = (bf16[128,256]{1,0:T(8,128)(2,1)S(1)}, bf16[128,256]{1,0:T(8,128)(2,1)S(1)}, u32[]{:S(2)}, u32[]{:S(2)}) collective-permute-start(bf16[128,256]{1,0:T(8,128)(2,1)S(1)} %get-tuple-element.49.delta_ref.d0), channel_id=1, source_target_pairs={{0,16},{8,24},{16,0},{24,8},{1,17},{9,25},{17,1},{25,9},{2,18},{10... | collective-permute-start | bytes 196616 | tf_op jit(solution)/shard_map/ppermute | solution.py:597
  25.4 3.2 %collective-permute-start.9 = (bf16[128,256]{1,0:T(8,128)(2,1)S(1)}, bf16[128,256]{1,0:T(8,128)(2,1)S(1)}, u32[]{:S(2)}, u32[]{:S(2)}) collective-permute-start(bf16[128,256]{1,0:T(8,128)(2,1)S(1)} %get-tuple-element.49.delta_ref.d0), channel_id=1, source_target_pairs={{0,8},{8,0},{16,24},{24,16},{1,9},{9,1},{17,25},{25,17},{2,10},{10... | collective-permute-start | bytes 196616 | tf_op jit(solution)/shard_map/ppermute | solution.py:597
  25.4 6.2 %copy-start.4 = (s32[4,33]{1,0:T(4,128)S(1)}, s32[4,33]{1,0:T(4,128)}, u32[]{:S(2)}) copy-start(s32[4,33]{1,0:T(4,128)} %constant.48.clone.table) | copy-start | bytes 1588
  28.5 1.5 %collective-permute-start.18 = (bf16[8,64,128]{2,1,0:T(8,128)(2,1)S(1)}, bf16[8,64,128]{2,1,0:T(8,128)(2,1)S(1)}, u32[]{:S(2)}, u32[]{:S(2)}) collective-permute-start(bf16[8,64,128]{2,1,0:T(8,128)(2,1)S(1)} %get-tuple-element.73), channel_id=1, source_target_pairs={{0,8},{8,0},{16,24},{24,16},{1,9},{9,1},{17,25},{25,17},{2,10},{10... | collective-permute-start | bytes 393224 | tf_op jit(solution)/shard_map/ppermute | solution.py:597
  29.0 2.5 %collective-permute-start.14 = (bf16[2,256,128]{2,1,0:T(8,128)(2,1)S(1)}, bf16[2,256,128]{2,1,0:T(8,128)(2,1)S(1)}, u32[]{:S(2)}, u32[]{:S(2)}) collective-permute-start(bf16[2,256,128]{2,1,0:T(8,128)(2,1)S(1)} %collective-permute-done.8.e2), channel_id=1, source_target_pairs={{0,8},{8,0},{16,24},{24,16},{1,9},{9,1},{17,25},{25,17},{2,10},{10... | collective-permute-start | bytes 393224 | tf_op jit(solution)/shard_map/ppermute | solution.py:597
  29.1 2.5 %collective-permute-start.15 = (bf16[2,256,128]{2,1,0:T(8,128)(2,1)S(1)}, bf16[2,256,128]{2,1,0:T(8,128)(2,1)S(1)}, u32[]{:S(2)}, u32[]{:S(2)}) collective-permute-start(bf16[2,256,128]{2,1,0:T(8,128)(2,1)S(1)} %collective-permute-done.11.m2), channel_id=1, source_target_pairs={{0,8},{8,0},{16,24},{24,16},{1,9},{9,1},{17,25},{25,17},{2,10},{10... | collective-permute-start | bytes 393224 | tf_op jit(solution)/shard_map/ppermute | solution.py:597
  29.5 2.0 %collective-permute-start.16 = (bf16[128,256]{1,0:T(8,128)(2,1)S(1)}, bf16[128,256]{1,0:T(8,128)(2,1)S(1)}, u32[]{:S(2)}, u32[]{:S(2)}) collective-permute-start(bf16[128,256]{1,0:T(8,128)(2,1)S(1)} %collective-permute-done.7.d2), channel_id=1, source_target_pairs={{0,8},{8,0},{16,24},{24,16},{1,9},{9,1},{17,25},{25,17},{2,10},{10... | collective-permute-start | bytes 196616 | tf_op jit(solution)/shard_map/ppermute | solution.py:597
  29.6 3.8 %collective-permute-start.17 = (bf16[8,64,128]{2,1,0:T(8,128)(2,1)S(1)}, bf16[8,64,128]{2,1,0:T(8,128)(2,1)S(1)}, u32[]{:S(2)}, u32[]{:S(2)}) collective-permute-start(bf16[8,64,128]{2,1,0:T(8,128)(2,1)S(1)} %get-tuple-element.71), channel_id=1, source_target_pairs={{0,8},{8,0},{16,24},{24,16},{1,9},{9,1},{17,25},{25,17},{2,10},{10... | collective-permute-start | bytes 393224 | tf_op jit(solution)/shard_map/ppermute | solution.py:597
  30.1 5.8 %collective-permute-start.19 = (bf16[2,4,64,128]{3,2,1,0:T(8,128)(2,1)S(1)}, bf16[2,4,64,128]{3,2,1,0:T(8,128)(2,1)S(1)}, u32[]{:S(2)}, u32[]{:S(2)}) collective-permute-start(bf16[2,4,64,128]{3,2,1,0:T(8,128)(2,1)S(1)} %bitcast.40), channel_id=1, source_target_pairs={{0,16},{8,24},{16,0},{24,8},{1,17},{9,25},{17,1},{25,9},{2,18},{10... | collective-permute-start | bytes 393224 | tf_op jit(solution)/shard_map/ppermute | solution.py:597
  35.9 8.5 %collective-permute-start.20 = (bf16[4,288,128]{2,1,0:T(8,128)(2,1)S(1)}, bf16[4,288,128]{2,1,0:T(8,128)(2,1)S(1)}, u32[]{:S(2)}, u32[]{:S(2)}) collective-permute-start(bf16[4,288,128]{2,1,0:T(8,128)(2,1)S(1)} %pad_maximum_fusion), channel_id=1, source_target_pairs={{0,1},{1,0},{2,3},{3,2},{4,5},{5,4},{6,7},{7,6},{8,9},{9,8},{10,11... | collective-permute-start | bytes 884744 | tf_op jit(solution)/shard_map/ppermute | solution.py:597
  44.6 5.0 %collective-permute-start.21 = (bf16[288,128]{1,0:T(8,128)(2,1)S(1)}, bf16[288,128]{1,0:T(8,128)(2,1)S(1)}, u32[]{:S(2)}, u32[]{:S(2)}) collective-permute-start(bf16[288,128]{1,0:T(8,128)(2,1)S(1)} %get-tuple-element.76), channel_id=1, source_target_pairs={{0,2},{1,3},{2,0},{3,1},{4,6},{5,7},{6,4},{7,5},{8,10},{9,11},{10,... | collective-permute-start | bytes 221192 | tf_op jit(solution)/shard_map/ppermute | solution.py:597
  46.4 6.8 %collective-permute-start.22 = (bf16[288,128]{1,0:T(8,128)(2,1)S(1)}, bf16[288,128]{1,0:T(8,128)(2,1)S(1)}, u32[]{:S(2)}, u32[]{:S(2)}) collective-permute-start(bf16[288,128]{1,0:T(8,128)(2,1)S(1)} %get-tuple-element.78), channel_id=1, source_target_pairs={{0,4},{1,5},{2,6},{3,7},{4,0},{5,1},{6,2},{7,3},{8,12},{9,13},{10,... | collective-permute-start | bytes 221192 | tf_op jit(solution)/shard_map/ppermute | solution.py:597
  49.0 6.7 %collective-permute-start.23 = (bf16[288,128]{1,0:T(8,128)(2,1)S(1)}, bf16[288,128]{1,0:T(8,128)(2,1)S(1)}, u32[]{:S(2)}, u32[]{:S(2)}) collective-permute-start(bf16[288,128]{1,0:T(8,128)(2,1)S(1)} %get-tuple-element.77), channel_id=1, source_target_pairs={{0,6},{1,7},{2,4},{3,5},{4,2},{5,3},{6,0},{7,1},{8,14},{9,15},{10,... | collective-permute-start | bytes 221192 | tf_op jit(solution)/shard_map/ppermute | solution.py:597
  55.7 5.7 %collective-permute-start.24 = (bf16[288,128]{1,0:T(8,128)(2,1)S(1)}, bf16[288,128]{1,0:T(8,128)(2,1)S(1)}, u32[]{:S(2)}, u32[]{:S(2)}) collective-permute-start(bf16[288,128]{1,0:T(8,128)(2,1)S(1)} %fusion.2.refs_0_), channel_id=1, source_target_pairs={{0,2},{1,3},{2,0},{3,1},{4,6},{5,7},{6,4},{7,5},{8,10},{9,11},{10,... | collective-permute-start | bytes 221192 | tf_op jit(solution)/shard_map/ppermute | solution.py:597
  55.8 5.9 %collective-permute-start.25 = (bf16[288,128]{1,0:T(8,128)(2,1)S(1)}, bf16[288,128]{1,0:T(8,128)(2,1)S(1)}, u32[]{:S(2)}, u32[]{:S(2)}) collective-permute-start(bf16[288,128]{1,0:T(8,128)(2,1)S(1)} %fusion.2.refs_0_), channel_id=1, source_target_pairs={{0,4},{1,5},{2,6},{3,7},{4,0},{5,1},{6,2},{7,3},{8,12},{9,13},{10,... | collective-permute-start | bytes 221192 | tf_op jit(solution)/shard_map/ppermute | solution.py:597
  56.9 6.7 %collective-permute-start.26 = (bf16[288,128]{1,0:T(8,128)(2,1)S(1)}, bf16[288,128]{1,0:T(8,128)(2,1)S(1)}, u32[]{:S(2)}, u32[]{:S(2)}) collective-permute-start(bf16[288,128]{1,0:T(8,128)(2,1)S(1)} %fusion.2.refs_0_), channel_id=1, source_target_pairs={{0,6},{1,7},{2,4},{3,5},{4,2},{5,3},{6,0},{7,1},{8,14},{9,15},{10,... | collective-permute-start | bytes 221192 | tf_op jit(solution)/shard_map/ppermute | solution.py:597
  60.2 6.8 %collective-permute-start.13 = (bf16[512,128]{1,0:T(8,128)(2,1)S(1)}, bf16[512,128]{1,0:T(8,128)(2,1)S(1)}, u32[]{:S(2)}, u32[]{:S(2)}) collective-permute-start(bf16[512,128]{1,0:T(8,128)(2,1)S(1)} %get-tuple-element.63), channel_id=1, source_target_pairs={{1,0},{2,1},{3,2},{4,3},{5,4},{6,5},{7,6},{9,8},{10,9},{11,10},{12... | collective-permute-start | bytes 393224 | tf_op jit(solution)/shard_map/ppermute | solution.py:603
  63.7 6.8 %collective-permute-start.27 = (bf16[4,288,128]{2,1,0:T(8,128)(2,1)S(1)}, bf16[4,288,128]{2,1,0:T(8,128)(2,1)S(1)}, u32[]{:S(2)}, u32[]{:S(2)}) collective-permute-start(bf16[4,288,128]{2,1,0:T(8,128)(2,1)S(1)} %pad_maximum_fusion.1), channel_id=1, source_target_pairs={{0,1},{1,0},{2,3},{3,2},{4,5},{5,4},{6,7},{7,6},{8,9},{9,8},{10,11... | collective-permute-start | bytes 884744 | tf_op jit(solution)/shard_map/ppermute | solution.py:597

commit v7 on v6

--- a/solution.py
+++ b/solution.py
@@ -94,7 +94,7 @@
     shape = (count, *volume.shape[1:])
     return pl.pallas_call(
         last_planes_kernel,
-        out_shape=sds(shape, BF16),
+        out_shape=pltpu.VMEM(shape, BF16),
         in_specs=[pl.BlockSpec(memory_space=pltpu.HBM)],
         out_specs=pl.BlockSpec(memory_space=pltpu.VMEM),
         scratch_shapes=[pltpu.SemaphoreType.DMA],
@@ -271,8 +271,8 @@
     for index, out in enumerate(outs):
         count, size, _ = out.shape
         for place in range(count):
-            row = pl.multiple_of(order[place] * size, 16)
-            out[place] = flat[slots[index], pl.ds(row, size), :]
+            row = pl.multiple_of(order[place] * size, 8)
+            out[place] = flat[slots[index], pl.ds(row, size), :].astype(BF16)
 
 
 def forward_second_kernel(
@@ -345,7 +345,7 @@
                 windows[at : at + size, tap * 128 : (tap + 1) * 128] = block.astype(BF16)
     product[...] = lax.dot_general(
         windows[...], deltas[...], (((0,), (0,)), ((), ())), preferred_element_type=F32
-    ).astype(BF16)
+    )
     lanes = product.shape[1] // 128
     count, piece, _ = out_ref.shape
     shard = 27 * 128 // 4
@@ -355,9 +355,10 @@
         ]
     rest = flat.shape[0] - lanes * shard
     if rest:
-        flat[lanes * shard :, :] = jnp.zeros((rest, 128), BF16)
+        flat[lanes * shard :, :] = jnp.zeros((rest, 128), F32)
     for place in range(count):
-        out_ref[place] = flat[pl.ds(pl.multiple_of(order[place] * piece, 16), piece), :]
+        row = pl.multiple_of(order[place] * piece, 8)
+        out_ref[place] = flat[pl.ds(row, piece), :].astype(BF16)
 
 
 def second_rows(edges, middles, deltas, data, order, places, size):
@@ -383,8 +384,8 @@
             pltpu.VMEM((4 * cells, rows // 32, 2, 2, 8, 128), F32),
             pltpu.VMEM((4 * cellrows, taps * 128), BF16),
             pltpu.VMEM((4 * cellrows, features), BF16),
-            pltpu.VMEM((taps * 128, features), BF16),
-            pltpu.VMEM((places * size, 128), BF16),
+            pltpu.VMEM((taps * 128, features), F32),
+            pltpu.VMEM((places * size, 128), F32),
         ],
         *edges, *middles, *deltas,
         smem=(data.reshape(1), jnp.array(table, jnp.int32), order),
@@ -450,7 +451,7 @@
     tally = jnp.dot(flipped, columns[...], preferred_element_type=F32)
     shard_rows = 9 * 192 // 4
     for tap in range(9):
-        turned = jnp.transpose(tally[:, tap * 256 : (tap + 1) * 256])[64:].astype(BF16)
+        turned = jnp.transpose(tally[:, tap * 256 : (tap + 1) * 256])[64:]
         at = tap * 192
         while at < (tap + 1) * 192:
             shard = at // shard_rows
@@ -461,7 +462,7 @@
             at = to
     rest = flat.shape[1] - shard_rows
     if rest:
-        flat[:, shard_rows:, :] = jnp.zeros((4, rest, 128), BF16)
+        flat[:, shard_rows:, :] = jnp.zeros((4, rest, 128), F32)
     put_pieces(flat, (g0, g1, g2, g3), slots, order)
 
 
@@ -483,7 +484,7 @@
             pltpu.VMEM((delta.shape[0], 4 * rows), F32),
             pltpu.VMEM(((cells + 1) * width, 9 * 256), BF16),
             pltpu.VMEM(((cells + 1) * width, 128), BF16),
-            pltpu.VMEM((4, places * size, 128), BF16),
+            pltpu.VMEM((4, places * size, 128), F32),
         ],
         delta, *shards, *slopes, sorted_volume, halo,
         smem=(offsets, slots, order),
@@ -572,16 +573,16 @@
     big = flat_second.shape[0] // (2 * high)
     for low in range(2):
         for index in range(high):
-            chunk = other.at[index] if low else chunks[index]
+            chunk = (other[index] if low else chunks[index][...]).astype(F32)
             place = order[low * high + index]
-            flat_second[pl.ds(pl.multiple_of(place * big, 16), big), :] = chunk[:big, :]
-            flat_first[pl.ds(pl.multiple_of(place * small, 16), small), :] = chunk[big:, :]
+            flat_second[pl.ds(pl.multiple_of(place * big, 8), big), :] = chunk[:big, :]
+            flat_first[pl.ds(pl.multiple_of(place * small, 8), small), :] = chunk[big:, :]
     rows, features = second_ref.shape
     for lane in range(features // 128):
         second_ref[:, lane * 128 : (lane + 1) * 128] = (
-            flat_second[lane * rows : (lane + 1) * rows, :].astype(F32) * scale_second
+            flat_second[lane * rows : (lane + 1) * rows, :] * scale_second
         )
-    first_ref[...] = flat_first[: first_ref.shape[0], :].astype(F32) * scale_first
+    first_ref[...] = flat_first[: first_ref.shape[0], :] * scale_first
 
 
 def wide_sum(*pieces):
@@ -618,12 +619,11 @@
     steps = jnp.arange(spaces, dtype=jnp.int32)
     order = place ^ (2 * (steps % high) + steps // high)
     lanes = weight_second.shape[1] // 128
-    size_first = -(-small // (16 * spaces)) * 16
-    size_second = -(-lanes * big // (16 * spaces)) * 16
+    size_first = -(-small // (8 * spaces)) * 8
+    size_second = -(-lanes * big // (8 * spaces)) * 8
 
     inputs = volume.reshape(planes, side, width)
     uppermost = last_planes(inputs, 3)
-    weight_first, uppermost = lax.optimization_barrier((weight_first, uppermost))
     first_x = swap(weight_first, "dp", 2)
     first_core = swap(weight_first, "dp", 1)
     second_x = swap(weight_second, "dp", 2)
@@ -643,6 +643,8 @@
     slope_low, windows, sorted_halo, edge, edge_there = forward_lower(
         halo, hidden, partial, padded, alive, x_side.reshape(1)
     )
+    windows, middle_x, middle_core = lax.optimization_barrier((windows, middle_x, middle_core))
+    middle_far = swap(middle_x, "dp", 1)
     cot = cotangent.reshape(cotangent.shape[1:])
     activations, delta_second = forward_second(windows, cot, shards_second, offsets_second)
     edge_x, edge_core = swap(edge_there, "dp", 2), swap(edge, "dp", 1)
@@ -651,14 +653,12 @@
         delta_second, shards_second, (slope_low, slope), sorted_volume, sorted_halo,
         offsets_second, slots, order, spaces, size_first,
     )
-    first, down, delta_x, edge_x, delta_core, edge_core, middle_x, middle_core = (
-        lax.optimization_barrier(
-            (first, down, delta_x, edge_x, delta_core, edge_core, middle_x, middle_core)
-        )
+    first, down, delta_x, edge_x, delta_core, edge_core, middle_far = lax.optimization_barrier(
+        (first, down, delta_x, edge_x, delta_core, edge_core, middle_far)
     )
     second = second_rows(
         (edge, edge_core, edge_x, swap(edge_x, "dp", 1)),
-        (middle, middle_core, middle_x, swap(middle_x, "dp", 1)),
+        (middle, middle_core, middle_x, middle_far),
         (delta_second, delta_core, delta_x, swap(delta_x, "dp", 1)),
         data, order, spaces, size_second,
     )
@@ -669,15 +669,17 @@
 
     far, near = pieces(swap(first[3], "dp", 1)), pieces(swap(first[1], "dp", 1))
     own, there = pieces(first[0]), pieces(first[2])
-    got_x = swap(added(there, far), "dp", 2)
+    both = [
+        (d * spaces + s, (d ^ 2) * spaces + (s ^ 1)) for d in range(4) for s in range(spaces)
+    ]
     second = pieces(second)
-    got_y = swap(
-        jnp.concatenate([second[1], added(own[1], near[1], got_x[1])], axis=1), "space", 1
-    )
+    got_y = swap(jnp.concatenate([second[1], added(own[1], near[1])], axis=1), "space", 1)
+    got_x = swap(added(there[0], far[0]), "dp", 2)
+    got_xy = lax.ppermute(added(there[1], far[1]), ("dp", "space"), both)
     held = jnp.concatenate(
         [
             added(second[0], got_y[:, :size_second]),
-            added(own[0], near[0], got_x[0], got_y[:, size_second:]),
+            added(own[0], near[0], got_x, got_xy, got_y[:, size_second:]),
         ],
         axis=1,
     )
@@ -693,8 +695,8 @@
         functools.partial(unpack_kernel, float(cells_first) ** -0.5, float(cells_second) ** -0.5),
         (sds(weight_first.shape, F32), sds(weight_second.shape, F32)),
         [
-            pltpu.VMEM((spaces * size_first, 128), BF16),
-            pltpu.VMEM((spaces * size_second, 128), BF16),
+            pltpu.VMEM((spaces * size_first, 128), F32),
+            pltpu.VMEM((spaces * size_second, 128), F32),
         ],
         *chunks,
         smem=(order,),

time: 72.4 us -> 73.3 us (1.012)
  local copies, waits for them, and re-layouts: 2.01 us -> 3.75 us
  Pallas kernels: 16.2 us -> 15.4 us
    unnamed x18 -> x22, local copies, waits for them, and re-layouts: 1.99 us -> 3.73 us
    ppermute x0 -> x1, starting transfers between devices: none -> 1.28 us  [local(): got_xy = lax.ppermute(added(there[1], far[1]), ('dp', 'space'), both)]
    ppermute x26, starting transfers between devices: 22.5 us -> 21.3 us  [swap(): return lax.ppermute(value, axis, [(i, i ^ bits) for i in range(size)])]
    pallas_call x1, Pallas kernels: 1.75 us -> 1 us  [last_planes(): pl.pallas_call(last_planes_kernel, out_shape=pltpu.VMEM(shape, BF16), in_...]
  transfers between devices with their start and end apart: 28 -> 29, of which waited for: 12 -> 13; matrix products, arithmetic and copies ran while one was open for 0% -> 0% of each run, Pallas kernels for 18% -> 19%
where the time goes in v7:
time: 73.3 us; the launch traced here: 73 us
  starting transfers between devices  27.5 us (38%)
  waiting for transfers between devices  25.1 us (34%)
  Pallas kernels  15.4 us (21%)
  local copies, waits for them, and re-layouts  3.75 us (5%)
  between operations  0.93 us (1%)
    ppermute x26, waiting for transfers between devices, swap(): return lax.ppermute(value, axis, [(i, i ^ bits) for i in range(size)])  22.4 us
    ppermute x26, starting transfers between devices, swap(): return lax.ppermute(value, axis, [(i, i ^ bits) for i in range(size)])  21.3 us
    pallas_call x8, Pallas kernels, call(): pl.pallas_call(kernel, out_shape=out_shape, in_specs=specs, out_specs=jax...  14.4 us
    ppermute x2, starting transfers between devices, shifted(): return lax.ppermute(value, axis, pairs)  4.98 us
    unnamed x22, local copies, waits for them, and re-layouts  3.73 us
    ppermute x2, waiting for transfers between devices, shifted(): return lax.ppermute(value, axis, pairs)  2.64 us
  transfers between devices with their start and end apart: 29, of which 13 were waited for; matrix products, arithmetic and copies ran while one was open for 0% of the time, Pallas kernels for 19%

profile of v7, /device:TPU:0, one launch (start us, length us, event | category | flops | bytes accessed | tf_op | source)
XLA Modules:
  0.0 73.0 jit_solution(4466735223502986365)
XLA Ops:
  0.6 3.0 %collective-permute-start.3 = (bf16[432,128]{1,0:T(8,128)(2,1)}, bf16[432,128]{1,0:T(8,128)(2,1)S(1)}, u32[]{:S(2)}, u32[]{:S(2)}) collective-permute-start(bf16[432,128]{1,0:T(8,128)(2,1)} %w0.7), channel_id=1, source_target_pairs={{0,16},{8,24},{16,0},{24,8},{1,17},{9,25},{17,1},{25,9},{2,18},{10... | collective-permute-start | bytes 331784 | tf_op jit(solution)/shard_map/ppermute | solution.py:598
  3.6 0.2 collective-permute-start.1
  3.8 0.4 collective-permute-start.7
  4.1 1.0 %shard_map.84 = bf16[3,32,2048]{2,1,0:T(8,128)(2,1)S(1)} custom-call(bf16[8,32,2048]{2,1,0:T(8,128)(2,1)} %bitcast.22), custom_call_target="tpu_custom_call" | custom-call | bytes 786432 | tf_op jit(solution)/shard_map/pallas_call | solution.py:95
  5.2 3.7 %collective-permute-start = (bf16[3,32,2048]{2,1,0:T(8,128)(2,1)S(1)}, bf16[3,32,2048]{2,1,0:T(8,128)(2,1)S(1)}, u32[]{:S(2)}, u32[]{:S(2)}) collective-permute-start(bf16[3,32,2048]{2,1,0:T(8,128)(2,1)S(1)} %shard_map.84), channel_id=1, source_target_pairs={{0,1},{1,2},{2,3},{3,4},{4,5},{5,6},{6,7},{8,9},{9,10},{10,11},{11... | collective-permute-start | bytes 1179656 | tf_op jit(solution)/shard_map/ppermute | solution.py:604
  8.9 1.2 %copy-done = bf16[1,8,32,2048]{3,2,1,0:T(8,128)(2,1)S(1)} copy-done((bf16[1,8,32,2048]{3,2,1,0:T(8,128)(2,1)S(1)}, bf16[1,8,32,2048]{3,2,1,0:T(8,128)(2,1)}, u32[]{:S(2)}) %copy-start) | copy-done | bytes 1048600
  10.1 0.3 shard_map.85.sorted_ref
  10.5 0.1 collective-permute-start.4
  10.6 1.3 %collective-permute-done.4.w3 = bf16[432,128]{1,0:T(8,128)(2,1)S(1)} collective-permute-done((bf16[432,128]{1,0:T(8,128)(2,1)S(1)}, bf16[432,128]{1,0:T(8,128)(2,1)S(1)}, u32[]{:S(2)}, u32[]{:S(2)}) %collective-permute-start.4) | collective-permute-done | bytes 110624 | tf_op jit(solution)/shard_map/ppermute | solution.py:598
  11.9 2.1 %shard_map.86 = (f32[768,128]{1,0:T(8,128)S(1)}, f32[3,8,2,2,8,128]{5,4,3,2,1,0:T(8,128)S(1)}, bf16[2,256,128]{2,1,0:T(8,128)(2,1)S(1)}, f32[256,128]{1,0:T(8,128)S(1)}, bf16[2304,128]{1,0:T(8,128)(2,1)S(1)}) custom-call(s32[4]{0:T(128)S(1)} %broadcast_multiply_fusion.offsets, bf16[8,3,256,128]{3,2,1,0:T(8,128)(2,1)S(1)} %shard_map.85.sorted_ref, ...), custom_call_target="tpu_custom_call" | custom-call | flops 2875000064 | bytes 3653632 | tf_op jit(solution)/shard_map/pallas_call | solution.py:49
  14.0 0.7 %copy-done.7 = f32[3,8,2,2,8,128]{5,4,3,2,1,0:T(8,128)} copy-done((f32[3,8,2,2,8,128]{5,4,3,2,1,0:T(8,128)}, f32[3,8,2,2,8,128]{5,4,3,2,1,0:T(8,128)S(1)}, u32[]{:S(2)}) %copy-start.7) | copy-done | bytes 393240
  14.7 0.7 %copy-done.9 = f32[768,128]{1,0:T(8,128)} copy-done((f32[768,128]{1,0:T(8,128)}, f32[768,128]{1,0:T(8,128)S(1)}, u32[]{:S(2)}) %copy-start.9) | copy-done | bytes 393240
  15.5 1.0 %collective-permute-done.1.w2 = bf16[864,256]{1,0:T(8,128)(2,1)S(1)} collective-permute-done((bf16[864,256]{1,0:T(8,128)(2,1)}, bf16[864,256]{1,0:T(8,128)(2,1)S(1)}, u32[]{:S(2)}, u32[]{:S(2)}) %collective-permute-start.1) | collective-permute-done | bytes 442400 | tf_op jit(solution)/shard_map/ppermute | solution.py:598
  16.5 1.8 %collective-permute-start.5 = (bf16[2,256,128]{2,1,0:T(8,128)(2,1)S(1)}, bf16[2,256,128]{2,1,0:T(8,128)(2,1)S(1)}, u32[]{:S(2)}, u32[]{:S(2)}) collective-permute-start(bf16[2,256,128]{2,1,0:T(8,128)(2,1)S(1)} %get-tuple-element.45.m0), channel_id=1, source_target_pairs={{0,16},{8,24},{16,0},{24,8},{1,17},{9,25},{17,1},{25,9},{2,18},{10... | collective-permute-start | bytes 393224 | tf_op jit(solution)/shard_map/ppermute | solution.py:598
  18.2 0.2 collective-permute-start.6
  18.4 1.0 %copy-done.8 = f32[3,8,2,2,8,128]{5,4,3,2,1,0:T(8,128)S(1)} copy-done((f32[3,8,2,2,8,128]{5,4,3,2,1,0:T(8,128)S(1)}, f32[3,8,2,2,8,128]{5,4,3,2,1,0:T(8,128)}, u32[]{:S(2)}) %copy-start.8) | copy-done | bytes 393240
  19.4 0.9 %shard_map.87 = (f32[512,128]{1,0:T(8,128)S(1)}, bf16[128,3456]{1,0:T(8,128)(2,1)S(1)}, bf16[3,3,256,128]{3,2,1,0:T(8,128)(2,1)S(1)}, bf16[2,256,128]{2,1,0:T(8,128)(2,1)S(1)}, bf16[2,256,128]{2,1,0:T(8,128)(2,1)S(1)}) custom-call(f32[1]{0:T(128)} %bitcast.alive, s32[1]{0:T(128)} %bitcast.1.side, bf16[3,32,2048]{2,1,0:T(8,128)(2,1)S(1)} %collective-permute-done.halo_ref, ...), custom_call_target="tpu_custom_call" | custom-call | flops 1724999936 | bytes 3506176 | tf_op jit(solution)/shard_map/pallas_call | solution.py:49
  20.4 2.1 %collective-permute-done.5.m2 = bf16[2,256,128]{2,1,0:T(8,128)(2,1)S(1)} collective-permute-done((bf16[2,256,128]{2,1,0:T(8,128)(2,1)S(1)}, bf16[2,256,128]{2,1,0:T(8,128)(2,1)S(1)}, u32[]{:S(2)}, u32[]{:S(2)}) %collective-permute-start.5) | collective-permute-done | bytes 131104 | tf_op jit(solution)/shard_map/ppermute | solution.py:598
  22.4 0.5 collective-permute-start.12
  22.9 1.7 %collective-permute-start.10 = (bf16[2,256,128]{2,1,0:T(8,128)(2,1)S(1)}, bf16[2,256,128]{2,1,0:T(8,128)(2,1)S(1)}, u32[]{:S(2)}, u32[]{:S(2)}) collective-permute-start(bf16[2,256,128]{2,1,0:T(8,128)(2,1)S(1)} %get-tuple-element.60), channel_id=1, source_target_pairs={{0,16},{8,24},{16,0},{24,8},{1,17},{9,25},{17,1},{25,9},{2,18},{10... | collective-permute-start | bytes 393224 | tf_op jit(solution)/shard_map/ppermute | solution.py:598
  24.7 1.8 %shard_map.88 = (bf16[2,8,2048]{2,1,0:T(8,128)(2,1)}, bf16[128,256]{1,0:T(8,128)(2,1)S(1)}) custom-call(s32[4]{0:T(128)S(1)} %get-tuple-element.82.offsets, bf16[128,3456]{1,0:T(8,128)(2,1)S(1)} %get-tuple-element.46.windows_ref, bf16[2,8,2048]{2,1,0:T(8,128)(2,1)S(1)} %bitcast.28, bf16[864,256]{1,0:T(8,128)(2,1)S(1)} %copy-done.1, ...), custom_call_target="tpu_custom_call" | custom-call | flops 1724999936 | bytes 2850816 | tf_op jit(solution)/shard_map/pallas_call | solution.py:49
  26.5 0.3 collective-permute-start.9
  26.8 3.0 %shard_map.89 = (bf16[768,128]{1,0:T(8,128)(2,1)S(1)}, f32[256,128]{1,0:T(8,128)S(1)}, bf16[512,128]{1,0:T(8,128)(2,1)S(1)}, bf16[8,56,128]{2,1,0:T(8,128)(2,1)S...) custom-call(s32[4]{0:T(128)S(1)} %get-tuple-element.82.offsets, ...), custom_call_target="tpu_custom_call" | custom-call | flops 4024999936 | bytes 5570560 | tf_op jit(solution)/shard_map/pallas_call | solution.py:49
  29.9 1.1 %collective-permute-done.9.d2 = bf16[128,256]{1,0:T(8,128)(2,1)S(1)} collective-permute-done((bf16[128,256]{1,0:T(8,128)(2,1)S(1)}, bf16[128,256]{1,0:T(8,128)(2,1)S(1)}, u32[]{:S(2)}, u32[]{:S(2)}) %collective-permute-start.9) | collective-permute-done | bytes 65568 | tf_op jit(solution)/shard_map/ppermute | solution.py:598
  31.0 0.5 collective-permute-start.19
  31.5 0.5 collective-permute-start.16
  32.0 0.3 collective-permute-done.17
  32.3 0.6 collective-permute-done.16.d3
  32.9 1.8 %shard_map.91 = bf16[8,216,128]{2,1,0:T(8,128)(2,1)S(1)} custom-call(s32[1]{0:T(128)} %bitcast.6.data, s32[4,33]{1,0:T(4,128)S(1)} %copy-done.4, s32[8]{0:T(128)S(1)} %fusion.12.order, bf16[2,256,128]{2,1,0:T(8,128)(2,1)S(1)} %get-tuple-element.61.e0, bf16[2,256,128]{2,1,0:T(8,128)(2,1)S(1)} %collective-permute-done.12.e1, ...), custom_call_target="tpu_custom_call" | custom-call | flops 2300000000 | bytes 1753088 | tf_op jit(solution)/shard_map/pallas_call | solution.py:49
  34.8 1.6 %collective-permute-start.18 = (bf16[4,272,128]{2,1,0:T(8,128)(2,1)S(1)}, bf16[4,272,128]{2,1,0:T(8,128)(2,1)S(1)}, u32[]{:S(2)}, u32[]{:S(2)}) collective-permute-start(bf16[4,272,128]{2,1,0:T(8,128)(2,1)S(1)} %pad_maximum_fusion), channel_id=1, source_target_pairs={{0,1},{1,0},{2,3},{3,2},{4,5},{5,4},{6,7},{7,6},{8,9},{9,8},{10,11... | collective-permute-start | bytes 835592 | tf_op jit(solution)/shard_map/ppermute | solution.py:598
  36.5 0.7 %collective-permute-start.20 = (bf16[4,56,128]{2,1,0:T(8,128)(2,1)S(1)}, bf16[4,56,128]{2,1,0:T(8,128)(2,1)S(1)}, u32[]{:S(2)}, u32[]{:S(2)}) collective-permute-start(bf16[4,56,128]{2,1,0:T(8,128)(2,1)S(1)} %get-tuple-element.79), channel_id=1, source_target_pairs={{0,16},{8,24},{16,0},{24,8},{1,17},{9,25},{17,1},{25,9},{2,18},{10... | collective-permute-start | bytes 172040 | tf_op jit(solution)/shard_map/ppermute | solution.py:598
  37.2 1.3 %collective-permute-start.21 = (bf16[4,56,128]{2,1,0:T(8,128)(2,1)S(1)}, bf16[4,56,128]{2,1,0:T(8,128)(2,1)S(1)}, u32[]{:S(2)}, u32[]{:S(2)}) collective-permute-start(bf16[4,56,128]{2,1,0:T(8,128)(2,1)S(1)} %get-tuple-element.80), channel_id=1, source_target_pairs={{0,17},{1,16},{2,19},{3,18},{4,21},{5,20},{6,23},{7,22},{8,25},{9,... | collective-permute-start | bytes 172040 | tf_op jit(solution)/shard_map/ppermute | solution.py:678
  38.5 6.5 %collective-permute-done.18 = bf16[4,272,128]{2,1,0:T(8,128)(2,1)S(1)} collective-permute-done((bf16[4,272,128]{2,1,0:T(8,128)(2,1)S(1)}, bf16[4,272,128]{2,1,0:T(8,128)(2,1)S(1)}, u32[]{:S(2)}, u32[]{:S(2)}) %collective-permute-start.18) | collective-permute-done | bytes 278560 | tf_op jit(solution)/shard_map/ppermute | solution.py:598
  45.2 1.6 %collective-permute-start.22 = (bf16[272,128]{1,0:T(8,128)(2,1)S(1)}, bf16[272,128]{1,0:T(8,128)(2,1)S(1)}, u32[]{:S(2)}, u32[]{:S(2)}) collective-permute-start(bf16[272,128]{1,0:T(8,128)(2,1)S(1)} %get-tuple-element.76), channel_id=1, source_target_pairs={{0,2},{1,3},{2,0},{3,1},{4,6},{5,7},{6,4},{7,5},{8,10},{9,11},{10,... | collective-permute-start | bytes 208904 | tf_op jit(solution)/shard_map/ppermute | solution.py:598
  46.8 2.6 %collective-permute-start.23 = (bf16[272,128]{1,0:T(8,128)(2,1)S(1)}, bf16[272,128]{1,0:T(8,128)(2,1)S(1)}, u32[]{:S(2)}, u32[]{:S(2)}) collective-permute-start(bf16[272,128]{1,0:T(8,128)(2,1)S(1)} %get-tuple-element.78), channel_id=1, source_target_pairs={{0,4},{1,5},{2,6},{3,7},{4,0},{5,1},{6,2},{7,3},{8,12},{9,13},{10,... | collective-permute-start | bytes 208904 | tf_op jit(solution)/shard_map/ppermute | solution.py:598
  49.4 0.2 collective-permute-start.24
  49.6 4.4 %collective-permute-done.23 = bf16[272,128]{1,0:T(8,128)(2,1)S(1)} collective-permute-done((bf16[272,128]{1,0:T(8,128)(2,1)S(1)}, bf16[272,128]{1,0:T(8,128)(2,1)S(1)}, u32[]{:S(2)}, u32[]{:S(2)}) %collective-permute-start.23) | collective-permute-done | bytes 69664 | tf_op jit(solution)/shard_map/ppermute | solution.py:598
  54.0 1.5 %collective-permute-done.24 = bf16[272,128]{1,0:T(8,128)(2,1)S(1)} collective-permute-done((bf16[272,128]{1,0:T(8,128)(2,1)S(1)}, bf16[272,128]{1,0:T(8,128)(2,1)S(1)}, u32[]{:S(2)}, u32[]{:S(2)}) %collective-permute-start.24) | collective-permute-done | bytes 69664 | tf_op jit(solution)/shard_map/ppermute | solution.py:598
  55.6 2.3 %collective-permute-start.26 = (bf16[272,128]{1,0:T(8,128)(2,1)S(1)}, bf16[272,128]{1,0:T(8,128)(2,1)S(1)}, u32[]{:S(2)}, u32[]{:S(2)}) collective-permute-start(bf16[272,128]{1,0:T(8,128)(2,1)S(1)} %fusion.2.refs_0_), channel_id=1, source_target_pairs={{0,4},{1,5},{2,6},{3,7},{4,0},{5,1},{6,2},{7,3},{8,12},{9,13},{10,... | collective-permute-start | bytes 208904 | tf_op jit(solution)/shard_map/ppermute | solution.py:598
  57.9 2.1 %collective-permute-start.27 = (bf16[272,128]{1,0:T(8,128)(2,1)S(1)}, bf16[272,128]{1,0:T(8,128)(2,1)S(1)}, u32[]{:S(2)}, u32[]{:S(2)}) collective-permute-start(bf16[272,128]{1,0:T(8,128)(2,1)S(1)} %fusion.2.refs_0_), channel_id=1, source_target_pairs={{0,6},{1,7},{2,4},{3,5},{4,2},{5,3},{6,0},{7,1},{8,14},{9,15},{10,... | collective-permute-start | bytes 208904 | tf_op jit(solution)/shard_map/ppermute | solution.py:598
  60.0 1.3 %collective-permute-start.14 = (bf16[512,128]{1,0:T(8,128)(2,1)S(1)}, bf16[512,128]{1,0:T(8,128)(2,1)S(1)}, u32[]{:S(2)}, u32[]{:S(2)}) collective-permute-start(bf16[512,128]{1,0:T(8,128)(2,1)S(1)} %get-tuple-element.63), channel_id=1, source_target_pairs={{1,0},{2,1},{3,2},{4,3},{5,4},{6,5},{7,6},{9,8},{10,9},{11,10},{12... | collective-permute-start | bytes 393224 | tf_op jit(solution)/shard_map/ppermute | solution.py:604
  61.3 1.1 %collective-permute-done.26.refs_2_ = bf16[272,128]{1,0:T(8,128)(2,1)S(1)} collective-permute-done((bf16[272,128]{1,0:T(8,128)(2,1)S(1)}, bf16[272,128]{1,0:T(8,128)(2,1)S(1)}, u32[]{:S(2)}, u32[]{:S(2)}) %collective-permute-start.26) | collective-permute-done | bytes 69664 | tf_op jit(solution)/shard_map/ppermute | solution.py:598
  62.4 2.3 %collective-permute-done.27.refs_3_ = bf16[272,128]{1,0:T(8,128)(2,1)S(1)} collective-permute-done((bf16[272,128]{1,0:T(8,128)(2,1)S(1)}, bf16[272,128]{1,0:T(8,128)(2,1)S(1)}, u32[]{:S(2)}, u32[]{:S(2)}) %collective-permute-start.27) | collective-permute-done | bytes 69664 | tf_op jit(solution)/shard_map/ppermute | solution.py:598
  64.7 0.9 %collective-permute-start.28 = (bf16[4,272,128]{2,1,0:T(8,128)(2,1)S(1)}, bf16[4,272,128]{2,1,0:T(8,128)(2,1)S(1)}, u32[]{:S(2)}, u32[]{:S(2)}) collective-permute-start(bf16[4,272,128]{2,1,0:T(8,128)(2,1)S(1)} %pad_maximum_fusion.1), channel_id=1, source_target_pairs={{0,1},{1,0},{2,3},{3,2},{4,5},{5,4},{6,7},{7,6},{8,9},{9,8},{10,11... | collective-permute-start | bytes 835592 | tf_op jit(solution)/shard_map/ppermute | solution.py:598
  65.6 2.6 %collective-permute-done.14.upper_ref = bf16[512,128]{1,0:T(8,128)(2,1)S(1)} collective-permute-done((bf16[512,128]{1,0:T(8,128)(2,1)S(1)}, bf16[512,128]{1,0:T(8,128)(2,1)S(1)}, u32[]{:S(2)}, u32[]{:S(2)}) %collective-permute-start.14) | collective-permute-done | bytes 131104 | tf_op jit(solution)/shard_map/ppermute | solution.py:604
  68.3 2.8 %shard_map.90 = bf16[8,32,2048]{2,1,0:T(8,128)(2,1)} custom-call(s32[4]{0:T(128)S(1)} %broadcast_multiply_fusion.offsets, bf16[768,128]{1,0:T(8,128)(2,1)S(1)} %get-tuple-element.53.low_ref, f32[256,128]{1,0:T(8,128)S(1)} %get-tuple-element.54.last_ref, f32[768,128]{1,0:T(8,128)S(1)} %copy-done.10, bf16[512,128]{1,0:T(8,128)(2,1)S(1)} %collective-permute-done.14.upper_ref, ...), custom_call_target="tpu_custom_call" | custom-call | flops 3449999872 | bytes 2342912 | tf_op jit(solution)/shard_map/pallas_call | solution.py:49
  71.1 0.3 collective-permute-done.28.refs_4_
  71.3 1.7 %shard_map.92 = (f32[432,128]{1,0:T(8,128)}, f32[864,256]{1,0:T(8,128)}) custom-call(s32[8]{0:T(128)S(1)} %fusion.12.order, bf16[272,128]{1,0:T(8,128)(2,1)S(1)} %fusion.2.refs_0_, bf16[272,128]{1,0:T(8,128)(2,1)S(1)} %collective-permute-done.25.refs_1_, bf16[272,128]{1,0:T(8,128)(2,1)S(1)} %collective-permute-done.26.refs_2_, ...), custom_call_target="tpu_custom_call" | custom-call | flops 1150000000 | bytes 1662976 | tf_op jit(solution)/shard_map/pallas_call | solution.py:49
  (53 shorter events, 0.5 us)
Async XLA Ops:
  0.6 9.8 %collective-permute-start.3 = (bf16[432,128]{1,0:T(8,128)(2,1)}, bf16[432,128]{1,0:T(8,128)(2,1)S(1)}, u32[]{:S(2)}, u32[]{:S(2)}) collective-permute-start(bf16[432,128]{1,0:T(8,128)(2,1)} %w0.7), channel_id=1, source_target_pairs={{0,16},{8,24},{16,0},{24,8},{1,17},{9,25},{17,1},{25,9},{2,18},{10... | collective-permute-start | bytes 331784 | tf_op jit(solution)/shard_map/ppermute | solution.py:598
  3.6 6.9 %collective-permute-start.2 = (bf16[432,128]{1,0:T(8,128)(2,1)}, bf16[432,128]{1,0:T(8,128)(2,1)S(1)}, u32[]{:S(2)}, u32[]{:S(2)}) collective-permute-start(bf16[432,128]{1,0:T(8,128)(2,1)} %w0.7), channel_id=1, source_target_pairs={{0,8},{8,0},{16,24},{24,16},{1,9},{9,1},{17,25},{25,17},{2,10},{10... | collective-permute-start | bytes 331784 | tf_op jit(solution)/shard_map/ppermute | solution.py:598
  3.6 12.8 %collective-permute-start.1 = (bf16[864,256]{1,0:T(8,128)(2,1)}, bf16[864,256]{1,0:T(8,128)(2,1)S(1)}, u32[]{:S(2)}, u32[]{:S(2)}) collective-permute-start(bf16[864,256]{1,0:T(8,128)(2,1)} %w0.6), channel_id=1, source_target_pairs={{0,16},{8,24},{16,0},{24,8},{1,17},{9,25},{17,1},{25,9},{2,18},{10... | collective-permute-start | bytes 1327112 | tf_op jit(solution)/shard_map/ppermute | solution.py:598
  3.8 20.8 %collective-permute-start.7 = (bf16[864,256]{1,0:T(8,128)(2,1)}, bf16[864,256]{1,0:T(8,128)(2,1)S(1)}, u32[]{:S(2)}, u32[]{:S(2)}) collective-permute-start(bf16[864,256]{1,0:T(8,128)(2,1)} %w0.6), channel_id=1, source_target_pairs={{0,8},{8,0},{16,24},{24,16},{1,9},{9,1},{17,25},{25,17},{2,10},{10... | collective-permute-start | bytes 1327112 | tf_op jit(solution)/shard_map/ppermute | solution.py:598
  5.2 13.3 %collective-permute-start = (bf16[3,32,2048]{2,1,0:T(8,128)(2,1)S(1)}, bf16[3,32,2048]{2,1,0:T(8,128)(2,1)S(1)}, u32[]{:S(2)}, u32[]{:S(2)}) collective-permute-start(bf16[3,32,2048]{2,1,0:T(8,128)(2,1)S(1)} %shard_map.84), channel_id=1, source_target_pairs={{0,1},{1,2},{2,3},{3,4},{4,5},{5,6},{6,7},{8,9},{9,10},{10,11},{11... | collective-permute-start | bytes 1179656 | tf_op jit(solution)/shard_map/ppermute | solution.py:604
  8.9 1.2 %copy-start = (bf16[1,8,32,2048]{3,2,1,0:T(8,128)(2,1)S(1)}, bf16[1,8,32,2048]{3,2,1,0:T(8,128)(2,1)}, u32[]{:S(2)}) copy-start(bf16[1,8,32,2048]{3,2,1,0:T(8,128)(2,1)} %param.5) | copy-start | bytes 3145732
  10.1 1.8 %copy-start.2 = (bf16[432,128]{1,0:T(8,128)(2,1)S(1)}, bf16[432,128]{1,0:T(8,128)(2,1)}, u32[]{:S(2)}) copy-start(bf16[432,128]{1,0:T(8,128)(2,1)} %w0.7) | copy-start | bytes 331780
  10.5 3.5 %copy-start.5 = (bf16[8,3,256,128]{3,2,1,0:T(8,128)(2,1)}, bf16[8,3,256,128]{3,2,1,0:T(8,128)(2,1)S(1)}, u32[]{:S(2)}) copy-start(bf16[8,3,256,128]{3,2,1,0:T(8,128)(2,1)S(1)} %shard_map.85.sorted_ref) | copy-start | bytes 4718596
  10.5 1.4 %collective-permute-start.4 = (bf16[432,128]{1,0:T(8,128)(2,1)S(1)}, bf16[432,128]{1,0:T(8,128)(2,1)S(1)}, u32[]{:S(2)}, u32[]{:S(2)}) collective-permute-start(bf16[432,128]{1,0:T(8,128)(2,1)S(1)} %collective-permute-done.3.w2), channel_id=1, source_target_pairs={{0,8},{8,0},{16,24},{24,16},{1,9},{9,1},{17,25},{25,17},{2,10},{10... | collective-permute-start | bytes 331784 | tf_op jit(solution)/shard_map/ppermute | solution.py:598
  14.0 0.7 %copy-start.7 = (f32[3,8,2,2,8,128]{5,4,3,2,1,0:T(8,128)}, f32[3,8,2,2,8,128]{5,4,3,2,1,0:T(8,128)S(1)}, u32[]{:S(2)}) copy-start(f32[3,8,2,2,8,128]{5,4,3,2,1,0:T(8,128)S(1)} %get-tuple-element.41.hidden_ref) | copy-start | bytes 1179652
  14.7 0.7 %copy-start.9 = (f32[768,128]{1,0:T(8,128)}, f32[768,128]{1,0:T(8,128)S(1)}, u32[]{:S(2)}) copy-start(f32[768,128]{1,0:T(8,128)S(1)} %get-tuple-element.51.slope_ref) | copy-start | bytes 1179652
  16.4 8.2 %collective-permute-start.8 = (bf16[864,256]{1,0:T(8,128)(2,1)S(1)}, bf16[864,256]{1,0:T(8,128)(2,1)S(1)}, u32[]{:S(2)}, u32[]{:S(2)}) collective-permute-start(bf16[864,256]{1,0:T(8,128)(2,1)S(1)} %collective-permute-done.1.w2), channel_id=1, source_target_pairs={{0,8},{8,0},{16,24},{24,16},{1,9},{9,1},{17,25},{25,17},{2,10},{10... | collective-permute-start | bytes 1327112 | tf_op jit(solution)/shard_map/ppermute | solution.py:598
  16.5 6.0 %collective-permute-start.5 = (bf16[2,256,128]{2,1,0:T(8,128)(2,1)S(1)}, bf16[2,256,128]{2,1,0:T(8,128)(2,1)S(1)}, u32[]{:S(2)}, u32[]{:S(2)}) collective-permute-start(bf16[2,256,128]{2,1,0:T(8,128)(2,1)S(1)} %get-tuple-element.45.m0), channel_id=1, source_target_pairs={{0,16},{8,24},{16,0},{24,8},{1,17},{9,25},{17,1},{25,9},{2,18},{10... | collective-permute-start | bytes 393224 | tf_op jit(solution)/shard_map/ppermute | solution.py:598
  18.2 4.2 %collective-permute-start.6 = (bf16[2,256,128]{2,1,0:T(8,128)(2,1)S(1)}, bf16[2,256,128]{2,1,0:T(8,128)(2,1)S(1)}, u32[]{:S(2)}, u32[]{:S(2)}) collective-permute-start(bf16[2,256,128]{2,1,0:T(8,128)(2,1)S(1)} %get-tuple-element.45.m0), channel_id=1, source_target_pairs={{0,8},{8,0},{16,24},{24,16},{1,9},{9,1},{17,25},{25,17},{2,10},{10... | collective-permute-start | bytes 393224 | tf_op jit(solution)/shard_map/ppermute | solution.py:598
  18.4 1.0 %copy-start.8 = (f32[3,8,2,2,8,128]{5,4,3,2,1,0:T(8,128)S(1)}, f32[3,8,2,2,8,128]{5,4,3,2,1,0:T(8,128)}, u32[]{:S(2)}) copy-start(f32[3,8,2,2,8,128]{5,4,3,2,1,0:T(8,128)} %copy-done.7) | copy-start | bytes 1179652
  19.4 5.2 %copy-start.1 = (bf16[864,256]{1,0:T(8,128)(2,1)S(1)}, bf16[864,256]{1,0:T(8,128)(2,1)}, u32[]{:S(2)}) copy-start(bf16[864,256]{1,0:T(8,128)(2,1)} %w0.6) | copy-start | bytes 1327108
  19.4 5.2 %copy-start.3 = (bf16[1,2,8,2048]{3,2,1,0:T(8,128)(2,1)S(1)}, bf16[1,2,8,2048]{3,2,1,0:T(8,128)(2,1)}, u32[]{:S(2)}) copy-start(bf16[1,2,8,2048]{3,2,1,0:T(8,128)(2,1)} %param.8) | copy-start | bytes 196612
  22.4 7.4 %collective-permute-start.13 = (bf16[2,256,128]{2,1,0:T(8,128)(2,1)S(1)}, bf16[2,256,128]{2,1,0:T(8,128)(2,1)S(1)}, u32[]{:S(2)}, u32[]{:S(2)}) collective-permute-start(bf16[2,256,128]{2,1,0:T(8,128)(2,1)S(1)} %collective-permute-done.5.m2), channel_id=1, source_target_pairs={{0,8},{8,0},{16,24},{24,16},{1,9},{9,1},{17,25},{25,17},{2,10},{10... | collective-permute-start | bytes 393224 | tf_op jit(solution)/shard_map/ppermute | solution.py:598
  22.4 7.4 %collective-permute-start.12 = (bf16[2,256,128]{2,1,0:T(8,128)(2,1)S(1)}, bf16[2,256,128]{2,1,0:T(8,128)(2,1)S(1)}, u32[]{:S(2)}, u32[]{:S(2)}) collective-permute-start(bf16[2,256,128]{2,1,0:T(8,128)(2,1)S(1)} %get-tuple-element.61.e0), channel_id=1, source_target_pairs={{0,8},{8,0},{16,24},{24,16},{1,9},{9,1},{17,25},{25,17},{2,10},{10... | collective-permute-start | bytes 393224 | tf_op jit(solution)/shard_map/ppermute | solution.py:598
  22.9 6.9 %collective-permute-start.10 = (bf16[2,256,128]{2,1,0:T(8,128)(2,1)S(1)}, bf16[2,256,128]{2,1,0:T(8,128)(2,1)S(1)}, u32[]{:S(2)}, u32[]{:S(2)}) collective-permute-start(bf16[2,256,128]{2,1,0:T(8,128)(2,1)S(1)} %get-tuple-element.60), channel_id=1, source_target_pairs={{0,16},{8,24},{16,0},{24,8},{1,17},{9,25},{17,1},{25,9},{2,18},{10... | collective-permute-start | bytes 393224 | tf_op jit(solution)/shard_map/ppermute | solution.py:598
  24.6 2.2 %copy-start.6 = (bf16[8,3,256,128]{3,2,1,0:T(8,128)(2,1)S(1)}, bf16[8,3,256,128]{3,2,1,0:T(8,128)(2,1)}, u32[]{:S(2)}) copy-start(bf16[8,3,256,128]{3,2,1,0:T(8,128)(2,1)} %copy-done.5) | copy-start | bytes 4718596
  24.7 2.2 %copy-start.10 = (f32[768,128]{1,0:T(8,128)S(1)}, f32[768,128]{1,0:T(8,128)}, u32[]{:S(2)}) copy-start(f32[768,128]{1,0:T(8,128)} %copy-done.9) | copy-start | bytes 1179652
  26.5 3.4 %collective-permute-start.11 = (bf16[128,256]{1,0:T(8,128)(2,1)S(1)}, bf16[128,256]{1,0:T(8,128)(2,1)S(1)}, u32[]{:S(2)}, u32[]{:S(2)}) collective-permute-start(bf16[128,256]{1,0:T(8,128)(2,1)S(1)} %get-tuple-element.49.delta_ref.d0), channel_id=1, source_target_pairs={{0,8},{8,0},{16,24},{24,16},{1,9},{9,1},{17,25},{25,17},{2,10},{10... | collective-permute-start | bytes 196616 | tf_op jit(solution)/shard_map/ppermute | solution.py:598
  26.5 4.5 %collective-permute-start.9 = (bf16[128,256]{1,0:T(8,128)(2,1)S(1)}, bf16[128,256]{1,0:T(8,128)(2,1)S(1)}, u32[]{:S(2)}, u32[]{:S(2)}) collective-permute-start(bf16[128,256]{1,0:T(8,128)(2,1)S(1)} %get-tuple-element.49.delta_ref.d0), channel_id=1, source_target_pairs={{0,16},{8,24},{16,0},{24,8},{1,17},{9,25},{17,1},{25,9},{2,18},{10... | collective-permute-start | bytes 196616 | tf_op jit(solution)/shard_map/ppermute | solution.py:598
  26.8 6.1 %copy-start.4 = (s32[4,33]{1,0:T(4,128)S(1)}, s32[4,33]{1,0:T(4,128)}, u32[]{:S(2)}) copy-start(s32[4,33]{1,0:T(4,128)} %constant.48.clone.table) | copy-start | bytes 1588
  31.0 1.3 %collective-permute-start.17 = (bf16[8,56,128]{2,1,0:T(8,128)(2,1)S(1)}, bf16[8,56,128]{2,1,0:T(8,128)(2,1)S(1)}, u32[]{:S(2)}, u32[]{:S(2)}) collective-permute-start(bf16[8,56,128]{2,1,0:T(8,128)(2,1)S(1)} %get-tuple-element.71), channel_id=1, source_target_pairs={{0,8},{8,0},{16,24},{24,16},{1,9},{9,1},{17,25},{25,17},{2,10},{10... | collective-permute-start | bytes 344072 | tf_op jit(solution)/shard_map/ppermute | solution.py:598
  31.0 5.4 %collective-permute-start.19 = (bf16[8,56,128]{2,1,0:T(8,128)(2,1)S(1)}, bf16[8,56,128]{2,1,0:T(8,128)(2,1)S(1)}, u32[]{:S(2)}, u32[]{:S(2)}) collective-permute-start(bf16[8,56,128]{2,1,0:T(8,128)(2,1)S(1)} %get-tuple-element.73), channel_id=1, source_target_pairs={{0,8},{8,0},{16,24},{24,16},{1,9},{9,1},{17,25},{25,17},{2,10},{10... | collective-permute-start | bytes 344072 | tf_op jit(solution)/shard_map/ppermute | solution.py:598
  31.5 1.4 %collective-permute-start.15 = (bf16[2,256,128]{2,1,0:T(8,128)(2,1)S(1)}, bf16[2,256,128]{2,1,0:T(8,128)(2,1)S(1)}, u32[]{:S(2)}, u32[]{:S(2)}) collective-permute-start(bf16[2,256,128]{2,1,0:T(8,128)(2,1)S(1)} %collective-permute-done.10.e2), channel_id=1, source_target_pairs={{0,8},{8,0},{16,24},{24,16},{1,9},{9,1},{17,25},{25,17},{2,10},{10... | collective-permute-start | bytes 393224 | tf_op jit(solution)/shard_map/ppermute | solution.py:598
  31.5 1.4 %collective-permute-start.16 = (bf16[128,256]{1,0:T(8,128)(2,1)S(1)}, bf16[128,256]{1,0:T(8,128)(2,1)S(1)}, u32[]{:S(2)}, u32[]{:S(2)}) collective-permute-start(bf16[128,256]{1,0:T(8,128)(2,1)S(1)} %collective-permute-done.9.d2), channel_id=1, source_target_pairs={{0,8},{8,0},{16,24},{24,16},{1,9},{9,1},{17,25},{25,17},{2,10},{10... | collective-permute-start | bytes 196616 | tf_op jit(solution)/shard_map/ppermute | solution.py:598
  34.8 10.2 %collective-permute-start.18 = (bf16[4,272,128]{2,1,0:T(8,128)(2,1)S(1)}, bf16[4,272,128]{2,1,0:T(8,128)(2,1)S(1)}, u32[]{:S(2)}, u32[]{:S(2)}) collective-permute-start(bf16[4,272,128]{2,1,0:T(8,128)(2,1)S(1)} %pad_maximum_fusion), channel_id=1, source_target_pairs={{0,1},{1,0},{2,3},{3,2},{4,5},{5,4},{6,7},{7,6},{8,9},{9,8},{10,11... | collective-permute-start | bytes 835592 | tf_op jit(solution)/shard_map/ppermute | solution.py:598
  36.5 8.6 %collective-permute-start.20 = (bf16[4,56,128]{2,1,0:T(8,128)(2,1)S(1)}, bf16[4,56,128]{2,1,0:T(8,128)(2,1)S(1)}, u32[]{:S(2)}, u32[]{:S(2)}) collective-permute-start(bf16[4,56,128]{2,1,0:T(8,128)(2,1)S(1)} %get-tuple-element.79), channel_id=1, source_target_pairs={{0,16},{8,24},{16,0},{24,8},{1,17},{9,25},{17,1},{25,9},{2,18},{10... | collective-permute-start | bytes 172040 | tf_op jit(solution)/shard_map/ppermute | solution.py:598
  37.2 7.9 %collective-permute-start.21 = (bf16[4,56,128]{2,1,0:T(8,128)(2,1)S(1)}, bf16[4,56,128]{2,1,0:T(8,128)(2,1)S(1)}, u32[]{:S(2)}, u32[]{:S(2)}) collective-permute-start(bf16[4,56,128]{2,1,0:T(8,128)(2,1)S(1)} %get-tuple-element.80), channel_id=1, source_target_pairs={{0,17},{1,16},{2,19},{3,18},{4,21},{5,20},{6,23},{7,22},{8,25},{9,... | collective-permute-start | bytes 172040 | tf_op jit(solution)/shard_map/ppermute | solution.py:678
  45.2 4.5 %collective-permute-start.22 = (bf16[272,128]{1,0:T(8,128)(2,1)S(1)}, bf16[272,128]{1,0:T(8,128)(2,1)S(1)}, u32[]{:S(2)}, u32[]{:S(2)}) collective-permute-start(bf16[272,128]{1,0:T(8,128)(2,1)S(1)} %get-tuple-element.76), channel_id=1, source_target_pairs={{0,2},{1,3},{2,0},{3,1},{4,6},{5,7},{6,4},{7,5},{8,10},{9,11},{10,... | collective-permute-start | bytes 208904 | tf_op jit(solution)/shard_map/ppermute | solution.py:598
  46.8 7.2 %collective-permute-start.23 = (bf16[272,128]{1,0:T(8,128)(2,1)S(1)}, bf16[272,128]{1,0:T(8,128)(2,1)S(1)}, u32[]{:S(2)}, u32[]{:S(2)}) collective-permute-start(bf16[272,128]{1,0:T(8,128)(2,1)S(1)} %get-tuple-element.78), channel_id=1, source_target_pairs={{0,4},{1,5},{2,6},{3,7},{4,0},{5,1},{6,2},{7,3},{8,12},{9,13},{10,... | collective-permute-start | bytes 208904 | tf_op jit(solution)/shard_map/ppermute | solution.py:598
  49.4 6.1 %collective-permute-start.24 = (bf16[272,128]{1,0:T(8,128)(2,1)S(1)}, bf16[272,128]{1,0:T(8,128)(2,1)S(1)}, u32[]{:S(2)}, u32[]{:S(2)}) collective-permute-start(bf16[272,128]{1,0:T(8,128)(2,1)S(1)} %get-tuple-element.77), channel_id=1, source_target_pairs={{0,6},{1,7},{2,4},{3,5},{4,2},{5,3},{6,0},{7,1},{8,14},{9,15},{10,... | collective-permute-start | bytes 208904 | tf_op jit(solution)/shard_map/ppermute | solution.py:598
  55.5 5.7 %collective-permute-start.25 = (bf16[272,128]{1,0:T(8,128)(2,1)S(1)}, bf16[272,128]{1,0:T(8,128)(2,1)S(1)}, u32[]{:S(2)}, u32[]{:S(2)}) collective-permute-start(bf16[272,128]{1,0:T(8,128)(2,1)S(1)} %fusion.2.refs_0_), channel_id=1, source_target_pairs={{0,2},{1,3},{2,0},{3,1},{4,6},{5,7},{6,4},{7,5},{8,10},{9,11},{10,... | collective-permute-start | bytes 208904 | tf_op jit(solution)/shard_map/ppermute | solution.py:598
  55.6 6.7 %collective-permute-start.26 = (bf16[272,128]{1,0:T(8,128)(2,1)S(1)}, bf16[272,128]{1,0:T(8,128)(2,1)S(1)}, u32[]{:S(2)}, u32[]{:S(2)}) collective-permute-start(bf16[272,128]{1,0:T(8,128)(2,1)S(1)} %fusion.2.refs_0_), channel_id=1, source_target_pairs={{0,4},{1,5},{2,6},{3,7},{4,0},{5,1},{6,2},{7,3},{8,12},{9,13},{10,... | collective-permute-start | bytes 208904 | tf_op jit(solution)/shard_map/ppermute | solution.py:598
  57.9 6.8 %collective-permute-start.27 = (bf16[272,128]{1,0:T(8,128)(2,1)S(1)}, bf16[272,128]{1,0:T(8,128)(2,1)S(1)}, u32[]{:S(2)}, u32[]{:S(2)}) collective-permute-start(bf16[272,128]{1,0:T(8,128)(2,1)S(1)} %fusion.2.refs_0_), channel_id=1, source_target_pairs={{0,6},{1,7},{2,4},{3,5},{4,2},{5,3},{6,0},{7,1},{8,14},{9,15},{10,... | collective-permute-start | bytes 208904 | tf_op jit(solution)/shard_map/ppermute | solution.py:598
  60.0 8.3 %collective-permute-start.14 = (bf16[512,128]{1,0:T(8,128)(2,1)S(1)}, bf16[512,128]{1,0:T(8,128)(2,1)S(1)}, u32[]{:S(2)}, u32[]{:S(2)}) collective-permute-start(bf16[512,128]{1,0:T(8,128)(2,1)S(1)} %get-tuple-element.63), channel_id=1, source_target_pairs={{1,0},{2,1},{3,2},{4,3},{5,4},{6,5},{7,6},{9,8},{10,9},{11,10},{12... | collective-permute-start | bytes 393224 | tf_op jit(solution)/shard_map/ppermute | solution.py:604
  64.7 6.6 %collective-permute-start.28 = (bf16[4,272,128]{2,1,0:T(8,128)(2,1)S(1)}, bf16[4,272,128]{2,1,0:T(8,128)(2,1)S(1)}, u32[]{:S(2)}, u32[]{:S(2)}) collective-permute-start(bf16[4,272,128]{2,1,0:T(8,128)(2,1)S(1)} %pad_maximum_fusion.1), channel_id=1, source_target_pairs={{0,1},{1,0},{2,3},{3,2},{4,5},{5,4},{6,7},{7,6},{8,9},{9,8},{10,11... | collective-permute-start | bytes 835592 | tf_op jit(solution)/shard_map/ppermute | solution.py:598

commit v8 on v7

--- a/solution.py
+++ b/solution.py
@@ -43,7 +43,7 @@
 
 
 def call(kernel, out_shape, scratch, *operands, smem=(), micros=1.0):
-    nbytes = sum(a.size * a.dtype.itemsize for a in (*operands, *jax.tree.leaves(out_shape)))
+    nbytes = sum(a.size * a.dtype.itemsize for a in operands)
     specs = [pl.BlockSpec(memory_space=pltpu.SMEM)] * len(smem)
     specs += [pl.BlockSpec(memory_space=pltpu.VMEM)] * len(operands)
     return pl.pallas_call(
@@ -61,6 +61,10 @@
 
 def sds(shape, dtype):
     return jax.ShapeDtypeStruct(shape, dtype)
+
+
+def near(shape, dtype):
+    return pltpu.VMEM(shape, dtype)
 
 
 def sort_kernel(planes, in_ref, out_ref, wide):
@@ -109,7 +113,7 @@
     pairs = width // 128
     return call(
         functools.partial(sort_kernel, planes),
-        sds((planes, 3, pairs * 16, 128), BF16),
+        near((planes, 3, pairs * 16, 128), BF16),
         [pltpu.VMEM((pairs, rows, 128), F32)],
         volume,
     )
@@ -188,11 +192,11 @@
     return call(
         forward_upper_kernel,
         (
-            sds((some, 128), F32),
-            sds((cells - 1, rows // 32, 2, 2, 8, 128), F32),
+            near((some, 128), F32),
+            near((cells - 1, rows // 32, 2, 2, 8, 128), F32),
             sds((cells - 2, rows, 128), BF16),
-            sds((rows, 128), F32),
-            sds((9 * 256, 128), BF16),
+            near((rows, 128), F32),
+            near((9 * 256, 128), BF16),
         ),
         [
             pltpu.VMEM((some, 9 * 256), BF16),
@@ -248,9 +252,9 @@
     return call(
         forward_lower_kernel,
         (
-            sds((2 * rows, 128), F32),
-            sds((cells * rows // 8, 27 * 128), BF16),
-            sds((halo.shape[0], 3, rows, 128), BF16),
+            near((2 * rows, 128), F32),
+            near((cells * rows // 8, 27 * 128), BF16),
+            near((halo.shape[0], 3, rows, 128), BF16),
             sds((2, rows, 128), BF16),
             sds((2, rows, 128), BF16),
         ),
@@ -474,8 +478,8 @@
     return call(
         back_second_kernel,
         (
-            sds(((cells - 1) * width, 128), BF16),
-            sds((width, 128), F32),
+            near(((cells - 1) * width, 128), BF16),
+            near((width, 128), F32),
             sds((2 * width, 128), BF16),
             piece, piece, piece, piece,
         ),
@@ -643,8 +647,6 @@
     slope_low, windows, sorted_halo, edge, edge_there = forward_lower(
         halo, hidden, partial, padded, alive, x_side.reshape(1)
     )
-    windows, middle_x, middle_core = lax.optimization_barrier((windows, middle_x, middle_core))
-    middle_far = swap(middle_x, "dp", 1)
     cot = cotangent.reshape(cotangent.shape[1:])
     activations, delta_second = forward_second(windows, cot, shards_second, offsets_second)
     edge_x, edge_core = swap(edge_there, "dp", 2), swap(edge, "dp", 1)
@@ -653,12 +655,14 @@
         delta_second, shards_second, (slope_low, slope), sorted_volume, sorted_halo,
         offsets_second, slots, order, spaces, size_first,
     )
-    first, down, delta_x, edge_x, delta_core, edge_core, middle_far = lax.optimization_barrier(
-        (first, down, delta_x, edge_x, delta_core, edge_core, middle_far)
+    first, down, delta_x, edge_x, delta_core, edge_core, middle_x, middle_core = (
+        lax.optimization_barrier(
+            (first, down, delta_x, edge_x, delta_core, edge_core, middle_x, middle_core)
+        )
     )
     second = second_rows(
         (edge, edge_core, edge_x, swap(edge_x, "dp", 1)),
-        (middle, middle_core, middle_x, middle_far),
+        (middle, middle_core, middle_x, swap(middle_x, "dp", 1)),
         (delta_second, delta_core, delta_x, swap(delta_x, "dp", 1)),
         data, order, spaces, size_second,
     )
@@ -667,19 +671,19 @@
     def pieces(value):
         return value.reshape(2, high, -1, 128)
 
-    far, near = pieces(swap(first[3], "dp", 1)), pieces(swap(first[1], "dp", 1))
+    far, beside = pieces(swap(first[3], "dp", 1)), pieces(swap(first[1], "dp", 1))
     own, there = pieces(first[0]), pieces(first[2])
     both = [
         (d * spaces + s, (d ^ 2) * spaces + (s ^ 1)) for d in range(4) for s in range(spaces)
     ]
     second = pieces(second)
-    got_y = swap(jnp.concatenate([second[1], added(own[1], near[1])], axis=1), "space", 1)
+    got_y = swap(jnp.concatenate([second[1], added(own[1], beside[1])], axis=1), "space", 1)
     got_x = swap(added(there[0], far[0]), "dp", 2)
     got_xy = lax.ppermute(added(there[1], far[1]), ("dp", "space"), both)
     held = jnp.concatenate(
         [
             added(second[0], got_y[:, :size_second]),
-            added(own[0], near[0], got_x, got_xy, got_y[:, size_second:]),
+            added(own[0], beside[0], got_x, got_xy, got_y[:, size_second:]),
         ],
         axis=1,
     )

time: 73.3 us -> 71.5 us (0.975)
  waiting for transfers between devices: 25.1 us -> 22.8 us
    ppermute x26, waiting for transfers between devices: 22.4 us -> 19.3 us  [swap(): return lax.ppermute(value, axis, [(i, i ^ bits) for i in range(size)])]
    ppermute x26, starting transfers between devices: 21.3 us -> 22.5 us  [swap(): return lax.ppermute(value, axis, [(i, i ^ bits) for i in range(size)])]
    ppermute x2, waiting for transfers between devices: 2.64 us -> 3.49 us  [shifted(): return lax.ppermute(value, axis, pairs)]
    ppermute x1, starting transfers between devices: 1.28 us -> 0.45 us  [local(): got_xy = lax.ppermute(added(there[1], far[1]), ('dp', 'space'), both)]
  transfers between devices with their start and end apart: 29 -> 29, of which waited for: 13 -> 11; matrix products, arithmetic and copies ran while one was open for 0% -> 0% of each run, Pallas kernels for 19% -> 19%
where the time goes in v8:
time: 71.5 us; the launch traced here: 71.2 us
  starting transfers between devices  27.9 us (39%)
  waiting for transfers between devices  22.8 us (32%)
  Pallas kernels  15.5 us (22%)
  local copies, waits for them, and re-layouts  3.75 us (5%)
  between operations  0.94 us (1%)
    ppermute x26, starting transfers between devices, swap(): return lax.ppermute(value, axis, [(i, i ^ bits) for i in range(size)])  22.5 us
    ppermute x26, waiting for transfers between devices, swap(): return lax.ppermute(value, axis, [(i, i ^ bits) for i in range(size)])  19.3 us
    pallas_call x8, Pallas kernels, call(): pl.pallas_call(kernel, out_shape=out_shape, in_specs=specs, out_specs=jax...  14.5 us
    ppermute x2, starting transfers between devices, shifted(): return lax.ppermute(value, axis, pairs)  4.98 us
    unnamed x22, local copies, waits for them, and re-layouts  3.73 us
    ppermute x2, waiting for transfers between devices, shifted(): return lax.ppermute(value, axis, pairs)  3.49 us
  transfers between devices with their start and end apart: 29, of which 11 were waited for; matrix products, arithmetic and copies ran while one was open for 0% of the time, Pallas kernels for 19%

profile of v8, /device:TPU:0, one launch (start us, length us, event | category | flops | bytes accessed | tf_op | source)
XLA Modules:
  0.0 71.2 jit_solution(10099597143435643094)
XLA Ops:
  0.6 3.0 %collective-permute-start.3 = (bf16[432,128]{1,0:T(8,128)(2,1)}, bf16[432,128]{1,0:T(8,128)(2,1)S(1)}, u32[]{:S(2)}, u32[]{:S(2)}) collective-permute-start(bf16[432,128]{1,0:T(8,128)(2,1)} %w0.7), channel_id=1, source_target_pairs={{0,16},{8,24},{16,0},{24,8},{1,17},{9,25},{17,1},{25,9},{2,18},{10... | collective-permute-start | bytes 331784 | tf_op jit(solution)/shard_map/ppermute | solution.py:602
  3.6 0.2 collective-permute-start.1
  3.8 0.4 collective-permute-start.5
  4.1 1.0 %shard_map.84 = bf16[3,32,2048]{2,1,0:T(8,128)(2,1)S(1)} custom-call(bf16[8,32,2048]{2,1,0:T(8,128)(2,1)} %bitcast.22), custom_call_target="tpu_custom_call" | custom-call | bytes 786432 | tf_op jit(solution)/shard_map/pallas_call | solution.py:99
  5.2 3.7 %collective-permute-start = (bf16[3,32,2048]{2,1,0:T(8,128)(2,1)S(1)}, bf16[3,32,2048]{2,1,0:T(8,128)(2,1)S(1)}, u32[]{:S(2)}, u32[]{:S(2)}) collective-permute-start(bf16[3,32,2048]{2,1,0:T(8,128)(2,1)S(1)} %shard_map.84), channel_id=1, source_target_pairs={{0,1},{1,2},{2,3},{3,4},{4,5},{5,6},{6,7},{8,9},{9,10},{10,11},{11... | collective-permute-start | bytes 1179656 | tf_op jit(solution)/shard_map/ppermute | solution.py:608
  8.9 1.2 %copy-done = bf16[1,8,32,2048]{3,2,1,0:T(8,128)(2,1)S(1)} copy-done((bf16[1,8,32,2048]{3,2,1,0:T(8,128)(2,1)S(1)}, bf16[1,8,32,2048]{3,2,1,0:T(8,128)(2,1)}, u32[]{:S(2)}) %copy-start) | copy-done | bytes 1048600
  10.1 0.3 shard_map.85.sorted_ref
  10.5 0.1 collective-permute-start.4
  10.6 1.3 %collective-permute-done.4.w3 = bf16[432,128]{1,0:T(8,128)(2,1)S(1)} collective-permute-done((bf16[432,128]{1,0:T(8,128)(2,1)S(1)}, bf16[432,128]{1,0:T(8,128)(2,1)S(1)}, u32[]{:S(2)}, u32[]{:S(2)}) %collective-permute-start.4) | collective-permute-done | bytes 110624 | tf_op jit(solution)/shard_map/ppermute | solution.py:602
  11.9 2.1 %shard_map.86 = (f32[768,128]{1,0:T(8,128)S(1)}, f32[3,8,2,2,8,128]{5,4,3,2,1,0:T(8,128)S(1)}, bf16[2,256,128]{2,1,0:T(8,128)(2,1)S(1)}, f32[256,128]{1,0:T(8,128)S(1)}, bf16[2304,128]{1,0:T(8,128)(2,1)S(1)}) custom-call(s32[4]{0:T(128)S(1)} %broadcast_multiply_fusion.offsets, bf16[8,3,256,128]{3,2,1,0:T(8,128)(2,1)S(1)} %shard_map.85.sorted_ref, ...), custom_call_target="tpu_custom_call" | custom-call | flops 2875000064 | bytes 2015232 | tf_op jit(solution)/shard_map/pallas_call | solution.py:49
  14.0 0.7 %copy-done.7 = f32[3,8,2,2,8,128]{5,4,3,2,1,0:T(8,128)} copy-done((f32[3,8,2,2,8,128]{5,4,3,2,1,0:T(8,128)}, f32[3,8,2,2,8,128]{5,4,3,2,1,0:T(8,128)S(1)}, u32[]{:S(2)}) %copy-start.7) | copy-done | bytes 393240
  14.7 0.7 %copy-done.9 = f32[768,128]{1,0:T(8,128)} copy-done((f32[768,128]{1,0:T(8,128)}, f32[768,128]{1,0:T(8,128)S(1)}, u32[]{:S(2)}) %copy-start.9) | copy-done | bytes 393240
  15.5 1.0 %collective-permute-done.1.w2 = bf16[864,256]{1,0:T(8,128)(2,1)S(1)} collective-permute-done((bf16[864,256]{1,0:T(8,128)(2,1)}, bf16[864,256]{1,0:T(8,128)(2,1)S(1)}, u32[]{:S(2)}, u32[]{:S(2)}) %collective-permute-start.1) | collective-permute-done | bytes 442400 | tf_op jit(solution)/shard_map/ppermute | solution.py:602
  16.5 1.8 %collective-permute-start.11 = (bf16[2,256,128]{2,1,0:T(8,128)(2,1)S(1)}, bf16[2,256,128]{2,1,0:T(8,128)(2,1)S(1)}, u32[]{:S(2)}, u32[]{:S(2)}) collective-permute-start(bf16[2,256,128]{2,1,0:T(8,128)(2,1)S(1)} %get-tuple-element.58.m0), channel_id=1, source_target_pairs={{0,16},{8,24},{16,0},{24,8},{1,17},{9,25},{17,1},{25,9},{2,18},{10... | collective-permute-start | bytes 393224 | tf_op jit(solution)/shard_map/ppermute | solution.py:602
  18.2 0.2 collective-permute-start.12
  18.4 1.0 %copy-done.8 = f32[3,8,2,2,8,128]{5,4,3,2,1,0:T(8,128)S(1)} copy-done((f32[3,8,2,2,8,128]{5,4,3,2,1,0:T(8,128)S(1)}, f32[3,8,2,2,8,128]{5,4,3,2,1,0:T(8,128)}, u32[]{:S(2)}) %copy-start.8) | copy-done | bytes 393240
  19.4 0.9 %shard_map.87 = (f32[512,128]{1,0:T(8,128)S(1)}, bf16[128,3456]{1,0:T(8,128)(2,1)S(1)}, bf16[3,3,256,128]{3,2,1,0:T(8,128)(2,1)S(1)}, bf16[2,256,128]{2,1,0:T(8,128)(2,1)S(1)}, bf16[2,256,128]{2,1,0:T(8,128)(2,1)S(1)}) custom-call(f32[1]{0:T(128)} %bitcast.alive, s32[1]{0:T(128)} %bitcast.1.side, bf16[3,32,2048]{2,1,0:T(8,128)(2,1)S(1)} %collective-permute-done.halo_ref, ...), custom_call_target="tpu_custom_call" | custom-call | flops 1724999936 | bytes 1507328 | tf_op jit(solution)/shard_map/pallas_call | solution.py:49
  20.4 0.4 collective-permute-start.10
  20.7 0.5 collective-permute-start.8
  21.3 1.8 %shard_map.88 = (bf16[2,8,2048]{2,1,0:T(8,128)(2,1)}, bf16[128,256]{1,0:T(8,128)(2,1)S(1)}) custom-call(s32[4]{0:T(128)S(1)} %get-tuple-element.78.offsets, bf16[128,3456]{1,0:T(8,128)(2,1)S(1)} %get-tuple-element.42.windows_ref, bf16[2,8,2048]{2,1,0:T(8,128)(2,1)S(1)} %bitcast.28, bf16[864,256]{1,0:T(8,128)(2,1)S(1)} %copy-done.1, ...), custom_call_target="tpu_custom_call" | custom-call | flops 1724999936 | bytes 2719744 | tf_op jit(solution)/shard_map/pallas_call | solution.py:49
  23.1 1.5 %collective-permute-start.7 = (bf16[128,256]{1,0:T(8,128)(2,1)S(1)}, bf16[128,256]{1,0:T(8,128)(2,1)S(1)}, u32[]{:S(2)}, u32[]{:S(2)}) collective-permute-start(bf16[128,256]{1,0:T(8,128)(2,1)S(1)} %get-tuple-element.45.delta_ref.d0), channel_id=1, source_target_pairs={{0,16},{8,24},{16,0},{24,8},{1,17},{9,25},{17,1},{25,9},{2,18},{10... | collective-permute-start | bytes 196616 | tf_op jit(solution)/shard_map/ppermute | solution.py:602
  24.6 3.0 %shard_map.89 = (bf16[768,128]{1,0:T(8,128)(2,1)S(1)}, f32[256,128]{1,0:T(8,128)S(1)}, bf16[512,128]{1,0:T(8,128)(2,1)S(1)}, bf16[8,56,128]{2,1,0:T(8,128)(2,1)S...) custom-call(s32[4]{0:T(128)S(1)} %get-tuple-element.78.offsets, ...), custom_call_target="tpu_custom_call" | custom-call | flops 4024999936 | bytes 4653056 | tf_op jit(solution)/shard_map/pallas_call | solution.py:49
  27.7 0.1 collective-permute-done.7.d2
  27.8 0.5 collective-permute-start.17
  28.2 0.1 collective-permute-start.19
  28.3 0.4 collective-permute-start.14
  28.8 0.1 collective-permute-start.15
  28.8 0.4 collective-permute-start.16
  29.3 0.9 %collective-permute-done.16.d3 = bf16[128,256]{1,0:T(8,128)(2,1)S(1)} collective-permute-done((bf16[128,256]{1,0:T(8,128)(2,1)S(1)}, bf16[128,256]{1,0:T(8,128)(2,1)S(1)}, u32[]{:S(2)}, u32[]{:S(2)}) %collective-permute-start.16) | collective-permute-done | bytes 65568 | tf_op jit(solution)/shard_map/ppermute | solution.py:602
  30.2 1.8 %shard_map.91 = bf16[8,216,128]{2,1,0:T(8,128)(2,1)S(1)} custom-call(s32[1]{0:T(128)} %bitcast.6.data, s32[4,33]{1,0:T(4,128)S(1)} %copy-done.4, s32[8]{0:T(128)S(1)} %fusion.12.order, bf16[2,256,128]{2,1,0:T(8,128)(2,1)S(1)} %get-tuple-element.57.e0, bf16[2,256,128]{2,1,0:T(8,128)(2,1)S(1)} %collective-permute-done.10.e1, ...), custom_call_target="tpu_custom_call" | custom-call | flops 2300000000 | bytes 1310720 | tf_op jit(solution)/shard_map/pallas_call | solution.py:49
  32.1 2.0 %collective-permute-start.18 = (bf16[4,272,128]{2,1,0:T(8,128)(2,1)S(1)}, bf16[4,272,128]{2,1,0:T(8,128)(2,1)S(1)}, u32[]{:S(2)}, u32[]{:S(2)}) collective-permute-start(bf16[4,272,128]{2,1,0:T(8,128)(2,1)S(1)} %pad_maximum_fusion), channel_id=1, source_target_pairs={{0,1},{1,0},{2,3},{3,2},{4,5},{5,4},{6,7},{7,6},{8,9},{9,8},{10,11... | collective-permute-start | bytes 835592 | tf_op jit(solution)/shard_map/ppermute | solution.py:602
  34.1 1.2 %collective-permute-start.20 = (bf16[4,56,128]{2,1,0:T(8,128)(2,1)S(1)}, bf16[4,56,128]{2,1,0:T(8,128)(2,1)S(1)}, u32[]{:S(2)}, u32[]{:S(2)}) collective-permute-start(bf16[4,56,128]{2,1,0:T(8,128)(2,1)S(1)} %get-tuple-element.75), channel_id=1, source_target_pairs={{0,16},{8,24},{16,0},{24,8},{1,17},{9,25},{17,1},{25,9},{2,18},{10... | collective-permute-start | bytes 172040 | tf_op jit(solution)/shard_map/ppermute | solution.py:602
  35.3 0.4 collective-permute-start.21
  35.7 6.6 %collective-permute-done.18 = bf16[4,272,128]{2,1,0:T(8,128)(2,1)S(1)} collective-permute-done((bf16[4,272,128]{2,1,0:T(8,128)(2,1)S(1)}, bf16[4,272,128]{2,1,0:T(8,128)(2,1)S(1)}, u32[]{:S(2)}, u32[]{:S(2)}) %collective-permute-start.18) | collective-permute-done | bytes 278560 | tf_op jit(solution)/shard_map/ppermute | solution.py:602
  42.5 2.8 %collective-permute-start.22 = (bf16[272,128]{1,0:T(8,128)(2,1)S(1)}, bf16[272,128]{1,0:T(8,128)(2,1)S(1)}, u32[]{:S(2)}, u32[]{:S(2)}) collective-permute-start(bf16[272,128]{1,0:T(8,128)(2,1)S(1)} %get-tuple-element.72), channel_id=1, source_target_pairs={{0,2},{1,3},{2,0},{3,1},{4,6},{5,7},{6,4},{7,5},{8,10},{9,11},{10,... | collective-permute-start | bytes 208904 | tf_op jit(solution)/shard_map/ppermute | solution.py:602
  45.2 2.6 %collective-permute-start.23 = (bf16[272,128]{1,0:T(8,128)(2,1)S(1)}, bf16[272,128]{1,0:T(8,128)(2,1)S(1)}, u32[]{:S(2)}, u32[]{:S(2)}) collective-permute-start(bf16[272,128]{1,0:T(8,128)(2,1)S(1)} %get-tuple-element.74), channel_id=1, source_target_pairs={{0,4},{1,5},{2,6},{3,7},{4,0},{5,1},{6,2},{7,3},{8,12},{9,13},{10,... | collective-permute-start | bytes 208904 | tf_op jit(solution)/shard_map/ppermute | solution.py:602
  47.8 4.5 %collective-permute-done.23 = bf16[272,128]{1,0:T(8,128)(2,1)S(1)} collective-permute-done((bf16[272,128]{1,0:T(8,128)(2,1)S(1)}, bf16[272,128]{1,0:T(8,128)(2,1)S(1)}, u32[]{:S(2)}, u32[]{:S(2)}) %collective-permute-start.23) | collective-permute-done | bytes 69664 | tf_op jit(solution)/shard_map/ppermute | solution.py:602
  52.3 1.7 %collective-permute-done.24 = bf16[272,128]{1,0:T(8,128)(2,1)S(1)} collective-permute-done((bf16[272,128]{1,0:T(8,128)(2,1)S(1)}, bf16[272,128]{1,0:T(8,128)(2,1)S(1)}, u32[]{:S(2)}, u32[]{:S(2)}) %collective-permute-start.24) | collective-permute-done | bytes 69664 | tf_op jit(solution)/shard_map/ppermute | solution.py:602
  54.0 2.1 %collective-permute-start.26 = (bf16[272,128]{1,0:T(8,128)(2,1)S(1)}, bf16[272,128]{1,0:T(8,128)(2,1)S(1)}, u32[]{:S(2)}, u32[]{:S(2)}) collective-permute-start(bf16[272,128]{1,0:T(8,128)(2,1)S(1)} %fusion.2.refs_0_), channel_id=1, source_target_pairs={{0,4},{1,5},{2,6},{3,7},{4,0},{5,1},{6,2},{7,3},{8,12},{9,13},{10,... | collective-permute-start | bytes 208904 | tf_op jit(solution)/shard_map/ppermute | solution.py:602
  56.2 2.2 %collective-permute-start.27 = (bf16[272,128]{1,0:T(8,128)(2,1)S(1)}, bf16[272,128]{1,0:T(8,128)(2,1)S(1)}, u32[]{:S(2)}, u32[]{:S(2)}) collective-permute-start(bf16[272,128]{1,0:T(8,128)(2,1)S(1)} %fusion.2.refs_0_), channel_id=1, source_target_pairs={{0,6},{1,7},{2,4},{3,5},{4,2},{5,3},{6,0},{7,1},{8,14},{9,15},{10,... | collective-permute-start | bytes 208904 | tf_op jit(solution)/shard_map/ppermute | solution.py:602
  58.4 1.3 %collective-permute-start.13 = (bf16[512,128]{1,0:T(8,128)(2,1)S(1)}, bf16[512,128]{1,0:T(8,128)(2,1)S(1)}, u32[]{:S(2)}, u32[]{:S(2)}) collective-permute-start(bf16[512,128]{1,0:T(8,128)(2,1)S(1)} %get-tuple-element.59), channel_id=1, source_target_pairs={{1,0},{2,1},{3,2},{4,3},{5,4},{6,5},{7,6},{9,8},{10,9},{11,10},{12... | collective-permute-start | bytes 393224 | tf_op jit(solution)/shard_map/ppermute | solution.py:608
  59.7 1.2 %collective-permute-done.26.refs_2_ = bf16[272,128]{1,0:T(8,128)(2,1)S(1)} collective-permute-done((bf16[272,128]{1,0:T(8,128)(2,1)S(1)}, bf16[272,128]{1,0:T(8,128)(2,1)S(1)}, u32[]{:S(2)}, u32[]{:S(2)}) %collective-permute-start.26) | collective-permute-done | bytes 69664 | tf_op jit(solution)/shard_map/ppermute | solution.py:602
  60.9 2.0 %collective-permute-done.27.refs_3_ = bf16[272,128]{1,0:T(8,128)(2,1)S(1)} collective-permute-done((bf16[272,128]{1,0:T(8,128)(2,1)S(1)}, bf16[272,128]{1,0:T(8,128)(2,1)S(1)}, u32[]{:S(2)}, u32[]{:S(2)}) %collective-permute-start.27) | collective-permute-done | bytes 69664 | tf_op jit(solution)/shard_map/ppermute | solution.py:602
  62.9 0.1 collective-permute-start.28
  63.0 3.5 %collective-permute-done.13.upper_ref = bf16[512,128]{1,0:T(8,128)(2,1)S(1)} collective-permute-done((bf16[512,128]{1,0:T(8,128)(2,1)S(1)}, bf16[512,128]{1,0:T(8,128)(2,1)S(1)}, u32[]{:S(2)}, u32[]{:S(2)}) %collective-permute-start.13) | collective-permute-done | bytes 131104 | tf_op jit(solution)/shard_map/ppermute | solution.py:608
  66.5 2.8 %shard_map.90 = bf16[8,32,2048]{2,1,0:T(8,128)(2,1)} custom-call(s32[4]{0:T(128)S(1)} %broadcast_multiply_fusion.offsets, bf16[768,128]{1,0:T(8,128)(2,1)S(1)} %get-tuple-element.49.low_ref, f32[256,128]{1,0:T(8,128)S(1)} %get-tuple-element.50.last_ref, f32[768,128]{1,0:T(8,128)S(1)} %copy-done.10, bf16[512,128]{1,0:T(8,128)(2,1)S(1)} %collective-permute-done.13.upper_ref, ...), custom_call_target="tpu_custom_call" | custom-call | flops 3449999872 | bytes 1294336 | tf_op jit(solution)/shard_map/pallas_call | solution.py:49
  69.3 0.2 collective-permute-done.28.refs_4_
  69.5 1.7 %shard_map.92 = (f32[432,128]{1,0:T(8,128)}, f32[864,256]{1,0:T(8,128)}) custom-call(s32[8]{0:T(128)S(1)} %fusion.12.order, bf16[272,128]{1,0:T(8,128)(2,1)S(1)} %fusion.2.refs_0_, bf16[272,128]{1,0:T(8,128)(2,1)S(1)} %collective-permute-done.25.refs_1_, bf16[272,128]{1,0:T(8,128)(2,1)S(1)} %collective-permute-done.26.refs_2_, ...), custom_call_target="tpu_custom_call" | custom-call | flops 1150000000 | bytes 557056 | tf_op jit(solution)/shard_map/pallas_call | solution.py:49
  (53 shorter events, 0.5 us)
Async XLA Ops:
  0.6 9.8 %collective-permute-start.3 = (bf16[432,128]{1,0:T(8,128)(2,1)}, bf16[432,128]{1,0:T(8,128)(2,1)S(1)}, u32[]{:S(2)}, u32[]{:S(2)}) collective-permute-start(bf16[432,128]{1,0:T(8,128)(2,1)} %w0.7), channel_id=1, source_target_pairs={{0,16},{8,24},{16,0},{24,8},{1,17},{9,25},{17,1},{25,9},{2,18},{10... | collective-permute-start | bytes 331784 | tf_op jit(solution)/shard_map/ppermute | solution.py:602
  3.6 6.9 %collective-permute-start.2 = (bf16[432,128]{1,0:T(8,128)(2,1)}, bf16[432,128]{1,0:T(8,128)(2,1)S(1)}, u32[]{:S(2)}, u32[]{:S(2)}) collective-permute-start(bf16[432,128]{1,0:T(8,128)(2,1)} %w0.7), channel_id=1, source_target_pairs={{0,8},{8,0},{16,24},{24,16},{1,9},{9,1},{17,25},{25,17},{2,10},{10... | collective-permute-start | bytes 331784 | tf_op jit(solution)/shard_map/ppermute | solution.py:602
  3.6 12.8 %collective-permute-start.1 = (bf16[864,256]{1,0:T(8,128)(2,1)}, bf16[864,256]{1,0:T(8,128)(2,1)S(1)}, u32[]{:S(2)}, u32[]{:S(2)}) collective-permute-start(bf16[864,256]{1,0:T(8,128)(2,1)} %w0.6), channel_id=1, source_target_pairs={{0,16},{8,24},{16,0},{24,8},{1,17},{9,25},{17,1},{25,9},{2,18},{10... | collective-permute-start | bytes 1327112 | tf_op jit(solution)/shard_map/ppermute | solution.py:602
  3.8 16.9 %collective-permute-start.5 = (bf16[864,256]{1,0:T(8,128)(2,1)}, bf16[864,256]{1,0:T(8,128)(2,1)S(1)}, u32[]{:S(2)}, u32[]{:S(2)}) collective-permute-start(bf16[864,256]{1,0:T(8,128)(2,1)} %w0.6), channel_id=1, source_target_pairs={{0,8},{8,0},{16,24},{24,16},{1,9},{9,1},{17,25},{25,17},{2,10},{10... | collective-permute-start | bytes 1327112 | tf_op jit(solution)/shard_map/ppermute | solution.py:602
  5.2 13.3 %collective-permute-start = (bf16[3,32,2048]{2,1,0:T(8,128)(2,1)S(1)}, bf16[3,32,2048]{2,1,0:T(8,128)(2,1)S(1)}, u32[]{:S(2)}, u32[]{:S(2)}) collective-permute-start(bf16[3,32,2048]{2,1,0:T(8,128)(2,1)S(1)} %shard_map.84), channel_id=1, source_target_pairs={{0,1},{1,2},{2,3},{3,4},{4,5},{5,6},{6,7},{8,9},{9,10},{10,11},{11... | collective-permute-start | bytes 1179656 | tf_op jit(solution)/shard_map/ppermute | solution.py:608
  8.9 1.2 %copy-start = (bf16[1,8,32,2048]{3,2,1,0:T(8,128)(2,1)S(1)}, bf16[1,8,32,2048]{3,2,1,0:T(8,128)(2,1)}, u32[]{:S(2)}) copy-start(bf16[1,8,32,2048]{3,2,1,0:T(8,128)(2,1)} %param.5) | copy-start | bytes 3145732
  10.1 1.8 %copy-start.2 = (bf16[432,128]{1,0:T(8,128)(2,1)S(1)}, bf16[432,128]{1,0:T(8,128)(2,1)}, u32[]{:S(2)}) copy-start(bf16[432,128]{1,0:T(8,128)(2,1)} %w0.7) | copy-start | bytes 331780
  10.5 3.5 %copy-start.5 = (bf16[8,3,256,128]{3,2,1,0:T(8,128)(2,1)}, bf16[8,3,256,128]{3,2,1,0:T(8,128)(2,1)S(1)}, u32[]{:S(2)}) copy-start(bf16[8,3,256,128]{3,2,1,0:T(8,128)(2,1)S(1)} %shard_map.85.sorted_ref) | copy-start | bytes 4718596
  10.5 1.4 %collective-permute-start.4 = (bf16[432,128]{1,0:T(8,128)(2,1)S(1)}, bf16[432,128]{1,0:T(8,128)(2,1)S(1)}, u32[]{:S(2)}, u32[]{:S(2)}) collective-permute-start(bf16[432,128]{1,0:T(8,128)(2,1)S(1)} %collective-permute-done.3.w2), channel_id=1, source_target_pairs={{0,8},{8,0},{16,24},{24,16},{1,9},{9,1},{17,25},{25,17},{2,10},{10... | collective-permute-start | bytes 331784 | tf_op jit(solution)/shard_map/ppermute | solution.py:602
  14.0 0.7 %copy-start.7 = (f32[3,8,2,2,8,128]{5,4,3,2,1,0:T(8,128)}, f32[3,8,2,2,8,128]{5,4,3,2,1,0:T(8,128)S(1)}, u32[]{:S(2)}) copy-start(f32[3,8,2,2,8,128]{5,4,3,2,1,0:T(8,128)S(1)} %get-tuple-element.39.hidden_ref) | copy-start | bytes 1179652
  14.7 0.7 %copy-start.9 = (f32[768,128]{1,0:T(8,128)}, f32[768,128]{1,0:T(8,128)S(1)}, u32[]{:S(2)}) copy-start(f32[768,128]{1,0:T(8,128)S(1)} %get-tuple-element.47.slope_ref) | copy-start | bytes 1179652
  16.4 4.8 %collective-permute-start.6 = (bf16[864,256]{1,0:T(8,128)(2,1)S(1)}, bf16[864,256]{1,0:T(8,128)(2,1)S(1)}, u32[]{:S(2)}, u32[]{:S(2)}) collective-permute-start(bf16[864,256]{1,0:T(8,128)(2,1)S(1)} %collective-permute-done.1.w2), channel_id=1, source_target_pairs={{0,8},{8,0},{16,24},{24,16},{1,9},{9,1},{17,25},{25,17},{2,10},{10... | collective-permute-start | bytes 1327112 | tf_op jit(solution)/shard_map/ppermute | solution.py:602
  16.5 8.2 %collective-permute-start.11 = (bf16[2,256,128]{2,1,0:T(8,128)(2,1)S(1)}, bf16[2,256,128]{2,1,0:T(8,128)(2,1)S(1)}, u32[]{:S(2)}, u32[]{:S(2)}) collective-permute-start(bf16[2,256,128]{2,1,0:T(8,128)(2,1)S(1)} %get-tuple-element.58.m0), channel_id=1, source_target_pairs={{0,16},{8,24},{16,0},{24,8},{1,17},{9,25},{17,1},{25,9},{2,18},{10... | collective-permute-start | bytes 393224 | tf_op jit(solution)/shard_map/ppermute | solution.py:602
  18.2 9.4 %collective-permute-start.12 = (bf16[2,256,128]{2,1,0:T(8,128)(2,1)S(1)}, bf16[2,256,128]{2,1,0:T(8,128)(2,1)S(1)}, u32[]{:S(2)}, u32[]{:S(2)}) collective-permute-start(bf16[2,256,128]{2,1,0:T(8,128)(2,1)S(1)} %get-tuple-element.58.m0), channel_id=1, source_target_pairs={{0,8},{8,0},{16,24},{24,16},{1,9},{9,1},{17,25},{25,17},{2,10},{10... | collective-permute-start | bytes 393224 | tf_op jit(solution)/shard_map/ppermute | solution.py:602
  18.4 1.0 %copy-start.8 = (f32[3,8,2,2,8,128]{5,4,3,2,1,0:T(8,128)S(1)}, f32[3,8,2,2,8,128]{5,4,3,2,1,0:T(8,128)}, u32[]{:S(2)}) copy-start(f32[3,8,2,2,8,128]{5,4,3,2,1,0:T(8,128)} %copy-done.7) | copy-start | bytes 1179652
  19.4 1.8 %copy-start.1 = (bf16[864,256]{1,0:T(8,128)(2,1)S(1)}, bf16[864,256]{1,0:T(8,128)(2,1)}, u32[]{:S(2)}) copy-start(bf16[864,256]{1,0:T(8,128)(2,1)} %w0.6) | copy-start | bytes 1327108
  19.4 1.8 %copy-start.3 = (bf16[1,2,8,2048]{3,2,1,0:T(8,128)(2,1)S(1)}, bf16[1,2,8,2048]{3,2,1,0:T(8,128)(2,1)}, u32[]{:S(2)}) copy-start(bf16[1,2,8,2048]{3,2,1,0:T(8,128)(2,1)} %param.8) | copy-start | bytes 196612
  20.4 7.3 %collective-permute-start.10 = (bf16[2,256,128]{2,1,0:T(8,128)(2,1)S(1)}, bf16[2,256,128]{2,1,0:T(8,128)(2,1)S(1)}, u32[]{:S(2)}, u32[]{:S(2)}) collective-permute-start(bf16[2,256,128]{2,1,0:T(8,128)(2,1)S(1)} %get-tuple-element.57.e0), channel_id=1, source_target_pairs={{0,8},{8,0},{16,24},{24,16},{1,9},{9,1},{17,25},{25,17},{2,10},{10... | collective-permute-start | bytes 393224 | tf_op jit(solution)/shard_map/ppermute | solution.py:602
  20.7 6.9 %collective-permute-start.8 = (bf16[2,256,128]{2,1,0:T(8,128)(2,1)S(1)}, bf16[2,256,128]{2,1,0:T(8,128)(2,1)S(1)}, u32[]{:S(2)}, u32[]{:S(2)}) collective-permute-start(bf16[2,256,128]{2,1,0:T(8,128)(2,1)S(1)} %get-tuple-element.56), channel_id=1, source_target_pairs={{0,16},{8,24},{16,0},{24,8},{1,17},{9,25},{17,1},{25,9},{2,18},{10... | collective-permute-start | bytes 393224 | tf_op jit(solution)/shard_map/ppermute | solution.py:602
  21.2 3.4 %copy-start.6 = (bf16[8,3,256,128]{3,2,1,0:T(8,128)(2,1)S(1)}, bf16[8,3,256,128]{3,2,1,0:T(8,128)(2,1)}, u32[]{:S(2)}) copy-start(bf16[8,3,256,128]{3,2,1,0:T(8,128)(2,1)} %copy-done.5) | copy-start | bytes 4718596
  21.2 3.4 %copy-start.10 = (f32[768,128]{1,0:T(8,128)S(1)}, f32[768,128]{1,0:T(8,128)}, u32[]{:S(2)}) copy-start(f32[768,128]{1,0:T(8,128)} %copy-done.9) | copy-start | bytes 1179652
  23.1 4.7 %collective-permute-start.7 = (bf16[128,256]{1,0:T(8,128)(2,1)S(1)}, bf16[128,256]{1,0:T(8,128)(2,1)S(1)}, u32[]{:S(2)}, u32[]{:S(2)}) collective-permute-start(bf16[128,256]{1,0:T(8,128)(2,1)S(1)} %get-tuple-element.45.delta_ref.d0), channel_id=1, source_target_pairs={{0,16},{8,24},{16,0},{24,8},{1,17},{9,25},{17,1},{25,9},{2,18},{10... | collective-permute-start | bytes 196616 | tf_op jit(solution)/shard_map/ppermute | solution.py:602
  24.6 3.2 %collective-permute-start.9 = (bf16[128,256]{1,0:T(8,128)(2,1)S(1)}, bf16[128,256]{1,0:T(8,128)(2,1)S(1)}, u32[]{:S(2)}, u32[]{:S(2)}) collective-permute-start(bf16[128,256]{1,0:T(8,128)(2,1)S(1)} %get-tuple-element.45.delta_ref.d0), channel_id=1, source_target_pairs={{0,8},{8,0},{16,24},{24,16},{1,9},{9,1},{17,25},{25,17},{2,10},{10... | collective-permute-start | bytes 196616 | tf_op jit(solution)/shard_map/ppermute | solution.py:602
  24.6 5.6 %copy-start.4 = (s32[4,33]{1,0:T(4,128)S(1)}, s32[4,33]{1,0:T(4,128)}, u32[]{:S(2)}) copy-start(s32[4,33]{1,0:T(4,128)} %constant.48.clone.table) | copy-start | bytes 1588
  27.8 1.5 %collective-permute-start.17 = (bf16[8,56,128]{2,1,0:T(8,128)(2,1)S(1)}, bf16[8,56,128]{2,1,0:T(8,128)(2,1)S(1)}, u32[]{:S(2)}, u32[]{:S(2)}) collective-permute-start(bf16[8,56,128]{2,1,0:T(8,128)(2,1)S(1)} %get-tuple-element.67), channel_id=1, source_target_pairs={{0,8},{8,0},{16,24},{24,16},{1,9},{9,1},{17,25},{25,17},{2,10},{10... | collective-permute-start | bytes 344072 | tf_op jit(solution)/shard_map/ppermute | solution.py:602
  28.2 5.8 %collective-permute-start.19 = (bf16[8,56,128]{2,1,0:T(8,128)(2,1)S(1)}, bf16[8,56,128]{2,1,0:T(8,128)(2,1)S(1)}, u32[]{:S(2)}, u32[]{:S(2)}) collective-permute-start(bf16[8,56,128]{2,1,0:T(8,128)(2,1)S(1)} %get-tuple-element.69), channel_id=1, source_target_pairs={{0,8},{8,0},{16,24},{24,16},{1,9},{9,1},{17,25},{25,17},{2,10},{10... | collective-permute-start | bytes 344072 | tf_op jit(solution)/shard_map/ppermute | solution.py:602
  28.3 1.9 %collective-permute-start.14 = (bf16[2,256,128]{2,1,0:T(8,128)(2,1)S(1)}, bf16[2,256,128]{2,1,0:T(8,128)(2,1)S(1)}, u32[]{:S(2)}, u32[]{:S(2)}) collective-permute-start(bf16[2,256,128]{2,1,0:T(8,128)(2,1)S(1)} %collective-permute-done.8.e2), channel_id=1, source_target_pairs={{0,8},{8,0},{16,24},{24,16},{1,9},{9,1},{17,25},{25,17},{2,10},{10... | collective-permute-start | bytes 393224 | tf_op jit(solution)/shard_map/ppermute | solution.py:602
  28.8 1.4 %collective-permute-start.15 = (bf16[2,256,128]{2,1,0:T(8,128)(2,1)S(1)}, bf16[2,256,128]{2,1,0:T(8,128)(2,1)S(1)}, u32[]{:S(2)}, u32[]{:S(2)}) collective-permute-start(bf16[2,256,128]{2,1,0:T(8,128)(2,1)S(1)} %collective-permute-done.11.m2), channel_id=1, source_target_pairs={{0,8},{8,0},{16,24},{24,16},{1,9},{9,1},{17,25},{25,17},{2,10},{10... | collective-permute-start | bytes 393224 | tf_op jit(solution)/shard_map/ppermute | solution.py:602
  28.8 1.4 %collective-permute-start.16 = (bf16[128,256]{1,0:T(8,128)(2,1)S(1)}, bf16[128,256]{1,0:T(8,128)(2,1)S(1)}, u32[]{:S(2)}, u32[]{:S(2)}) collective-permute-start(bf16[128,256]{1,0:T(8,128)(2,1)S(1)} %collective-permute-done.7.d2), channel_id=1, source_target_pairs={{0,8},{8,0},{16,24},{24,16},{1,9},{9,1},{17,25},{25,17},{2,10},{10... | collective-permute-start | bytes 196616 | tf_op jit(solution)/shard_map/ppermute | solution.py:602
  32.1 10.2 %collective-permute-start.18 = (bf16[4,272,128]{2,1,0:T(8,128)(2,1)S(1)}, bf16[4,272,128]{2,1,0:T(8,128)(2,1)S(1)}, u32[]{:S(2)}, u32[]{:S(2)}) collective-permute-start(bf16[4,272,128]{2,1,0:T(8,128)(2,1)S(1)} %pad_maximum_fusion), channel_id=1, source_target_pairs={{0,1},{1,0},{2,3},{3,2},{4,5},{5,4},{6,7},{7,6},{8,9},{9,8},{10,11... | collective-permute-start | bytes 835592 | tf_op jit(solution)/shard_map/ppermute | solution.py:602
  34.1 8.3 %collective-permute-start.20 = (bf16[4,56,128]{2,1,0:T(8,128)(2,1)S(1)}, bf16[4,56,128]{2,1,0:T(8,128)(2,1)S(1)}, u32[]{:S(2)}, u32[]{:S(2)}) collective-permute-start(bf16[4,56,128]{2,1,0:T(8,128)(2,1)S(1)} %get-tuple-element.75), channel_id=1, source_target_pairs={{0,16},{8,24},{16,0},{24,8},{1,17},{9,25},{17,1},{25,9},{2,18},{10... | collective-permute-start | bytes 172040 | tf_op jit(solution)/shard_map/ppermute | solution.py:602
  35.3 7.1 %collective-permute-start.21 = (bf16[4,56,128]{2,1,0:T(8,128)(2,1)S(1)}, bf16[4,56,128]{2,1,0:T(8,128)(2,1)S(1)}, u32[]{:S(2)}, u32[]{:S(2)}) collective-permute-start(bf16[4,56,128]{2,1,0:T(8,128)(2,1)S(1)} %get-tuple-element.76), channel_id=1, source_target_pairs={{0,17},{1,16},{2,19},{3,18},{4,21},{5,20},{6,23},{7,22},{8,25},{9,... | collective-permute-start | bytes 172040 | tf_op jit(solution)/shard_map/ppermute | solution.py:682
  42.5 5.4 %collective-permute-start.22 = (bf16[272,128]{1,0:T(8,128)(2,1)S(1)}, bf16[272,128]{1,0:T(8,128)(2,1)S(1)}, u32[]{:S(2)}, u32[]{:S(2)}) collective-permute-start(bf16[272,128]{1,0:T(8,128)(2,1)S(1)} %get-tuple-element.72), channel_id=1, source_target_pairs={{0,2},{1,3},{2,0},{3,1},{4,6},{5,7},{6,4},{7,5},{8,10},{9,11},{10,... | collective-permute-start | bytes 208904 | tf_op jit(solution)/shard_map/ppermute | solution.py:602
  45.2 7.0 %collective-permute-start.23 = (bf16[272,128]{1,0:T(8,128)(2,1)S(1)}, bf16[272,128]{1,0:T(8,128)(2,1)S(1)}, u32[]{:S(2)}, u32[]{:S(2)}) collective-permute-start(bf16[272,128]{1,0:T(8,128)(2,1)S(1)} %get-tuple-element.74), channel_id=1, source_target_pairs={{0,4},{1,5},{2,6},{3,7},{4,0},{5,1},{6,2},{7,3},{8,12},{9,13},{10,... | collective-permute-start | bytes 208904 | tf_op jit(solution)/shard_map/ppermute | solution.py:602
  47.8 6.1 %collective-permute-start.24 = (bf16[272,128]{1,0:T(8,128)(2,1)S(1)}, bf16[272,128]{1,0:T(8,128)(2,1)S(1)}, u32[]{:S(2)}, u32[]{:S(2)}) collective-permute-start(bf16[272,128]{1,0:T(8,128)(2,1)S(1)} %get-tuple-element.73), channel_id=1, source_target_pairs={{0,6},{1,7},{2,4},{3,5},{4,2},{5,3},{6,0},{7,1},{8,14},{9,15},{10,... | collective-permute-start | bytes 208904 | tf_op jit(solution)/shard_map/ppermute | solution.py:602
  54.0 5.7 %collective-permute-start.25 = (bf16[272,128]{1,0:T(8,128)(2,1)S(1)}, bf16[272,128]{1,0:T(8,128)(2,1)S(1)}, u32[]{:S(2)}, u32[]{:S(2)}) collective-permute-start(bf16[272,128]{1,0:T(8,128)(2,1)S(1)} %fusion.2.refs_0_), channel_id=1, source_target_pairs={{0,2},{1,3},{2,0},{3,1},{4,6},{5,7},{6,4},{7,5},{8,10},{9,11},{10,... | collective-permute-start | bytes 208904 | tf_op jit(solution)/shard_map/ppermute | solution.py:602
  54.0 6.8 %collective-permute-start.26 = (bf16[272,128]{1,0:T(8,128)(2,1)S(1)}, bf16[272,128]{1,0:T(8,128)(2,1)S(1)}, u32[]{:S(2)}, u32[]{:S(2)}) collective-permute-start(bf16[272,128]{1,0:T(8,128)(2,1)S(1)} %fusion.2.refs_0_), channel_id=1, source_target_pairs={{0,4},{1,5},{2,6},{3,7},{4,0},{5,1},{6,2},{7,3},{8,12},{9,13},{10,... | collective-permute-start | bytes 208904 | tf_op jit(solution)/shard_map/ppermute | solution.py:602
  56.2 6.7 %collective-permute-start.27 = (bf16[272,128]{1,0:T(8,128)(2,1)S(1)}, bf16[272,128]{1,0:T(8,128)(2,1)S(1)}, u32[]{:S(2)}, u32[]{:S(2)}) collective-permute-start(bf16[272,128]{1,0:T(8,128)(2,1)S(1)} %fusion.2.refs_0_), channel_id=1, source_target_pairs={{0,6},{1,7},{2,4},{3,5},{4,2},{5,3},{6,0},{7,1},{8,14},{9,15},{10,... | collective-permute-start | bytes 208904 | tf_op jit(solution)/shard_map/ppermute | solution.py:602
  58.4 8.1 %collective-permute-start.13 = (bf16[512,128]{1,0:T(8,128)(2,1)S(1)}, bf16[512,128]{1,0:T(8,128)(2,1)S(1)}, u32[]{:S(2)}, u32[]{:S(2)}) collective-permute-start(bf16[512,128]{1,0:T(8,128)(2,1)S(1)} %get-tuple-element.59), channel_id=1, source_target_pairs={{1,0},{2,1},{3,2},{4,3},{5,4},{6,5},{7,6},{9,8},{10,9},{11,10},{12... | collective-permute-start | bytes 393224 | tf_op jit(solution)/shard_map/ppermute | solution.py:608
  62.9 6.6 %collective-permute-start.28 = (bf16[4,272,128]{2,1,0:T(8,128)(2,1)S(1)}, bf16[4,272,128]{2,1,0:T(8,128)(2,1)S(1)}, u32[]{:S(2)}, u32[]{:S(2)}) collective-permute-start(bf16[4,272,128]{2,1,0:T(8,128)(2,1)S(1)} %pad_maximum_fusion.1), channel_id=1, source_target_pairs={{0,1},{1,0},{2,3},{3,2},{4,5},{5,4},{6,7},{7,6},{8,9},{9,8},{10,11... | collective-permute-start | bytes 835592 | tf_op jit(solution)/shard_map/ppermute | solution.py:602

commit v9 on v8

--- a/solution.py
+++ b/solution.py
@@ -150,7 +150,7 @@
         padded[tap * 256 + 64 : (tap + 1) * 256, :] = whole[tap * 192 : (tap + 1) * 192, :]
 
 
-def take_windows(read, dst, out, a, half):
+def take_windows(read, dst, row, left, half):
     for e in range(3):
         for f in range(3):
             block = read(0 if f == 1 else 1, 0 if e == 1 else 1)
@@ -160,13 +160,14 @@
                 block = jnp.concatenate(
                     [jnp.zeros((8, 128), F32), block[: half * 8 - 8]], axis=0
                 )
-            left = ((a * 3 + e) * 3 + f) * 128
-            dst[out * half * 8 : (out + 1) * half * 8, left : left + 128] = block.astype(BF16)
+            at = left + (e * 3 + f) * 128
+            dst[row : row + half * 8, at : at + 128] = block.astype(BF16)
 
 
 def forward_upper_kernel(
     offsets, sorted_ref, w0, w1, w2, w3,
-    slope_ref, hidden_ref, middle_ref, partial_ref, padded_ref, columns, some, whole,
+    slope_ref, windows_ref, middle_ref, top_ref, partial_ref, padded_ref,
+    columns, some, whole, upper,
 ):
     cells = sorted_ref.shape[0] // 2
     put_rows(whole, (w0, w1, w2, w3), offsets)
@@ -174,10 +175,21 @@
     gather_taps(columns, sorted_ref, None, 1, cells - 1)
     linear = jnp.dot(columns[...], padded_ref[...], preferred_element_type=F32)
     hidden = activate(linear)
-    hidden_ref[...] = hidden.reshape(hidden_ref.shape)
+    upper[...] = hidden.reshape(upper.shape)
     count = middle_ref.shape[0] * middle_ref.shape[1]
     middle_ref[...] = hidden[:count].reshape(middle_ref.shape).astype(BF16)
+    top_ref[...] = hidden[count:].astype(BF16)
     slope_ref[...] = activate_slope(linear)
+    half = upper.shape[1]
+    for out in range(cells // 2):
+        for a in range(3):
+            plane = 2 * out - 1 + a
+            if plane > 0:
+
+                def read(column, row):
+                    return upper[plane - 1, :, column, row].reshape(half * 8, 128)
+
+                take_windows(read, windows_ref, out * half * 8, a * 9 * 128, half)
     for a in range(1, 3):
         for e in range(3):
             put_tap(some, 0, ((a - 1) * 3 + e) * 256, sorted_ref.at[a - 1, e])
@@ -193,8 +205,9 @@
         forward_upper_kernel,
         (
             near((some, 128), F32),
-            near((cells - 1, rows // 32, 2, 2, 8, 128), F32),
+            near((cells * rows // 8, 27 * 128), BF16),
             sds((cells - 2, rows, 128), BF16),
+            near((rows, 128), BF16),
             near((rows, 128), F32),
             near((9 * 256, 128), BF16),
         ),
@@ -202,6 +215,7 @@
             pltpu.VMEM((some, 9 * 256), BF16),
             pltpu.VMEM((rows, 6 * 256), BF16),
             pltpu.VMEM((4 * shard, 128), BF16),
+            pltpu.VMEM((cells - 1, rows // 32, 2, 2, 8, 128), F32),
         ],
         sorted_volume, *shards,
         smem=(offsets,),
@@ -210,11 +224,10 @@
 
 
 def forward_lower_kernel(
-    alive, side, halo_ref, hidden_ref, partial_ref, padded_ref,
+    alive, side, halo_ref, top_ref, partial_ref, padded_ref,
     slope_ref, windows_ref, sorted_ref, here_ref, there_ref, wide, columns, some, lowest, planes,
 ):
     rows = partial_ref.shape[0]
-    cells = hidden_ref.shape[0] + 1
     half = rows // 32
     sort_kernel(halo_ref.shape[0], halo_ref, sorted_ref, wide)
     for e in range(3):
@@ -232,28 +245,24 @@
     planes[0] = lowest[0].reshape(rows, 128).astype(BF16)
     planes[1] = lowest[1].reshape(rows, 128).astype(BF16)
     planes[2] = planes[1]
-    planes[3] = hidden_ref[cells - 2].reshape(rows, 128).astype(BF16)
+    planes[3] = top_ref[...]
     here_ref[...] = planes[pl.ds(2 * side[0], 2)]
     there_ref[...] = planes[pl.ds(2 - 2 * side[0], 2)]
-    for out in range(cells // 2):
-        for a in range(3):
-            plane = 2 * out - 1 + a
-            source = lowest.at[plane + 1] if plane < 1 else hidden_ref.at[plane - 1]
-
-            def read(column, row):
-                return source[:, column, row].reshape(half * 8, 128)
-
-            take_windows(read, windows_ref, out, a, half)
-
-
-def forward_lower(halo, hidden, partial, padded, alive, side):
+    for a in range(2):
+
+        def read(column, row):
+            return lowest[a, :, column, row].reshape(half * 8, 128)
+
+        take_windows(read, windows_ref, 0, a * 9 * 128, half)
+
+
+def forward_lower(halo, top, partial, padded, alive, side):
     rows = partial.shape[0]
-    cells = hidden.shape[0] + 1
     return call(
         forward_lower_kernel,
         (
             near((2 * rows, 128), F32),
-            near((cells * rows // 8, 27 * 128), BF16),
+            near((rows // 4, 2 * 9 * 128), BF16),
             near((halo.shape[0], 3, rows, 128), BF16),
             sds((2, rows, 128), BF16),
             sds((2, rows, 128), BF16),
@@ -262,10 +271,10 @@
             pltpu.VMEM((rows // 16, halo.shape[1], 128), F32),
             pltpu.VMEM((rows, 9 * 256), BF16),
             pltpu.VMEM((rows, 3 * 256), BF16),
-            pltpu.VMEM((2, *hidden.shape[1:]), F32),
+            pltpu.VMEM((2, rows // 32, 2, 2, 8, 128), F32),
             pltpu.VMEM((4, rows, 128), BF16),
         ],
-        halo, hidden, partial, padded,
+        halo, top, partial, padded,
         smem=(alive, side),
         micros=1.5,
     )
@@ -280,10 +289,14 @@
 
 
 def forward_second_kernel(
-    offsets, windows_ref, cot_ref, w0, w1, w2, w3, act_ref, delta_ref, whole
+    offsets, upper_ref, lower_ref, cot_ref, w0, w1, w2, w3, act_ref, delta_ref, whole, windows
 ):
     put_rows(whole, (w0, w1, w2, w3), offsets)
-    linear = jnp.dot(windows_ref[...], whole[...], preferred_element_type=F32)
+    low, width = lower_ref.shape
+    windows[:low, :width] = lower_ref[...]
+    windows[:low, width:] = upper_ref[:low, width:]
+    windows[low:, :] = upper_ref[low:, :]
+    linear = jnp.dot(windows[...], whole[...], preferred_element_type=F32)
     outs, _, width = cot_ref.shape
     features = linear.shape[1]
     count = width // features
@@ -304,13 +317,13 @@
     delta_ref[...] = (jnp.concatenate(deltas, axis=0) * slope).astype(BF16)
 
 
-def forward_second(windows, cot, shards, offsets):
+def forward_second(upper, lower, cot, shards, offsets):
     rows, features = shards[0].shape
     return call(
         forward_second_kernel,
-        (sds(cot.shape, BF16), sds((windows.shape[0], features), BF16)),
-        [pltpu.VMEM((4 * rows, features), BF16)],
-        windows, cot, *shards,
+        (sds(cot.shape, BF16), sds((upper.shape[0], features), BF16)),
+        [pltpu.VMEM((4 * rows, features), BF16), pltpu.VMEM(upper.shape, BF16)],
+        upper, lower, cot, *shards,
         smem=(offsets,),
         micros=1.5,
     )
@@ -637,32 +650,34 @@
     shards_first = (weight_first, first_core, first_x, first_far)
 
     sorted_volume = sorted_planes(inputs)
-    slope, hidden, middle, partial, padded = forward_upper(
+    slope, windows, middle, top, partial, padded = forward_upper(
         sorted_volume, shards_first, offsets_first
     )
     middle_x, middle_core = swap(middle, "dp", 2), swap(middle, "dp", 1)
-    second_x, hidden = lax.optimization_barrier((second_x, hidden))
+    second_x, partial = lax.optimization_barrier((second_x, partial))
     second_far = swap(second_x, "dp", 1)
     shards_second = (weight_second, second_core, second_x, second_far)
-    slope_low, windows, sorted_halo, edge, edge_there = forward_lower(
-        halo, hidden, partial, padded, alive, x_side.reshape(1)
+    slope_low, windows_low, sorted_halo, edge, edge_there = forward_lower(
+        halo, top, partial, padded, alive, x_side.reshape(1)
     )
     cot = cotangent.reshape(cotangent.shape[1:])
-    activations, delta_second = forward_second(windows, cot, shards_second, offsets_second)
+    activations, delta_second = forward_second(
+        windows, windows_low, cot, shards_second, offsets_second
+    )
+    delta_second, middle_x = lax.optimization_barrier((delta_second, middle_x))
     edge_x, edge_core = swap(edge_there, "dp", 2), swap(edge, "dp", 1)
     delta_x, delta_core = swap(delta_second, "dp", 2), swap(delta_second, "dp", 1)
     low, last, down, *first = back_second(
         delta_second, shards_second, (slope_low, slope), sorted_volume, sorted_halo,
         offsets_second, slots, order, spaces, size_first,
     )
-    first, down, delta_x, edge_x, delta_core, edge_core, middle_x, middle_core = (
-        lax.optimization_barrier(
-            (first, down, delta_x, edge_x, delta_core, edge_core, middle_x, middle_core)
-        )
+    middle_far = swap(middle_x, "dp", 1)
+    first, down, delta_x, edge_x, delta_core, edge_core, middle_far = lax.optimization_barrier(
+        (first, down, delta_x, edge_x, delta_core, edge_core, middle_far)
     )
     second = second_rows(
         (edge, edge_core, edge_x, swap(edge_x, "dp", 1)),
-        (middle, middle_core, middle_x, swap(middle_x, "dp", 1)),
+        (middle, middle_core, middle_x, middle_far),
         (delta_second, delta_core, delta_x, swap(delta_x, "dp", 1)),
         data, order, spaces, size_second,
     )
@@ -677,17 +692,30 @@
         (d * spaces + s, (d ^ 2) * spaces + (s ^ 1)) for d in range(4) for s in range(spaces)
     ]
     second = pieces(second)
-    got_y = swap(jnp.concatenate([second[1], added(own[1], beside[1])], axis=1), "space", 1)
+    sent_y = jnp.concatenate([second[1], added(own[1], beside[1])], axis=1)
+    got_y = swap(sent_y[1:], "space", 1)
     got_x = swap(added(there[0], far[0]), "dp", 2)
+    sent_own, got_x = lax.optimization_barrier((sent_y[:1], got_x))
+    got_y_own = swap(sent_own, "space", 1)
     got_xy = lax.ppermute(added(there[1], far[1]), ("dp", "space"), both)
-    held = jnp.concatenate(
-        [
-            added(second[0], got_y[:, :size_second]),
-            added(own[0], beside[0], got_x, got_xy, got_y[:, size_second:]),
-        ],
-        axis=1,
-    )
-    mine = added(held[0], *(swap(held[k], "space", 2 * k) for k in range(1, high)))
+
+    def held(places, got):
+        return jnp.concatenate(
+            [
+                wide_sum(second[0][places], got[:, :size_second]),
+                wide_sum(
+                    own[0][places], beside[0][places], got_x[places], got_xy[places],
+                    got[:, size_second:],
+                ),
+            ],
+            axis=1,
+        )
+
+    sent = held(slice(1, high), got_y).astype(BF16)
+    mine = added(
+        held(slice(0, 1), got_y_own)[0],
+        *(swap(sent[k - 1], "space", 2 * k) for k in range(1, high)),
+    )
     chunks = [mine] + [swap(mine, "space", 2 * k) for k in range(1, high)]
     chunks.append(swap(jnp.stack(chunks), "space", 1))
 

time: 71.5 us -> 70 us (0.979)
  waiting for transfers between devices: 22.8 us -> 20.1 us
  starting transfers between devices: 27.9 us -> 30 us
  local copies, waits for them, and re-layouts: 3.75 us -> 2.92 us
    ppermute x26 -> x27, waiting for transfers between devices: 19.3 us -> 17.9 us  [swap(): return lax.ppermute(value, axis, [(i, i ^ bits) for i in range(size)])]
    ppermute x2, waiting for transfers between devices: 3.49 us -> 2.21 us  [shifted(): return lax.ppermute(value, axis, pairs)]
    ppermute x1, starting transfers between devices: 0.45 us -> 1.48 us  [local(): got_xy = lax.ppermute(added(there[1], far[1]), ('dp', 'space'), both)]
    ppermute x26 -> x27, starting transfers between devices: 22.5 us -> 23.5 us  [swap(): return lax.ppermute(value, axis, [(i, i ^ bits) for i in range(size)])]
    unnamed x22, local copies, waits for them, and re-layouts: 3.73 us -> 2.9 us
  transfers between devices with their start and end apart: 29 -> 30, of which waited for: 11 -> 11; matrix products, arithmetic and copies ran while one was open for 0% -> 0% of each run, Pallas kernels for 19% -> 20%
where the time goes in v9:
time: 70 us; the launch traced here: 69.8 us
  starting transfers between devices  30 us (43%)
  waiting for transfers between devices  20.1 us (29%)
  Pallas kernels  15.4 us (22%)
  local copies, waits for them, and re-layouts  2.92 us (4%)
  between operations  1 us (1%)
    ppermute x27, starting transfers between devices, swap(): return lax.ppermute(value, axis, [(i, i ^ bits) for i in range(size)])  23.5 us
    ppermute x27, waiting for transfers between devices, swap(): return lax.ppermute(value, axis, [(i, i ^ bits) for i in range(size)])  17.9 us
    pallas_call x8, Pallas kernels, call(): pl.pallas_call(kernel, out_shape=out_shape, in_specs=specs, out_specs=jax...  14.4 us
    ppermute x2, starting transfers between devices, shifted(): return lax.ppermute(value, axis, pairs)  4.98 us
    unnamed x22, local copies, waits for them, and re-layouts  2.9 us
    ppermute x2, waiting for transfers between devices, shifted(): return lax.ppermute(value, axis, pairs)  2.21 us
    ppermute x1, starting transfers between devices, local(): got_xy = lax.ppermute(added(there[1], far[1]), ('dp', 'space'), both)  1.48 us
  transfers between devices with their start and end apart: 30, of which 11 were waited for; matrix products, arithmetic and copies ran while one was open for 0% of the time, Pallas kernels for 20%

profile of v9, /device:TPU:0, one launch (start us, length us, event | category | flops | bytes accessed | tf_op | source)
XLA Modules:
  0.0 69.8 jit_solution(12533622631135337922)
XLA Ops:
  0.6 3.0 %collective-permute-start.1 = (bf16[432,128]{1,0:T(8,128)(2,1)}, bf16[432,128]{1,0:T(8,128)(2,1)S(1)}, u32[]{:S(2)}, u32[]{:S(2)}) collective-permute-start(bf16[432,128]{1,0:T(8,128)(2,1)} %w0.7), channel_id=1, source_target_pairs={{0,16},{8,24},{16,0},{24,8},{1,17},{9,25},{17,1},{25,9},{2,18},{10... | collective-permute-start | bytes 331784 | tf_op jit(solution)/shard_map/ppermute | solution.py:615
  3.6 0.2 collective-permute-start.4
  3.8 0.4 collective-permute-start.5
  4.1 1.0 %shard_map.86 = bf16[3,32,2048]{2,1,0:T(8,128)(2,1)S(1)} custom-call(bf16[8,32,2048]{2,1,0:T(8,128)(2,1)} %bitcast.27), custom_call_target="tpu_custom_call" | custom-call | bytes 786432 | tf_op jit(solution)/shard_map/pallas_call | solution.py:99
  5.2 3.7 %collective-permute-start.3 = (bf16[3,32,2048]{2,1,0:T(8,128)(2,1)S(1)}, bf16[3,32,2048]{2,1,0:T(8,128)(2,1)S(1)}, u32[]{:S(2)}, u32[]{:S(2)}) collective-permute-start(bf16[3,32,2048]{2,1,0:T(8,128)(2,1)S(1)} %shard_map.86), channel_id=1, source_target_pairs={{0,1},{1,2},{2,3},{3,4},{4,5},{5,6},{6,7},{8,9},{9,10},{10,11},{11... | collective-permute-start | bytes 1179656 | tf_op jit(solution)/shard_map/ppermute | solution.py:621
  8.9 1.2 %copy-done = bf16[1,8,32,2048]{3,2,1,0:T(8,128)(2,1)S(1)} copy-done((bf16[1,8,32,2048]{3,2,1,0:T(8,128)(2,1)S(1)}, bf16[1,8,32,2048]{3,2,1,0:T(8,128)(2,1)}, u32[]{:S(2)}) %copy-start) | copy-done | bytes 1048600
  10.1 0.3 shard_map.84.sorted_ref
  10.5 0.1 collective-permute-start.2
  10.6 1.3 %collective-permute-done.2.w3 = bf16[432,128]{1,0:T(8,128)(2,1)S(1)} collective-permute-done((bf16[432,128]{1,0:T(8,128)(2,1)S(1)}, bf16[432,128]{1,0:T(8,128)(2,1)S(1)}, u32[]{:S(2)}, u32[]{:S(2)}) %collective-permute-start.2) | collective-permute-done | bytes 110624 | tf_op jit(solution)/shard_map/ppermute | solution.py:615
  11.9 2.2 %shard_map.85 = (f32[768,128]{1,0:T(8,128)S(1)}, bf16[128,3456]{1,0:T(8,128)(2,1)S(1)}, bf16[2,256,128]{2,1,0:T(8,128)(2,1)S(1)}, bf16[256,128]{1,0:T(8,128)(2,1...) custom-call(s32[4]{0:T(128)S(1)} %broadcast_multiply_fusion.offsets, ...), custom_call_target="tpu_custom_call" | custom-call | flops 2875000064 | bytes 2015232 | tf_op jit(solution)/shard_map/pallas_call | solution.py:49
  14.1 0.9 %copy-done.7 = bf16[128,3456]{1,0:T(8,128)(2,1)} copy-done((bf16[128,3456]{1,0:T(8,128)(2,1)}, bf16[128,3456]{1,0:T(8,128)(2,1)S(1)}, u32[]{:S(2)}) %copy-start.7) | copy-done | bytes 884760
  15.0 0.7 %copy-done.9 = f32[768,128]{1,0:T(8,128)} copy-done((f32[768,128]{1,0:T(8,128)}, f32[768,128]{1,0:T(8,128)S(1)}, u32[]{:S(2)}) %copy-start.9) | copy-done | bytes 393240
  15.7 0.7 %collective-permute-done.4.w2 = bf16[864,256]{1,0:T(8,128)(2,1)S(1)} collective-permute-done((bf16[864,256]{1,0:T(8,128)(2,1)}, bf16[864,256]{1,0:T(8,128)(2,1)S(1)}, u32[]{:S(2)}, u32[]{:S(2)}) %collective-permute-start.4) | collective-permute-done | bytes 442400 | tf_op jit(solution)/shard_map/ppermute | solution.py:615
  16.5 1.8 %collective-permute-start.7 = (bf16[2,256,128]{2,1,0:T(8,128)(2,1)S(1)}, bf16[2,256,128]{2,1,0:T(8,128)(2,1)S(1)}, u32[]{:S(2)}, u32[]{:S(2)}) collective-permute-start(bf16[2,256,128]{2,1,0:T(8,128)(2,1)S(1)} %get-tuple-element.51.m0), channel_id=1, source_target_pairs={{0,16},{8,24},{16,0},{24,8},{1,17},{9,25},{17,1},{25,9},{2,18},{10... | collective-permute-start | bytes 393224 | tf_op jit(solution)/shard_map/ppermute | solution.py:615
  18.2 0.9 %shard_map.87 = (f32[512,128]{1,0:T(8,128)S(1)}, bf16[64,2304]{1,0:T(8,128)(2,1)S(1)}, bf16[3,3,256,128]{3,2,1,0:T(8,128)(2,1)S(1)}, bf16[2,256,128]{2,1,0:T(8,128)(2,1)S(1)}, bf16[2,256,128]{2,1,0:T(8,128)(2,1)S(1)}) custom-call(f32[1]{0:T(128)} %bitcast.1.alive, s32[1]{0:T(128)} %bitcast.2.side, bf16[3,32,2048]{2,1,0:T(8,128)(2,1)S(1)} %collective-permute-done.3.halo_ref, ...), custom_call_target="tpu_custom_call" | custom-call | flops 1724999936 | bytes 1179648 | tf_op jit(solution)/shard_map/pallas_call | solution.py:49
  19.1 0.3 collective-permute-start.11
  19.4 0.8 %collective-permute-start.9 = (bf16[2,256,128]{2,1,0:T(8,128)(2,1)S(1)}, bf16[2,256,128]{2,1,0:T(8,128)(2,1)S(1)}, u32[]{:S(2)}, u32[]{:S(2)}) collective-permute-start(bf16[2,256,128]{2,1,0:T(8,128)(2,1)S(1)} %get-tuple-element.63), channel_id=1, source_target_pairs={{0,16},{8,24},{16,0},{24,8},{1,17},{9,25},{17,1},{25,9},{2,18},{10... | collective-permute-start | bytes 393224 | tf_op jit(solution)/shard_map/ppermute | solution.py:615
  20.2 1.8 %shard_map.88 = (bf16[2,8,2048]{2,1,0:T(8,128)(2,1)}, bf16[128,256]{1,0:T(8,128)(2,1)S(1)}) custom-call(s32[4]{0:T(128)S(1)} %get-tuple-element.86.offsets, bf16[128,3456]{1,0:T(8,128)(2,1)S(1)} %copy-done.8, bf16[64,2304]{1,0:T(8,128)(2,1)S(1)} %get-tuple-element.47.lower_ref, bf16[2,8,2048]{2,1,0:T(8,128)(2,1)S(1)} %bitcast.33, ...), custom_call_target="tpu_custom_call" | custom-call | flops 1724999936 | bytes 3014656 | tf_op jit(solution)/shard_map/pallas_call | solution.py:49
  22.0 0.5 collective-permute-done.7.m2
  22.5 2.0 %collective-permute-start.8 = (bf16[128,256]{1,0:T(8,128)(2,1)S(1)}, bf16[128,256]{1,0:T(8,128)(2,1)S(1)}, u32[]{:S(2)}, u32[]{:S(2)}) collective-permute-start(bf16[128,256]{1,0:T(8,128)(2,1)S(1)} %get-tuple-element.52.delta_ref.d0), channel_id=1, source_target_pairs={{0,16},{8,24},{16,0},{24,8},{1,17},{9,25},{17,1},{25,9},{2,18},{10... | collective-permute-start | bytes 196616 | tf_op jit(solution)/shard_map/ppermute | solution.py:615
  24.5 0.2 collective-permute-start.12
  24.7 3.0 %shard_map.89 = (bf16[768,128]{1,0:T(8,128)(2,1)S(1)}, f32[256,128]{1,0:T(8,128)S(1)}, bf16[512,128]{1,0:T(8,128)(2,1)S(1)}, bf16[8,56,128]{2,1,0:T(8,128)(2,1)S...) custom-call(s32[4]{0:T(128)S(1)} %get-tuple-element.86.offsets, ...), custom_call_target="tpu_custom_call" | custom-call | flops 4024999936 | bytes 4653056 | tf_op jit(solution)/shard_map/pallas_call | solution.py:49
  27.8 0.3 collective-permute-start.18
  28.1 0.2 collective-permute-start.15
  28.4 0.3 collective-permute-start.14
  28.6 0.2 collective-permute-start.16
  28.9 0.3 collective-permute-start.17
  29.2 1.2 %collective-permute-start.19 = (bf16[4,56,128]{2,1,0:T(8,128)(2,1)S(1)}, bf16[4,56,128]{2,1,0:T(8,128)(2,1)S(1)}, u32[]{:S(2)}, u32[]{:S(2)}) collective-permute-start(bf16[4,56,128]{2,1,0:T(8,128)(2,1)S(1)} %get-tuple-element.81), channel_id=1, source_target_pairs={{0,16},{8,24},{16,0},{24,8},{1,17},{9,25},{17,1},{25,9},{2,18},{10... | collective-permute-start | bytes 172040 | tf_op jit(solution)/shard_map/ppermute | solution.py:615
  30.4 1.5 %collective-permute-start.21 = (bf16[4,56,128]{2,1,0:T(8,128)(2,1)S(1)}, bf16[4,56,128]{2,1,0:T(8,128)(2,1)S(1)}, u32[]{:S(2)}, u32[]{:S(2)}) collective-permute-start(bf16[4,56,128]{2,1,0:T(8,128)(2,1)S(1)} %get-tuple-element.80), channel_id=1, source_target_pairs={{0,17},{1,16},{2,19},{3,18},{4,21},{5,20},{6,23},{7,22},{8,25},{9,... | collective-permute-start | bytes 172040 | tf_op jit(solution)/shard_map/ppermute | solution.py:700
  32.0 1.8 %shard_map.91 = bf16[8,216,128]{2,1,0:T(8,128)(2,1)S(1)} custom-call(s32[1]{0:T(128)} %bitcast.6.data, s32[4,33]{1,0:T(4,128)S(1)} %copy-done.4, s32[8]{0:T(128)S(1)} %fusion.11.order, bf16[2,256,128]{2,1,0:T(8,128)(2,1)S(1)} %get-tuple-element.64.e0, bf16[2,256,128]{2,1,0:T(8,128)(2,1)S(1)} %collective-permute-done.11.e1, ...), custom_call_target="tpu_custom_call" | custom-call | flops 2300000000 | bytes 1310720 | tf_op jit(solution)/shard_map/pallas_call | solution.py:49
  33.9 1.0 %collective-permute-start.20 = (bf16[1,272,128]{2,1,0:T(8,128)(2,1)S(1)}, bf16[1,272,128]{2,1,0:T(8,128)(2,1)S(1)}, u32[]{:S(2)}, u32[]{:S(2)}) collective-permute-start(bf16[1,272,128]{2,1,0:T(8,128)(2,1)S(1)} %pad_maximum_fusion.3), channel_id=1, source_target_pairs={{0,1},{1,0},{2,3},{3,2},{4,5},{5,4},{6,7},{7,6},{8,9},{9,8},{10,11... | collective-permute-start | bytes 208904 | tf_op jit(solution)/shard_map/ppermute | solution.py:615
  34.8 1.2 %collective-permute-start.22 = (bf16[3,272,128]{2,1,0:T(8,128)(2,1)S(1)}, bf16[3,272,128]{2,1,0:T(8,128)(2,1)S(1)}, u32[]{:S(2)}, u32[]{:S(2)}) collective-permute-start(bf16[3,272,128]{2,1,0:T(8,128)(2,1)S(1)} %pad_maximum_fusion.1), channel_id=1, source_target_pairs={{0,1},{1,0},{2,3},{3,2},{4,5},{5,4},{6,7},{7,6},{8,9},{9,8},{10,11... | collective-permute-start | bytes 626696 | tf_op jit(solution)/shard_map/ppermute | solution.py:615
  36.0 3.0 %collective-permute-done.20 = bf16[1,272,128]{2,1,0:T(8,128)(2,1)S(1)} collective-permute-done((bf16[1,272,128]{2,1,0:T(8,128)(2,1)S(1)}, bf16[1,272,128]{2,1,0:T(8,128)(2,1)S(1)}, u32[]{:S(2)}, u32[]{:S(2)}) %collective-permute-start.20) | collective-permute-done | bytes 69664 | tf_op jit(solution)/shard_map/ppermute | solution.py:615
  39.0 3.4 %collective-permute-done.22 = bf16[3,272,128]{2,1,0:T(8,128)(2,1)S(1)} collective-permute-done((bf16[3,272,128]{2,1,0:T(8,128)(2,1)S(1)}, bf16[3,272,128]{2,1,0:T(8,128)(2,1)S(1)}, u32[]{:S(2)}, u32[]{:S(2)}) %collective-permute-start.22) | collective-permute-done | bytes 208928 | tf_op jit(solution)/shard_map/ppermute | solution.py:615
  42.5 2.1 %collective-permute-start.23 = (bf16[272,128]{1,0:T(8,128)(2,1)S(1)}, bf16[272,128]{1,0:T(8,128)(2,1)S(1)}, u32[]{:S(2)}, u32[]{:S(2)}) collective-permute-start(bf16[272,128]{1,0:T(8,128)(2,1)S(1)} %get-tuple-element.82), channel_id=1, source_target_pairs={{0,2},{1,3},{2,0},{3,1},{4,6},{5,7},{6,4},{7,5},{8,10},{9,11},{10,... | collective-permute-start | bytes 208904 | tf_op jit(solution)/shard_map/ppermute | solution.py:615
  44.6 2.6 %collective-permute-start.24 = (bf16[272,128]{1,0:T(8,128)(2,1)S(1)}, bf16[272,128]{1,0:T(8,128)(2,1)S(1)}, u32[]{:S(2)}, u32[]{:S(2)}) collective-permute-start(bf16[272,128]{1,0:T(8,128)(2,1)S(1)} %get-tuple-element.84), channel_id=1, source_target_pairs={{0,4},{1,5},{2,6},{3,7},{4,0},{5,1},{6,2},{7,3},{8,12},{9,13},{10,... | collective-permute-start | bytes 208904 | tf_op jit(solution)/shard_map/ppermute | solution.py:615
  47.2 4.2 %collective-permute-done.24 = bf16[272,128]{1,0:T(8,128)(2,1)S(1)} collective-permute-done((bf16[272,128]{1,0:T(8,128)(2,1)S(1)}, bf16[272,128]{1,0:T(8,128)(2,1)S(1)}, u32[]{:S(2)}, u32[]{:S(2)}) %collective-permute-start.24) | collective-permute-done | bytes 69664 | tf_op jit(solution)/shard_map/ppermute | solution.py:615
  51.4 1.9 %collective-permute-done.25 = bf16[272,128]{1,0:T(8,128)(2,1)S(1)} collective-permute-done((bf16[272,128]{1,0:T(8,128)(2,1)S(1)}, bf16[272,128]{1,0:T(8,128)(2,1)S(1)}, u32[]{:S(2)}, u32[]{:S(2)}) %collective-permute-start.25) | collective-permute-done | bytes 69664 | tf_op jit(solution)/shard_map/ppermute | solution.py:615
  53.4 1.8 %collective-permute-start.27 = (bf16[272,128]{1,0:T(8,128)(2,1)S(1)}, bf16[272,128]{1,0:T(8,128)(2,1)S(1)}, u32[]{:S(2)}, u32[]{:S(2)}) collective-permute-start(bf16[272,128]{1,0:T(8,128)(2,1)S(1)} %fusion.3.refs_0_), channel_id=1, source_target_pairs={{0,4},{1,5},{2,6},{3,7},{4,0},{5,1},{6,2},{7,3},{8,12},{9,13},{10,... | collective-permute-start | bytes 208904 | tf_op jit(solution)/shard_map/ppermute | solution.py:615
  55.2 2.5 %collective-permute-start.28 = (bf16[272,128]{1,0:T(8,128)(2,1)S(1)}, bf16[272,128]{1,0:T(8,128)(2,1)S(1)}, u32[]{:S(2)}, u32[]{:S(2)}) collective-permute-start(bf16[272,128]{1,0:T(8,128)(2,1)S(1)} %fusion.3.refs_0_), channel_id=1, source_target_pairs={{0,6},{1,7},{2,4},{3,5},{4,2},{5,3},{6,0},{7,1},{8,14},{9,15},{10,... | collective-permute-start | bytes 208904 | tf_op jit(solution)/shard_map/ppermute | solution.py:615
  57.8 1.3 %collective-permute-start.13 = (bf16[512,128]{1,0:T(8,128)(2,1)S(1)}, bf16[512,128]{1,0:T(8,128)(2,1)S(1)}, u32[]{:S(2)}, u32[]{:S(2)}) collective-permute-start(bf16[512,128]{1,0:T(8,128)(2,1)S(1)} %get-tuple-element.66), channel_id=1, source_target_pairs={{1,0},{2,1},{3,2},{4,3},{5,4},{6,5},{7,6},{9,8},{10,9},{11,10},{12... | collective-permute-start | bytes 393224 | tf_op jit(solution)/shard_map/ppermute | solution.py:621
  59.1 0.1 collective-permute-done.27.refs_2_
  59.2 2.2 %collective-permute-done.28.refs_3_ = bf16[272,128]{1,0:T(8,128)(2,1)S(1)} collective-permute-done((bf16[272,128]{1,0:T(8,128)(2,1)S(1)}, bf16[272,128]{1,0:T(8,128)(2,1)S(1)}, u32[]{:S(2)}, u32[]{:S(2)}) %collective-permute-start.28) | collective-permute-done | bytes 69664 | tf_op jit(solution)/shard_map/ppermute | solution.py:615
  61.5 1.0 %collective-permute-start.29 = (bf16[4,272,128]{2,1,0:T(8,128)(2,1)S(1)}, bf16[4,272,128]{2,1,0:T(8,128)(2,1)S(1)}, u32[]{:S(2)}, u32[]{:S(2)}) collective-permute-start(bf16[4,272,128]{2,1,0:T(8,128)(2,1)S(1)} %pad_maximum_fusion), channel_id=1, source_target_pairs={{0,1},{1,0},{2,3},{3,2},{4,5},{5,4},{6,7},{7,6},{8,9},{9,8},{10,11... | collective-permute-start | bytes 835592 | tf_op jit(solution)/shard_map/ppermute | solution.py:615
  62.5 2.2 %collective-permute-done.13.upper_ref = bf16[512,128]{1,0:T(8,128)(2,1)S(1)} collective-permute-done((bf16[512,128]{1,0:T(8,128)(2,1)S(1)}, bf16[512,128]{1,0:T(8,128)(2,1)S(1)}, u32[]{:S(2)}, u32[]{:S(2)}) %collective-permute-start.13) | collective-permute-done | bytes 131104 | tf_op jit(solution)/shard_map/ppermute | solution.py:621
  64.7 2.8 %shard_map.90 = bf16[8,32,2048]{2,1,0:T(8,128)(2,1)} custom-call(s32[4]{0:T(128)S(1)} %broadcast_multiply_fusion.offsets, bf16[768,128]{1,0:T(8,128)(2,1)S(1)} %get-tuple-element.56.low_ref, f32[256,128]{1,0:T(8,128)S(1)} %get-tuple-element.57.last_ref, f32[768,128]{1,0:T(8,128)S(1)} %copy-done.10, bf16[512,128]{1,0:T(8,128)(2,1)S(1)} %collective-permute-done.13.upper_ref, ...), custom_call_target="tpu_custom_call" | custom-call | flops 3449999872 | bytes 1294336 | tf_op jit(solution)/shard_map/pallas_call | solution.py:49
  67.5 0.6 collective-permute-done.29.refs_4_
  68.1 1.7 %shard_map.92 = (f32[432,128]{1,0:T(8,128)}, f32[864,256]{1,0:T(8,128)}) custom-call(s32[8]{0:T(128)S(1)} %fusion.11.order, bf16[272,128]{1,0:T(8,128)(2,1)S(1)} %fusion.3.refs_0_, bf16[272,128]{1,0:T(8,128)(2,1)S(1)} %collective-permute-done.26.refs_1_, bf16[272,128]{1,0:T(8,128)(2,1)S(1)} %collective-permute-done.27.refs_2_, ...), custom_call_target="tpu_custom_call" | custom-call | flops 1150000000 | bytes 557056 | tf_op jit(solution)/shard_map/pallas_call | solution.py:49
  (58 shorter events, 0.5 us)
Async XLA Ops:
  0.6 9.8 %collective-permute-start.1 = (bf16[432,128]{1,0:T(8,128)(2,1)}, bf16[432,128]{1,0:T(8,128)(2,1)S(1)}, u32[]{:S(2)}, u32[]{:S(2)}) collective-permute-start(bf16[432,128]{1,0:T(8,128)(2,1)} %w0.7), channel_id=1, source_target_pairs={{0,16},{8,24},{16,0},{24,8},{1,17},{9,25},{17,1},{25,9},{2,18},{10... | collective-permute-start | bytes 331784 | tf_op jit(solution)/shard_map/ppermute | solution.py:615
  3.6 6.9 %collective-permute-start = (bf16[432,128]{1,0:T(8,128)(2,1)}, bf16[432,128]{1,0:T(8,128)(2,1)S(1)}, u32[]{:S(2)}, u32[]{:S(2)}) collective-permute-start(bf16[432,128]{1,0:T(8,128)(2,1)} %w0.7), channel_id=1, source_target_pairs={{0,8},{8,0},{16,24},{24,16},{1,9},{9,1},{17,25},{25,17},{2,10},{10... | collective-permute-start | bytes 331784 | tf_op jit(solution)/shard_map/ppermute | solution.py:615
  3.6 12.8 %collective-permute-start.4 = (bf16[864,256]{1,0:T(8,128)(2,1)}, bf16[864,256]{1,0:T(8,128)(2,1)S(1)}, u32[]{:S(2)}, u32[]{:S(2)}) collective-permute-start(bf16[864,256]{1,0:T(8,128)(2,1)} %w0.6), channel_id=1, source_target_pairs={{0,16},{8,24},{16,0},{24,8},{1,17},{9,25},{17,1},{25,9},{2,18},{10... | collective-permute-start | bytes 1327112 | tf_op jit(solution)/shard_map/ppermute | solution.py:615
  3.8 16.4 %collective-permute-start.5 = (bf16[864,256]{1,0:T(8,128)(2,1)}, bf16[864,256]{1,0:T(8,128)(2,1)S(1)}, u32[]{:S(2)}, u32[]{:S(2)}) collective-permute-start(bf16[864,256]{1,0:T(8,128)(2,1)} %w0.6), channel_id=1, source_target_pairs={{0,8},{8,0},{16,24},{24,16},{1,9},{9,1},{17,25},{25,17},{2,10},{10... | collective-permute-start | bytes 1327112 | tf_op jit(solution)/shard_map/ppermute | solution.py:615
  5.2 13.1 %collective-permute-start.3 = (bf16[3,32,2048]{2,1,0:T(8,128)(2,1)S(1)}, bf16[3,32,2048]{2,1,0:T(8,128)(2,1)S(1)}, u32[]{:S(2)}, u32[]{:S(2)}) collective-permute-start(bf16[3,32,2048]{2,1,0:T(8,128)(2,1)S(1)} %shard_map.86), channel_id=1, source_target_pairs={{0,1},{1,2},{2,3},{3,4},{4,5},{5,6},{6,7},{8,9},{9,10},{10,11},{11... | collective-permute-start | bytes 1179656 | tf_op jit(solution)/shard_map/ppermute | solution.py:621
  8.9 1.2 %copy-start = (bf16[1,8,32,2048]{3,2,1,0:T(8,128)(2,1)S(1)}, bf16[1,8,32,2048]{3,2,1,0:T(8,128)(2,1)}, u32[]{:S(2)}) copy-start(bf16[1,8,32,2048]{3,2,1,0:T(8,128)(2,1)} %param.5) | copy-start | bytes 3145732
  10.1 1.8 %copy-start.2 = (bf16[432,128]{1,0:T(8,128)(2,1)S(1)}, bf16[432,128]{1,0:T(8,128)(2,1)}, u32[]{:S(2)}) copy-start(bf16[432,128]{1,0:T(8,128)(2,1)} %w0.7) | copy-start | bytes 331780
  10.5 3.6 %copy-start.5 = (bf16[8,3,256,128]{3,2,1,0:T(8,128)(2,1)}, bf16[8,3,256,128]{3,2,1,0:T(8,128)(2,1)S(1)}, u32[]{:S(2)}) copy-start(bf16[8,3,256,128]{3,2,1,0:T(8,128)(2,1)S(1)} %shard_map.84.sorted_ref) | copy-start | bytes 4718596
  10.5 1.4 %collective-permute-start.2 = (bf16[432,128]{1,0:T(8,128)(2,1)S(1)}, bf16[432,128]{1,0:T(8,128)(2,1)S(1)}, u32[]{:S(2)}, u32[]{:S(2)}) collective-permute-start(bf16[432,128]{1,0:T(8,128)(2,1)S(1)} %collective-permute-done.1.w2), channel_id=1, source_target_pairs={{0,8},{8,0},{16,24},{24,16},{1,9},{9,1},{17,25},{25,17},{2,10},{10... | collective-permute-start | bytes 331784 | tf_op jit(solution)/shard_map/ppermute | solution.py:615
  14.0 0.9 %copy-start.7 = (bf16[128,3456]{1,0:T(8,128)(2,1)}, bf16[128,3456]{1,0:T(8,128)(2,1)S(1)}, u32[]{:S(2)}) copy-start(bf16[128,3456]{1,0:T(8,128)(2,1)S(1)} %get-tuple-element.42.upper_ref) | copy-start | bytes 2654212
  15.0 0.7 %copy-start.9 = (f32[768,128]{1,0:T(8,128)}, f32[768,128]{1,0:T(8,128)S(1)}, u32[]{:S(2)}) copy-start(f32[768,128]{1,0:T(8,128)S(1)} %get-tuple-element.54.slope_ref) | copy-start | bytes 1179652
  16.4 3.7 %collective-permute-start.6 = (bf16[864,256]{1,0:T(8,128)(2,1)S(1)}, bf16[864,256]{1,0:T(8,128)(2,1)S(1)}, u32[]{:S(2)}, u32[]{:S(2)}) collective-permute-start(bf16[864,256]{1,0:T(8,128)(2,1)S(1)} %collective-permute-done.4.w2), channel_id=1, source_target_pairs={{0,8},{8,0},{16,24},{24,16},{1,9},{9,1},{17,25},{25,17},{2,10},{10... | collective-permute-start | bytes 1327112 | tf_op jit(solution)/shard_map/ppermute | solution.py:615
  16.5 6.1 %collective-permute-start.7 = (bf16[2,256,128]{2,1,0:T(8,128)(2,1)S(1)}, bf16[2,256,128]{2,1,0:T(8,128)(2,1)S(1)}, u32[]{:S(2)}, u32[]{:S(2)}) collective-permute-start(bf16[2,256,128]{2,1,0:T(8,128)(2,1)S(1)} %get-tuple-element.51.m0), channel_id=1, source_target_pairs={{0,16},{8,24},{16,0},{24,8},{1,17},{9,25},{17,1},{25,9},{2,18},{10... | collective-permute-start | bytes 393224 | tf_op jit(solution)/shard_map/ppermute | solution.py:615
  18.2 1.9 %copy-start.1 = (bf16[864,256]{1,0:T(8,128)(2,1)S(1)}, bf16[864,256]{1,0:T(8,128)(2,1)}, u32[]{:S(2)}) copy-start(bf16[864,256]{1,0:T(8,128)(2,1)} %w0.6) | copy-start | bytes 1327108
  18.2 1.9 %copy-start.3 = (bf16[1,2,8,2048]{3,2,1,0:T(8,128)(2,1)S(1)}, bf16[1,2,8,2048]{3,2,1,0:T(8,128)(2,1)}, u32[]{:S(2)}) copy-start(bf16[1,2,8,2048]{3,2,1,0:T(8,128)(2,1)} %param.8) | copy-start | bytes 196612
  18.2 2.0 %copy-start.8 = (bf16[128,3456]{1,0:T(8,128)(2,1)S(1)}, bf16[128,3456]{1,0:T(8,128)(2,1)}, u32[]{:S(2)}) copy-start(bf16[128,3456]{1,0:T(8,128)(2,1)} %copy-done.7) | copy-start | bytes 2654212
  19.1 8.6 %collective-permute-start.11 = (bf16[2,256,128]{2,1,0:T(8,128)(2,1)S(1)}, bf16[2,256,128]{2,1,0:T(8,128)(2,1)S(1)}, u32[]{:S(2)}, u32[]{:S(2)}) collective-permute-start(bf16[2,256,128]{2,1,0:T(8,128)(2,1)S(1)} %get-tuple-element.64.e0), channel_id=1, source_target_pairs={{0,8},{8,0},{16,24},{24,16},{1,9},{9,1},{17,25},{25,17},{2,10},{10... | collective-permute-start | bytes 393224 | tf_op jit(solution)/shard_map/ppermute | solution.py:615
  19.4 8.4 %collective-permute-start.9 = (bf16[2,256,128]{2,1,0:T(8,128)(2,1)S(1)}, bf16[2,256,128]{2,1,0:T(8,128)(2,1)S(1)}, u32[]{:S(2)}, u32[]{:S(2)}) collective-permute-start(bf16[2,256,128]{2,1,0:T(8,128)(2,1)S(1)} %get-tuple-element.63), channel_id=1, source_target_pairs={{0,16},{8,24},{16,0},{24,8},{1,17},{9,25},{17,1},{25,9},{2,18},{10... | collective-permute-start | bytes 393224 | tf_op jit(solution)/shard_map/ppermute | solution.py:615
  20.2 4.6 %copy-start.6 = (bf16[8,3,256,128]{3,2,1,0:T(8,128)(2,1)S(1)}, bf16[8,3,256,128]{3,2,1,0:T(8,128)(2,1)}, u32[]{:S(2)}) copy-start(bf16[8,3,256,128]{3,2,1,0:T(8,128)(2,1)} %copy-done.5) | copy-start | bytes 4718596
  20.2 4.6 %copy-start.10 = (f32[768,128]{1,0:T(8,128)S(1)}, f32[768,128]{1,0:T(8,128)}, u32[]{:S(2)}) copy-start(f32[768,128]{1,0:T(8,128)} %copy-done.9) | copy-start | bytes 1179652
  22.5 5.2 %collective-permute-start.10 = (bf16[128,256]{1,0:T(8,128)(2,1)S(1)}, bf16[128,256]{1,0:T(8,128)(2,1)S(1)}, u32[]{:S(2)}, u32[]{:S(2)}) collective-permute-start(bf16[128,256]{1,0:T(8,128)(2,1)S(1)} %get-tuple-element.52.delta_ref.d0), channel_id=1, source_target_pairs={{0,8},{8,0},{16,24},{24,16},{1,9},{9,1},{17,25},{25,17},{2,10},{10... | collective-permute-start | bytes 196616 | tf_op jit(solution)/shard_map/ppermute | solution.py:615
  22.5 5.2 %collective-permute-start.8 = (bf16[128,256]{1,0:T(8,128)(2,1)S(1)}, bf16[128,256]{1,0:T(8,128)(2,1)S(1)}, u32[]{:S(2)}, u32[]{:S(2)}) collective-permute-start(bf16[128,256]{1,0:T(8,128)(2,1)S(1)} %get-tuple-element.52.delta_ref.d0), channel_id=1, source_target_pairs={{0,16},{8,24},{16,0},{24,8},{1,17},{9,25},{17,1},{25,9},{2,18},{10... | collective-permute-start | bytes 196616 | tf_op jit(solution)/shard_map/ppermute | solution.py:615
  24.5 3.3 %collective-permute-start.12 = (bf16[2,256,128]{2,1,0:T(8,128)(2,1)S(1)}, bf16[2,256,128]{2,1,0:T(8,128)(2,1)S(1)}, u32[]{:S(2)}, u32[]{:S(2)}) collective-permute-start(bf16[2,256,128]{2,1,0:T(8,128)(2,1)S(1)} %collective-permute-done.7.m2), channel_id=1, source_target_pairs={{0,8},{8,0},{16,24},{24,16},{1,9},{9,1},{17,25},{25,17},{2,10},{10... | collective-permute-start | bytes 393224 | tf_op jit(solution)/shard_map/ppermute | solution.py:615
  24.7 7.2 %copy-start.4 = (s32[4,33]{1,0:T(4,128)S(1)}, s32[4,33]{1,0:T(4,128)}, u32[]{:S(2)}) copy-start(s32[4,33]{1,0:T(4,128)} %constant.48.clone.table) | copy-start | bytes 1588
  27.8 1.4 %collective-permute-start.18 = (bf16[8,56,128]{2,1,0:T(8,128)(2,1)S(1)}, bf16[8,56,128]{2,1,0:T(8,128)(2,1)S(1)}, u32[]{:S(2)}, u32[]{:S(2)}) collective-permute-start(bf16[8,56,128]{2,1,0:T(8,128)(2,1)S(1)} %get-tuple-element.75), channel_id=1, source_target_pairs={{0,8},{8,0},{16,24},{24,16},{1,9},{9,1},{17,25},{25,17},{2,10},{10... | collective-permute-start | bytes 344072 | tf_op jit(solution)/shard_map/ppermute | solution.py:615
  28.1 3.8 %collective-permute-start.15 = (bf16[2,256,128]{2,1,0:T(8,128)(2,1)S(1)}, bf16[2,256,128]{2,1,0:T(8,128)(2,1)S(1)}, u32[]{:S(2)}, u32[]{:S(2)}) collective-permute-start(bf16[2,256,128]{2,1,0:T(8,128)(2,1)S(1)} %get-tuple-element.51.m0), channel_id=1, source_target_pairs={{0,8},{8,0},{16,24},{24,16},{1,9},{9,1},{17,25},{25,17},{2,10},{10... | collective-permute-start | bytes 393224 | tf_op jit(solution)/shard_map/ppermute | solution.py:615
  28.4 3.6 %collective-permute-start.14 = (bf16[2,256,128]{2,1,0:T(8,128)(2,1)S(1)}, bf16[2,256,128]{2,1,0:T(8,128)(2,1)S(1)}, u32[]{:S(2)}, u32[]{:S(2)}) collective-permute-start(bf16[2,256,128]{2,1,0:T(8,128)(2,1)S(1)} %collective-permute-done.9.e2), channel_id=1, source_target_pairs={{0,8},{8,0},{16,24},{24,16},{1,9},{9,1},{17,25},{25,17},{2,10},{10... | collective-permute-start | bytes 393224 | tf_op jit(solution)/shard_map/ppermute | solution.py:615
  28.6 3.3 %collective-permute-start.16 = (bf16[128,256]{1,0:T(8,128)(2,1)S(1)}, bf16[128,256]{1,0:T(8,128)(2,1)S(1)}, u32[]{:S(2)}, u32[]{:S(2)}) collective-permute-start(bf16[128,256]{1,0:T(8,128)(2,1)S(1)} %collective-permute-done.8.d2), channel_id=1, source_target_pairs={{0,8},{8,0},{16,24},{24,16},{1,9},{9,1},{17,25},{25,17},{2,10},{10... | collective-permute-start | bytes 196616 | tf_op jit(solution)/shard_map/ppermute | solution.py:615
  28.9 1.6 %collective-permute-start.17 = (bf16[8,56,128]{2,1,0:T(8,128)(2,1)S(1)}, bf16[8,56,128]{2,1,0:T(8,128)(2,1)S(1)}, u32[]{:S(2)}, u32[]{:S(2)}) collective-permute-start(bf16[8,56,128]{2,1,0:T(8,128)(2,1)S(1)} %get-tuple-element.73), channel_id=1, source_target_pairs={{0,8},{8,0},{16,24},{24,16},{1,9},{9,1},{17,25},{25,17},{2,10},{10... | collective-permute-start | bytes 344072 | tf_op jit(solution)/shard_map/ppermute | solution.py:615
  29.2 4.6 %collective-permute-start.19 = (bf16[4,56,128]{2,1,0:T(8,128)(2,1)S(1)}, bf16[4,56,128]{2,1,0:T(8,128)(2,1)S(1)}, u32[]{:S(2)}, u32[]{:S(2)}) collective-permute-start(bf16[4,56,128]{2,1,0:T(8,128)(2,1)S(1)} %get-tuple-element.81), channel_id=1, source_target_pairs={{0,16},{8,24},{16,0},{24,8},{1,17},{9,25},{17,1},{25,9},{2,18},{10... | collective-permute-start | bytes 172040 | tf_op jit(solution)/shard_map/ppermute | solution.py:615
  30.4 12.0 %collective-permute-start.21 = (bf16[4,56,128]{2,1,0:T(8,128)(2,1)S(1)}, bf16[4,56,128]{2,1,0:T(8,128)(2,1)S(1)}, u32[]{:S(2)}, u32[]{:S(2)}) collective-permute-start(bf16[4,56,128]{2,1,0:T(8,128)(2,1)S(1)} %get-tuple-element.80), channel_id=1, source_target_pairs={{0,17},{1,16},{2,19},{3,18},{4,21},{5,20},{6,23},{7,22},{8,25},{9,... | collective-permute-start | bytes 172040 | tf_op jit(solution)/shard_map/ppermute | solution.py:700
  33.9 5.1 %collective-permute-start.20 = (bf16[1,272,128]{2,1,0:T(8,128)(2,1)S(1)}, bf16[1,272,128]{2,1,0:T(8,128)(2,1)S(1)}, u32[]{:S(2)}, u32[]{:S(2)}) collective-permute-start(bf16[1,272,128]{2,1,0:T(8,128)(2,1)S(1)} %pad_maximum_fusion.3), channel_id=1, source_target_pairs={{0,1},{1,0},{2,3},{3,2},{4,5},{5,4},{6,7},{7,6},{8,9},{9,8},{10,11... | collective-permute-start | bytes 208904 | tf_op jit(solution)/shard_map/ppermute | solution.py:615
  34.8 7.5 %collective-permute-start.22 = (bf16[3,272,128]{2,1,0:T(8,128)(2,1)S(1)}, bf16[3,272,128]{2,1,0:T(8,128)(2,1)S(1)}, u32[]{:S(2)}, u32[]{:S(2)}) collective-permute-start(bf16[3,272,128]{2,1,0:T(8,128)(2,1)S(1)} %pad_maximum_fusion.1), channel_id=1, source_target_pairs={{0,1},{1,0},{2,3},{3,2},{4,5},{5,4},{6,7},{7,6},{8,9},{9,8},{10,11... | collective-permute-start | bytes 626696 | tf_op jit(solution)/shard_map/ppermute | solution.py:615
  42.5 4.7 %collective-permute-start.23 = (bf16[272,128]{1,0:T(8,128)(2,1)S(1)}, bf16[272,128]{1,0:T(8,128)(2,1)S(1)}, u32[]{:S(2)}, u32[]{:S(2)}) collective-permute-start(bf16[272,128]{1,0:T(8,128)(2,1)S(1)} %get-tuple-element.82), channel_id=1, source_target_pairs={{0,2},{1,3},{2,0},{3,1},{4,6},{5,7},{6,4},{7,5},{8,10},{9,11},{10,... | collective-permute-start | bytes 208904 | tf_op jit(solution)/shard_map/ppermute | solution.py:615
  44.6 6.8 %collective-permute-start.24 = (bf16[272,128]{1,0:T(8,128)(2,1)S(1)}, bf16[272,128]{1,0:T(8,128)(2,1)S(1)}, u32[]{:S(2)}, u32[]{:S(2)}) collective-permute-start(bf16[272,128]{1,0:T(8,128)(2,1)S(1)} %get-tuple-element.84), channel_id=1, source_target_pairs={{0,4},{1,5},{2,6},{3,7},{4,0},{5,1},{6,2},{7,3},{8,12},{9,13},{10,... | collective-permute-start | bytes 208904 | tf_op jit(solution)/shard_map/ppermute | solution.py:615
  47.2 6.1 %collective-permute-start.25 = (bf16[272,128]{1,0:T(8,128)(2,1)S(1)}, bf16[272,128]{1,0:T(8,128)(2,1)S(1)}, u32[]{:S(2)}, u32[]{:S(2)}) collective-permute-start(bf16[272,128]{1,0:T(8,128)(2,1)S(1)} %get-tuple-element.83), channel_id=1, source_target_pairs={{0,6},{1,7},{2,4},{3,5},{4,2},{5,3},{6,0},{7,1},{8,14},{9,15},{10,... | collective-permute-start | bytes 208904 | tf_op jit(solution)/shard_map/ppermute | solution.py:615
  53.3 5.7 %collective-permute-start.26 = (bf16[272,128]{1,0:T(8,128)(2,1)S(1)}, bf16[272,128]{1,0:T(8,128)(2,1)S(1)}, u32[]{:S(2)}, u32[]{:S(2)}) collective-permute-start(bf16[272,128]{1,0:T(8,128)(2,1)S(1)} %fusion.3.refs_0_), channel_id=1, source_target_pairs={{0,2},{1,3},{2,0},{3,1},{4,6},{5,7},{6,4},{7,5},{8,10},{9,11},{10,... | collective-permute-start | bytes 208904 | tf_op jit(solution)/shard_map/ppermute | solution.py:615
  53.4 5.8 %collective-permute-start.27 = (bf16[272,128]{1,0:T(8,128)(2,1)S(1)}, bf16[272,128]{1,0:T(8,128)(2,1)S(1)}, u32[]{:S(2)}, u32[]{:S(2)}) collective-permute-start(bf16[272,128]{1,0:T(8,128)(2,1)S(1)} %fusion.3.refs_0_), channel_id=1, source_target_pairs={{0,4},{1,5},{2,6},{3,7},{4,0},{5,1},{6,2},{7,3},{8,12},{9,13},{10,... | collective-permute-start | bytes 208904 | tf_op jit(solution)/shard_map/ppermute | solution.py:615
  55.2 6.2 %collective-permute-start.28 = (bf16[272,128]{1,0:T(8,128)(2,1)S(1)}, bf16[272,128]{1,0:T(8,128)(2,1)S(1)}, u32[]{:S(2)}, u32[]{:S(2)}) collective-permute-start(bf16[272,128]{1,0:T(8,128)(2,1)S(1)} %fusion.3.refs_0_), channel_id=1, source_target_pairs={{0,6},{1,7},{2,4},{3,5},{4,2},{5,3},{6,0},{7,1},{8,14},{9,15},{10,... | collective-permute-start | bytes 208904 | tf_op jit(solution)/shard_map/ppermute | solution.py:615
  57.8 6.9 %collective-permute-start.13 = (bf16[512,128]{1,0:T(8,128)(2,1)S(1)}, bf16[512,128]{1,0:T(8,128)(2,1)S(1)}, u32[]{:S(2)}, u32[]{:S(2)}) collective-permute-start(bf16[512,128]{1,0:T(8,128)(2,1)S(1)} %get-tuple-element.66), channel_id=1, source_target_pairs={{1,0},{2,1},{3,2},{4,3},{5,4},{6,5},{7,6},{9,8},{10,9},{11,10},{12... | collective-permute-start | bytes 393224 | tf_op jit(solution)/shard_map/ppermute | solution.py:621
  61.5 6.6 %collective-permute-start.29 = (bf16[4,272,128]{2,1,0:T(8,128)(2,1)S(1)}, bf16[4,272,128]{2,1,0:T(8,128)(2,1)S(1)}, u32[]{:S(2)}, u32[]{:S(2)}) collective-permute-start(bf16[4,272,128]{2,1,0:T(8,128)(2,1)S(1)} %pad_maximum_fusion), channel_id=1, source_target_pairs={{0,1},{1,0},{2,3},{3,2},{4,5},{5,4},{6,7},{7,6},{8,9},{9,8},{10,11... | collective-permute-start | bytes 835592 | tf_op jit(solution)/shard_map/ppermute | solution.py:615

commit v10 on v9

--- a/solution.py
+++ b/solution.py
@@ -695,8 +695,7 @@
     sent_y = jnp.concatenate([second[1], added(own[1], beside[1])], axis=1)
     got_y = swap(sent_y[1:], "space", 1)
     got_x = swap(added(there[0], far[0]), "dp", 2)
-    sent_own, got_x = lax.optimization_barrier((sent_y[:1], got_x))
-    got_y_own = swap(sent_own, "space", 1)
+    got_y_own = swap(sent_y[:1], "space", 1)
     got_xy = lax.ppermute(added(there[1], far[1]), ("dp", "space"), both)
 
     def held(places, got):
@@ -712,10 +711,10 @@
         )
 
     sent = held(slice(1, high), got_y).astype(BF16)
-    mine = added(
-        held(slice(0, 1), got_y_own)[0],
-        *(swap(sent[k - 1], "space", 2 * k) for k in range(1, high)),
-    )
+    *received, got_y_own = lax.optimization_barrier(
+        (*(swap(sent[k - 1], "space", 2 * k) for k in range(1, high)), got_y_own)
+    )
+    mine = added(held(slice(0, 1), got_y_own)[0], *received)
     chunks = [mine] + [swap(mine, "space", 2 * k) for k in range(1, high)]
     chunks.append(swap(jnp.stack(chunks), "space", 1))
 

time: 70 us -> 68.8 us (0.983)
    ppermute x27, waiting for transfers between devices: 17.9 us -> 16.8 us  [swap(): return lax.ppermute(value, axis, [(i, i ^ bits) for i in range(size)])]
  transfers between devices with their start and end apart: 30 -> 30, of which waited for: 11 -> 13; matrix products, arithmetic and copies ran while one was open for 0% -> 0% of each run, Pallas kernels for 20% -> 20%
where the time goes in v10:
time: 68.8 us; the launch traced here: 68.6 us
  starting transfers between devices  29.4 us (43%)
  waiting for transfers between devices  19.6 us (28%)
  Pallas kernels  15.4 us (22%)
  local copies, waits for them, and re-layouts  2.92 us (4%)
  between operations  0.97 us (1%)
    ppermute x27, starting transfers between devices, swap(): return lax.ppermute(value, axis, [(i, i ^ bits) for i in range(size)])  23.1 us
    ppermute x27, waiting for transfers between devices, swap(): return lax.ppermute(value, axis, [(i, i ^ bits) for i in range(size)])  16.8 us
    pallas_call x8, Pallas kernels, call(): pl.pallas_call(kernel, out_shape=out_shape, in_specs=specs, out_specs=jax...  14.4 us
    ppermute x2, starting transfers between devices, shifted(): return lax.ppermute(value, axis, pairs)  4.98 us
    unnamed x22, local copies, waits for them, and re-layouts  2.9 us
    ppermute x2, waiting for transfers between devices, shifted(): return lax.ppermute(value, axis, pairs)  2.78 us
  transfers between devices with their start and end apart: 30, of which 13 were waited for; matrix products, arithmetic and copies ran while one was open for 0% of the time, Pallas kernels for 20%

profile of v10, /device:TPU:0, one launch (start us, length us, event | category | flops | bytes accessed | tf_op | source)
XLA Modules:
  0.0 68.6 jit_solution(10751320137513680070)
XLA Ops:
  0.6 3.0 %collective-permute-start.1 = (bf16[432,128]{1,0:T(8,128)(2,1)}, bf16[432,128]{1,0:T(8,128)(2,1)S(1)}, u32[]{:S(2)}, u32[]{:S(2)}) collective-permute-start(bf16[432,128]{1,0:T(8,128)(2,1)} %w0.7), channel_id=1, source_target_pairs={{0,16},{8,24},{16,0},{24,8},{1,17},{9,25},{17,1},{25,9},{2,18},{10... | collective-permute-start | bytes 331784 | tf_op jit(solution)/shard_map/ppermute | solution.py:615
  3.8 0.4 collective-permute-start.5
  4.1 1.0 %shard_map.86 = bf16[3,32,2048]{2,1,0:T(8,128)(2,1)S(1)} custom-call(bf16[8,32,2048]{2,1,0:T(8,128)(2,1)} %bitcast.27), custom_call_target="tpu_custom_call" | custom-call | bytes 786432 | tf_op jit(solution)/shard_map/pallas_call | solution.py:99
  5.2 3.7 %collective-permute-start.3 = (bf16[3,32,2048]{2,1,0:T(8,128)(2,1)S(1)}, bf16[3,32,2048]{2,1,0:T(8,128)(2,1)S(1)}, u32[]{:S(2)}, u32[]{:S(2)}) collective-permute-start(bf16[3,32,2048]{2,1,0:T(8,128)(2,1)S(1)} %shard_map.86), channel_id=1, source_target_pairs={{0,1},{1,2},{2,3},{3,4},{4,5},{5,6},{6,7},{8,9},{9,10},{10,11},{11... | collective-permute-start | bytes 1179656 | tf_op jit(solution)/shard_map/ppermute | solution.py:621
  8.9 1.2 %copy-done = bf16[1,8,32,2048]{3,2,1,0:T(8,128)(2,1)S(1)} copy-done((bf16[1,8,32,2048]{3,2,1,0:T(8,128)(2,1)S(1)}, bf16[1,8,32,2048]{3,2,1,0:T(8,128)(2,1)}, u32[]{:S(2)}) %copy-start) | copy-done | bytes 1048600
  10.1 0.3 shard_map.84.sorted_ref
  10.6 1.3 %collective-permute-done.2.w3 = bf16[432,128]{1,0:T(8,128)(2,1)S(1)} collective-permute-done((bf16[432,128]{1,0:T(8,128)(2,1)S(1)}, bf16[432,128]{1,0:T(8,128)(2,1)S(1)}, u32[]{:S(2)}, u32[]{:S(2)}) %collective-permute-start.2) | collective-permute-done | bytes 110624 | tf_op jit(solution)/shard_map/ppermute | solution.py:615
  11.9 2.2 %shard_map.85 = (f32[768,128]{1,0:T(8,128)S(1)}, bf16[128,3456]{1,0:T(8,128)(2,1)S(1)}, bf16[2,256,128]{2,1,0:T(8,128)(2,1)S(1)}, bf16[256,128]{1,0:T(8,128)(2,1...) custom-call(s32[4]{0:T(128)S(1)} %broadcast_multiply_fusion.offsets, ...), custom_call_target="tpu_custom_call" | custom-call | flops 2875000064 | bytes 2015232 | tf_op jit(solution)/shard_map/pallas_call | solution.py:49
  14.1 0.9 %copy-done.7 = bf16[128,3456]{1,0:T(8,128)(2,1)} copy-done((bf16[128,3456]{1,0:T(8,128)(2,1)}, bf16[128,3456]{1,0:T(8,128)(2,1)S(1)}, u32[]{:S(2)}) %copy-start.7) | copy-done | bytes 884760
  15.0 0.7 %copy-done.9 = f32[768,128]{1,0:T(8,128)} copy-done((f32[768,128]{1,0:T(8,128)}, f32[768,128]{1,0:T(8,128)S(1)}, u32[]{:S(2)}) %copy-start.9) | copy-done | bytes 393240
  15.7 0.7 %collective-permute-done.4.w2 = bf16[864,256]{1,0:T(8,128)(2,1)S(1)} collective-permute-done((bf16[864,256]{1,0:T(8,128)(2,1)}, bf16[864,256]{1,0:T(8,128)(2,1)S(1)}, u32[]{:S(2)}, u32[]{:S(2)}) %collective-permute-start.4) | collective-permute-done | bytes 442400 | tf_op jit(solution)/shard_map/ppermute | solution.py:615
  16.5 1.8 %collective-permute-start.7 = (bf16[2,256,128]{2,1,0:T(8,128)(2,1)S(1)}, bf16[2,256,128]{2,1,0:T(8,128)(2,1)S(1)}, u32[]{:S(2)}, u32[]{:S(2)}) collective-permute-start(bf16[2,256,128]{2,1,0:T(8,128)(2,1)S(1)} %get-tuple-element.53.m0), channel_id=1, source_target_pairs={{0,16},{8,24},{16,0},{24,8},{1,17},{9,25},{17,1},{25,9},{2,18},{10... | collective-permute-start | bytes 393224 | tf_op jit(solution)/shard_map/ppermute | solution.py:615
  18.2 0.9 %shard_map.87 = (f32[512,128]{1,0:T(8,128)S(1)}, bf16[64,2304]{1,0:T(8,128)(2,1)S(1)}, bf16[3,3,256,128]{3,2,1,0:T(8,128)(2,1)S(1)}, bf16[2,256,128]{2,1,0:T(8,128)(2,1)S(1)}, bf16[2,256,128]{2,1,0:T(8,128)(2,1)S(1)}) custom-call(f32[1]{0:T(128)} %bitcast.1.alive, s32[1]{0:T(128)} %bitcast.2.side, bf16[3,32,2048]{2,1,0:T(8,128)(2,1)S(1)} %collective-permute-done.3.halo_ref, ...), custom_call_target="tpu_custom_call" | custom-call | flops 1724999936 | bytes 1179648 | tf_op jit(solution)/shard_map/pallas_call | solution.py:49
  19.1 0.3 collective-permute-start.11
  19.4 0.8 %collective-permute-start.9 = (bf16[2,256,128]{2,1,0:T(8,128)(2,1)S(1)}, bf16[2,256,128]{2,1,0:T(8,128)(2,1)S(1)}, u32[]{:S(2)}, u32[]{:S(2)}) collective-permute-start(bf16[2,256,128]{2,1,0:T(8,128)(2,1)S(1)} %get-tuple-element.65), channel_id=1, source_target_pairs={{0,16},{8,24},{16,0},{24,8},{1,17},{9,25},{17,1},{25,9},{2,18},{10... | collective-permute-start | bytes 393224 | tf_op jit(solution)/shard_map/ppermute | solution.py:615
  20.2 1.8 %shard_map.88 = (bf16[2,8,2048]{2,1,0:T(8,128)(2,1)}, bf16[128,256]{1,0:T(8,128)(2,1)S(1)}) custom-call(s32[4]{0:T(128)S(1)} %get-tuple-element.90.offsets, bf16[128,3456]{1,0:T(8,128)(2,1)S(1)} %copy-done.8, bf16[64,2304]{1,0:T(8,128)(2,1)S(1)} %get-tuple-element.49.lower_ref, bf16[2,8,2048]{2,1,0:T(8,128)(2,1)S(1)} %bitcast.33, ...), custom_call_target="tpu_custom_call" | custom-call | flops 1724999936 | bytes 3014656 | tf_op jit(solution)/shard_map/pallas_call | solution.py:49
  22.0 0.5 collective-permute-done.7.m2
  22.5 2.0 %collective-permute-start.8 = (bf16[128,256]{1,0:T(8,128)(2,1)S(1)}, bf16[128,256]{1,0:T(8,128)(2,1)S(1)}, u32[]{:S(2)}, u32[]{:S(2)}) collective-permute-start(bf16[128,256]{1,0:T(8,128)(2,1)S(1)} %get-tuple-element.54.delta_ref.d0), channel_id=1, source_target_pairs={{0,16},{8,24},{16,0},{24,8},{1,17},{9,25},{17,1},{25,9},{2,18},{10... | collective-permute-start | bytes 196616 | tf_op jit(solution)/shard_map/ppermute | solution.py:615
  24.5 0.2 collective-permute-start.12
  24.7 3.0 %shard_map.89 = (bf16[768,128]{1,0:T(8,128)(2,1)S(1)}, f32[256,128]{1,0:T(8,128)S(1)}, bf16[512,128]{1,0:T(8,128)(2,1)S(1)}, bf16[8,56,128]{2,1,0:T(8,128)(2,1)S...) custom-call(s32[4]{0:T(128)S(1)} %get-tuple-element.90.offsets, ...), custom_call_target="tpu_custom_call" | custom-call | flops 4024999936 | bytes 4653056 | tf_op jit(solution)/shard_map/pallas_call | solution.py:49
  27.8 0.3 collective-permute-start.17
  28.1 0.2 collective-permute-start.15
  28.4 0.3 collective-permute-start.14
  28.6 0.2 collective-permute-start.16
  28.9 0.3 collective-permute-start.19
  29.2 0.3 collective-permute-done.15.m1
  29.5 0.4 collective-permute-done.16.d3
  29.9 1.8 %shard_map.91 = bf16[8,216,128]{2,1,0:T(8,128)(2,1)S(1)} custom-call(s32[1]{0:T(128)} %bitcast.6.data, s32[4,33]{1,0:T(4,128)S(1)} %copy-done.4, s32[8]{0:T(128)S(1)} %fusion.12.order, bf16[2,256,128]{2,1,0:T(8,128)(2,1)S(1)} %get-tuple-element.66.e0, bf16[2,256,128]{2,1,0:T(8,128)(2,1)S(1)} %collective-permute-done.11.e1, ...), custom_call_target="tpu_custom_call" | custom-call | flops 2300000000 | bytes 1310720 | tf_op jit(solution)/shard_map/pallas_call | solution.py:49
  31.8 1.2 %collective-permute-start.18 = (bf16[3,272,128]{2,1,0:T(8,128)(2,1)S(1)}, bf16[3,272,128]{2,1,0:T(8,128)(2,1)S(1)}, u32[]{:S(2)}, u32[]{:S(2)}) collective-permute-start(bf16[3,272,128]{2,1,0:T(8,128)(2,1)S(1)} %fusion), channel_id=1, source_target_pairs={{0,1},{1,0},{2,3},{3,2},{4,5},{5,4},{6,7},{7,6},{8,9},{9,8},{10,11... | collective-permute-start | bytes 626696 | tf_op jit(solution)/shard_map/ppermute | solution.py:615
  33.0 1.1 %collective-permute-start.20 = (bf16[4,56,128]{2,1,0:T(8,128)(2,1)S(1)}, bf16[4,56,128]{2,1,0:T(8,128)(2,1)S(1)}, u32[]{:S(2)}, u32[]{:S(2)}) collective-permute-start(bf16[4,56,128]{2,1,0:T(8,128)(2,1)S(1)} %get-tuple-element.84), channel_id=1, source_target_pairs={{0,16},{8,24},{16,0},{24,8},{1,17},{9,25},{17,1},{25,9},{2,18},{10... | collective-permute-start | bytes 172040 | tf_op jit(solution)/shard_map/ppermute | solution.py:615
  34.1 1.3 %collective-permute-start.21 = (bf16[4,56,128]{2,1,0:T(8,128)(2,1)S(1)}, bf16[4,56,128]{2,1,0:T(8,128)(2,1)S(1)}, u32[]{:S(2)}, u32[]{:S(2)}) collective-permute-start(bf16[4,56,128]{2,1,0:T(8,128)(2,1)S(1)} %get-tuple-element.85), channel_id=1, source_target_pairs={{0,17},{1,16},{2,19},{3,18},{4,21},{5,20},{6,23},{7,22},{8,25},{9,... | collective-permute-start | bytes 172040 | tf_op jit(solution)/shard_map/ppermute | solution.py:699
  35.4 1.1 %collective-permute-start.25 = (bf16[1,272,128]{2,1,0:T(8,128)(2,1)S(1)}, bf16[1,272,128]{2,1,0:T(8,128)(2,1)S(1)}, u32[]{:S(2)}, u32[]{:S(2)}) collective-permute-start(bf16[1,272,128]{2,1,0:T(8,128)(2,1)S(1)} %pad_maximum_fusion.1), channel_id=1, source_target_pairs={{0,1},{1,0},{2,3},{3,2},{4,5},{5,4},{6,7},{7,6},{8,9},{9,8},{10,11... | collective-permute-start | bytes 208904 | tf_op jit(solution)/shard_map/ppermute | solution.py:615
  36.6 4.5 %collective-permute-done.18 = bf16[3,272,128]{2,1,0:T(8,128)(2,1)S(1)} collective-permute-done((bf16[3,272,128]{2,1,0:T(8,128)(2,1)S(1)}, bf16[3,272,128]{2,1,0:T(8,128)(2,1)S(1)}, u32[]{:S(2)}, u32[]{:S(2)}) %collective-permute-start.18) | collective-permute-done | bytes 208928 | tf_op jit(solution)/shard_map/ppermute | solution.py:615
  41.2 2.1 %collective-permute-start.22 = (bf16[272,128]{1,0:T(8,128)(2,1)S(1)}, bf16[272,128]{1,0:T(8,128)(2,1)S(1)}, u32[]{:S(2)}, u32[]{:S(2)}) collective-permute-start(bf16[272,128]{1,0:T(8,128)(2,1)S(1)} %get-tuple-element.87), channel_id=1, source_target_pairs={{0,2},{1,3},{2,0},{3,1},{4,6},{5,7},{6,4},{7,5},{8,10},{9,11},{10,... | collective-permute-start | bytes 208904 | tf_op jit(solution)/shard_map/ppermute | solution.py:615
  43.3 2.6 %collective-permute-start.23 = (bf16[272,128]{1,0:T(8,128)(2,1)S(1)}, bf16[272,128]{1,0:T(8,128)(2,1)S(1)}, u32[]{:S(2)}, u32[]{:S(2)}) collective-permute-start(bf16[272,128]{1,0:T(8,128)(2,1)S(1)} %get-tuple-element.88), channel_id=1, source_target_pairs={{0,4},{1,5},{2,6},{3,7},{4,0},{5,1},{6,2},{7,3},{8,12},{9,13},{10,... | collective-permute-start | bytes 208904 | tf_op jit(solution)/shard_map/ppermute | solution.py:615
  45.9 0.4 collective-permute-done.22
  46.3 3.7 %collective-permute-done.23 = bf16[272,128]{1,0:T(8,128)(2,1)S(1)} collective-permute-done((bf16[272,128]{1,0:T(8,128)(2,1)S(1)}, bf16[272,128]{1,0:T(8,128)(2,1)S(1)}, u32[]{:S(2)}, u32[]{:S(2)}) %collective-permute-start.23) | collective-permute-done | bytes 69664 | tf_op jit(solution)/shard_map/ppermute | solution.py:615
  50.0 2.3 %collective-permute-done.24 = bf16[272,128]{1,0:T(8,128)(2,1)S(1)} collective-permute-done((bf16[272,128]{1,0:T(8,128)(2,1)S(1)}, bf16[272,128]{1,0:T(8,128)(2,1)S(1)}, u32[]{:S(2)}, u32[]{:S(2)}) %collective-permute-start.24) | collective-permute-done | bytes 69664 | tf_op jit(solution)/shard_map/ppermute | solution.py:615
  52.4 1.4 %collective-permute-start.27 = (bf16[272,128]{1,0:T(8,128)(2,1)S(1)}, bf16[272,128]{1,0:T(8,128)(2,1)S(1)}, u32[]{:S(2)}, u32[]{:S(2)}) collective-permute-start(bf16[272,128]{1,0:T(8,128)(2,1)S(1)} %fusion.4.refs_0_), channel_id=1, source_target_pairs={{0,4},{1,5},{2,6},{3,7},{4,0},{5,1},{6,2},{7,3},{8,12},{9,13},{10,... | collective-permute-start | bytes 208904 | tf_op jit(solution)/shard_map/ppermute | solution.py:615
  53.8 2.9 %collective-permute-start.28 = (bf16[272,128]{1,0:T(8,128)(2,1)S(1)}, bf16[272,128]{1,0:T(8,128)(2,1)S(1)}, u32[]{:S(2)}, u32[]{:S(2)}) collective-permute-start(bf16[272,128]{1,0:T(8,128)(2,1)S(1)} %fusion.4.refs_0_), channel_id=1, source_target_pairs={{0,6},{1,7},{2,4},{3,5},{4,2},{5,3},{6,0},{7,1},{8,14},{9,15},{10,... | collective-permute-start | bytes 208904 | tf_op jit(solution)/shard_map/ppermute | solution.py:615
  56.8 1.3 %collective-permute-start.13 = (bf16[512,128]{1,0:T(8,128)(2,1)S(1)}, bf16[512,128]{1,0:T(8,128)(2,1)S(1)}, u32[]{:S(2)}, u32[]{:S(2)}) collective-permute-start(bf16[512,128]{1,0:T(8,128)(2,1)S(1)} %get-tuple-element.68), channel_id=1, source_target_pairs={{1,0},{2,1},{3,2},{4,3},{5,4},{6,5},{7,6},{9,8},{10,9},{11,10},{12... | collective-permute-start | bytes 393224 | tf_op jit(solution)/shard_map/ppermute | solution.py:621
  58.1 0.4 collective-permute-done.27.refs_2_
  58.5 1.7 %collective-permute-done.28.refs_3_ = bf16[272,128]{1,0:T(8,128)(2,1)S(1)} collective-permute-done((bf16[272,128]{1,0:T(8,128)(2,1)S(1)}, bf16[272,128]{1,0:T(8,128)(2,1)S(1)}, u32[]{:S(2)}, u32[]{:S(2)}) %collective-permute-start.28) | collective-permute-done | bytes 69664 | tf_op jit(solution)/shard_map/ppermute | solution.py:615
  60.3 0.6 collective-permute-start.29
  60.8 2.8 %collective-permute-done.13.upper_ref = bf16[512,128]{1,0:T(8,128)(2,1)S(1)} collective-permute-done((bf16[512,128]{1,0:T(8,128)(2,1)S(1)}, bf16[512,128]{1,0:T(8,128)(2,1)S(1)}, u32[]{:S(2)}, u32[]{:S(2)}) %collective-permute-start.13) | collective-permute-done | bytes 131104 | tf_op jit(solution)/shard_map/ppermute | solution.py:621
  63.6 2.8 %shard_map.90 = bf16[8,32,2048]{2,1,0:T(8,128)(2,1)} custom-call(s32[4]{0:T(128)S(1)} %broadcast_multiply_fusion.offsets, bf16[768,128]{1,0:T(8,128)(2,1)S(1)} %get-tuple-element.58.low_ref, f32[256,128]{1,0:T(8,128)S(1)} %get-tuple-element.59.last_ref, f32[768,128]{1,0:T(8,128)S(1)} %copy-done.10, bf16[512,128]{1,0:T(8,128)(2,1)S(1)} %collective-permute-done.13.upper_ref, ...), custom_call_target="tpu_custom_call" | custom-call | flops 3449999872 | bytes 1294336 | tf_op jit(solution)/shard_map/pallas_call | solution.py:49
  66.4 0.5 collective-permute-done.29.refs_4_
  66.9 1.7 %shard_map.92 = (f32[432,128]{1,0:T(8,128)}, f32[864,256]{1,0:T(8,128)}) custom-call(s32[8]{0:T(128)S(1)} %fusion.12.order, bf16[272,128]{1,0:T(8,128)(2,1)S(1)} %fusion.4.refs_0_, bf16[272,128]{1,0:T(8,128)(2,1)S(1)} %collective-permute-done.26.refs_1_, bf16[272,128]{1,0:T(8,128)(2,1)S(1)} %collective-permute-done.27.refs_2_, ...), custom_call_target="tpu_custom_call" | custom-call | flops 1150000000 | bytes 557056 | tf_op jit(solution)/shard_map/pallas_call | solution.py:49
  (58 shorter events, 0.7 us)
Async XLA Ops:
  0.6 9.8 %collective-permute-start.1 = (bf16[432,128]{1,0:T(8,128)(2,1)}, bf16[432,128]{1,0:T(8,128)(2,1)S(1)}, u32[]{:S(2)}, u32[]{:S(2)}) collective-permute-start(bf16[432,128]{1,0:T(8,128)(2,1)} %w0.7), channel_id=1, source_target_pairs={{0,16},{8,24},{16,0},{24,8},{1,17},{9,25},{17,1},{25,9},{2,18},{10... | collective-permute-start | bytes 331784 | tf_op jit(solution)/shard_map/ppermute | solution.py:615
  3.6 6.9 %collective-permute-start = (bf16[432,128]{1,0:T(8,128)(2,1)}, bf16[432,128]{1,0:T(8,128)(2,1)S(1)}, u32[]{:S(2)}, u32[]{:S(2)}) collective-permute-start(bf16[432,128]{1,0:T(8,128)(2,1)} %w0.7), channel_id=1, source_target_pairs={{0,8},{8,0},{16,24},{24,16},{1,9},{9,1},{17,25},{25,17},{2,10},{10... | collective-permute-start | bytes 331784 | tf_op jit(solution)/shard_map/ppermute | solution.py:615
  3.6 12.8 %collective-permute-start.4 = (bf16[864,256]{1,0:T(8,128)(2,1)}, bf16[864,256]{1,0:T(8,128)(2,1)S(1)}, u32[]{:S(2)}, u32[]{:S(2)}) collective-permute-start(bf16[864,256]{1,0:T(8,128)(2,1)} %w0.6), channel_id=1, source_target_pairs={{0,16},{8,24},{16,0},{24,8},{1,17},{9,25},{17,1},{25,9},{2,18},{10... | collective-permute-start | bytes 1327112 | tf_op jit(solution)/shard_map/ppermute | solution.py:615
  3.8 16.4 %collective-permute-start.5 = (bf16[864,256]{1,0:T(8,128)(2,1)}, bf16[864,256]{1,0:T(8,128)(2,1)S(1)}, u32[]{:S(2)}, u32[]{:S(2)}) collective-permute-start(bf16[864,256]{1,0:T(8,128)(2,1)} %w0.6), channel_id=1, source_target_pairs={{0,8},{8,0},{16,24},{24,16},{1,9},{9,1},{17,25},{25,17},{2,10},{10... | collective-permute-start | bytes 1327112 | tf_op jit(solution)/shard_map/ppermute | solution.py:615
  5.2 13.1 %collective-permute-start.3 = (bf16[3,32,2048]{2,1,0:T(8,128)(2,1)S(1)}, bf16[3,32,2048]{2,1,0:T(8,128)(2,1)S(1)}, u32[]{:S(2)}, u32[]{:S(2)}) collective-permute-start(bf16[3,32,2048]{2,1,0:T(8,128)(2,1)S(1)} %shard_map.86), channel_id=1, source_target_pairs={{0,1},{1,2},{2,3},{3,4},{4,5},{5,6},{6,7},{8,9},{9,10},{10,11},{11... | collective-permute-start | bytes 1179656 | tf_op jit(solution)/shard_map/ppermute | solution.py:621
  8.9 1.2 %copy-start = (bf16[1,8,32,2048]{3,2,1,0:T(8,128)(2,1)S(1)}, bf16[1,8,32,2048]{3,2,1,0:T(8,128)(2,1)}, u32[]{:S(2)}) copy-start(bf16[1,8,32,2048]{3,2,1,0:T(8,128)(2,1)} %param.5) | copy-start | bytes 3145732
  10.1 1.8 %copy-start.2 = (bf16[432,128]{1,0:T(8,128)(2,1)S(1)}, bf16[432,128]{1,0:T(8,128)(2,1)}, u32[]{:S(2)}) copy-start(bf16[432,128]{1,0:T(8,128)(2,1)} %w0.7) | copy-start | bytes 331780
  10.5 3.6 %copy-start.5 = (bf16[8,3,256,128]{3,2,1,0:T(8,128)(2,1)}, bf16[8,3,256,128]{3,2,1,0:T(8,128)(2,1)S(1)}, u32[]{:S(2)}) copy-start(bf16[8,3,256,128]{3,2,1,0:T(8,128)(2,1)S(1)} %shard_map.84.sorted_ref) | copy-start | bytes 4718596
  10.5 1.4 %collective-permute-start.2 = (bf16[432,128]{1,0:T(8,128)(2,1)S(1)}, bf16[432,128]{1,0:T(8,128)(2,1)S(1)}, u32[]{:S(2)}, u32[]{:S(2)}) collective-permute-start(bf16[432,128]{1,0:T(8,128)(2,1)S(1)} %collective-permute-done.1.w2), channel_id=1, source_target_pairs={{0,8},{8,0},{16,24},{24,16},{1,9},{9,1},{17,25},{25,17},{2,10},{10... | collective-permute-start | bytes 331784 | tf_op jit(solution)/shard_map/ppermute | solution.py:615
  14.0 0.9 %copy-start.7 = (bf16[128,3456]{1,0:T(8,128)(2,1)}, bf16[128,3456]{1,0:T(8,128)(2,1)S(1)}, u32[]{:S(2)}) copy-start(bf16[128,3456]{1,0:T(8,128)(2,1)S(1)} %get-tuple-element.44.upper_ref) | copy-start | bytes 2654212
  15.0 0.7 %copy-start.9 = (f32[768,128]{1,0:T(8,128)}, f32[768,128]{1,0:T(8,128)S(1)}, u32[]{:S(2)}) copy-start(f32[768,128]{1,0:T(8,128)S(1)} %get-tuple-element.56.slope_ref) | copy-start | bytes 1179652
  16.4 3.7 %collective-permute-start.6 = (bf16[864,256]{1,0:T(8,128)(2,1)S(1)}, bf16[864,256]{1,0:T(8,128)(2,1)S(1)}, u32[]{:S(2)}, u32[]{:S(2)}) collective-permute-start(bf16[864,256]{1,0:T(8,128)(2,1)S(1)} %collective-permute-done.4.w2), channel_id=1, source_target_pairs={{0,8},{8,0},{16,24},{24,16},{1,9},{9,1},{17,25},{25,17},{2,10},{10... | collective-permute-start | bytes 1327112 | tf_op jit(solution)/shard_map/ppermute | solution.py:615
  16.5 6.1 %collective-permute-start.7 = (bf16[2,256,128]{2,1,0:T(8,128)(2,1)S(1)}, bf16[2,256,128]{2,1,0:T(8,128)(2,1)S(1)}, u32[]{:S(2)}, u32[]{:S(2)}) collective-permute-start(bf16[2,256,128]{2,1,0:T(8,128)(2,1)S(1)} %get-tuple-element.53.m0), channel_id=1, source_target_pairs={{0,16},{8,24},{16,0},{24,8},{1,17},{9,25},{17,1},{25,9},{2,18},{10... | collective-permute-start | bytes 393224 | tf_op jit(solution)/shard_map/ppermute | solution.py:615
  18.2 1.9 %copy-start.1 = (bf16[864,256]{1,0:T(8,128)(2,1)S(1)}, bf16[864,256]{1,0:T(8,128)(2,1)}, u32[]{:S(2)}) copy-start(bf16[864,256]{1,0:T(8,128)(2,1)} %w0.6) | copy-start | bytes 1327108
  18.2 1.9 %copy-start.3 = (bf16[1,2,8,2048]{3,2,1,0:T(8,128)(2,1)S(1)}, bf16[1,2,8,2048]{3,2,1,0:T(8,128)(2,1)}, u32[]{:S(2)}) copy-start(bf16[1,2,8,2048]{3,2,1,0:T(8,128)(2,1)} %param.8) | copy-start | bytes 196612
  18.2 2.0 %copy-start.8 = (bf16[128,3456]{1,0:T(8,128)(2,1)S(1)}, bf16[128,3456]{1,0:T(8,128)(2,1)}, u32[]{:S(2)}) copy-start(bf16[128,3456]{1,0:T(8,128)(2,1)} %copy-done.7) | copy-start | bytes 2654212
  19.1 8.6 %collective-permute-start.11 = (bf16[2,256,128]{2,1,0:T(8,128)(2,1)S(1)}, bf16[2,256,128]{2,1,0:T(8,128)(2,1)S(1)}, u32[]{:S(2)}, u32[]{:S(2)}) collective-permute-start(bf16[2,256,128]{2,1,0:T(8,128)(2,1)S(1)} %get-tuple-element.66.e0), channel_id=1, source_target_pairs={{0,8},{8,0},{16,24},{24,16},{1,9},{9,1},{17,25},{25,17},{2,10},{10... | collective-permute-start | bytes 393224 | tf_op jit(solution)/shard_map/ppermute | solution.py:615
  19.4 8.4 %collective-permute-start.9 = (bf16[2,256,128]{2,1,0:T(8,128)(2,1)S(1)}, bf16[2,256,128]{2,1,0:T(8,128)(2,1)S(1)}, u32[]{:S(2)}, u32[]{:S(2)}) collective-permute-start(bf16[2,256,128]{2,1,0:T(8,128)(2,1)S(1)} %get-tuple-element.65), channel_id=1, source_target_pairs={{0,16},{8,24},{16,0},{24,8},{1,17},{9,25},{17,1},{25,9},{2,18},{10... | collective-permute-start | bytes 393224 | tf_op jit(solution)/shard_map/ppermute | solution.py:615
  20.2 4.6 %copy-start.6 = (bf16[8,3,256,128]{3,2,1,0:T(8,128)(2,1)S(1)}, bf16[8,3,256,128]{3,2,1,0:T(8,128)(2,1)}, u32[]{:S(2)}) copy-start(bf16[8,3,256,128]{3,2,1,0:T(8,128)(2,1)} %copy-done.5) | copy-start | bytes 4718596
  20.2 4.6 %copy-start.10 = (f32[768,128]{1,0:T(8,128)S(1)}, f32[768,128]{1,0:T(8,128)}, u32[]{:S(2)}) copy-start(f32[768,128]{1,0:T(8,128)} %copy-done.9) | copy-start | bytes 1179652
  22.5 5.2 %collective-permute-start.10 = (bf16[128,256]{1,0:T(8,128)(2,1)S(1)}, bf16[128,256]{1,0:T(8,128)(2,1)S(1)}, u32[]{:S(2)}, u32[]{:S(2)}) collective-permute-start(bf16[128,256]{1,0:T(8,128)(2,1)S(1)} %get-tuple-element.54.delta_ref.d0), channel_id=1, source_target_pairs={{0,8},{8,0},{16,24},{24,16},{1,9},{9,1},{17,25},{25,17},{2,10},{10... | collective-permute-start | bytes 196616 | tf_op jit(solution)/shard_map/ppermute | solution.py:615
  22.5 5.2 %collective-permute-start.8 = (bf16[128,256]{1,0:T(8,128)(2,1)S(1)}, bf16[128,256]{1,0:T(8,128)(2,1)S(1)}, u32[]{:S(2)}, u32[]{:S(2)}) collective-permute-start(bf16[128,256]{1,0:T(8,128)(2,1)S(1)} %get-tuple-element.54.delta_ref.d0), channel_id=1, source_target_pairs={{0,16},{8,24},{16,0},{24,8},{1,17},{9,25},{17,1},{25,9},{2,18},{10... | collective-permute-start | bytes 196616 | tf_op jit(solution)/shard_map/ppermute | solution.py:615
  24.5 3.3 %collective-permute-start.12 = (bf16[2,256,128]{2,1,0:T(8,128)(2,1)S(1)}, bf16[2,256,128]{2,1,0:T(8,128)(2,1)S(1)}, u32[]{:S(2)}, u32[]{:S(2)}) collective-permute-start(bf16[2,256,128]{2,1,0:T(8,128)(2,1)S(1)} %collective-permute-done.7.m2), channel_id=1, source_target_pairs={{0,8},{8,0},{16,24},{24,16},{1,9},{9,1},{17,25},{25,17},{2,10},{10... | collective-permute-start | bytes 393224 | tf_op jit(solution)/shard_map/ppermute | solution.py:615
  24.7 5.2 %copy-start.4 = (s32[4,33]{1,0:T(4,128)S(1)}, s32[4,33]{1,0:T(4,128)}, u32[]{:S(2)}) copy-start(s32[4,33]{1,0:T(4,128)} %constant.48.clone.table) | copy-start | bytes 1588
  27.8 1.4 %collective-permute-start.17 = (bf16[8,56,128]{2,1,0:T(8,128)(2,1)S(1)}, bf16[8,56,128]{2,1,0:T(8,128)(2,1)S(1)}, u32[]{:S(2)}, u32[]{:S(2)}) collective-permute-start(bf16[8,56,128]{2,1,0:T(8,128)(2,1)S(1)} %get-tuple-element.75), channel_id=1, source_target_pairs={{0,8},{8,0},{16,24},{24,16},{1,9},{9,1},{17,25},{25,17},{2,10},{10... | collective-permute-start | bytes 344072 | tf_op jit(solution)/shard_map/ppermute | solution.py:615
  28.1 1.3 %collective-permute-start.15 = (bf16[2,256,128]{2,1,0:T(8,128)(2,1)S(1)}, bf16[2,256,128]{2,1,0:T(8,128)(2,1)S(1)}, u32[]{:S(2)}, u32[]{:S(2)}) collective-permute-start(bf16[2,256,128]{2,1,0:T(8,128)(2,1)S(1)} %get-tuple-element.53.m0), channel_id=1, source_target_pairs={{0,8},{8,0},{16,24},{24,16},{1,9},{9,1},{17,25},{25,17},{2,10},{10... | collective-permute-start | bytes 393224 | tf_op jit(solution)/shard_map/ppermute | solution.py:615
  28.4 1.5 %collective-permute-start.14 = (bf16[2,256,128]{2,1,0:T(8,128)(2,1)S(1)}, bf16[2,256,128]{2,1,0:T(8,128)(2,1)S(1)}, u32[]{:S(2)}, u32[]{:S(2)}) collective-permute-start(bf16[2,256,128]{2,1,0:T(8,128)(2,1)S(1)} %collective-permute-done.9.e2), channel_id=1, source_target_pairs={{0,8},{8,0},{16,24},{24,16},{1,9},{9,1},{17,25},{25,17},{2,10},{10... | collective-permute-start | bytes 393224 | tf_op jit(solution)/shard_map/ppermute | solution.py:615
  28.6 1.3 %collective-permute-start.16 = (bf16[128,256]{1,0:T(8,128)(2,1)S(1)}, bf16[128,256]{1,0:T(8,128)(2,1)S(1)}, u32[]{:S(2)}, u32[]{:S(2)}) collective-permute-start(bf16[128,256]{1,0:T(8,128)(2,1)S(1)} %collective-permute-done.8.d2), channel_id=1, source_target_pairs={{0,8},{8,0},{16,24},{24,16},{1,9},{9,1},{17,25},{25,17},{2,10},{10... | collective-permute-start | bytes 196616 | tf_op jit(solution)/shard_map/ppermute | solution.py:615
  28.9 4.1 %collective-permute-start.19 = (bf16[8,56,128]{2,1,0:T(8,128)(2,1)S(1)}, bf16[8,56,128]{2,1,0:T(8,128)(2,1)S(1)}, u32[]{:S(2)}, u32[]{:S(2)}) collective-permute-start(bf16[8,56,128]{2,1,0:T(8,128)(2,1)S(1)} %get-tuple-element.77), channel_id=1, source_target_pairs={{0,8},{8,0},{16,24},{24,16},{1,9},{9,1},{17,25},{25,17},{2,10},{10... | collective-permute-start | bytes 344072 | tf_op jit(solution)/shard_map/ppermute | solution.py:615
  31.8 9.3 %collective-permute-start.18 = (bf16[3,272,128]{2,1,0:T(8,128)(2,1)S(1)}, bf16[3,272,128]{2,1,0:T(8,128)(2,1)S(1)}, u32[]{:S(2)}, u32[]{:S(2)}) collective-permute-start(bf16[3,272,128]{2,1,0:T(8,128)(2,1)S(1)} %fusion), channel_id=1, source_target_pairs={{0,1},{1,0},{2,3},{3,2},{4,5},{5,4},{6,7},{7,6},{8,9},{9,8},{10,11... | collective-permute-start | bytes 626696 | tf_op jit(solution)/shard_map/ppermute | solution.py:615
  33.0 8.1 %collective-permute-start.20 = (bf16[4,56,128]{2,1,0:T(8,128)(2,1)S(1)}, bf16[4,56,128]{2,1,0:T(8,128)(2,1)S(1)}, u32[]{:S(2)}, u32[]{:S(2)}) collective-permute-start(bf16[4,56,128]{2,1,0:T(8,128)(2,1)S(1)} %get-tuple-element.84), channel_id=1, source_target_pairs={{0,16},{8,24},{16,0},{24,8},{1,17},{9,25},{17,1},{25,9},{2,18},{10... | collective-permute-start | bytes 172040 | tf_op jit(solution)/shard_map/ppermute | solution.py:615
  34.1 7.0 %collective-permute-start.21 = (bf16[4,56,128]{2,1,0:T(8,128)(2,1)S(1)}, bf16[4,56,128]{2,1,0:T(8,128)(2,1)S(1)}, u32[]{:S(2)}, u32[]{:S(2)}) collective-permute-start(bf16[4,56,128]{2,1,0:T(8,128)(2,1)S(1)} %get-tuple-element.85), channel_id=1, source_target_pairs={{0,17},{1,16},{2,19},{3,18},{4,21},{5,20},{6,23},{7,22},{8,25},{9,... | collective-permute-start | bytes 172040 | tf_op jit(solution)/shard_map/ppermute | solution.py:699
  35.4 10.4 %collective-permute-start.25 = (bf16[1,272,128]{2,1,0:T(8,128)(2,1)S(1)}, bf16[1,272,128]{2,1,0:T(8,128)(2,1)S(1)}, u32[]{:S(2)}, u32[]{:S(2)}) collective-permute-start(bf16[1,272,128]{2,1,0:T(8,128)(2,1)S(1)} %pad_maximum_fusion.1), channel_id=1, source_target_pairs={{0,1},{1,0},{2,3},{3,2},{4,5},{5,4},{6,7},{7,6},{8,9},{9,8},{10,11... | collective-permute-start | bytes 208904 | tf_op jit(solution)/shard_map/ppermute | solution.py:615
  41.2 5.1 %collective-permute-start.22 = (bf16[272,128]{1,0:T(8,128)(2,1)S(1)}, bf16[272,128]{1,0:T(8,128)(2,1)S(1)}, u32[]{:S(2)}, u32[]{:S(2)}) collective-permute-start(bf16[272,128]{1,0:T(8,128)(2,1)S(1)} %get-tuple-element.87), channel_id=1, source_target_pairs={{0,2},{1,3},{2,0},{3,1},{4,6},{5,7},{6,4},{7,5},{8,10},{9,11},{10,... | collective-permute-start | bytes 208904 | tf_op jit(solution)/shard_map/ppermute | solution.py:615
  43.3 6.7 %collective-permute-start.23 = (bf16[272,128]{1,0:T(8,128)(2,1)S(1)}, bf16[272,128]{1,0:T(8,128)(2,1)S(1)}, u32[]{:S(2)}, u32[]{:S(2)}) collective-permute-start(bf16[272,128]{1,0:T(8,128)(2,1)S(1)} %get-tuple-element.88), channel_id=1, source_target_pairs={{0,4},{1,5},{2,6},{3,7},{4,0},{5,1},{6,2},{7,3},{8,12},{9,13},{10,... | collective-permute-start | bytes 208904 | tf_op jit(solution)/shard_map/ppermute | solution.py:615
  45.9 6.4 %collective-permute-start.24 = (bf16[272,128]{1,0:T(8,128)(2,1)S(1)}, bf16[272,128]{1,0:T(8,128)(2,1)S(1)}, u32[]{:S(2)}, u32[]{:S(2)}) collective-permute-start(bf16[272,128]{1,0:T(8,128)(2,1)S(1)} %get-tuple-element.86), channel_id=1, source_target_pairs={{0,6},{1,7},{2,4},{3,5},{4,2},{5,3},{6,0},{7,1},{8,14},{9,15},{10,... | collective-permute-start | bytes 208904 | tf_op jit(solution)/shard_map/ppermute | solution.py:615
  52.3 5.7 %collective-permute-start.26 = (bf16[272,128]{1,0:T(8,128)(2,1)S(1)}, bf16[272,128]{1,0:T(8,128)(2,1)S(1)}, u32[]{:S(2)}, u32[]{:S(2)}) collective-permute-start(bf16[272,128]{1,0:T(8,128)(2,1)S(1)} %fusion.4.refs_0_), channel_id=1, source_target_pairs={{0,2},{1,3},{2,0},{3,1},{4,6},{5,7},{6,4},{7,5},{8,10},{9,11},{10,... | collective-permute-start | bytes 208904 | tf_op jit(solution)/shard_map/ppermute | solution.py:615
  52.4 6.1 %collective-permute-start.27 = (bf16[272,128]{1,0:T(8,128)(2,1)S(1)}, bf16[272,128]{1,0:T(8,128)(2,1)S(1)}, u32[]{:S(2)}, u32[]{:S(2)}) collective-permute-start(bf16[272,128]{1,0:T(8,128)(2,1)S(1)} %fusion.4.refs_0_), channel_id=1, source_target_pairs={{0,4},{1,5},{2,6},{3,7},{4,0},{5,1},{6,2},{7,3},{8,12},{9,13},{10,... | collective-permute-start | bytes 208904 | tf_op jit(solution)/shard_map/ppermute | solution.py:615
  53.8 6.4 %collective-permute-start.28 = (bf16[272,128]{1,0:T(8,128)(2,1)S(1)}, bf16[272,128]{1,0:T(8,128)(2,1)S(1)}, u32[]{:S(2)}, u32[]{:S(2)}) collective-permute-start(bf16[272,128]{1,0:T(8,128)(2,1)S(1)} %fusion.4.refs_0_), channel_id=1, source_target_pairs={{0,6},{1,7},{2,4},{3,5},{4,2},{5,3},{6,0},{7,1},{8,14},{9,15},{10,... | collective-permute-start | bytes 208904 | tf_op jit(solution)/shard_map/ppermute | solution.py:615
  56.8 6.8 %collective-permute-start.13 = (bf16[512,128]{1,0:T(8,128)(2,1)S(1)}, bf16[512,128]{1,0:T(8,128)(2,1)S(1)}, u32[]{:S(2)}, u32[]{:S(2)}) collective-permute-start(bf16[512,128]{1,0:T(8,128)(2,1)S(1)} %get-tuple-element.68), channel_id=1, source_target_pairs={{1,0},{2,1},{3,2},{4,3},{5,4},{6,5},{7,6},{9,8},{10,9},{11,10},{12... | collective-permute-start | bytes 393224 | tf_op jit(solution)/shard_map/ppermute | solution.py:621
  60.3 6.6 %collective-permute-start.29 = (bf16[4,272,128]{2,1,0:T(8,128)(2,1)S(1)}, bf16[4,272,128]{2,1,0:T(8,128)(2,1)S(1)}, u32[]{:S(2)}, u32[]{:S(2)}) collective-permute-start(bf16[4,272,128]{2,1,0:T(8,128)(2,1)S(1)} %pad_maximum_fusion), channel_id=1, source_target_pairs={{0,1},{1,0},{2,3},{3,2},{4,5},{5,4},{6,7},{7,6},{8,9},{9,8},{10,11... | collective-permute-start | bytes 835592 | tf_op jit(solution)/shard_map/ppermute | solution.py:615

commit v11 on v10

--- a/solution.py
+++ b/solution.py
@@ -584,13 +584,16 @@
 
 
 def unpack_kernel(scale_first, scale_second, order, *refs):
-    *chunks, other, first_ref, second_ref, flat_first, flat_second = refs
-    high = len(chunks)
+    *chunks, first_ref, second_ref, flat_first, flat_second = refs
+    high = order.shape[0] // 2
     small = flat_first.shape[0] // (2 * high)
     big = flat_second.shape[0] // (2 * high)
     for low in range(2):
         for index in range(high):
-            chunk = (other[index] if low else chunks[index][...]).astype(F32)
+            if low and index:
+                chunk = chunks[high + 1][index - 1].astype(F32)
+            else:
+                chunk = chunks[index + low * high][...].astype(F32)
             place = order[low * high + index]
             flat_second[pl.ds(pl.multiple_of(place * big, 8), big), :] = chunk[:big, :]
             flat_first[pl.ds(pl.multiple_of(place * small, 8), small), :] = chunk[big:, :]
@@ -681,6 +684,7 @@
         (delta_second, delta_core, delta_x, swap(delta_x, "dp", 1)),
         data, order, spaces, size_second,
     )
+    second, down = lax.optimization_barrier((second, down))
     upper = shifted(down, "space", -1)
 
     def pieces(value):
@@ -711,12 +715,17 @@
         )
 
     sent = held(slice(1, high), got_y).astype(BF16)
-    *received, got_y_own = lax.optimization_barrier(
-        (*(swap(sent[k - 1], "space", 2 * k) for k in range(1, high)), got_y_own)
+    *received, got_y_own, upper = lax.optimization_barrier(
+        (*(swap(sent[k - 1], "space", 2 * k) for k in range(1, high)), got_y_own, upper)
     )
     mine = added(held(slice(0, 1), got_y_own)[0], *received)
-    chunks = [mine] + [swap(mine, "space", 2 * k) for k in range(1, high)]
-    chunks.append(swap(jnp.stack(chunks), "space", 1))
+    others = [swap(mine, "space", 2 * k) for k in range(1, high)]
+    mine_y = swap(mine, "space", 1)
+    chunks = [mine, *others, mine_y]
+    if others:
+        chunks.append(swap(jnp.stack(others), "space", 1))
+    upper, mine_y = lax.optimization_barrier((upper, mine_y))
+    chunks[high] = mine_y
 
     gradient = back_input(low, last, slope, upper, shards_first, offsets_first, inputs.shape)
 

time: 68.8 us -> 67.8 us (0.985)
  waiting for transfers between devices: 19.6 us -> 17.1 us
  starting transfers between devices: 29.4 us -> 30.8 us
    ppermute x2, waiting for transfers between devices: 2.78 us -> 0.01 us  [shifted(): return lax.ppermute(value, axis, pairs)]
    ppermute x27 -> x28, starting transfers between devices: 23.1 us -> 24.6 us  [swap(): return lax.ppermute(value, axis, [(i, i ^ bits) for i in range(size)])]
    ppermute x27 -> x28, waiting for transfers between devices: 16.8 us -> 17.1 us  [swap(): return lax.ppermute(value, axis, [(i, i ^ bits) for i in range(size)])]
  transfers between devices with their start and end apart: 30 -> 31, of which waited for: 13 -> 13; matrix products, arithmetic and copies ran while one was open for 0% -> 0% of each run, Pallas kernels for 20% -> 20%
where the time goes in v11:
time: 67.8 us; the launch traced here: 67.6 us
  starting transfers between devices  30.8 us (45%)
  waiting for transfers between devices  17.1 us (25%)
  Pallas kernels  15.4 us (23%)
  local copies, waits for them, and re-layouts  2.92 us (4%)
  between operations  0.96 us (1%)
    ppermute x28, starting transfers between devices, swap(): return lax.ppermute(value, axis, [(i, i ^ bits) for i in range(size)])  24.6 us
    ppermute x28, waiting for transfers between devices, swap(): return lax.ppermute(value, axis, [(i, i ^ bits) for i in range(size)])  17.1 us
    pallas_call x8, Pallas kernels, call(): pl.pallas_call(kernel, out_shape=out_shape, in_specs=specs, out_specs=jax...  14.4 us
    ppermute x2, starting transfers between devices, shifted(): return lax.ppermute(value, axis, pairs)  4.98 us
    unnamed x22, local copies, waits for them, and re-layouts  2.9 us
  transfers between devices with their start and end apart: 31, of which 13 were waited for; matrix products, arithmetic and copies ran while one was open for 0% of the time, Pallas kernels for 20%

profile of v11, /device:TPU:0, one launch (start us, length us, event | category | flops | bytes accessed | tf_op | source)
XLA Modules:
  0.0 67.6 jit_solution(2734633666135288136)
XLA Ops:
  0.6 3.0 %collective-permute-start.1 = (bf16[432,128]{1,0:T(8,128)(2,1)}, bf16[432,128]{1,0:T(8,128)(2,1)S(1)}, u32[]{:S(2)}, u32[]{:S(2)}) collective-permute-start(bf16[432,128]{1,0:T(8,128)(2,1)} %w0.7), channel_id=1, source_target_pairs={{0,16},{8,24},{16,0},{24,8},{1,17},{9,25},{17,1},{25,9},{2,18},{10... | collective-permute-start | bytes 331784 | tf_op jit(solution)/shard_map/ppermute | solution.py:618
  3.8 0.4 collective-permute-start.5
  4.1 1.0 %shard_map.86 = bf16[3,32,2048]{2,1,0:T(8,128)(2,1)S(1)} custom-call(bf16[8,32,2048]{2,1,0:T(8,128)(2,1)} %bitcast.26), custom_call_target="tpu_custom_call" | custom-call | bytes 786432 | tf_op jit(solution)/shard_map/pallas_call | solution.py:99
  5.2 3.7 %collective-permute-start.3 = (bf16[3,32,2048]{2,1,0:T(8,128)(2,1)S(1)}, bf16[3,32,2048]{2,1,0:T(8,128)(2,1)S(1)}, u32[]{:S(2)}, u32[]{:S(2)}) collective-permute-start(bf16[3,32,2048]{2,1,0:T(8,128)(2,1)S(1)} %shard_map.86), channel_id=1, source_target_pairs={{0,1},{1,2},{2,3},{3,4},{4,5},{5,6},{6,7},{8,9},{9,10},{10,11},{11... | collective-permute-start | bytes 1179656 | tf_op jit(solution)/shard_map/ppermute | solution.py:624
  8.9 1.2 %copy-done = bf16[1,8,32,2048]{3,2,1,0:T(8,128)(2,1)S(1)} copy-done((bf16[1,8,32,2048]{3,2,1,0:T(8,128)(2,1)S(1)}, bf16[1,8,32,2048]{3,2,1,0:T(8,128)(2,1)}, u32[]{:S(2)}) %copy-start) | copy-done | bytes 1048600
  10.1 0.3 shard_map.84.sorted_ref
  10.6 1.3 %collective-permute-done.2.w3 = bf16[432,128]{1,0:T(8,128)(2,1)S(1)} collective-permute-done((bf16[432,128]{1,0:T(8,128)(2,1)S(1)}, bf16[432,128]{1,0:T(8,128)(2,1)S(1)}, u32[]{:S(2)}, u32[]{:S(2)}) %collective-permute-start.2) | collective-permute-done | bytes 110624 | tf_op jit(solution)/shard_map/ppermute | solution.py:618
  11.9 2.2 %shard_map.85 = (f32[768,128]{1,0:T(8,128)S(1)}, bf16[128,3456]{1,0:T(8,128)(2,1)S(1)}, bf16[2,256,128]{2,1,0:T(8,128)(2,1)S(1)}, bf16[256,128]{1,0:T(8,128)(2,1...) custom-call(s32[4]{0:T(128)S(1)} %broadcast_multiply_fusion.offsets, ...), custom_call_target="tpu_custom_call" | custom-call | flops 2875000064 | bytes 2015232 | tf_op jit(solution)/shard_map/pallas_call | solution.py:49
  14.1 0.9 %copy-done.7 = bf16[128,3456]{1,0:T(8,128)(2,1)} copy-done((bf16[128,3456]{1,0:T(8,128)(2,1)}, bf16[128,3456]{1,0:T(8,128)(2,1)S(1)}, u32[]{:S(2)}) %copy-start.7) | copy-done | bytes 884760
  15.0 0.7 %copy-done.9 = f32[768,128]{1,0:T(8,128)} copy-done((f32[768,128]{1,0:T(8,128)}, f32[768,128]{1,0:T(8,128)S(1)}, u32[]{:S(2)}) %copy-start.9) | copy-done | bytes 393240
  15.7 0.7 %collective-permute-done.4.w2 = bf16[864,256]{1,0:T(8,128)(2,1)S(1)} collective-permute-done((bf16[864,256]{1,0:T(8,128)(2,1)}, bf16[864,256]{1,0:T(8,128)(2,1)S(1)}, u32[]{:S(2)}, u32[]{:S(2)}) %collective-permute-start.4) | collective-permute-done | bytes 442400 | tf_op jit(solution)/shard_map/ppermute | solution.py:618
  16.5 1.8 %collective-permute-start.7 = (bf16[2,256,128]{2,1,0:T(8,128)(2,1)S(1)}, bf16[2,256,128]{2,1,0:T(8,128)(2,1)S(1)}, u32[]{:S(2)}, u32[]{:S(2)}) collective-permute-start(bf16[2,256,128]{2,1,0:T(8,128)(2,1)S(1)} %get-tuple-element.58.m0), channel_id=1, source_target_pairs={{0,16},{8,24},{16,0},{24,8},{1,17},{9,25},{17,1},{25,9},{2,18},{10... | collective-permute-start | bytes 393224 | tf_op jit(solution)/shard_map/ppermute | solution.py:618
  18.2 0.9 %shard_map.87 = (f32[512,128]{1,0:T(8,128)S(1)}, bf16[64,2304]{1,0:T(8,128)(2,1)S(1)}, bf16[3,3,256,128]{3,2,1,0:T(8,128)(2,1)S(1)}, bf16[2,256,128]{2,1,0:T(8,128)(2,1)S(1)}, bf16[2,256,128]{2,1,0:T(8,128)(2,1)S(1)}) custom-call(f32[1]{0:T(128)} %bitcast.1.alive, s32[1]{0:T(128)} %bitcast.2.side, bf16[3,32,2048]{2,1,0:T(8,128)(2,1)S(1)} %collective-permute-done.3.halo_ref, ...), custom_call_target="tpu_custom_call" | custom-call | flops 1724999936 | bytes 1179648 | tf_op jit(solution)/shard_map/pallas_call | solution.py:49
  19.1 0.3 collective-permute-start.11
  19.4 0.8 %collective-permute-start.9 = (bf16[2,256,128]{2,1,0:T(8,128)(2,1)S(1)}, bf16[2,256,128]{2,1,0:T(8,128)(2,1)S(1)}, u32[]{:S(2)}, u32[]{:S(2)}) collective-permute-start(bf16[2,256,128]{2,1,0:T(8,128)(2,1)S(1)} %get-tuple-element.71), channel_id=1, source_target_pairs={{0,16},{8,24},{16,0},{24,8},{1,17},{9,25},{17,1},{25,9},{2,18},{10... | collective-permute-start | bytes 393224 | tf_op jit(solution)/shard_map/ppermute | solution.py:618
  20.2 1.8 %shard_map.88 = (bf16[2,8,2048]{2,1,0:T(8,128)(2,1)}, bf16[128,256]{1,0:T(8,128)(2,1)S(1)}) custom-call(s32[4]{0:T(128)S(1)} %get-tuple-element.100.offsets, bf16[128,3456]{1,0:T(8,128)(2,1)S(1)} %copy-done.8, bf16[64,2304]{1,0:T(8,128)(2,1)S(1)} %get-tuple-element.54.lower_ref, bf16[2,8,2048]{2,1,0:T(8,128)(2,1)S(1)} %bitcast.31, ...), custom_call_target="tpu_custom_call" | custom-call | flops 1724999936 | bytes 3014656 | tf_op jit(solution)/shard_map/pallas_call | solution.py:49
  22.0 0.5 collective-permute-done.7.m2
  22.5 2.0 %collective-permute-start.8 = (bf16[128,256]{1,0:T(8,128)(2,1)S(1)}, bf16[128,256]{1,0:T(8,128)(2,1)S(1)}, u32[]{:S(2)}, u32[]{:S(2)}) collective-permute-start(bf16[128,256]{1,0:T(8,128)(2,1)S(1)} %get-tuple-element.59.delta_ref.d0), channel_id=1, source_target_pairs={{0,16},{8,24},{16,0},{24,8},{1,17},{9,25},{17,1},{25,9},{2,18},{10... | collective-permute-start | bytes 196616 | tf_op jit(solution)/shard_map/ppermute | solution.py:618
  24.5 0.2 collective-permute-start.12
  24.7 3.0 %shard_map.89 = (bf16[768,128]{1,0:T(8,128)(2,1)S(1)}, f32[256,128]{1,0:T(8,128)S(1)}, bf16[512,128]{1,0:T(8,128)(2,1)S(1)}, bf16[8,56,128]{2,1,0:T(8,128)(2,1)S...) custom-call(s32[4]{0:T(128)S(1)} %get-tuple-element.100.offsets, ...), custom_call_target="tpu_custom_call" | custom-call | flops 4024999936 | bytes 4653056 | tf_op jit(solution)/shard_map/pallas_call | solution.py:49
  27.8 0.4 collective-permute-start.16
  28.1 0.2 collective-permute-start.14
  28.3 0.3 collective-permute-start.13
  28.6 0.2 collective-permute-start.15
  28.9 0.3 collective-permute-start.18
  29.2 0.3 collective-permute-done.14.m1
  29.5 0.4 collective-permute-done.15.d3
  29.9 1.8 %shard_map.90 = bf16[8,216,128]{2,1,0:T(8,128)(2,1)S(1)} custom-call(s32[1]{0:T(128)} %bitcast.5.data, s32[4,33]{1,0:T(4,128)S(1)} %copy-done.4, s32[8]{0:T(128)S(1)} %fusion.12.order, bf16[2,256,128]{2,1,0:T(8,128)(2,1)S(1)} %get-tuple-element.65.e0, bf16[2,256,128]{2,1,0:T(8,128)(2,1)S(1)} %collective-permute-done.11.e1, ...), custom_call_target="tpu_custom_call" | custom-call | flops 2300000000 | bytes 1310720 | tf_op jit(solution)/shard_map/pallas_call | solution.py:49
  31.8 1.2 %collective-permute-start.17 = (bf16[3,272,128]{2,1,0:T(8,128)(2,1)S(1)}, bf16[3,272,128]{2,1,0:T(8,128)(2,1)S(1)}, u32[]{:S(2)}, u32[]{:S(2)}) collective-permute-start(bf16[3,272,128]{2,1,0:T(8,128)(2,1)S(1)} %fusion), channel_id=1, source_target_pairs={{0,1},{1,0},{2,3},{3,2},{4,5},{5,4},{6,7},{7,6},{8,9},{9,8},{10,11... | collective-permute-start | bytes 626696 | tf_op jit(solution)/shard_map/ppermute | solution.py:618
  33.0 1.2 %collective-permute-start.19 = (bf16[4,56,128]{2,1,0:T(8,128)(2,1)S(1)}, bf16[4,56,128]{2,1,0:T(8,128)(2,1)S(1)}, u32[]{:S(2)}, u32[]{:S(2)}) collective-permute-start(bf16[4,56,128]{2,1,0:T(8,128)(2,1)S(1)} %get-tuple-element.94), channel_id=1, source_target_pairs={{0,16},{8,24},{16,0},{24,8},{1,17},{9,25},{17,1},{25,9},{2,18},{10... | collective-permute-start | bytes 172040 | tf_op jit(solution)/shard_map/ppermute | solution.py:618
  34.1 1.3 %collective-permute-start.20 = (bf16[4,56,128]{2,1,0:T(8,128)(2,1)S(1)}, bf16[4,56,128]{2,1,0:T(8,128)(2,1)S(1)}, u32[]{:S(2)}, u32[]{:S(2)}) collective-permute-start(bf16[4,56,128]{2,1,0:T(8,128)(2,1)S(1)} %get-tuple-element.95), channel_id=1, source_target_pairs={{0,17},{1,16},{2,19},{3,18},{4,21},{5,20},{6,23},{7,22},{8,25},{9,... | collective-permute-start | bytes 172040 | tf_op jit(solution)/shard_map/ppermute | solution.py:703
  35.4 1.1 %collective-permute-start.24 = (bf16[1,272,128]{2,1,0:T(8,128)(2,1)S(1)}, bf16[1,272,128]{2,1,0:T(8,128)(2,1)S(1)}, u32[]{:S(2)}, u32[]{:S(2)}) collective-permute-start(bf16[1,272,128]{2,1,0:T(8,128)(2,1)S(1)} %pad_maximum_fusion.1), channel_id=1, source_target_pairs={{0,1},{1,0},{2,3},{3,2},{4,5},{5,4},{6,7},{7,6},{8,9},{9,8},{10,11... | collective-permute-start | bytes 208904 | tf_op jit(solution)/shard_map/ppermute | solution.py:618
  36.6 1.3 %collective-permute-start.25 = (bf16[512,128]{1,0:T(8,128)(2,1)S(1)}, bf16[512,128]{1,0:T(8,128)(2,1)S(1)}, u32[]{:S(2)}, u32[]{:S(2)}) collective-permute-start(bf16[512,128]{1,0:T(8,128)(2,1)S(1)} %get-tuple-element.84), channel_id=1, source_target_pairs={{1,0},{2,1},{3,2},{4,3},{5,4},{6,5},{7,6},{9,8},{10,9},{11,10},{12... | collective-permute-start | bytes 393224 | tf_op jit(solution)/shard_map/ppermute | solution.py:624
  37.8 3.2 %collective-permute-done.17 = bf16[3,272,128]{2,1,0:T(8,128)(2,1)S(1)} collective-permute-done((bf16[3,272,128]{2,1,0:T(8,128)(2,1)S(1)}, bf16[3,272,128]{2,1,0:T(8,128)(2,1)S(1)}, u32[]{:S(2)}, u32[]{:S(2)}) %collective-permute-start.17) | collective-permute-done | bytes 208928 | tf_op jit(solution)/shard_map/ppermute | solution.py:618
  41.2 2.1 %collective-permute-start.21 = (bf16[272,128]{1,0:T(8,128)(2,1)S(1)}, bf16[272,128]{1,0:T(8,128)(2,1)S(1)}, u32[]{:S(2)}, u32[]{:S(2)}) collective-permute-start(bf16[272,128]{1,0:T(8,128)(2,1)S(1)} %get-tuple-element.97), channel_id=1, source_target_pairs={{0,2},{1,3},{2,0},{3,1},{4,6},{5,7},{6,4},{7,5},{8,10},{9,11},{10,... | collective-permute-start | bytes 208904 | tf_op jit(solution)/shard_map/ppermute | solution.py:618
  43.3 2.6 %collective-permute-start.22 = (bf16[272,128]{1,0:T(8,128)(2,1)S(1)}, bf16[272,128]{1,0:T(8,128)(2,1)S(1)}, u32[]{:S(2)}, u32[]{:S(2)}) collective-permute-start(bf16[272,128]{1,0:T(8,128)(2,1)S(1)} %get-tuple-element.98), channel_id=1, source_target_pairs={{0,4},{1,5},{2,6},{3,7},{4,0},{5,1},{6,2},{7,3},{8,12},{9,13},{10,... | collective-permute-start | bytes 208904 | tf_op jit(solution)/shard_map/ppermute | solution.py:618
  45.9 0.5 collective-permute-done.21
  46.3 4.1 %collective-permute-done.22 = bf16[272,128]{1,0:T(8,128)(2,1)S(1)} collective-permute-done((bf16[272,128]{1,0:T(8,128)(2,1)S(1)}, bf16[272,128]{1,0:T(8,128)(2,1)S(1)}, u32[]{:S(2)}, u32[]{:S(2)}) %collective-permute-start.22) | collective-permute-done | bytes 69664 | tf_op jit(solution)/shard_map/ppermute | solution.py:618
  50.4 1.8 %collective-permute-done.23 = bf16[272,128]{1,0:T(8,128)(2,1)S(1)} collective-permute-done((bf16[272,128]{1,0:T(8,128)(2,1)S(1)}, bf16[272,128]{1,0:T(8,128)(2,1)S(1)}, u32[]{:S(2)}, u32[]{:S(2)}) %collective-permute-start.23) | collective-permute-done | bytes 69664 | tf_op jit(solution)/shard_map/ppermute | solution.py:618
  52.4 1.4 %collective-permute-start.28 = (bf16[272,128]{1,0:T(8,128)(2,1)S(1)}, bf16[272,128]{1,0:T(8,128)(2,1)S(1)}, u32[]{:S(2)}, u32[]{:S(2)}) collective-permute-start(bf16[272,128]{1,0:T(8,128)(2,1)S(1)} %fusion.4.refs_0_), channel_id=1, source_target_pairs={{0,4},{1,5},{2,6},{3,7},{4,0},{5,1},{6,2},{7,3},{8,12},{9,13},{10,... | collective-permute-start | bytes 208904 | tf_op jit(solution)/shard_map/ppermute | solution.py:618
  53.8 2.9 %collective-permute-start.29 = (bf16[272,128]{1,0:T(8,128)(2,1)S(1)}, bf16[272,128]{1,0:T(8,128)(2,1)S(1)}, u32[]{:S(2)}, u32[]{:S(2)}) collective-permute-start(bf16[272,128]{1,0:T(8,128)(2,1)S(1)} %fusion.4.refs_0_), channel_id=1, source_target_pairs={{0,6},{1,7},{2,4},{3,5},{4,2},{5,3},{6,0},{7,1},{8,14},{9,15},{10,... | collective-permute-start | bytes 208904 | tf_op jit(solution)/shard_map/ppermute | solution.py:618
  56.8 0.7 %collective-permute-start.26 = (bf16[272,128]{1,0:T(8,128)(2,1)S(1)}, bf16[272,128]{1,0:T(8,128)(2,1)S(1)}, u32[]{:S(2)}, u32[]{:S(2)}) collective-permute-start(bf16[272,128]{1,0:T(8,128)(2,1)S(1)} %fusion.4.refs_0_), channel_id=1, source_target_pairs={{0,1},{1,0},{2,3},{3,2},{4,5},{5,4},{6,7},{7,6},{8,9},{9,8},{10,11... | collective-permute-start | bytes 208904 | tf_op jit(solution)/shard_map/ppermute | solution.py:618
  57.7 2.3 %collective-permute-done.29.refs_3_ = bf16[272,128]{1,0:T(8,128)(2,1)S(1)} collective-permute-done((bf16[272,128]{1,0:T(8,128)(2,1)S(1)}, bf16[272,128]{1,0:T(8,128)(2,1)S(1)}, u32[]{:S(2)}, u32[]{:S(2)}) %collective-permute-start.29) | collective-permute-done | bytes 69664 | tf_op jit(solution)/shard_map/ppermute | solution.py:618
  60.0 1.3 %collective-permute-start.30 = (bf16[3,272,128]{2,1,0:T(8,128)(2,1)S(1)}, bf16[3,272,128]{2,1,0:T(8,128)(2,1)S(1)}, u32[]{:S(2)}, u32[]{:S(2)}) collective-permute-start(bf16[3,272,128]{2,1,0:T(8,128)(2,1)S(1)} %pad_maximum_fusion), channel_id=1, source_target_pairs={{0,1},{1,0},{2,3},{3,2},{4,5},{5,4},{6,7},{7,6},{8,9},{9,8},{10,11... | collective-permute-start | bytes 626696 | tf_op jit(solution)/shard_map/ppermute | solution.py:618
  61.3 0.4 collective-permute-done.26.refs_4_
  61.7 2.8 %shard_map.91 = bf16[8,32,2048]{2,1,0:T(8,128)(2,1)} custom-call(s32[4]{0:T(128)S(1)} %broadcast_multiply_fusion.offsets, bf16[768,128]{1,0:T(8,128)(2,1)S(1)} %get-tuple-element.63.low_ref, f32[256,128]{1,0:T(8,128)S(1)} %get-tuple-element.64.last_ref, f32[768,128]{1,0:T(8,128)S(1)} %copy-done.10, bf16[512,128]{1,0:T(8,128)(2,1)S(1)} %collective-permute-done.25.upper_ref, ...), custom_call_target="tpu_custom_call" | custom-call | flops 3449999872 | bytes 1294336 | tf_op jit(solution)/shard_map/pallas_call | solution.py:49
  64.5 1.4 %collective-permute-done.30.refs_5_ = bf16[3,272,128]{2,1,0:T(8,128)(2,1)S(1)} collective-permute-done((bf16[3,272,128]{2,1,0:T(8,128)(2,1)S(1)}, bf16[3,272,128]{2,1,0:T(8,128)(2,1)S(1)}, u32[]{:S(2)}, u32[]{:S(2)}) %collective-permute-start.30) | collective-permute-done | bytes 208928 | tf_op jit(solution)/shard_map/ppermute | solution.py:618
  65.9 1.7 %shard_map.92 = (f32[432,128]{1,0:T(8,128)}, f32[864,256]{1,0:T(8,128)}) custom-call(s32[8]{0:T(128)S(1)} %fusion.12.order, bf16[272,128]{1,0:T(8,128)(2,1)S(1)} %fusion.4.refs_0_, bf16[272,128]{1,0:T(8,128)(2,1)S(1)} %collective-permute-done.27.refs_1_, bf16[272,128]{1,0:T(8,128)(2,1)S(1)} %collective-permute-done.28.refs_2_, ...), custom_call_target="tpu_custom_call" | custom-call | flops 1150000000 | bytes 557056 | tf_op jit(solution)/shard_map/pallas_call | solution.py:49
  (60 shorter events, 0.9 us)
Async XLA Ops:
  0.6 9.8 %collective-permute-start.1 = (bf16[432,128]{1,0:T(8,128)(2,1)}, bf16[432,128]{1,0:T(8,128)(2,1)S(1)}, u32[]{:S(2)}, u32[]{:S(2)}) collective-permute-start(bf16[432,128]{1,0:T(8,128)(2,1)} %w0.7), channel_id=1, source_target_pairs={{0,16},{8,24},{16,0},{24,8},{1,17},{9,25},{17,1},{25,9},{2,18},{10... | collective-permute-start | bytes 331784 | tf_op jit(solution)/shard_map/ppermute | solution.py:618
  3.6 6.9 %collective-permute-start = (bf16[432,128]{1,0:T(8,128)(2,1)}, bf16[432,128]{1,0:T(8,128)(2,1)S(1)}, u32[]{:S(2)}, u32[]{:S(2)}) collective-permute-start(bf16[432,128]{1,0:T(8,128)(2,1)} %w0.7), channel_id=1, source_target_pairs={{0,8},{8,0},{16,24},{24,16},{1,9},{9,1},{17,25},{25,17},{2,10},{10... | collective-permute-start | bytes 331784 | tf_op jit(solution)/shard_map/ppermute | solution.py:618
  3.6 12.8 %collective-permute-start.4 = (bf16[864,256]{1,0:T(8,128)(2,1)}, bf16[864,256]{1,0:T(8,128)(2,1)S(1)}, u32[]{:S(2)}, u32[]{:S(2)}) collective-permute-start(bf16[864,256]{1,0:T(8,128)(2,1)} %w0.6), channel_id=1, source_target_pairs={{0,16},{8,24},{16,0},{24,8},{1,17},{9,25},{17,1},{25,9},{2,18},{10... | collective-permute-start | bytes 1327112 | tf_op jit(solution)/shard_map/ppermute | solution.py:618
  3.8 16.4 %collective-permute-start.5 = (bf16[864,256]{1,0:T(8,128)(2,1)}, bf16[864,256]{1,0:T(8,128)(2,1)S(1)}, u32[]{:S(2)}, u32[]{:S(2)}) collective-permute-start(bf16[864,256]{1,0:T(8,128)(2,1)} %w0.6), channel_id=1, source_target_pairs={{0,8},{8,0},{16,24},{24,16},{1,9},{9,1},{17,25},{25,17},{2,10},{10... | collective-permute-start | bytes 1327112 | tf_op jit(solution)/shard_map/ppermute | solution.py:618
  5.2 13.1 %collective-permute-start.3 = (bf16[3,32,2048]{2,1,0:T(8,128)(2,1)S(1)}, bf16[3,32,2048]{2,1,0:T(8,128)(2,1)S(1)}, u32[]{:S(2)}, u32[]{:S(2)}) collective-permute-start(bf16[3,32,2048]{2,1,0:T(8,128)(2,1)S(1)} %shard_map.86), channel_id=1, source_target_pairs={{0,1},{1,2},{2,3},{3,4},{4,5},{5,6},{6,7},{8,9},{9,10},{10,11},{11... | collective-permute-start | bytes 1179656 | tf_op jit(solution)/shard_map/ppermute | solution.py:624
  8.9 1.2 %copy-start = (bf16[1,8,32,2048]{3,2,1,0:T(8,128)(2,1)S(1)}, bf16[1,8,32,2048]{3,2,1,0:T(8,128)(2,1)}, u32[]{:S(2)}) copy-start(bf16[1,8,32,2048]{3,2,1,0:T(8,128)(2,1)} %param.5) | copy-start | bytes 3145732
  10.1 1.8 %copy-start.2 = (bf16[432,128]{1,0:T(8,128)(2,1)S(1)}, bf16[432,128]{1,0:T(8,128)(2,1)}, u32[]{:S(2)}) copy-start(bf16[432,128]{1,0:T(8,128)(2,1)} %w0.7) | copy-start | bytes 331780
  10.5 3.6 %copy-start.5 = (bf16[8,3,256,128]{3,2,1,0:T(8,128)(2,1)}, bf16[8,3,256,128]{3,2,1,0:T(8,128)(2,1)S(1)}, u32[]{:S(2)}) copy-start(bf16[8,3,256,128]{3,2,1,0:T(8,128)(2,1)S(1)} %shard_map.84.sorted_ref) | copy-start | bytes 4718596
  10.5 1.4 %collective-permute-start.2 = (bf16[432,128]{1,0:T(8,128)(2,1)S(1)}, bf16[432,128]{1,0:T(8,128)(2,1)S(1)}, u32[]{:S(2)}, u32[]{:S(2)}) collective-permute-start(bf16[432,128]{1,0:T(8,128)(2,1)S(1)} %collective-permute-done.1.w2), channel_id=1, source_target_pairs={{0,8},{8,0},{16,24},{24,16},{1,9},{9,1},{17,25},{25,17},{2,10},{10... | collective-permute-start | bytes 331784 | tf_op jit(solution)/shard_map/ppermute | solution.py:618
  14.0 0.9 %copy-start.7 = (bf16[128,3456]{1,0:T(8,128)(2,1)}, bf16[128,3456]{1,0:T(8,128)(2,1)S(1)}, u32[]{:S(2)}) copy-start(bf16[128,3456]{1,0:T(8,128)(2,1)S(1)} %get-tuple-element.49.upper_ref) | copy-start | bytes 2654212
  15.0 0.7 %copy-start.9 = (f32[768,128]{1,0:T(8,128)}, f32[768,128]{1,0:T(8,128)S(1)}, u32[]{:S(2)}) copy-start(f32[768,128]{1,0:T(8,128)S(1)} %get-tuple-element.61.slope_ref) | copy-start | bytes 1179652
  16.4 3.7 %collective-permute-start.6 = (bf16[864,256]{1,0:T(8,128)(2,1)S(1)}, bf16[864,256]{1,0:T(8,128)(2,1)S(1)}, u32[]{:S(2)}, u32[]{:S(2)}) collective-permute-start(bf16[864,256]{1,0:T(8,128)(2,1)S(1)} %collective-permute-done.4.w2), channel_id=1, source_target_pairs={{0,8},{8,0},{16,24},{24,16},{1,9},{9,1},{17,25},{25,17},{2,10},{10... | collective-permute-start | bytes 1327112 | tf_op jit(solution)/shard_map/ppermute | solution.py:618
  16.5 6.1 %collective-permute-start.7 = (bf16[2,256,128]{2,1,0:T(8,128)(2,1)S(1)}, bf16[2,256,128]{2,1,0:T(8,128)(2,1)S(1)}, u32[]{:S(2)}, u32[]{:S(2)}) collective-permute-start(bf16[2,256,128]{2,1,0:T(8,128)(2,1)S(1)} %get-tuple-element.58.m0), channel_id=1, source_target_pairs={{0,16},{8,24},{16,0},{24,8},{1,17},{9,25},{17,1},{25,9},{2,18},{10... | collective-permute-start | bytes 393224 | tf_op jit(solution)/shard_map/ppermute | solution.py:618
  18.2 1.9 %copy-start.1 = (bf16[864,256]{1,0:T(8,128)(2,1)S(1)}, bf16[864,256]{1,0:T(8,128)(2,1)}, u32[]{:S(2)}) copy-start(bf16[864,256]{1,0:T(8,128)(2,1)} %w0.6) | copy-start | bytes 1327108
  18.2 1.9 %copy-start.3 = (bf16[1,2,8,2048]{3,2,1,0:T(8,128)(2,1)S(1)}, bf16[1,2,8,2048]{3,2,1,0:T(8,128)(2,1)}, u32[]{:S(2)}) copy-start(bf16[1,2,8,2048]{3,2,1,0:T(8,128)(2,1)} %param.8) | copy-start | bytes 196612
  18.2 2.0 %copy-start.8 = (bf16[128,3456]{1,0:T(8,128)(2,1)S(1)}, bf16[128,3456]{1,0:T(8,128)(2,1)}, u32[]{:S(2)}) copy-start(bf16[128,3456]{1,0:T(8,128)(2,1)} %copy-done.7) | copy-start | bytes 2654212
  19.1 8.6 %collective-permute-start.11 = (bf16[2,256,128]{2,1,0:T(8,128)(2,1)S(1)}, bf16[2,256,128]{2,1,0:T(8,128)(2,1)S(1)}, u32[]{:S(2)}, u32[]{:S(2)}) collective-permute-start(bf16[2,256,128]{2,1,0:T(8,128)(2,1)S(1)} %get-tuple-element.65.e0), channel_id=1, source_target_pairs={{0,8},{8,0},{16,24},{24,16},{1,9},{9,1},{17,25},{25,17},{2,10},{10... | collective-permute-start | bytes 393224 | tf_op jit(solution)/shard_map/ppermute | solution.py:618
  19.4 8.4 %collective-permute-start.9 = (bf16[2,256,128]{2,1,0:T(8,128)(2,1)S(1)}, bf16[2,256,128]{2,1,0:T(8,128)(2,1)S(1)}, u32[]{:S(2)}, u32[]{:S(2)}) collective-permute-start(bf16[2,256,128]{2,1,0:T(8,128)(2,1)S(1)} %get-tuple-element.71), channel_id=1, source_target_pairs={{0,16},{8,24},{16,0},{24,8},{1,17},{9,25},{17,1},{25,9},{2,18},{10... | collective-permute-start | bytes 393224 | tf_op jit(solution)/shard_map/ppermute | solution.py:618
  20.2 4.6 %copy-start.6 = (bf16[8,3,256,128]{3,2,1,0:T(8,128)(2,1)S(1)}, bf16[8,3,256,128]{3,2,1,0:T(8,128)(2,1)}, u32[]{:S(2)}) copy-start(bf16[8,3,256,128]{3,2,1,0:T(8,128)(2,1)} %copy-done.5) | copy-start | bytes 4718596
  20.2 4.6 %copy-start.10 = (f32[768,128]{1,0:T(8,128)S(1)}, f32[768,128]{1,0:T(8,128)}, u32[]{:S(2)}) copy-start(f32[768,128]{1,0:T(8,128)} %copy-done.9) | copy-start | bytes 1179652
  22.5 5.2 %collective-permute-start.10 = (bf16[128,256]{1,0:T(8,128)(2,1)S(1)}, bf16[128,256]{1,0:T(8,128)(2,1)S(1)}, u32[]{:S(2)}, u32[]{:S(2)}) collective-permute-start(bf16[128,256]{1,0:T(8,128)(2,1)S(1)} %get-tuple-element.59.delta_ref.d0), channel_id=1, source_target_pairs={{0,8},{8,0},{16,24},{24,16},{1,9},{9,1},{17,25},{25,17},{2,10},{10... | collective-permute-start | bytes 196616 | tf_op jit(solution)/shard_map/ppermute | solution.py:618
  22.5 5.2 %collective-permute-start.8 = (bf16[128,256]{1,0:T(8,128)(2,1)S(1)}, bf16[128,256]{1,0:T(8,128)(2,1)S(1)}, u32[]{:S(2)}, u32[]{:S(2)}) collective-permute-start(bf16[128,256]{1,0:T(8,128)(2,1)S(1)} %get-tuple-element.59.delta_ref.d0), channel_id=1, source_target_pairs={{0,16},{8,24},{16,0},{24,8},{1,17},{9,25},{17,1},{25,9},{2,18},{10... | collective-permute-start | bytes 196616 | tf_op jit(solution)/shard_map/ppermute | solution.py:618
  24.5 3.3 %collective-permute-start.12 = (bf16[2,256,128]{2,1,0:T(8,128)(2,1)S(1)}, bf16[2,256,128]{2,1,0:T(8,128)(2,1)S(1)}, u32[]{:S(2)}, u32[]{:S(2)}) collective-permute-start(bf16[2,256,128]{2,1,0:T(8,128)(2,1)S(1)} %collective-permute-done.7.m2), channel_id=1, source_target_pairs={{0,8},{8,0},{16,24},{24,16},{1,9},{9,1},{17,25},{25,17},{2,10},{10... | collective-permute-start | bytes 393224 | tf_op jit(solution)/shard_map/ppermute | solution.py:618
  24.7 5.2 %copy-start.4 = (s32[4,33]{1,0:T(4,128)S(1)}, s32[4,33]{1,0:T(4,128)}, u32[]{:S(2)}) copy-start(s32[4,33]{1,0:T(4,128)} %constant.48.clone.table) | copy-start | bytes 1588
  27.8 1.4 %collective-permute-start.16 = (bf16[8,56,128]{2,1,0:T(8,128)(2,1)S(1)}, bf16[8,56,128]{2,1,0:T(8,128)(2,1)S(1)}, u32[]{:S(2)}, u32[]{:S(2)}) collective-permute-start(bf16[8,56,128]{2,1,0:T(8,128)(2,1)S(1)} %get-tuple-element.81), channel_id=1, source_target_pairs={{0,8},{8,0},{16,24},{24,16},{1,9},{9,1},{17,25},{25,17},{2,10},{10... | collective-permute-start | bytes 344072 | tf_op jit(solution)/shard_map/ppermute | solution.py:618
  28.1 1.3 %collective-permute-start.14 = (bf16[2,256,128]{2,1,0:T(8,128)(2,1)S(1)}, bf16[2,256,128]{2,1,0:T(8,128)(2,1)S(1)}, u32[]{:S(2)}, u32[]{:S(2)}) collective-permute-start(bf16[2,256,128]{2,1,0:T(8,128)(2,1)S(1)} %get-tuple-element.58.m0), channel_id=1, source_target_pairs={{0,8},{8,0},{16,24},{24,16},{1,9},{9,1},{17,25},{25,17},{2,10},{10... | collective-permute-start | bytes 393224 | tf_op jit(solution)/shard_map/ppermute | solution.py:618
  28.3 1.5 %collective-permute-start.13 = (bf16[2,256,128]{2,1,0:T(8,128)(2,1)S(1)}, bf16[2,256,128]{2,1,0:T(8,128)(2,1)S(1)}, u32[]{:S(2)}, u32[]{:S(2)}) collective-permute-start(bf16[2,256,128]{2,1,0:T(8,128)(2,1)S(1)} %collective-permute-done.9.e2), channel_id=1, source_target_pairs={{0,8},{8,0},{16,24},{24,16},{1,9},{9,1},{17,25},{25,17},{2,10},{10... | collective-permute-start | bytes 393224 | tf_op jit(solution)/shard_map/ppermute | solution.py:618
  28.6 1.3 %collective-permute-start.15 = (bf16[128,256]{1,0:T(8,128)(2,1)S(1)}, bf16[128,256]{1,0:T(8,128)(2,1)S(1)}, u32[]{:S(2)}, u32[]{:S(2)}) collective-permute-start(bf16[128,256]{1,0:T(8,128)(2,1)S(1)} %collective-permute-done.8.d2), channel_id=1, source_target_pairs={{0,8},{8,0},{16,24},{24,16},{1,9},{9,1},{17,25},{25,17},{2,10},{10... | collective-permute-start | bytes 196616 | tf_op jit(solution)/shard_map/ppermute | solution.py:618
  28.9 4.1 %collective-permute-start.18 = (bf16[8,56,128]{2,1,0:T(8,128)(2,1)S(1)}, bf16[8,56,128]{2,1,0:T(8,128)(2,1)S(1)}, u32[]{:S(2)}, u32[]{:S(2)}) collective-permute-start(bf16[8,56,128]{2,1,0:T(8,128)(2,1)S(1)} %get-tuple-element.83), channel_id=1, source_target_pairs={{0,8},{8,0},{16,24},{24,16},{1,9},{9,1},{17,25},{25,17},{2,10},{10... | collective-permute-start | bytes 344072 | tf_op jit(solution)/shard_map/ppermute | solution.py:618
  31.8 9.3 %collective-permute-start.17 = (bf16[3,272,128]{2,1,0:T(8,128)(2,1)S(1)}, bf16[3,272,128]{2,1,0:T(8,128)(2,1)S(1)}, u32[]{:S(2)}, u32[]{:S(2)}) collective-permute-start(bf16[3,272,128]{2,1,0:T(8,128)(2,1)S(1)} %fusion), channel_id=1, source_target_pairs={{0,1},{1,0},{2,3},{3,2},{4,5},{5,4},{6,7},{7,6},{8,9},{9,8},{10,11... | collective-permute-start | bytes 626696 | tf_op jit(solution)/shard_map/ppermute | solution.py:618
  33.0 8.1 %collective-permute-start.19 = (bf16[4,56,128]{2,1,0:T(8,128)(2,1)S(1)}, bf16[4,56,128]{2,1,0:T(8,128)(2,1)S(1)}, u32[]{:S(2)}, u32[]{:S(2)}) collective-permute-start(bf16[4,56,128]{2,1,0:T(8,128)(2,1)S(1)} %get-tuple-element.94), channel_id=1, source_target_pairs={{0,16},{8,24},{16,0},{24,8},{1,17},{9,25},{17,1},{25,9},{2,18},{10... | collective-permute-start | bytes 172040 | tf_op jit(solution)/shard_map/ppermute | solution.py:618
  34.1 7.0 %collective-permute-start.20 = (bf16[4,56,128]{2,1,0:T(8,128)(2,1)S(1)}, bf16[4,56,128]{2,1,0:T(8,128)(2,1)S(1)}, u32[]{:S(2)}, u32[]{:S(2)}) collective-permute-start(bf16[4,56,128]{2,1,0:T(8,128)(2,1)S(1)} %get-tuple-element.95), channel_id=1, source_target_pairs={{0,17},{1,16},{2,19},{3,18},{4,21},{5,20},{6,23},{7,22},{8,25},{9,... | collective-permute-start | bytes 172040 | tf_op jit(solution)/shard_map/ppermute | solution.py:703
  35.4 10.4 %collective-permute-start.24 = (bf16[1,272,128]{2,1,0:T(8,128)(2,1)S(1)}, bf16[1,272,128]{2,1,0:T(8,128)(2,1)S(1)}, u32[]{:S(2)}, u32[]{:S(2)}) collective-permute-start(bf16[1,272,128]{2,1,0:T(8,128)(2,1)S(1)} %pad_maximum_fusion.1), channel_id=1, source_target_pairs={{0,1},{1,0},{2,3},{3,2},{4,5},{5,4},{6,7},{7,6},{8,9},{9,8},{10,11... | collective-permute-start | bytes 208904 | tf_op jit(solution)/shard_map/ppermute | solution.py:618
  36.6 9.3 %collective-permute-start.25 = (bf16[512,128]{1,0:T(8,128)(2,1)S(1)}, bf16[512,128]{1,0:T(8,128)(2,1)S(1)}, u32[]{:S(2)}, u32[]{:S(2)}) collective-permute-start(bf16[512,128]{1,0:T(8,128)(2,1)S(1)} %get-tuple-element.84), channel_id=1, source_target_pairs={{1,0},{2,1},{3,2},{4,3},{5,4},{6,5},{7,6},{9,8},{10,9},{11,10},{12... | collective-permute-start | bytes 393224 | tf_op jit(solution)/shard_map/ppermute | solution.py:624
  41.2 5.1 %collective-permute-start.21 = (bf16[272,128]{1,0:T(8,128)(2,1)S(1)}, bf16[272,128]{1,0:T(8,128)(2,1)S(1)}, u32[]{:S(2)}, u32[]{:S(2)}) collective-permute-start(bf16[272,128]{1,0:T(8,128)(2,1)S(1)} %get-tuple-element.97), channel_id=1, source_target_pairs={{0,2},{1,3},{2,0},{3,1},{4,6},{5,7},{6,4},{7,5},{8,10},{9,11},{10,... | collective-permute-start | bytes 208904 | tf_op jit(solution)/shard_map/ppermute | solution.py:618
  43.3 7.1 %collective-permute-start.22 = (bf16[272,128]{1,0:T(8,128)(2,1)S(1)}, bf16[272,128]{1,0:T(8,128)(2,1)S(1)}, u32[]{:S(2)}, u32[]{:S(2)}) collective-permute-start(bf16[272,128]{1,0:T(8,128)(2,1)S(1)} %get-tuple-element.98), channel_id=1, source_target_pairs={{0,4},{1,5},{2,6},{3,7},{4,0},{5,1},{6,2},{7,3},{8,12},{9,13},{10,... | collective-permute-start | bytes 208904 | tf_op jit(solution)/shard_map/ppermute | solution.py:618
  45.9 6.4 %collective-permute-start.23 = (bf16[272,128]{1,0:T(8,128)(2,1)S(1)}, bf16[272,128]{1,0:T(8,128)(2,1)S(1)}, u32[]{:S(2)}, u32[]{:S(2)}) collective-permute-start(bf16[272,128]{1,0:T(8,128)(2,1)S(1)} %get-tuple-element.96), channel_id=1, source_target_pairs={{0,6},{1,7},{2,4},{3,5},{4,2},{5,3},{6,0},{7,1},{8,14},{9,15},{10,... | collective-permute-start | bytes 208904 | tf_op jit(solution)/shard_map/ppermute | solution.py:618
  52.3 5.2 %collective-permute-start.27 = (bf16[272,128]{1,0:T(8,128)(2,1)S(1)}, bf16[272,128]{1,0:T(8,128)(2,1)S(1)}, u32[]{:S(2)}, u32[]{:S(2)}) collective-permute-start(bf16[272,128]{1,0:T(8,128)(2,1)S(1)} %fusion.4.refs_0_), channel_id=1, source_target_pairs={{0,2},{1,3},{2,0},{3,1},{4,6},{5,7},{6,4},{7,5},{8,10},{9,11},{10,... | collective-permute-start | bytes 208904 | tf_op jit(solution)/shard_map/ppermute | solution.py:618
  52.4 5.3 %collective-permute-start.28 = (bf16[272,128]{1,0:T(8,128)(2,1)S(1)}, bf16[272,128]{1,0:T(8,128)(2,1)S(1)}, u32[]{:S(2)}, u32[]{:S(2)}) collective-permute-start(bf16[272,128]{1,0:T(8,128)(2,1)S(1)} %fusion.4.refs_0_), channel_id=1, source_target_pairs={{0,4},{1,5},{2,6},{3,7},{4,0},{5,1},{6,2},{7,3},{8,12},{9,13},{10,... | collective-permute-start | bytes 208904 | tf_op jit(solution)/shard_map/ppermute | solution.py:618
  53.8 6.2 %collective-permute-start.29 = (bf16[272,128]{1,0:T(8,128)(2,1)S(1)}, bf16[272,128]{1,0:T(8,128)(2,1)S(1)}, u32[]{:S(2)}, u32[]{:S(2)}) collective-permute-start(bf16[272,128]{1,0:T(8,128)(2,1)S(1)} %fusion.4.refs_0_), channel_id=1, source_target_pairs={{0,6},{1,7},{2,4},{3,5},{4,2},{5,3},{6,0},{7,1},{8,14},{9,15},{10,... | collective-permute-start | bytes 208904 | tf_op jit(solution)/shard_map/ppermute | solution.py:618
  56.8 4.9 %collective-permute-start.26 = (bf16[272,128]{1,0:T(8,128)(2,1)S(1)}, bf16[272,128]{1,0:T(8,128)(2,1)S(1)}, u32[]{:S(2)}, u32[]{:S(2)}) collective-permute-start(bf16[272,128]{1,0:T(8,128)(2,1)S(1)} %fusion.4.refs_0_), channel_id=1, source_target_pairs={{0,1},{1,0},{2,3},{3,2},{4,5},{5,4},{6,7},{7,6},{8,9},{9,8},{10,11... | collective-permute-start | bytes 208904 | tf_op jit(solution)/shard_map/ppermute | solution.py:618
  60.0 5.9 %collective-permute-start.30 = (bf16[3,272,128]{2,1,0:T(8,128)(2,1)S(1)}, bf16[3,272,128]{2,1,0:T(8,128)(2,1)S(1)}, u32[]{:S(2)}, u32[]{:S(2)}) collective-permute-start(bf16[3,272,128]{2,1,0:T(8,128)(2,1)S(1)} %pad_maximum_fusion), channel_id=1, source_target_pairs={{0,1},{1,0},{2,3},{3,2},{4,5},{5,4},{6,7},{7,6},{8,9},{9,8},{10,11... | collective-permute-start | bytes 626696 | tf_op jit(solution)/shard_map/ppermute | solution.py:618

commit v12 on v11

--- a/solution.py
+++ b/solution.py
@@ -590,7 +590,9 @@
     big = flat_second.shape[0] // (2 * high)
     for low in range(2):
         for index in range(high):
-            if low and index:
+            if low and index and index == high - 1:
+                chunk = chunks[-1][0].astype(F32)
+            elif low and index:
                 chunk = chunks[high + 1][index - 1].astype(F32)
             else:
                 chunk = chunks[index + low * high][...].astype(F32)
@@ -721,11 +723,10 @@
     mine = added(held(slice(0, 1), got_y_own)[0], *received)
     others = [swap(mine, "space", 2 * k) for k in range(1, high)]
     mine_y = swap(mine, "space", 1)
-    chunks = [mine, *others, mine_y]
-    if others:
-        chunks.append(swap(jnp.stack(others), "space", 1))
+    late = [swap(jnp.stack(others[-1:]), "space", 1)] if others else []
+    early = [swap(jnp.stack(others[:-1]), "space", 1)] if len(others) > 1 else []
     upper, mine_y = lax.optimization_barrier((upper, mine_y))
-    chunks[high] = mine_y
+    chunks = [mine, *others, mine_y, *early, *late]
 
     gradient = back_input(low, last, slope, upper, shards_first, offsets_first, inputs.shape)
 

time: 67.8 us -> 66.2 us (0.976)
  waiting for transfers between devices: 17.1 us -> 14.4 us
  starting transfers between devices: 30.8 us -> 32 us
    ppermute x28 -> x29, waiting for transfers between devices: 17.1 us -> 14.4 us  [swap(): return lax.ppermute(value, axis, [(i, i ^ bits) for i in range(size)])]
    ppermute x28 -> x29, starting transfers between devices: 24.6 us -> 25.7 us  [swap(): return lax.ppermute(value, axis, [(i, i ^ bits) for i in range(size)])]
  transfers between devices with their start and end apart: 31 -> 32, of which waited for: 13 -> 12; matrix products, arithmetic and copies ran while one was open for 0% -> 0% of each run, Pallas kernels for 20% -> 21%
where the time goes in v12:
time: 66.2 us; the launch traced here: 66 us
  starting transfers between devices  32 us (48%)
  Pallas kernels  15.4 us (23%)
  waiting for transfers between devices  14.4 us (22%)
  local copies, waits for them, and re-layouts  2.92 us (4%)
  between operations  0.96 us (1%)
    ppermute x29, starting transfers between devices, swap(): return lax.ppermute(value, axis, [(i, i ^ bits) for i in range(size)])  25.7 us
    ppermute x29, waiting for transfers between devices, swap(): return lax.ppermute(value, axis, [(i, i ^ bits) for i in range(size)])  14.4 us
    pallas_call x8, Pallas kernels, call(): pl.pallas_call(kernel, out_shape=out_shape, in_specs=specs, out_specs=jax...  14.4 us
    ppermute x2, starting transfers between devices, shifted(): return lax.ppermute(value, axis, pairs)  4.98 us
    unnamed x22, local copies, waits for them, and re-layouts  2.9 us
  transfers between devices with their start and end apart: 32, of which 12 were waited for; matrix products, arithmetic and copies ran while one was open for 0% of the time, Pallas kernels for 21%

profile of v12, /device:TPU:0, one launch (start us, length us, event | category | flops | bytes accessed | tf_op | source)
XLA Modules:
  0.0 66.0 jit_solution(2756066685507374530)
XLA Ops:
  0.6 3.0 %collective-permute-start.1 = (bf16[432,128]{1,0:T(8,128)(2,1)}, bf16[432,128]{1,0:T(8,128)(2,1)S(1)}, u32[]{:S(2)}, u32[]{:S(2)}) collective-permute-start(bf16[432,128]{1,0:T(8,128)(2,1)} %w0.7), channel_id=1, source_target_pairs={{0,16},{8,24},{16,0},{24,8},{1,17},{9,25},{17,1},{25,9},{2,18},{10... | collective-permute-start | bytes 331784 | tf_op jit(solution)/shard_map/ppermute | solution.py:620
  3.8 0.4 collective-permute-start.5
  4.1 1.0 %shard_map.86 = bf16[3,32,2048]{2,1,0:T(8,128)(2,1)S(1)} custom-call(bf16[8,32,2048]{2,1,0:T(8,128)(2,1)} %bitcast.26), custom_call_target="tpu_custom_call" | custom-call | bytes 786432 | tf_op jit(solution)/shard_map/pallas_call | solution.py:99
  5.2 3.7 %collective-permute-start.3 = (bf16[3,32,2048]{2,1,0:T(8,128)(2,1)S(1)}, bf16[3,32,2048]{2,1,0:T(8,128)(2,1)S(1)}, u32[]{:S(2)}, u32[]{:S(2)}) collective-permute-start(bf16[3,32,2048]{2,1,0:T(8,128)(2,1)S(1)} %shard_map.86), channel_id=1, source_target_pairs={{0,1},{1,2},{2,3},{3,4},{4,5},{5,6},{6,7},{8,9},{9,10},{10,11},{11... | collective-permute-start | bytes 1179656 | tf_op jit(solution)/shard_map/ppermute | solution.py:626
  8.9 1.2 %copy-done = bf16[1,8,32,2048]{3,2,1,0:T(8,128)(2,1)S(1)} copy-done((bf16[1,8,32,2048]{3,2,1,0:T(8,128)(2,1)S(1)}, bf16[1,8,32,2048]{3,2,1,0:T(8,128)(2,1)}, u32[]{:S(2)}) %copy-start) | copy-done | bytes 1048600
  10.1 0.3 shard_map.84.sorted_ref
  10.6 1.3 %collective-permute-done.2.w3 = bf16[432,128]{1,0:T(8,128)(2,1)S(1)} collective-permute-done((bf16[432,128]{1,0:T(8,128)(2,1)S(1)}, bf16[432,128]{1,0:T(8,128)(2,1)S(1)}, u32[]{:S(2)}, u32[]{:S(2)}) %collective-permute-start.2) | collective-permute-done | bytes 110624 | tf_op jit(solution)/shard_map/ppermute | solution.py:620
  11.9 2.2 %shard_map.85 = (f32[768,128]{1,0:T(8,128)S(1)}, bf16[128,3456]{1,0:T(8,128)(2,1)S(1)}, bf16[2,256,128]{2,1,0:T(8,128)(2,1)S(1)}, bf16[256,128]{1,0:T(8,128)(2,1...) custom-call(s32[4]{0:T(128)S(1)} %broadcast_multiply_fusion.offsets, ...), custom_call_target="tpu_custom_call" | custom-call | flops 2875000064 | bytes 2015232 | tf_op jit(solution)/shard_map/pallas_call | solution.py:49
  14.1 0.9 %copy-done.7 = bf16[128,3456]{1,0:T(8,128)(2,1)} copy-done((bf16[128,3456]{1,0:T(8,128)(2,1)}, bf16[128,3456]{1,0:T(8,128)(2,1)S(1)}, u32[]{:S(2)}) %copy-start.7) | copy-done | bytes 884760
  15.0 0.7 %copy-done.9 = f32[768,128]{1,0:T(8,128)} copy-done((f32[768,128]{1,0:T(8,128)}, f32[768,128]{1,0:T(8,128)S(1)}, u32[]{:S(2)}) %copy-start.9) | copy-done | bytes 393240
  15.7 0.7 %collective-permute-done.4.w2 = bf16[864,256]{1,0:T(8,128)(2,1)S(1)} collective-permute-done((bf16[864,256]{1,0:T(8,128)(2,1)}, bf16[864,256]{1,0:T(8,128)(2,1)S(1)}, u32[]{:S(2)}, u32[]{:S(2)}) %collective-permute-start.4) | collective-permute-done | bytes 442400 | tf_op jit(solution)/shard_map/ppermute | solution.py:620
  16.5 1.8 %collective-permute-start.7 = (bf16[2,256,128]{2,1,0:T(8,128)(2,1)S(1)}, bf16[2,256,128]{2,1,0:T(8,128)(2,1)S(1)}, u32[]{:S(2)}, u32[]{:S(2)}) collective-permute-start(bf16[2,256,128]{2,1,0:T(8,128)(2,1)S(1)} %get-tuple-element.58.m0), channel_id=1, source_target_pairs={{0,16},{8,24},{16,0},{24,8},{1,17},{9,25},{17,1},{25,9},{2,18},{10... | collective-permute-start | bytes 393224 | tf_op jit(solution)/shard_map/ppermute | solution.py:620
  18.2 0.9 %shard_map.87 = (f32[512,128]{1,0:T(8,128)S(1)}, bf16[64,2304]{1,0:T(8,128)(2,1)S(1)}, bf16[3,3,256,128]{3,2,1,0:T(8,128)(2,1)S(1)}, bf16[2,256,128]{2,1,0:T(8,128)(2,1)S(1)}, bf16[2,256,128]{2,1,0:T(8,128)(2,1)S(1)}) custom-call(f32[1]{0:T(128)} %bitcast.1.alive, s32[1]{0:T(128)} %bitcast.2.side, bf16[3,32,2048]{2,1,0:T(8,128)(2,1)S(1)} %collective-permute-done.3.halo_ref, ...), custom_call_target="tpu_custom_call" | custom-call | flops 1724999936 | bytes 1179648 | tf_op jit(solution)/shard_map/pallas_call | solution.py:49
  19.1 0.3 collective-permute-start.11
  19.4 0.8 %collective-permute-start.9 = (bf16[2,256,128]{2,1,0:T(8,128)(2,1)S(1)}, bf16[2,256,128]{2,1,0:T(8,128)(2,1)S(1)}, u32[]{:S(2)}, u32[]{:S(2)}) collective-permute-start(bf16[2,256,128]{2,1,0:T(8,128)(2,1)S(1)} %get-tuple-element.71), channel_id=1, source_target_pairs={{0,16},{8,24},{16,0},{24,8},{1,17},{9,25},{17,1},{25,9},{2,18},{10... | collective-permute-start | bytes 393224 | tf_op jit(solution)/shard_map/ppermute | solution.py:620
  20.2 1.8 %shard_map.88 = (bf16[2,8,2048]{2,1,0:T(8,128)(2,1)}, bf16[128,256]{1,0:T(8,128)(2,1)S(1)}) custom-call(s32[4]{0:T(128)S(1)} %get-tuple-element.100.offsets, bf16[128,3456]{1,0:T(8,128)(2,1)S(1)} %copy-done.8, bf16[64,2304]{1,0:T(8,128)(2,1)S(1)} %get-tuple-element.54.lower_ref, bf16[2,8,2048]{2,1,0:T(8,128)(2,1)S(1)} %bitcast.31, ...), custom_call_target="tpu_custom_call" | custom-call | flops 1724999936 | bytes 3014656 | tf_op jit(solution)/shard_map/pallas_call | solution.py:49
  22.0 0.5 collective-permute-done.7.m2
  22.5 2.0 %collective-permute-start.8 = (bf16[128,256]{1,0:T(8,128)(2,1)S(1)}, bf16[128,256]{1,0:T(8,128)(2,1)S(1)}, u32[]{:S(2)}, u32[]{:S(2)}) collective-permute-start(bf16[128,256]{1,0:T(8,128)(2,1)S(1)} %get-tuple-element.59.delta_ref.d0), channel_id=1, source_target_pairs={{0,16},{8,24},{16,0},{24,8},{1,17},{9,25},{17,1},{25,9},{2,18},{10... | collective-permute-start | bytes 196616 | tf_op jit(solution)/shard_map/ppermute | solution.py:620
  24.5 0.2 collective-permute-start.12
  24.7 3.0 %shard_map.89 = (bf16[768,128]{1,0:T(8,128)(2,1)S(1)}, f32[256,128]{1,0:T(8,128)S(1)}, bf16[512,128]{1,0:T(8,128)(2,1)S(1)}, bf16[8,56,128]{2,1,0:T(8,128)(2,1)S...) custom-call(s32[4]{0:T(128)S(1)} %get-tuple-element.100.offsets, ...), custom_call_target="tpu_custom_call" | custom-call | flops 4024999936 | bytes 4653056 | tf_op jit(solution)/shard_map/pallas_call | solution.py:49
  27.8 0.4 collective-permute-start.16
  28.1 0.2 collective-permute-start.14
  28.3 0.3 collective-permute-start.13
  28.6 0.2 collective-permute-start.15
  28.9 0.3 collective-permute-start.18
  29.2 0.3 collective-permute-done.14.m1
  29.5 0.4 collective-permute-done.15.d3
  29.9 1.8 %shard_map.90 = bf16[8,216,128]{2,1,0:T(8,128)(2,1)S(1)} custom-call(s32[1]{0:T(128)} %bitcast.5.data, s32[4,33]{1,0:T(4,128)S(1)} %copy-done.4, s32[8]{0:T(128)S(1)} %fusion.12.order, bf16[2,256,128]{2,1,0:T(8,128)(2,1)S(1)} %get-tuple-element.65.e0, bf16[2,256,128]{2,1,0:T(8,128)(2,1)S(1)} %collective-permute-done.11.e1, ...), custom_call_target="tpu_custom_call" | custom-call | flops 2300000000 | bytes 1310720 | tf_op jit(solution)/shard_map/pallas_call | solution.py:49
  31.8 1.2 %collective-permute-start.17 = (bf16[3,272,128]{2,1,0:T(8,128)(2,1)S(1)}, bf16[3,272,128]{2,1,0:T(8,128)(2,1)S(1)}, u32[]{:S(2)}, u32[]{:S(2)}) collective-permute-start(bf16[3,272,128]{2,1,0:T(8,128)(2,1)S(1)} %fusion), channel_id=1, source_target_pairs={{0,1},{1,0},{2,3},{3,2},{4,5},{5,4},{6,7},{7,6},{8,9},{9,8},{10,11... | collective-permute-start | bytes 626696 | tf_op jit(solution)/shard_map/ppermute | solution.py:620
  33.0 1.2 %collective-permute-start.19 = (bf16[4,56,128]{2,1,0:T(8,128)(2,1)S(1)}, bf16[4,56,128]{2,1,0:T(8,128)(2,1)S(1)}, u32[]{:S(2)}, u32[]{:S(2)}) collective-permute-start(bf16[4,56,128]{2,1,0:T(8,128)(2,1)S(1)} %get-tuple-element.94), channel_id=1, source_target_pairs={{0,16},{8,24},{16,0},{24,8},{1,17},{9,25},{17,1},{25,9},{2,18},{10... | collective-permute-start | bytes 172040 | tf_op jit(solution)/shard_map/ppermute | solution.py:620
  34.1 1.3 %collective-permute-start.20 = (bf16[4,56,128]{2,1,0:T(8,128)(2,1)S(1)}, bf16[4,56,128]{2,1,0:T(8,128)(2,1)S(1)}, u32[]{:S(2)}, u32[]{:S(2)}) collective-permute-start(bf16[4,56,128]{2,1,0:T(8,128)(2,1)S(1)} %get-tuple-element.95), channel_id=1, source_target_pairs={{0,17},{1,16},{2,19},{3,18},{4,21},{5,20},{6,23},{7,22},{8,25},{9,... | collective-permute-start | bytes 172040 | tf_op jit(solution)/shard_map/ppermute | solution.py:705
  35.4 1.1 %collective-permute-start.24 = (bf16[1,272,128]{2,1,0:T(8,128)(2,1)S(1)}, bf16[1,272,128]{2,1,0:T(8,128)(2,1)S(1)}, u32[]{:S(2)}, u32[]{:S(2)}) collective-permute-start(bf16[1,272,128]{2,1,0:T(8,128)(2,1)S(1)} %pad_maximum_fusion.1), channel_id=1, source_target_pairs={{0,1},{1,0},{2,3},{3,2},{4,5},{5,4},{6,7},{7,6},{8,9},{9,8},{10,11... | collective-permute-start | bytes 208904 | tf_op jit(solution)/shard_map/ppermute | solution.py:620
  36.6 1.3 %collective-permute-start.25 = (bf16[512,128]{1,0:T(8,128)(2,1)S(1)}, bf16[512,128]{1,0:T(8,128)(2,1)S(1)}, u32[]{:S(2)}, u32[]{:S(2)}) collective-permute-start(bf16[512,128]{1,0:T(8,128)(2,1)S(1)} %get-tuple-element.84), channel_id=1, source_target_pairs={{1,0},{2,1},{3,2},{4,3},{5,4},{6,5},{7,6},{9,8},{10,9},{11,10},{12... | collective-permute-start | bytes 393224 | tf_op jit(solution)/shard_map/ppermute | solution.py:626
  37.8 3.2 %collective-permute-done.17 = bf16[3,272,128]{2,1,0:T(8,128)(2,1)S(1)} collective-permute-done((bf16[3,272,128]{2,1,0:T(8,128)(2,1)S(1)}, bf16[3,272,128]{2,1,0:T(8,128)(2,1)S(1)}, u32[]{:S(2)}, u32[]{:S(2)}) %collective-permute-start.17) | collective-permute-done | bytes 208928 | tf_op jit(solution)/shard_map/ppermute | solution.py:620
  41.2 2.1 %collective-permute-start.21 = (bf16[272,128]{1,0:T(8,128)(2,1)S(1)}, bf16[272,128]{1,0:T(8,128)(2,1)S(1)}, u32[]{:S(2)}, u32[]{:S(2)}) collective-permute-start(bf16[272,128]{1,0:T(8,128)(2,1)S(1)} %get-tuple-element.97), channel_id=1, source_target_pairs={{0,2},{1,3},{2,0},{3,1},{4,6},{5,7},{6,4},{7,5},{8,10},{9,11},{10,... | collective-permute-start | bytes 208904 | tf_op jit(solution)/shard_map/ppermute | solution.py:620
  43.3 2.6 %collective-permute-start.22 = (bf16[272,128]{1,0:T(8,128)(2,1)S(1)}, bf16[272,128]{1,0:T(8,128)(2,1)S(1)}, u32[]{:S(2)}, u32[]{:S(2)}) collective-permute-start(bf16[272,128]{1,0:T(8,128)(2,1)S(1)} %get-tuple-element.98), channel_id=1, source_target_pairs={{0,4},{1,5},{2,6},{3,7},{4,0},{5,1},{6,2},{7,3},{8,12},{9,13},{10,... | collective-permute-start | bytes 208904 | tf_op jit(solution)/shard_map/ppermute | solution.py:620
  45.9 0.5 collective-permute-done.21
  46.3 4.1 %collective-permute-done.22 = bf16[272,128]{1,0:T(8,128)(2,1)S(1)} collective-permute-done((bf16[272,128]{1,0:T(8,128)(2,1)S(1)}, bf16[272,128]{1,0:T(8,128)(2,1)S(1)}, u32[]{:S(2)}, u32[]{:S(2)}) %collective-permute-start.22) | collective-permute-done | bytes 69664 | tf_op jit(solution)/shard_map/ppermute | solution.py:620
  50.4 1.8 %collective-permute-done.23 = bf16[272,128]{1,0:T(8,128)(2,1)S(1)} collective-permute-done((bf16[272,128]{1,0:T(8,128)(2,1)S(1)}, bf16[272,128]{1,0:T(8,128)(2,1)S(1)}, u32[]{:S(2)}, u32[]{:S(2)}) %collective-permute-start.23) | collective-permute-done | bytes 69664 | tf_op jit(solution)/shard_map/ppermute | solution.py:620
  52.4 1.4 %collective-permute-start.28 = (bf16[272,128]{1,0:T(8,128)(2,1)S(1)}, bf16[272,128]{1,0:T(8,128)(2,1)S(1)}, u32[]{:S(2)}, u32[]{:S(2)}) collective-permute-start(bf16[272,128]{1,0:T(8,128)(2,1)S(1)} %fusion.4.refs_0_), channel_id=1, source_target_pairs={{0,4},{1,5},{2,6},{3,7},{4,0},{5,1},{6,2},{7,3},{8,12},{9,13},{10,... | collective-permute-start | bytes 208904 | tf_op jit(solution)/shard_map/ppermute | solution.py:620
  53.8 2.9 %collective-permute-start.29 = (bf16[272,128]{1,0:T(8,128)(2,1)S(1)}, bf16[272,128]{1,0:T(8,128)(2,1)S(1)}, u32[]{:S(2)}, u32[]{:S(2)}) collective-permute-start(bf16[272,128]{1,0:T(8,128)(2,1)S(1)} %fusion.4.refs_0_), channel_id=1, source_target_pairs={{0,6},{1,7},{2,4},{3,5},{4,2},{5,3},{6,0},{7,1},{8,14},{9,15},{10,... | collective-permute-start | bytes 208904 | tf_op jit(solution)/shard_map/ppermute | solution.py:620
  56.8 0.7 %collective-permute-start.26 = (bf16[272,128]{1,0:T(8,128)(2,1)S(1)}, bf16[272,128]{1,0:T(8,128)(2,1)S(1)}, u32[]{:S(2)}, u32[]{:S(2)}) collective-permute-start(bf16[272,128]{1,0:T(8,128)(2,1)S(1)} %fusion.4.refs_0_), channel_id=1, source_target_pairs={{0,1},{1,0},{2,3},{3,2},{4,5},{5,4},{6,7},{7,6},{8,9},{9,8},{10,11... | collective-permute-start | bytes 208904 | tf_op jit(solution)/shard_map/ppermute | solution.py:620
  57.7 1.2 %collective-permute-start.30 = (bf16[2,272,128]{2,1,0:T(8,128)(2,1)S(1)}, bf16[2,272,128]{2,1,0:T(8,128)(2,1)S(1)}, u32[]{:S(2)}, u32[]{:S(2)}) collective-permute-start(bf16[2,272,128]{2,1,0:T(8,128)(2,1)S(1)} %pad_maximum_fusion), channel_id=1, source_target_pairs={{0,1},{1,0},{2,3},{3,2},{4,5},{5,4},{6,7},{7,6},{8,9},{9,8},{10,11... | collective-permute-start | bytes 417800 | tf_op jit(solution)/shard_map/ppermute | solution.py:620
  58.9 1.1 %collective-permute-done.29.refs_3_ = bf16[272,128]{1,0:T(8,128)(2,1)S(1)} collective-permute-done((bf16[272,128]{1,0:T(8,128)(2,1)S(1)}, bf16[272,128]{1,0:T(8,128)(2,1)S(1)}, u32[]{:S(2)}, u32[]{:S(2)}) %collective-permute-start.29) | collective-permute-done | bytes 69664 | tf_op jit(solution)/shard_map/ppermute | solution.py:620
  60.0 1.2 %collective-permute-start.31 = (bf16[1,272,128]{2,1,0:T(8,128)(2,1)S(1)}, bf16[1,272,128]{2,1,0:T(8,128)(2,1)S(1)}, u32[]{:S(2)}, u32[]{:S(2)}) collective-permute-start(bf16[1,272,128]{2,1,0:T(8,128)(2,1)S(1)} %bitcast.30), channel_id=1, source_target_pairs={{0,1},{1,0},{2,3},{3,2},{4,5},{5,4},{6,7},{7,6},{8,9},{9,8},{10,11... | collective-permute-start | bytes 208904 | tf_op jit(solution)/shard_map/ppermute | solution.py:620
  61.2 2.8 %shard_map.91 = bf16[8,32,2048]{2,1,0:T(8,128)(2,1)} custom-call(s32[4]{0:T(128)S(1)} %broadcast_multiply_fusion.offsets, bf16[768,128]{1,0:T(8,128)(2,1)S(1)} %get-tuple-element.63.low_ref, f32[256,128]{1,0:T(8,128)S(1)} %get-tuple-element.64.last_ref, f32[768,128]{1,0:T(8,128)S(1)} %copy-done.10, bf16[512,128]{1,0:T(8,128)(2,1)S(1)} %collective-permute-done.25.upper_ref, ...), custom_call_target="tpu_custom_call" | custom-call | flops 3449999872 | bytes 1294336 | tf_op jit(solution)/shard_map/pallas_call | solution.py:49
  64.0 0.3 collective-permute-done.31.refs_6_
  64.3 1.7 %shard_map.92 = (f32[432,128]{1,0:T(8,128)}, f32[864,256]{1,0:T(8,128)}) custom-call(s32[8]{0:T(128)S(1)} %fusion.12.order, bf16[272,128]{1,0:T(8,128)(2,1)S(1)} %fusion.4.refs_0_, bf16[272,128]{1,0:T(8,128)(2,1)S(1)} %collective-permute-done.27.refs_1_, bf16[272,128]{1,0:T(8,128)(2,1)S(1)} %collective-permute-done.28.refs_2_, ...), custom_call_target="tpu_custom_call" | custom-call | flops 1150000000 | bytes 557056 | tf_op jit(solution)/shard_map/pallas_call | solution.py:49
  (62 shorter events, 0.9 us)
Async XLA Ops:
  0.6 9.8 %collective-permute-start.1 = (bf16[432,128]{1,0:T(8,128)(2,1)}, bf16[432,128]{1,0:T(8,128)(2,1)S(1)}, u32[]{:S(2)}, u32[]{:S(2)}) collective-permute-start(bf16[432,128]{1,0:T(8,128)(2,1)} %w0.7), channel_id=1, source_target_pairs={{0,16},{8,24},{16,0},{24,8},{1,17},{9,25},{17,1},{25,9},{2,18},{10... | collective-permute-start | bytes 331784 | tf_op jit(solution)/shard_map/ppermute | solution.py:620
  3.6 6.9 %collective-permute-start = (bf16[432,128]{1,0:T(8,128)(2,1)}, bf16[432,128]{1,0:T(8,128)(2,1)S(1)}, u32[]{:S(2)}, u32[]{:S(2)}) collective-permute-start(bf16[432,128]{1,0:T(8,128)(2,1)} %w0.7), channel_id=1, source_target_pairs={{0,8},{8,0},{16,24},{24,16},{1,9},{9,1},{17,25},{25,17},{2,10},{10... | collective-permute-start | bytes 331784 | tf_op jit(solution)/shard_map/ppermute | solution.py:620
  3.6 12.8 %collective-permute-start.4 = (bf16[864,256]{1,0:T(8,128)(2,1)}, bf16[864,256]{1,0:T(8,128)(2,1)S(1)}, u32[]{:S(2)}, u32[]{:S(2)}) collective-permute-start(bf16[864,256]{1,0:T(8,128)(2,1)} %w0.6), channel_id=1, source_target_pairs={{0,16},{8,24},{16,0},{24,8},{1,17},{9,25},{17,1},{25,9},{2,18},{10... | collective-permute-start | bytes 1327112 | tf_op jit(solution)/shard_map/ppermute | solution.py:620
  3.8 16.4 %collective-permute-start.5 = (bf16[864,256]{1,0:T(8,128)(2,1)}, bf16[864,256]{1,0:T(8,128)(2,1)S(1)}, u32[]{:S(2)}, u32[]{:S(2)}) collective-permute-start(bf16[864,256]{1,0:T(8,128)(2,1)} %w0.6), channel_id=1, source_target_pairs={{0,8},{8,0},{16,24},{24,16},{1,9},{9,1},{17,25},{25,17},{2,10},{10... | collective-permute-start | bytes 1327112 | tf_op jit(solution)/shard_map/ppermute | solution.py:620
  5.2 13.1 %collective-permute-start.3 = (bf16[3,32,2048]{2,1,0:T(8,128)(2,1)S(1)}, bf16[3,32,2048]{2,1,0:T(8,128)(2,1)S(1)}, u32[]{:S(2)}, u32[]{:S(2)}) collective-permute-start(bf16[3,32,2048]{2,1,0:T(8,128)(2,1)S(1)} %shard_map.86), channel_id=1, source_target_pairs={{0,1},{1,2},{2,3},{3,4},{4,5},{5,6},{6,7},{8,9},{9,10},{10,11},{11... | collective-permute-start | bytes 1179656 | tf_op jit(solution)/shard_map/ppermute | solution.py:626
  8.9 1.2 %copy-start = (bf16[1,8,32,2048]{3,2,1,0:T(8,128)(2,1)S(1)}, bf16[1,8,32,2048]{3,2,1,0:T(8,128)(2,1)}, u32[]{:S(2)}) copy-start(bf16[1,8,32,2048]{3,2,1,0:T(8,128)(2,1)} %param.5) | copy-start | bytes 3145732
  10.1 1.8 %copy-start.2 = (bf16[432,128]{1,0:T(8,128)(2,1)S(1)}, bf16[432,128]{1,0:T(8,128)(2,1)}, u32[]{:S(2)}) copy-start(bf16[432,128]{1,0:T(8,128)(2,1)} %w0.7) | copy-start | bytes 331780
  10.5 3.6 %copy-start.5 = (bf16[8,3,256,128]{3,2,1,0:T(8,128)(2,1)}, bf16[8,3,256,128]{3,2,1,0:T(8,128)(2,1)S(1)}, u32[]{:S(2)}) copy-start(bf16[8,3,256,128]{3,2,1,0:T(8,128)(2,1)S(1)} %shard_map.84.sorted_ref) | copy-start | bytes 4718596
  10.5 1.4 %collective-permute-start.2 = (bf16[432,128]{1,0:T(8,128)(2,1)S(1)}, bf16[432,128]{1,0:T(8,128)(2,1)S(1)}, u32[]{:S(2)}, u32[]{:S(2)}) collective-permute-start(bf16[432,128]{1,0:T(8,128)(2,1)S(1)} %collective-permute-done.1.w2), channel_id=1, source_target_pairs={{0,8},{8,0},{16,24},{24,16},{1,9},{9,1},{17,25},{25,17},{2,10},{10... | collective-permute-start | bytes 331784 | tf_op jit(solution)/shard_map/ppermute | solution.py:620
  14.0 0.9 %copy-start.7 = (bf16[128,3456]{1,0:T(8,128)(2,1)}, bf16[128,3456]{1,0:T(8,128)(2,1)S(1)}, u32[]{:S(2)}) copy-start(bf16[128,3456]{1,0:T(8,128)(2,1)S(1)} %get-tuple-element.49.upper_ref) | copy-start | bytes 2654212
  15.0 0.7 %copy-start.9 = (f32[768,128]{1,0:T(8,128)}, f32[768,128]{1,0:T(8,128)S(1)}, u32[]{:S(2)}) copy-start(f32[768,128]{1,0:T(8,128)S(1)} %get-tuple-element.61.slope_ref) | copy-start | bytes 1179652
  16.4 3.7 %collective-permute-start.6 = (bf16[864,256]{1,0:T(8,128)(2,1)S(1)}, bf16[864,256]{1,0:T(8,128)(2,1)S(1)}, u32[]{:S(2)}, u32[]{:S(2)}) collective-permute-start(bf16[864,256]{1,0:T(8,128)(2,1)S(1)} %collective-permute-done.4.w2), channel_id=1, source_target_pairs={{0,8},{8,0},{16,24},{24,16},{1,9},{9,1},{17,25},{25,17},{2,10},{10... | collective-permute-start | bytes 1327112 | tf_op jit(solution)/shard_map/ppermute | solution.py:620
  16.5 6.1 %collective-permute-start.7 = (bf16[2,256,128]{2,1,0:T(8,128)(2,1)S(1)}, bf16[2,256,128]{2,1,0:T(8,128)(2,1)S(1)}, u32[]{:S(2)}, u32[]{:S(2)}) collective-permute-start(bf16[2,256,128]{2,1,0:T(8,128)(2,1)S(1)} %get-tuple-element.58.m0), channel_id=1, source_target_pairs={{0,16},{8,24},{16,0},{24,8},{1,17},{9,25},{17,1},{25,9},{2,18},{10... | collective-permute-start | bytes 393224 | tf_op jit(solution)/shard_map/ppermute | solution.py:620
  18.2 1.9 %copy-start.1 = (bf16[864,256]{1,0:T(8,128)(2,1)S(1)}, bf16[864,256]{1,0:T(8,128)(2,1)}, u32[]{:S(2)}) copy-start(bf16[864,256]{1,0:T(8,128)(2,1)} %w0.6) | copy-start | bytes 1327108
  18.2 1.9 %copy-start.3 = (bf16[1,2,8,2048]{3,2,1,0:T(8,128)(2,1)S(1)}, bf16[1,2,8,2048]{3,2,1,0:T(8,128)(2,1)}, u32[]{:S(2)}) copy-start(bf16[1,2,8,2048]{3,2,1,0:T(8,128)(2,1)} %param.8) | copy-start | bytes 196612
  18.2 2.0 %copy-start.8 = (bf16[128,3456]{1,0:T(8,128)(2,1)S(1)}, bf16[128,3456]{1,0:T(8,128)(2,1)}, u32[]{:S(2)}) copy-start(bf16[128,3456]{1,0:T(8,128)(2,1)} %copy-done.7) | copy-start | bytes 2654212
  19.1 8.6 %collective-permute-start.11 = (bf16[2,256,128]{2,1,0:T(8,128)(2,1)S(1)}, bf16[2,256,128]{2,1,0:T(8,128)(2,1)S(1)}, u32[]{:S(2)}, u32[]{:S(2)}) collective-permute-start(bf16[2,256,128]{2,1,0:T(8,128)(2,1)S(1)} %get-tuple-element.65.e0), channel_id=1, source_target_pairs={{0,8},{8,0},{16,24},{24,16},{1,9},{9,1},{17,25},{25,17},{2,10},{10... | collective-permute-start | bytes 393224 | tf_op jit(solution)/shard_map/ppermute | solution.py:620
  19.4 8.4 %collective-permute-start.9 = (bf16[2,256,128]{2,1,0:T(8,128)(2,1)S(1)}, bf16[2,256,128]{2,1,0:T(8,128)(2,1)S(1)}, u32[]{:S(2)}, u32[]{:S(2)}) collective-permute-start(bf16[2,256,128]{2,1,0:T(8,128)(2,1)S(1)} %get-tuple-element.71), channel_id=1, source_target_pairs={{0,16},{8,24},{16,0},{24,8},{1,17},{9,25},{17,1},{25,9},{2,18},{10... | collective-permute-start | bytes 393224 | tf_op jit(solution)/shard_map/ppermute | solution.py:620
  20.2 4.6 %copy-start.6 = (bf16[8,3,256,128]{3,2,1,0:T(8,128)(2,1)S(1)}, bf16[8,3,256,128]{3,2,1,0:T(8,128)(2,1)}, u32[]{:S(2)}) copy-start(bf16[8,3,256,128]{3,2,1,0:T(8,128)(2,1)} %copy-done.5) | copy-start | bytes 4718596
  20.2 4.6 %copy-start.10 = (f32[768,128]{1,0:T(8,128)S(1)}, f32[768,128]{1,0:T(8,128)}, u32[]{:S(2)}) copy-start(f32[768,128]{1,0:T(8,128)} %copy-done.9) | copy-start | bytes 1179652
  22.5 5.2 %collective-permute-start.10 = (bf16[128,256]{1,0:T(8,128)(2,1)S(1)}, bf16[128,256]{1,0:T(8,128)(2,1)S(1)}, u32[]{:S(2)}, u32[]{:S(2)}) collective-permute-start(bf16[128,256]{1,0:T(8,128)(2,1)S(1)} %get-tuple-element.59.delta_ref.d0), channel_id=1, source_target_pairs={{0,8},{8,0},{16,24},{24,16},{1,9},{9,1},{17,25},{25,17},{2,10},{10... | collective-permute-start | bytes 196616 | tf_op jit(solution)/shard_map/ppermute | solution.py:620
  22.5 5.2 %collective-permute-start.8 = (bf16[128,256]{1,0:T(8,128)(2,1)S(1)}, bf16[128,256]{1,0:T(8,128)(2,1)S(1)}, u32[]{:S(2)}, u32[]{:S(2)}) collective-permute-start(bf16[128,256]{1,0:T(8,128)(2,1)S(1)} %get-tuple-element.59.delta_ref.d0), channel_id=1, source_target_pairs={{0,16},{8,24},{16,0},{24,8},{1,17},{9,25},{17,1},{25,9},{2,18},{10... | collective-permute-start | bytes 196616 | tf_op jit(solution)/shard_map/ppermute | solution.py:620
  24.5 3.3 %collective-permute-start.12 = (bf16[2,256,128]{2,1,0:T(8,128)(2,1)S(1)}, bf16[2,256,128]{2,1,0:T(8,128)(2,1)S(1)}, u32[]{:S(2)}, u32[]{:S(2)}) collective-permute-start(bf16[2,256,128]{2,1,0:T(8,128)(2,1)S(1)} %collective-permute-done.7.m2), channel_id=1, source_target_pairs={{0,8},{8,0},{16,24},{24,16},{1,9},{9,1},{17,25},{25,17},{2,10},{10... | collective-permute-start | bytes 393224 | tf_op jit(solution)/shard_map/ppermute | solution.py:620
  24.7 5.2 %copy-start.4 = (s32[4,33]{1,0:T(4,128)S(1)}, s32[4,33]{1,0:T(4,128)}, u32[]{:S(2)}) copy-start(s32[4,33]{1,0:T(4,128)} %constant.48.clone.table) | copy-start | bytes 1588
  27.8 1.4 %collective-permute-start.16 = (bf16[8,56,128]{2,1,0:T(8,128)(2,1)S(1)}, bf16[8,56,128]{2,1,0:T(8,128)(2,1)S(1)}, u32[]{:S(2)}, u32[]{:S(2)}) collective-permute-start(bf16[8,56,128]{2,1,0:T(8,128)(2,1)S(1)} %get-tuple-element.81), channel_id=1, source_target_pairs={{0,8},{8,0},{16,24},{24,16},{1,9},{9,1},{17,25},{25,17},{2,10},{10... | collective-permute-start | bytes 344072 | tf_op jit(solution)/shard_map/ppermute | solution.py:620
  28.1 1.3 %collective-permute-start.14 = (bf16[2,256,128]{2,1,0:T(8,128)(2,1)S(1)}, bf16[2,256,128]{2,1,0:T(8,128)(2,1)S(1)}, u32[]{:S(2)}, u32[]{:S(2)}) collective-permute-start(bf16[2,256,128]{2,1,0:T(8,128)(2,1)S(1)} %get-tuple-element.58.m0), channel_id=1, source_target_pairs={{0,8},{8,0},{16,24},{24,16},{1,9},{9,1},{17,25},{25,17},{2,10},{10... | collective-permute-start | bytes 393224 | tf_op jit(solution)/shard_map/ppermute | solution.py:620
  28.3 1.5 %collective-permute-start.13 = (bf16[2,256,128]{2,1,0:T(8,128)(2,1)S(1)}, bf16[2,256,128]{2,1,0:T(8,128)(2,1)S(1)}, u32[]{:S(2)}, u32[]{:S(2)}) collective-permute-start(bf16[2,256,128]{2,1,0:T(8,128)(2,1)S(1)} %collective-permute-done.9.e2), channel_id=1, source_target_pairs={{0,8},{8,0},{16,24},{24,16},{1,9},{9,1},{17,25},{25,17},{2,10},{10... | collective-permute-start | bytes 393224 | tf_op jit(solution)/shard_map/ppermute | solution.py:620
  28.6 1.3 %collective-permute-start.15 = (bf16[128,256]{1,0:T(8,128)(2,1)S(1)}, bf16[128,256]{1,0:T(8,128)(2,1)S(1)}, u32[]{:S(2)}, u32[]{:S(2)}) collective-permute-start(bf16[128,256]{1,0:T(8,128)(2,1)S(1)} %collective-permute-done.8.d2), channel_id=1, source_target_pairs={{0,8},{8,0},{16,24},{24,16},{1,9},{9,1},{17,25},{25,17},{2,10},{10... | collective-permute-start | bytes 196616 | tf_op jit(solution)/shard_map/ppermute | solution.py:620
  28.9 4.1 %collective-permute-start.18 = (bf16[8,56,128]{2,1,0:T(8,128)(2,1)S(1)}, bf16[8,56,128]{2,1,0:T(8,128)(2,1)S(1)}, u32[]{:S(2)}, u32[]{:S(2)}) collective-permute-start(bf16[8,56,128]{2,1,0:T(8,128)(2,1)S(1)} %get-tuple-element.83), channel_id=1, source_target_pairs={{0,8},{8,0},{16,24},{24,16},{1,9},{9,1},{17,25},{25,17},{2,10},{10... | collective-permute-start | bytes 344072 | tf_op jit(solution)/shard_map/ppermute | solution.py:620
  31.8 9.3 %collective-permute-start.17 = (bf16[3,272,128]{2,1,0:T(8,128)(2,1)S(1)}, bf16[3,272,128]{2,1,0:T(8,128)(2,1)S(1)}, u32[]{:S(2)}, u32[]{:S(2)}) collective-permute-start(bf16[3,272,128]{2,1,0:T(8,128)(2,1)S(1)} %fusion), channel_id=1, source_target_pairs={{0,1},{1,0},{2,3},{3,2},{4,5},{5,4},{6,7},{7,6},{8,9},{9,8},{10,11... | collective-permute-start | bytes 626696 | tf_op jit(solution)/shard_map/ppermute | solution.py:620
  33.0 8.1 %collective-permute-start.19 = (bf16[4,56,128]{2,1,0:T(8,128)(2,1)S(1)}, bf16[4,56,128]{2,1,0:T(8,128)(2,1)S(1)}, u32[]{:S(2)}, u32[]{:S(2)}) collective-permute-start(bf16[4,56,128]{2,1,0:T(8,128)(2,1)S(1)} %get-tuple-element.94), channel_id=1, source_target_pairs={{0,16},{8,24},{16,0},{24,8},{1,17},{9,25},{17,1},{25,9},{2,18},{10... | collective-permute-start | bytes 172040 | tf_op jit(solution)/shard_map/ppermute | solution.py:620
  34.1 7.0 %collective-permute-start.20 = (bf16[4,56,128]{2,1,0:T(8,128)(2,1)S(1)}, bf16[4,56,128]{2,1,0:T(8,128)(2,1)S(1)}, u32[]{:S(2)}, u32[]{:S(2)}) collective-permute-start(bf16[4,56,128]{2,1,0:T(8,128)(2,1)S(1)} %get-tuple-element.95), channel_id=1, source_target_pairs={{0,17},{1,16},{2,19},{3,18},{4,21},{5,20},{6,23},{7,22},{8,25},{9,... | collective-permute-start | bytes 172040 | tf_op jit(solution)/shard_map/ppermute | solution.py:705
  35.4 10.4 %collective-permute-start.24 = (bf16[1,272,128]{2,1,0:T(8,128)(2,1)S(1)}, bf16[1,272,128]{2,1,0:T(8,128)(2,1)S(1)}, u32[]{:S(2)}, u32[]{:S(2)}) collective-permute-start(bf16[1,272,128]{2,1,0:T(8,128)(2,1)S(1)} %pad_maximum_fusion.1), channel_id=1, source_target_pairs={{0,1},{1,0},{2,3},{3,2},{4,5},{5,4},{6,7},{7,6},{8,9},{9,8},{10,11... | collective-permute-start | bytes 208904 | tf_op jit(solution)/shard_map/ppermute | solution.py:620
  36.6 9.3 %collective-permute-start.25 = (bf16[512,128]{1,0:T(8,128)(2,1)S(1)}, bf16[512,128]{1,0:T(8,128)(2,1)S(1)}, u32[]{:S(2)}, u32[]{:S(2)}) collective-permute-start(bf16[512,128]{1,0:T(8,128)(2,1)S(1)} %get-tuple-element.84), channel_id=1, source_target_pairs={{1,0},{2,1},{3,2},{4,3},{5,4},{6,5},{7,6},{9,8},{10,9},{11,10},{12... | collective-permute-start | bytes 393224 | tf_op jit(solution)/shard_map/ppermute | solution.py:626
  41.2 5.1 %collective-permute-start.21 = (bf16[272,128]{1,0:T(8,128)(2,1)S(1)}, bf16[272,128]{1,0:T(8,128)(2,1)S(1)}, u32[]{:S(2)}, u32[]{:S(2)}) collective-permute-start(bf16[272,128]{1,0:T(8,128)(2,1)S(1)} %get-tuple-element.97), channel_id=1, source_target_pairs={{0,2},{1,3},{2,0},{3,1},{4,6},{5,7},{6,4},{7,5},{8,10},{9,11},{10,... | collective-permute-start | bytes 208904 | tf_op jit(solution)/shard_map/ppermute | solution.py:620
  43.3 7.1 %collective-permute-start.22 = (bf16[272,128]{1,0:T(8,128)(2,1)S(1)}, bf16[272,128]{1,0:T(8,128)(2,1)S(1)}, u32[]{:S(2)}, u32[]{:S(2)}) collective-permute-start(bf16[272,128]{1,0:T(8,128)(2,1)S(1)} %get-tuple-element.98), channel_id=1, source_target_pairs={{0,4},{1,5},{2,6},{3,7},{4,0},{5,1},{6,2},{7,3},{8,12},{9,13},{10,... | collective-permute-start | bytes 208904 | tf_op jit(solution)/shard_map/ppermute | solution.py:620
  45.9 6.4 %collective-permute-start.23 = (bf16[272,128]{1,0:T(8,128)(2,1)S(1)}, bf16[272,128]{1,0:T(8,128)(2,1)S(1)}, u32[]{:S(2)}, u32[]{:S(2)}) collective-permute-start(bf16[272,128]{1,0:T(8,128)(2,1)S(1)} %get-tuple-element.96), channel_id=1, source_target_pairs={{0,6},{1,7},{2,4},{3,5},{4,2},{5,3},{6,0},{7,1},{8,14},{9,15},{10,... | collective-permute-start | bytes 208904 | tf_op jit(solution)/shard_map/ppermute | solution.py:620
  52.3 5.2 %collective-permute-start.27 = (bf16[272,128]{1,0:T(8,128)(2,1)S(1)}, bf16[272,128]{1,0:T(8,128)(2,1)S(1)}, u32[]{:S(2)}, u32[]{:S(2)}) collective-permute-start(bf16[272,128]{1,0:T(8,128)(2,1)S(1)} %fusion.4.refs_0_), channel_id=1, source_target_pairs={{0,2},{1,3},{2,0},{3,1},{4,6},{5,7},{6,4},{7,5},{8,10},{9,11},{10,... | collective-permute-start | bytes 208904 | tf_op jit(solution)/shard_map/ppermute | solution.py:620
  52.4 5.3 %collective-permute-start.28 = (bf16[272,128]{1,0:T(8,128)(2,1)S(1)}, bf16[272,128]{1,0:T(8,128)(2,1)S(1)}, u32[]{:S(2)}, u32[]{:S(2)}) collective-permute-start(bf16[272,128]{1,0:T(8,128)(2,1)S(1)} %fusion.4.refs_0_), channel_id=1, source_target_pairs={{0,4},{1,5},{2,6},{3,7},{4,0},{5,1},{6,2},{7,3},{8,12},{9,13},{10,... | collective-permute-start | bytes 208904 | tf_op jit(solution)/shard_map/ppermute | solution.py:620
  53.8 6.2 %collective-permute-start.29 = (bf16[272,128]{1,0:T(8,128)(2,1)S(1)}, bf16[272,128]{1,0:T(8,128)(2,1)S(1)}, u32[]{:S(2)}, u32[]{:S(2)}) collective-permute-start(bf16[272,128]{1,0:T(8,128)(2,1)S(1)} %fusion.4.refs_0_), channel_id=1, source_target_pairs={{0,6},{1,7},{2,4},{3,5},{4,2},{5,3},{6,0},{7,1},{8,14},{9,15},{10,... | collective-permute-start | bytes 208904 | tf_op jit(solution)/shard_map/ppermute | solution.py:620
  56.8 4.5 %collective-permute-start.26 = (bf16[272,128]{1,0:T(8,128)(2,1)S(1)}, bf16[272,128]{1,0:T(8,128)(2,1)S(1)}, u32[]{:S(2)}, u32[]{:S(2)}) collective-permute-start(bf16[272,128]{1,0:T(8,128)(2,1)S(1)} %fusion.4.refs_0_), channel_id=1, source_target_pairs={{0,1},{1,0},{2,3},{3,2},{4,5},{5,4},{6,7},{7,6},{8,9},{9,8},{10,11... | collective-permute-start | bytes 208904 | tf_op jit(solution)/shard_map/ppermute | solution.py:620
  57.7 6.6 %collective-permute-start.30 = (bf16[2,272,128]{2,1,0:T(8,128)(2,1)S(1)}, bf16[2,272,128]{2,1,0:T(8,128)(2,1)S(1)}, u32[]{:S(2)}, u32[]{:S(2)}) collective-permute-start(bf16[2,272,128]{2,1,0:T(8,128)(2,1)S(1)} %pad_maximum_fusion), channel_id=1, source_target_pairs={{0,1},{1,0},{2,3},{3,2},{4,5},{5,4},{6,7},{7,6},{8,9},{9,8},{10,11... | collective-permute-start | bytes 417800 | tf_op jit(solution)/shard_map/ppermute | solution.py:620
  60.0 4.3 %collective-permute-start.31 = (bf16[1,272,128]{2,1,0:T(8,128)(2,1)S(1)}, bf16[1,272,128]{2,1,0:T(8,128)(2,1)S(1)}, u32[]{:S(2)}, u32[]{:S(2)}) collective-permute-start(bf16[1,272,128]{2,1,0:T(8,128)(2,1)S(1)} %bitcast.30), channel_id=1, source_target_pairs={{0,1},{1,0},{2,3},{3,2},{4,5},{5,4},{6,7},{7,6},{8,9},{9,8},{10,11... | collective-permute-start | bytes 208904 | tf_op jit(solution)/shard_map/ppermute | solution.py:620

commit v13 on v12

--- a/solution.py
+++ b/solution.py
@@ -42,7 +42,7 @@
     return jnp.where(block_row(*block.shape) == 7, 0.0, moved)
 
 
-def call(kernel, out_shape, scratch, *operands, smem=(), micros=1.0):
+def call(kernel, out_shape, scratch, *operands, smem=(), micros=1.0, out_space=pltpu.VMEM):
     nbytes = sum(a.size * a.dtype.itemsize for a in operands)
     specs = [pl.BlockSpec(memory_space=pltpu.SMEM)] * len(smem)
     specs += [pl.BlockSpec(memory_space=pltpu.VMEM)] * len(operands)
@@ -50,7 +50,7 @@
         kernel,
         out_shape=out_shape,
         in_specs=specs,
-        out_specs=jax.tree.map(lambda _: pl.BlockSpec(memory_space=pltpu.VMEM), out_shape),
+        out_specs=jax.tree.map(lambda _: pl.BlockSpec(memory_space=out_space), out_shape),
         scratch_shapes=scratch,
         compiler_params=pltpu.CompilerParams(vmem_limit_bytes=VMEM_LIMIT),
         cost_estimate=pl.CostEstimate(
@@ -584,7 +584,7 @@
 
 
 def unpack_kernel(scale_first, scale_second, order, *refs):
-    *chunks, first_ref, second_ref, flat_first, flat_second = refs
+    *chunks, first_ref, second_ref, flat_first, flat_second, sems = refs
     high = order.shape[0] // 2
     small = flat_first.shape[0] // (2 * high)
     big = flat_second.shape[0] // (2 * high)
@@ -597,14 +597,26 @@
             else:
                 chunk = chunks[index + low * high][...].astype(F32)
             place = order[low * high + index]
-            flat_second[pl.ds(pl.multiple_of(place * big, 8), big), :] = chunk[:big, :]
-            flat_first[pl.ds(pl.multiple_of(place * small, 8), small), :] = chunk[big:, :]
+            flat_second[pl.ds(pl.multiple_of(place * big, 8), big), :] = chunk[:big, :] * scale_second
+            flat_first[pl.ds(pl.multiple_of(place * small, 8), small), :] = chunk[big:, :] * scale_first
     rows, features = second_ref.shape
-    for lane in range(features // 128):
-        second_ref[:, lane * 128 : (lane + 1) * 128] = (
-            flat_second[lane * rows : (lane + 1) * rows, :] * scale_second
+    copies = [
+        pltpu.make_async_copy(
+            flat_second.at[lane * rows : (lane + 1) * rows],
+            second_ref.at[:, lane * 128 : (lane + 1) * 128],
+            sems.at[lane],
         )
-    first_ref[...] = flat_first[: first_ref.shape[0], :] * scale_first
+        for lane in range(features // 128)
+    ]
+    copies.append(
+        pltpu.make_async_copy(
+            flat_first.at[: first_ref.shape[0]], first_ref, sems.at[features // 128]
+        )
+    )
+    for copy in copies:
+        copy.start()
+    for copy in copies:
+        copy.wait()
 
 
 def wide_sum(*pieces):
@@ -738,9 +750,11 @@
         [
             pltpu.VMEM((spaces * size_first, 128), F32),
             pltpu.VMEM((spaces * size_second, 128), F32),
+            pltpu.SemaphoreType.DMA((lanes + 1,)),
         ],
         *chunks,
         smem=(order,),
+        out_space=pltpu.HBM,
     )
     return (
         activations.reshape(cotangent.shape),

time: 66.2 us -> 66.1 us (level)
  no operation moved by 1% of the time
where the time goes in v13:
time: 66.1 us; the launch traced here: 65.9 us
  starting transfers between devices  32 us (48%)
  Pallas kernels  15.3 us (23%)
  waiting for transfers between devices  14.4 us (22%)
  local copies, waits for them, and re-layouts  2.92 us (4%)
  between operations  0.96 us (1%)
    ppermute x29, starting transfers between devices, swap(): return lax.ppermute(value, axis, [(i, i ^ bits) for i in range(size)])  25.7 us
    ppermute x29, waiting for transfers between devices, swap(): return lax.ppermute(value, axis, [(i, i ^ bits) for i in range(size)])  14.4 us
    pallas_call x8, Pallas kernels, call(): pl.pallas_call(kernel, out_shape=out_shape, in_specs=specs, out_specs=jax...  14.3 us
    ppermute x2, starting transfers between devices, shifted(): return lax.ppermute(value, axis, pairs)  4.98 us
    unnamed x22, local copies, waits for them, and re-layouts  2.9 us
  transfers between devices with their start and end apart: 32, of which 12 were waited for; matrix products, arithmetic and copies ran while one was open for 0% of the time, Pallas kernels for 21%

profile of v13, /device:TPU:0, one launch (start us, length us, event | category | flops | bytes accessed | tf_op | source)
XLA Modules:
  0.0 65.9 jit_solution(7435207737832498849)
XLA Ops:
  0.6 3.0 %collective-permute-start.1 = (bf16[432,128]{1,0:T(8,128)(2,1)}, bf16[432,128]{1,0:T(8,128)(2,1)S(1)}, u32[]{:S(2)}, u32[]{:S(2)}) collective-permute-start(bf16[432,128]{1,0:T(8,128)(2,1)} %w0.7), channel_id=1, source_target_pairs={{0,16},{8,24},{16,0},{24,8},{1,17},{9,25},{17,1},{25,9},{2,18},{10... | collective-permute-start | bytes 331784 | tf_op jit(solution)/shard_map/ppermute | solution.py:632
  3.8 0.4 collective-permute-start.5
  4.1 1.0 %shard_map.86 = bf16[3,32,2048]{2,1,0:T(8,128)(2,1)S(1)} custom-call(bf16[8,32,2048]{2,1,0:T(8,128)(2,1)} %bitcast.26), custom_call_target="tpu_custom_call" | custom-call | bytes 786432 | tf_op jit(solution)/shard_map/pallas_call | solution.py:99
  5.2 3.7 %collective-permute-start.3 = (bf16[3,32,2048]{2,1,0:T(8,128)(2,1)S(1)}, bf16[3,32,2048]{2,1,0:T(8,128)(2,1)S(1)}, u32[]{:S(2)}, u32[]{:S(2)}) collective-permute-start(bf16[3,32,2048]{2,1,0:T(8,128)(2,1)S(1)} %shard_map.86), channel_id=1, source_target_pairs={{0,1},{1,2},{2,3},{3,4},{4,5},{5,6},{6,7},{8,9},{9,10},{10,11},{11... | collective-permute-start | bytes 1179656 | tf_op jit(solution)/shard_map/ppermute | solution.py:638
  8.9 1.2 %copy-done = bf16[1,8,32,2048]{3,2,1,0:T(8,128)(2,1)S(1)} copy-done((bf16[1,8,32,2048]{3,2,1,0:T(8,128)(2,1)S(1)}, bf16[1,8,32,2048]{3,2,1,0:T(8,128)(2,1)}, u32[]{:S(2)}) %copy-start) | copy-done | bytes 1048600
  10.1 0.3 shard_map.84.sorted_ref
  10.6 1.3 %collective-permute-done.2.w3 = bf16[432,128]{1,0:T(8,128)(2,1)S(1)} collective-permute-done((bf16[432,128]{1,0:T(8,128)(2,1)S(1)}, bf16[432,128]{1,0:T(8,128)(2,1)S(1)}, u32[]{:S(2)}, u32[]{:S(2)}) %collective-permute-start.2) | collective-permute-done | bytes 110624 | tf_op jit(solution)/shard_map/ppermute | solution.py:632
  11.9 2.2 %shard_map.85 = (f32[768,128]{1,0:T(8,128)S(1)}, bf16[128,3456]{1,0:T(8,128)(2,1)S(1)}, bf16[2,256,128]{2,1,0:T(8,128)(2,1)S(1)}, bf16[256,128]{1,0:T(8,128)(2,1...) custom-call(s32[4]{0:T(128)S(1)} %broadcast_multiply_fusion.offsets, ...), custom_call_target="tpu_custom_call" | custom-call | flops 2875000064 | bytes 2015232 | tf_op jit(solution)/shard_map/pallas_call | solution.py:49
  14.1 0.9 %copy-done.7 = bf16[128,3456]{1,0:T(8,128)(2,1)} copy-done((bf16[128,3456]{1,0:T(8,128)(2,1)}, bf16[128,3456]{1,0:T(8,128)(2,1)S(1)}, u32[]{:S(2)}) %copy-start.7) | copy-done | bytes 884760
  15.0 0.7 %copy-done.9 = f32[768,128]{1,0:T(8,128)} copy-done((f32[768,128]{1,0:T(8,128)}, f32[768,128]{1,0:T(8,128)S(1)}, u32[]{:S(2)}) %copy-start.9) | copy-done | bytes 393240
  15.7 0.7 %collective-permute-done.4.w2 = bf16[864,256]{1,0:T(8,128)(2,1)S(1)} collective-permute-done((bf16[864,256]{1,0:T(8,128)(2,1)}, bf16[864,256]{1,0:T(8,128)(2,1)S(1)}, u32[]{:S(2)}, u32[]{:S(2)}) %collective-permute-start.4) | collective-permute-done | bytes 442400 | tf_op jit(solution)/shard_map/ppermute | solution.py:632
  16.5 1.8 %collective-permute-start.7 = (bf16[2,256,128]{2,1,0:T(8,128)(2,1)S(1)}, bf16[2,256,128]{2,1,0:T(8,128)(2,1)S(1)}, u32[]{:S(2)}, u32[]{:S(2)}) collective-permute-start(bf16[2,256,128]{2,1,0:T(8,128)(2,1)S(1)} %get-tuple-element.58.m0), channel_id=1, source_target_pairs={{0,16},{8,24},{16,0},{24,8},{1,17},{9,25},{17,1},{25,9},{2,18},{10... | collective-permute-start | bytes 393224 | tf_op jit(solution)/shard_map/ppermute | solution.py:632
  18.2 0.9 %shard_map.87 = (f32[512,128]{1,0:T(8,128)S(1)}, bf16[64,2304]{1,0:T(8,128)(2,1)S(1)}, bf16[3,3,256,128]{3,2,1,0:T(8,128)(2,1)S(1)}, bf16[2,256,128]{2,1,0:T(8,128)(2,1)S(1)}, bf16[2,256,128]{2,1,0:T(8,128)(2,1)S(1)}) custom-call(f32[1]{0:T(128)} %bitcast.1.alive, s32[1]{0:T(128)} %bitcast.2.side, bf16[3,32,2048]{2,1,0:T(8,128)(2,1)S(1)} %collective-permute-done.3.halo_ref, ...), custom_call_target="tpu_custom_call" | custom-call | flops 1724999936 | bytes 1179648 | tf_op jit(solution)/shard_map/pallas_call | solution.py:49
  19.1 0.3 collective-permute-start.11
  19.4 0.8 %collective-permute-start.9 = (bf16[2,256,128]{2,1,0:T(8,128)(2,1)S(1)}, bf16[2,256,128]{2,1,0:T(8,128)(2,1)S(1)}, u32[]{:S(2)}, u32[]{:S(2)}) collective-permute-start(bf16[2,256,128]{2,1,0:T(8,128)(2,1)S(1)} %get-tuple-element.71), channel_id=1, source_target_pairs={{0,16},{8,24},{16,0},{24,8},{1,17},{9,25},{17,1},{25,9},{2,18},{10... | collective-permute-start | bytes 393224 | tf_op jit(solution)/shard_map/ppermute | solution.py:632
  20.2 1.8 %shard_map.88 = (bf16[2,8,2048]{2,1,0:T(8,128)(2,1)}, bf16[128,256]{1,0:T(8,128)(2,1)S(1)}) custom-call(s32[4]{0:T(128)S(1)} %get-tuple-element.100.offsets, bf16[128,3456]{1,0:T(8,128)(2,1)S(1)} %copy-done.8, bf16[64,2304]{1,0:T(8,128)(2,1)S(1)} %get-tuple-element.54.lower_ref, bf16[2,8,2048]{2,1,0:T(8,128)(2,1)S(1)} %bitcast.31, ...), custom_call_target="tpu_custom_call" | custom-call | flops 1724999936 | bytes 3014656 | tf_op jit(solution)/shard_map/pallas_call | solution.py:49
  22.0 0.5 collective-permute-done.7.m2
  22.5 2.0 %collective-permute-start.8 = (bf16[128,256]{1,0:T(8,128)(2,1)S(1)}, bf16[128,256]{1,0:T(8,128)(2,1)S(1)}, u32[]{:S(2)}, u32[]{:S(2)}) collective-permute-start(bf16[128,256]{1,0:T(8,128)(2,1)S(1)} %get-tuple-element.59.delta_ref.d0), channel_id=1, source_target_pairs={{0,16},{8,24},{16,0},{24,8},{1,17},{9,25},{17,1},{25,9},{2,18},{10... | collective-permute-start | bytes 196616 | tf_op jit(solution)/shard_map/ppermute | solution.py:632
  24.5 0.2 collective-permute-start.12
  24.7 3.0 %shard_map.89 = (bf16[768,128]{1,0:T(8,128)(2,1)S(1)}, f32[256,128]{1,0:T(8,128)S(1)}, bf16[512,128]{1,0:T(8,128)(2,1)S(1)}, bf16[8,56,128]{2,1,0:T(8,128)(2,1)S...) custom-call(s32[4]{0:T(128)S(1)} %get-tuple-element.100.offsets, ...), custom_call_target="tpu_custom_call" | custom-call | flops 4024999936 | bytes 4653056 | tf_op jit(solution)/shard_map/pallas_call | solution.py:49
  27.8 0.4 collective-permute-start.16
  28.1 0.2 collective-permute-start.14
  28.3 0.3 collective-permute-start.13
  28.6 0.2 collective-permute-start.15
  28.9 0.3 collective-permute-start.18
  29.2 0.3 collective-permute-done.14.m1
  29.5 0.4 collective-permute-done.15.d3
  29.9 1.8 %shard_map.90 = bf16[8,216,128]{2,1,0:T(8,128)(2,1)S(1)} custom-call(s32[1]{0:T(128)} %bitcast.5.data, s32[4,33]{1,0:T(4,128)S(1)} %copy-done.4, s32[8]{0:T(128)S(1)} %fusion.12.order, bf16[2,256,128]{2,1,0:T(8,128)(2,1)S(1)} %get-tuple-element.65.e0, bf16[2,256,128]{2,1,0:T(8,128)(2,1)S(1)} %collective-permute-done.11.e1, ...), custom_call_target="tpu_custom_call" | custom-call | flops 2300000000 | bytes 1310720 | tf_op jit(solution)/shard_map/pallas_call | solution.py:49
  31.8 1.2 %collective-permute-start.17 = (bf16[3,272,128]{2,1,0:T(8,128)(2,1)S(1)}, bf16[3,272,128]{2,1,0:T(8,128)(2,1)S(1)}, u32[]{:S(2)}, u32[]{:S(2)}) collective-permute-start(bf16[3,272,128]{2,1,0:T(8,128)(2,1)S(1)} %fusion), channel_id=1, source_target_pairs={{0,1},{1,0},{2,3},{3,2},{4,5},{5,4},{6,7},{7,6},{8,9},{9,8},{10,11... | collective-permute-start | bytes 626696 | tf_op jit(solution)/shard_map/ppermute | solution.py:632
  33.0 1.2 %collective-permute-start.19 = (bf16[4,56,128]{2,1,0:T(8,128)(2,1)S(1)}, bf16[4,56,128]{2,1,0:T(8,128)(2,1)S(1)}, u32[]{:S(2)}, u32[]{:S(2)}) collective-permute-start(bf16[4,56,128]{2,1,0:T(8,128)(2,1)S(1)} %get-tuple-element.94), channel_id=1, source_target_pairs={{0,16},{8,24},{16,0},{24,8},{1,17},{9,25},{17,1},{25,9},{2,18},{10... | collective-permute-start | bytes 172040 | tf_op jit(solution)/shard_map/ppermute | solution.py:632
  34.1 1.3 %collective-permute-start.20 = (bf16[4,56,128]{2,1,0:T(8,128)(2,1)S(1)}, bf16[4,56,128]{2,1,0:T(8,128)(2,1)S(1)}, u32[]{:S(2)}, u32[]{:S(2)}) collective-permute-start(bf16[4,56,128]{2,1,0:T(8,128)(2,1)S(1)} %get-tuple-element.95), channel_id=1, source_target_pairs={{0,17},{1,16},{2,19},{3,18},{4,21},{5,20},{6,23},{7,22},{8,25},{9,... | collective-permute-start | bytes 172040 | tf_op jit(solution)/shard_map/ppermute | solution.py:717
  35.4 1.1 %collective-permute-start.24 = (bf16[1,272,128]{2,1,0:T(8,128)(2,1)S(1)}, bf16[1,272,128]{2,1,0:T(8,128)(2,1)S(1)}, u32[]{:S(2)}, u32[]{:S(2)}) collective-permute-start(bf16[1,272,128]{2,1,0:T(8,128)(2,1)S(1)} %pad_maximum_fusion.1), channel_id=1, source_target_pairs={{0,1},{1,0},{2,3},{3,2},{4,5},{5,4},{6,7},{7,6},{8,9},{9,8},{10,11... | collective-permute-start | bytes 208904 | tf_op jit(solution)/shard_map/ppermute | solution.py:632
  36.6 1.3 %collective-permute-start.25 = (bf16[512,128]{1,0:T(8,128)(2,1)S(1)}, bf16[512,128]{1,0:T(8,128)(2,1)S(1)}, u32[]{:S(2)}, u32[]{:S(2)}) collective-permute-start(bf16[512,128]{1,0:T(8,128)(2,1)S(1)} %get-tuple-element.84), channel_id=1, source_target_pairs={{1,0},{2,1},{3,2},{4,3},{5,4},{6,5},{7,6},{9,8},{10,9},{11,10},{12... | collective-permute-start | bytes 393224 | tf_op jit(solution)/shard_map/ppermute | solution.py:638
  37.8 3.2 %collective-permute-done.17 = bf16[3,272,128]{2,1,0:T(8,128)(2,1)S(1)} collective-permute-done((bf16[3,272,128]{2,1,0:T(8,128)(2,1)S(1)}, bf16[3,272,128]{2,1,0:T(8,128)(2,1)S(1)}, u32[]{:S(2)}, u32[]{:S(2)}) %collective-permute-start.17) | collective-permute-done | bytes 208928 | tf_op jit(solution)/shard_map/ppermute | solution.py:632
  41.2 2.1 %collective-permute-start.21 = (bf16[272,128]{1,0:T(8,128)(2,1)S(1)}, bf16[272,128]{1,0:T(8,128)(2,1)S(1)}, u32[]{:S(2)}, u32[]{:S(2)}) collective-permute-start(bf16[272,128]{1,0:T(8,128)(2,1)S(1)} %get-tuple-element.97), channel_id=1, source_target_pairs={{0,2},{1,3},{2,0},{3,1},{4,6},{5,7},{6,4},{7,5},{8,10},{9,11},{10,... | collective-permute-start | bytes 208904 | tf_op jit(solution)/shard_map/ppermute | solution.py:632
  43.3 2.6 %collective-permute-start.22 = (bf16[272,128]{1,0:T(8,128)(2,1)S(1)}, bf16[272,128]{1,0:T(8,128)(2,1)S(1)}, u32[]{:S(2)}, u32[]{:S(2)}) collective-permute-start(bf16[272,128]{1,0:T(8,128)(2,1)S(1)} %get-tuple-element.98), channel_id=1, source_target_pairs={{0,4},{1,5},{2,6},{3,7},{4,0},{5,1},{6,2},{7,3},{8,12},{9,13},{10,... | collective-permute-start | bytes 208904 | tf_op jit(solution)/shard_map/ppermute | solution.py:632
  45.9 0.5 collective-permute-done.21
  46.3 4.1 %collective-permute-done.22 = bf16[272,128]{1,0:T(8,128)(2,1)S(1)} collective-permute-done((bf16[272,128]{1,0:T(8,128)(2,1)S(1)}, bf16[272,128]{1,0:T(8,128)(2,1)S(1)}, u32[]{:S(2)}, u32[]{:S(2)}) %collective-permute-start.22) | collective-permute-done | bytes 69664 | tf_op jit(solution)/shard_map/ppermute | solution.py:632
  50.4 1.8 %collective-permute-done.23 = bf16[272,128]{1,0:T(8,128)(2,1)S(1)} collective-permute-done((bf16[272,128]{1,0:T(8,128)(2,1)S(1)}, bf16[272,128]{1,0:T(8,128)(2,1)S(1)}, u32[]{:S(2)}, u32[]{:S(2)}) %collective-permute-start.23) | collective-permute-done | bytes 69664 | tf_op jit(solution)/shard_map/ppermute | solution.py:632
  52.4 1.4 %collective-permute-start.28 = (bf16[272,128]{1,0:T(8,128)(2,1)S(1)}, bf16[272,128]{1,0:T(8,128)(2,1)S(1)}, u32[]{:S(2)}, u32[]{:S(2)}) collective-permute-start(bf16[272,128]{1,0:T(8,128)(2,1)S(1)} %fusion.4.refs_0_), channel_id=1, source_target_pairs={{0,4},{1,5},{2,6},{3,7},{4,0},{5,1},{6,2},{7,3},{8,12},{9,13},{10,... | collective-permute-start | bytes 208904 | tf_op jit(solution)/shard_map/ppermute | solution.py:632
  53.8 2.9 %collective-permute-start.29 = (bf16[272,128]{1,0:T(8,128)(2,1)S(1)}, bf16[272,128]{1,0:T(8,128)(2,1)S(1)}, u32[]{:S(2)}, u32[]{:S(2)}) collective-permute-start(bf16[272,128]{1,0:T(8,128)(2,1)S(1)} %fusion.4.refs_0_), channel_id=1, source_target_pairs={{0,6},{1,7},{2,4},{3,5},{4,2},{5,3},{6,0},{7,1},{8,14},{9,15},{10,... | collective-permute-start | bytes 208904 | tf_op jit(solution)/shard_map/ppermute | solution.py:632
  56.8 0.7 %collective-permute-start.26 = (bf16[272,128]{1,0:T(8,128)(2,1)S(1)}, bf16[272,128]{1,0:T(8,128)(2,1)S(1)}, u32[]{:S(2)}, u32[]{:S(2)}) collective-permute-start(bf16[272,128]{1,0:T(8,128)(2,1)S(1)} %fusion.4.refs_0_), channel_id=1, source_target_pairs={{0,1},{1,0},{2,3},{3,2},{4,5},{5,4},{6,7},{7,6},{8,9},{9,8},{10,11... | collective-permute-start | bytes 208904 | tf_op jit(solution)/shard_map/ppermute | solution.py:632
  57.7 1.2 %collective-permute-start.30 = (bf16[2,272,128]{2,1,0:T(8,128)(2,1)S(1)}, bf16[2,272,128]{2,1,0:T(8,128)(2,1)S(1)}, u32[]{:S(2)}, u32[]{:S(2)}) collective-permute-start(bf16[2,272,128]{2,1,0:T(8,128)(2,1)S(1)} %pad_maximum_fusion), channel_id=1, source_target_pairs={{0,1},{1,0},{2,3},{3,2},{4,5},{5,4},{6,7},{7,6},{8,9},{9,8},{10,11... | collective-permute-start | bytes 417800 | tf_op jit(solution)/shard_map/ppermute | solution.py:632
  58.9 1.1 %collective-permute-done.29.refs_3_ = bf16[272,128]{1,0:T(8,128)(2,1)S(1)} collective-permute-done((bf16[272,128]{1,0:T(8,128)(2,1)S(1)}, bf16[272,128]{1,0:T(8,128)(2,1)S(1)}, u32[]{:S(2)}, u32[]{:S(2)}) %collective-permute-start.29) | collective-permute-done | bytes 69664 | tf_op jit(solution)/shard_map/ppermute | solution.py:632
  60.0 1.2 %collective-permute-start.31 = (bf16[1,272,128]{2,1,0:T(8,128)(2,1)S(1)}, bf16[1,272,128]{2,1,0:T(8,128)(2,1)S(1)}, u32[]{:S(2)}, u32[]{:S(2)}) collective-permute-start(bf16[1,272,128]{2,1,0:T(8,128)(2,1)S(1)} %bitcast.30), channel_id=1, source_target_pairs={{0,1},{1,0},{2,3},{3,2},{4,5},{5,4},{6,7},{7,6},{8,9},{9,8},{10,11... | collective-permute-start | bytes 208904 | tf_op jit(solution)/shard_map/ppermute | solution.py:632
  61.2 2.8 %shard_map.91 = bf16[8,32,2048]{2,1,0:T(8,128)(2,1)} custom-call(s32[4]{0:T(128)S(1)} %broadcast_multiply_fusion.offsets, bf16[768,128]{1,0:T(8,128)(2,1)S(1)} %get-tuple-element.63.low_ref, f32[256,128]{1,0:T(8,128)S(1)} %get-tuple-element.64.last_ref, f32[768,128]{1,0:T(8,128)S(1)} %copy-done.10, bf16[512,128]{1,0:T(8,128)(2,1)S(1)} %collective-permute-done.25.upper_ref, ...), custom_call_target="tpu_custom_call" | custom-call | flops 3449999872 | bytes 1294336 | tf_op jit(solution)/shard_map/pallas_call | solution.py:49
  64.0 0.3 collective-permute-done.31.refs_6_
  64.3 1.6 %shard_map.92 = (f32[432,128]{1,0:T(8,128)}, f32[864,256]{1,0:T(8,128)}) custom-call(s32[8]{0:T(128)S(1)} %fusion.12.order, bf16[272,128]{1,0:T(8,128)(2,1)S(1)} %fusion.4.refs_0_, bf16[272,128]{1,0:T(8,128)(2,1)S(1)} %collective-permute-done.27.refs_1_, bf16[272,128]{1,0:T(8,128)(2,1)S(1)} %collective-permute-done.28.refs_2_, ...), custom_call_target="tpu_custom_call" | custom-call | flops 1150000000 | bytes 557056 | tf_op jit(solution)/shard_map/pallas_call | solution.py:49
  (62 shorter events, 0.9 us)
Async XLA Ops:
  0.6 9.8 %collective-permute-start.1 = (bf16[432,128]{1,0:T(8,128)(2,1)}, bf16[432,128]{1,0:T(8,128)(2,1)S(1)}, u32[]{:S(2)}, u32[]{:S(2)}) collective-permute-start(bf16[432,128]{1,0:T(8,128)(2,1)} %w0.7), channel_id=1, source_target_pairs={{0,16},{8,24},{16,0},{24,8},{1,17},{9,25},{17,1},{25,9},{2,18},{10... | collective-permute-start | bytes 331784 | tf_op jit(solution)/shard_map/ppermute | solution.py:632
  3.6 6.9 %collective-permute-start = (bf16[432,128]{1,0:T(8,128)(2,1)}, bf16[432,128]{1,0:T(8,128)(2,1)S(1)}, u32[]{:S(2)}, u32[]{:S(2)}) collective-permute-start(bf16[432,128]{1,0:T(8,128)(2,1)} %w0.7), channel_id=1, source_target_pairs={{0,8},{8,0},{16,24},{24,16},{1,9},{9,1},{17,25},{25,17},{2,10},{10... | collective-permute-start | bytes 331784 | tf_op jit(solution)/shard_map/ppermute | solution.py:632
  3.6 12.8 %collective-permute-start.4 = (bf16[864,256]{1,0:T(8,128)(2,1)}, bf16[864,256]{1,0:T(8,128)(2,1)S(1)}, u32[]{:S(2)}, u32[]{:S(2)}) collective-permute-start(bf16[864,256]{1,0:T(8,128)(2,1)} %w0.6), channel_id=1, source_target_pairs={{0,16},{8,24},{16,0},{24,8},{1,17},{9,25},{17,1},{25,9},{2,18},{10... | collective-permute-start | bytes 1327112 | tf_op jit(solution)/shard_map/ppermute | solution.py:632
  3.8 16.4 %collective-permute-start.5 = (bf16[864,256]{1,0:T(8,128)(2,1)}, bf16[864,256]{1,0:T(8,128)(2,1)S(1)}, u32[]{:S(2)}, u32[]{:S(2)}) collective-permute-start(bf16[864,256]{1,0:T(8,128)(2,1)} %w0.6), channel_id=1, source_target_pairs={{0,8},{8,0},{16,24},{24,16},{1,9},{9,1},{17,25},{25,17},{2,10},{10... | collective-permute-start | bytes 1327112 | tf_op jit(solution)/shard_map/ppermute | solution.py:632
  5.2 13.1 %collective-permute-start.3 = (bf16[3,32,2048]{2,1,0:T(8,128)(2,1)S(1)}, bf16[3,32,2048]{2,1,0:T(8,128)(2,1)S(1)}, u32[]{:S(2)}, u32[]{:S(2)}) collective-permute-start(bf16[3,32,2048]{2,1,0:T(8,128)(2,1)S(1)} %shard_map.86), channel_id=1, source_target_pairs={{0,1},{1,2},{2,3},{3,4},{4,5},{5,6},{6,7},{8,9},{9,10},{10,11},{11... | collective-permute-start | bytes 1179656 | tf_op jit(solution)/shard_map/ppermute | solution.py:638
  8.9 1.2 %copy-start = (bf16[1,8,32,2048]{3,2,1,0:T(8,128)(2,1)S(1)}, bf16[1,8,32,2048]{3,2,1,0:T(8,128)(2,1)}, u32[]{:S(2)}) copy-start(bf16[1,8,32,2048]{3,2,1,0:T(8,128)(2,1)} %param.5) | copy-start | bytes 3145732
  10.1 1.8 %copy-start.2 = (bf16[432,128]{1,0:T(8,128)(2,1)S(1)}, bf16[432,128]{1,0:T(8,128)(2,1)}, u32[]{:S(2)}) copy-start(bf16[432,128]{1,0:T(8,128)(2,1)} %w0.7) | copy-start | bytes 331780
  10.5 3.6 %copy-start.5 = (bf16[8,3,256,128]{3,2,1,0:T(8,128)(2,1)}, bf16[8,3,256,128]{3,2,1,0:T(8,128)(2,1)S(1)}, u32[]{:S(2)}) copy-start(bf16[8,3,256,128]{3,2,1,0:T(8,128)(2,1)S(1)} %shard_map.84.sorted_ref) | copy-start | bytes 4718596
  10.5 1.4 %collective-permute-start.2 = (bf16[432,128]{1,0:T(8,128)(2,1)S(1)}, bf16[432,128]{1,0:T(8,128)(2,1)S(1)}, u32[]{:S(2)}, u32[]{:S(2)}) collective-permute-start(bf16[432,128]{1,0:T(8,128)(2,1)S(1)} %collective-permute-done.1.w2), channel_id=1, source_target_pairs={{0,8},{8,0},{16,24},{24,16},{1,9},{9,1},{17,25},{25,17},{2,10},{10... | collective-permute-start | bytes 331784 | tf_op jit(solution)/shard_map/ppermute | solution.py:632
  14.0 0.9 %copy-start.7 = (bf16[128,3456]{1,0:T(8,128)(2,1)}, bf16[128,3456]{1,0:T(8,128)(2,1)S(1)}, u32[]{:S(2)}) copy-start(bf16[128,3456]{1,0:T(8,128)(2,1)S(1)} %get-tuple-element.49.upper_ref) | copy-start | bytes 2654212
  15.0 0.7 %copy-start.9 = (f32[768,128]{1,0:T(8,128)}, f32[768,128]{1,0:T(8,128)S(1)}, u32[]{:S(2)}) copy-start(f32[768,128]{1,0:T(8,128)S(1)} %get-tuple-element.61.slope_ref) | copy-start | bytes 1179652
  16.4 3.7 %collective-permute-start.6 = (bf16[864,256]{1,0:T(8,128)(2,1)S(1)}, bf16[864,256]{1,0:T(8,128)(2,1)S(1)}, u32[]{:S(2)}, u32[]{:S(2)}) collective-permute-start(bf16[864,256]{1,0:T(8,128)(2,1)S(1)} %collective-permute-done.4.w2), channel_id=1, source_target_pairs={{0,8},{8,0},{16,24},{24,16},{1,9},{9,1},{17,25},{25,17},{2,10},{10... | collective-permute-start | bytes 1327112 | tf_op jit(solution)/shard_map/ppermute | solution.py:632
  16.5 6.1 %collective-permute-start.7 = (bf16[2,256,128]{2,1,0:T(8,128)(2,1)S(1)}, bf16[2,256,128]{2,1,0:T(8,128)(2,1)S(1)}, u32[]{:S(2)}, u32[]{:S(2)}) collective-permute-start(bf16[2,256,128]{2,1,0:T(8,128)(2,1)S(1)} %get-tuple-element.58.m0), channel_id=1, source_target_pairs={{0,16},{8,24},{16,0},{24,8},{1,17},{9,25},{17,1},{25,9},{2,18},{10... | collective-permute-start | bytes 393224 | tf_op jit(solution)/shard_map/ppermute | solution.py:632
  18.2 1.9 %copy-start.1 = (bf16[864,256]{1,0:T(8,128)(2,1)S(1)}, bf16[864,256]{1,0:T(8,128)(2,1)}, u32[]{:S(2)}) copy-start(bf16[864,256]{1,0:T(8,128)(2,1)} %w0.6) | copy-start | bytes 1327108
  18.2 1.9 %copy-start.3 = (bf16[1,2,8,2048]{3,2,1,0:T(8,128)(2,1)S(1)}, bf16[1,2,8,2048]{3,2,1,0:T(8,128)(2,1)}, u32[]{:S(2)}) copy-start(bf16[1,2,8,2048]{3,2,1,0:T(8,128)(2,1)} %param.8) | copy-start | bytes 196612
  18.2 2.0 %copy-start.8 = (bf16[128,3456]{1,0:T(8,128)(2,1)S(1)}, bf16[128,3456]{1,0:T(8,128)(2,1)}, u32[]{:S(2)}) copy-start(bf16[128,3456]{1,0:T(8,128)(2,1)} %copy-done.7) | copy-start | bytes 2654212
  19.1 8.6 %collective-permute-start.11 = (bf16[2,256,128]{2,1,0:T(8,128)(2,1)S(1)}, bf16[2,256,128]{2,1,0:T(8,128)(2,1)S(1)}, u32[]{:S(2)}, u32[]{:S(2)}) collective-permute-start(bf16[2,256,128]{2,1,0:T(8,128)(2,1)S(1)} %get-tuple-element.65.e0), channel_id=1, source_target_pairs={{0,8},{8,0},{16,24},{24,16},{1,9},{9,1},{17,25},{25,17},{2,10},{10... | collective-permute-start | bytes 393224 | tf_op jit(solution)/shard_map/ppermute | solution.py:632
  19.4 8.4 %collective-permute-start.9 = (bf16[2,256,128]{2,1,0:T(8,128)(2,1)S(1)}, bf16[2,256,128]{2,1,0:T(8,128)(2,1)S(1)}, u32[]{:S(2)}, u32[]{:S(2)}) collective-permute-start(bf16[2,256,128]{2,1,0:T(8,128)(2,1)S(1)} %get-tuple-element.71), channel_id=1, source_target_pairs={{0,16},{8,24},{16,0},{24,8},{1,17},{9,25},{17,1},{25,9},{2,18},{10... | collective-permute-start | bytes 393224 | tf_op jit(solution)/shard_map/ppermute | solution.py:632
  20.2 4.6 %copy-start.6 = (bf16[8,3,256,128]{3,2,1,0:T(8,128)(2,1)S(1)}, bf16[8,3,256,128]{3,2,1,0:T(8,128)(2,1)}, u32[]{:S(2)}) copy-start(bf16[8,3,256,128]{3,2,1,0:T(8,128)(2,1)} %copy-done.5) | copy-start | bytes 4718596
  20.2 4.6 %copy-start.10 = (f32[768,128]{1,0:T(8,128)S(1)}, f32[768,128]{1,0:T(8,128)}, u32[]{:S(2)}) copy-start(f32[768,128]{1,0:T(8,128)} %copy-done.9) | copy-start | bytes 1179652
  22.5 5.2 %collective-permute-start.10 = (bf16[128,256]{1,0:T(8,128)(2,1)S(1)}, bf16[128,256]{1,0:T(8,128)(2,1)S(1)}, u32[]{:S(2)}, u32[]{:S(2)}) collective-permute-start(bf16[128,256]{1,0:T(8,128)(2,1)S(1)} %get-tuple-element.59.delta_ref.d0), channel_id=1, source_target_pairs={{0,8},{8,0},{16,24},{24,16},{1,9},{9,1},{17,25},{25,17},{2,10},{10... | collective-permute-start | bytes 196616 | tf_op jit(solution)/shard_map/ppermute | solution.py:632
  22.5 5.2 %collective-permute-start.8 = (bf16[128,256]{1,0:T(8,128)(2,1)S(1)}, bf16[128,256]{1,0:T(8,128)(2,1)S(1)}, u32[]{:S(2)}, u32[]{:S(2)}) collective-permute-start(bf16[128,256]{1,0:T(8,128)(2,1)S(1)} %get-tuple-element.59.delta_ref.d0), channel_id=1, source_target_pairs={{0,16},{8,24},{16,0},{24,8},{1,17},{9,25},{17,1},{25,9},{2,18},{10... | collective-permute-start | bytes 196616 | tf_op jit(solution)/shard_map/ppermute | solution.py:632
  24.5 3.3 %collective-permute-start.12 = (bf16[2,256,128]{2,1,0:T(8,128)(2,1)S(1)}, bf16[2,256,128]{2,1,0:T(8,128)(2,1)S(1)}, u32[]{:S(2)}, u32[]{:S(2)}) collective-permute-start(bf16[2,256,128]{2,1,0:T(8,128)(2,1)S(1)} %collective-permute-done.7.m2), channel_id=1, source_target_pairs={{0,8},{8,0},{16,24},{24,16},{1,9},{9,1},{17,25},{25,17},{2,10},{10... | collective-permute-start | bytes 393224 | tf_op jit(solution)/shard_map/ppermute | solution.py:632
  24.7 5.2 %copy-start.4 = (s32[4,33]{1,0:T(4,128)S(1)}, s32[4,33]{1,0:T(4,128)}, u32[]{:S(2)}) copy-start(s32[4,33]{1,0:T(4,128)} %constant.48.clone.table) | copy-start | bytes 1588
  27.8 1.4 %collective-permute-start.16 = (bf16[8,56,128]{2,1,0:T(8,128)(2,1)S(1)}, bf16[8,56,128]{2,1,0:T(8,128)(2,1)S(1)}, u32[]{:S(2)}, u32[]{:S(2)}) collective-permute-start(bf16[8,56,128]{2,1,0:T(8,128)(2,1)S(1)} %get-tuple-element.81), channel_id=1, source_target_pairs={{0,8},{8,0},{16,24},{24,16},{1,9},{9,1},{17,25},{25,17},{2,10},{10... | collective-permute-start | bytes 344072 | tf_op jit(solution)/shard_map/ppermute | solution.py:632
  28.1 1.3 %collective-permute-start.14 = (bf16[2,256,128]{2,1,0:T(8,128)(2,1)S(1)}, bf16[2,256,128]{2,1,0:T(8,128)(2,1)S(1)}, u32[]{:S(2)}, u32[]{:S(2)}) collective-permute-start(bf16[2,256,128]{2,1,0:T(8,128)(2,1)S(1)} %get-tuple-element.58.m0), channel_id=1, source_target_pairs={{0,8},{8,0},{16,24},{24,16},{1,9},{9,1},{17,25},{25,17},{2,10},{10... | collective-permute-start | bytes 393224 | tf_op jit(solution)/shard_map/ppermute | solution.py:632
  28.3 1.5 %collective-permute-start.13 = (bf16[2,256,128]{2,1,0:T(8,128)(2,1)S(1)}, bf16[2,256,128]{2,1,0:T(8,128)(2,1)S(1)}, u32[]{:S(2)}, u32[]{:S(2)}) collective-permute-start(bf16[2,256,128]{2,1,0:T(8,128)(2,1)S(1)} %collective-permute-done.9.e2), channel_id=1, source_target_pairs={{0,8},{8,0},{16,24},{24,16},{1,9},{9,1},{17,25},{25,17},{2,10},{10... | collective-permute-start | bytes 393224 | tf_op jit(solution)/shard_map/ppermute | solution.py:632
  28.6 1.3 %collective-permute-start.15 = (bf16[128,256]{1,0:T(8,128)(2,1)S(1)}, bf16[128,256]{1,0:T(8,128)(2,1)S(1)}, u32[]{:S(2)}, u32[]{:S(2)}) collective-permute-start(bf16[128,256]{1,0:T(8,128)(2,1)S(1)} %collective-permute-done.8.d2), channel_id=1, source_target_pairs={{0,8},{8,0},{16,24},{24,16},{1,9},{9,1},{17,25},{25,17},{2,10},{10... | collective-permute-start | bytes 196616 | tf_op jit(solution)/shard_map/ppermute | solution.py:632
  28.9 4.1 %collective-permute-start.18 = (bf16[8,56,128]{2,1,0:T(8,128)(2,1)S(1)}, bf16[8,56,128]{2,1,0:T(8,128)(2,1)S(1)}, u32[]{:S(2)}, u32[]{:S(2)}) collective-permute-start(bf16[8,56,128]{2,1,0:T(8,128)(2,1)S(1)} %get-tuple-element.83), channel_id=1, source_target_pairs={{0,8},{8,0},{16,24},{24,16},{1,9},{9,1},{17,25},{25,17},{2,10},{10... | collective-permute-start | bytes 344072 | tf_op jit(solution)/shard_map/ppermute | solution.py:632
  31.8 9.3 %collective-permute-start.17 = (bf16[3,272,128]{2,1,0:T(8,128)(2,1)S(1)}, bf16[3,272,128]{2,1,0:T(8,128)(2,1)S(1)}, u32[]{:S(2)}, u32[]{:S(2)}) collective-permute-start(bf16[3,272,128]{2,1,0:T(8,128)(2,1)S(1)} %fusion), channel_id=1, source_target_pairs={{0,1},{1,0},{2,3},{3,2},{4,5},{5,4},{6,7},{7,6},{8,9},{9,8},{10,11... | collective-permute-start | bytes 626696 | tf_op jit(solution)/shard_map/ppermute | solution.py:632
  33.0 8.1 %collective-permute-start.19 = (bf16[4,56,128]{2,1,0:T(8,128)(2,1)S(1)}, bf16[4,56,128]{2,1,0:T(8,128)(2,1)S(1)}, u32[]{:S(2)}, u32[]{:S(2)}) collective-permute-start(bf16[4,56,128]{2,1,0:T(8,128)(2,1)S(1)} %get-tuple-element.94), channel_id=1, source_target_pairs={{0,16},{8,24},{16,0},{24,8},{1,17},{9,25},{17,1},{25,9},{2,18},{10... | collective-permute-start | bytes 172040 | tf_op jit(solution)/shard_map/ppermute | solution.py:632
  34.1 7.0 %collective-permute-start.20 = (bf16[4,56,128]{2,1,0:T(8,128)(2,1)S(1)}, bf16[4,56,128]{2,1,0:T(8,128)(2,1)S(1)}, u32[]{:S(2)}, u32[]{:S(2)}) collective-permute-start(bf16[4,56,128]{2,1,0:T(8,128)(2,1)S(1)} %get-tuple-element.95), channel_id=1, source_target_pairs={{0,17},{1,16},{2,19},{3,18},{4,21},{5,20},{6,23},{7,22},{8,25},{9,... | collective-permute-start | bytes 172040 | tf_op jit(solution)/shard_map/ppermute | solution.py:717
  35.4 10.4 %collective-permute-start.24 = (bf16[1,272,128]{2,1,0:T(8,128)(2,1)S(1)}, bf16[1,272,128]{2,1,0:T(8,128)(2,1)S(1)}, u32[]{:S(2)}, u32[]{:S(2)}) collective-permute-start(bf16[1,272,128]{2,1,0:T(8,128)(2,1)S(1)} %pad_maximum_fusion.1), channel_id=1, source_target_pairs={{0,1},{1,0},{2,3},{3,2},{4,5},{5,4},{6,7},{7,6},{8,9},{9,8},{10,11... | collective-permute-start | bytes 208904 | tf_op jit(solution)/shard_map/ppermute | solution.py:632
  36.6 9.3 %collective-permute-start.25 = (bf16[512,128]{1,0:T(8,128)(2,1)S(1)}, bf16[512,128]{1,0:T(8,128)(2,1)S(1)}, u32[]{:S(2)}, u32[]{:S(2)}) collective-permute-start(bf16[512,128]{1,0:T(8,128)(2,1)S(1)} %get-tuple-element.84), channel_id=1, source_target_pairs={{1,0},{2,1},{3,2},{4,3},{5,4},{6,5},{7,6},{9,8},{10,9},{11,10},{12... | collective-permute-start | bytes 393224 | tf_op jit(solution)/shard_map/ppermute | solution.py:638
  41.2 5.1 %collective-permute-start.21 = (bf16[272,128]{1,0:T(8,128)(2,1)S(1)}, bf16[272,128]{1,0:T(8,128)(2,1)S(1)}, u32[]{:S(2)}, u32[]{:S(2)}) collective-permute-start(bf16[272,128]{1,0:T(8,128)(2,1)S(1)} %get-tuple-element.97), channel_id=1, source_target_pairs={{0,2},{1,3},{2,0},{3,1},{4,6},{5,7},{6,4},{7,5},{8,10},{9,11},{10,... | collective-permute-start | bytes 208904 | tf_op jit(solution)/shard_map/ppermute | solution.py:632
  43.3 7.1 %collective-permute-start.22 = (bf16[272,128]{1,0:T(8,128)(2,1)S(1)}, bf16[272,128]{1,0:T(8,128)(2,1)S(1)}, u32[]{:S(2)}, u32[]{:S(2)}) collective-permute-start(bf16[272,128]{1,0:T(8,128)(2,1)S(1)} %get-tuple-element.98), channel_id=1, source_target_pairs={{0,4},{1,5},{2,6},{3,7},{4,0},{5,1},{6,2},{7,3},{8,12},{9,13},{10,... | collective-permute-start | bytes 208904 | tf_op jit(solution)/shard_map/ppermute | solution.py:632
  45.9 6.4 %collective-permute-start.23 = (bf16[272,128]{1,0:T(8,128)(2,1)S(1)}, bf16[272,128]{1,0:T(8,128)(2,1)S(1)}, u32[]{:S(2)}, u32[]{:S(2)}) collective-permute-start(bf16[272,128]{1,0:T(8,128)(2,1)S(1)} %get-tuple-element.96), channel_id=1, source_target_pairs={{0,6},{1,7},{2,4},{3,5},{4,2},{5,3},{6,0},{7,1},{8,14},{9,15},{10,... | collective-permute-start | bytes 208904 | tf_op jit(solution)/shard_map/ppermute | solution.py:632
  52.3 5.2 %collective-permute-start.27 = (bf16[272,128]{1,0:T(8,128)(2,1)S(1)}, bf16[272,128]{1,0:T(8,128)(2,1)S(1)}, u32[]{:S(2)}, u32[]{:S(2)}) collective-permute-start(bf16[272,128]{1,0:T(8,128)(2,1)S(1)} %fusion.4.refs_0_), channel_id=1, source_target_pairs={{0,2},{1,3},{2,0},{3,1},{4,6},{5,7},{6,4},{7,5},{8,10},{9,11},{10,... | collective-permute-start | bytes 208904 | tf_op jit(solution)/shard_map/ppermute | solution.py:632
  52.4 5.3 %collective-permute-start.28 = (bf16[272,128]{1,0:T(8,128)(2,1)S(1)}, bf16[272,128]{1,0:T(8,128)(2,1)S(1)}, u32[]{:S(2)}, u32[]{:S(2)}) collective-permute-start(bf16[272,128]{1,0:T(8,128)(2,1)S(1)} %fusion.4.refs_0_), channel_id=1, source_target_pairs={{0,4},{1,5},{2,6},{3,7},{4,0},{5,1},{6,2},{7,3},{8,12},{9,13},{10,... | collective-permute-start | bytes 208904 | tf_op jit(solution)/shard_map/ppermute | solution.py:632
  53.8 6.2 %collective-permute-start.29 = (bf16[272,128]{1,0:T(8,128)(2,1)S(1)}, bf16[272,128]{1,0:T(8,128)(2,1)S(1)}, u32[]{:S(2)}, u32[]{:S(2)}) collective-permute-start(bf16[272,128]{1,0:T(8,128)(2,1)S(1)} %fusion.4.refs_0_), channel_id=1, source_target_pairs={{0,6},{1,7},{2,4},{3,5},{4,2},{5,3},{6,0},{7,1},{8,14},{9,15},{10,... | collective-permute-start | bytes 208904 | tf_op jit(solution)/shard_map/ppermute | solution.py:632
  56.8 4.5 %collective-permute-start.26 = (bf16[272,128]{1,0:T(8,128)(2,1)S(1)}, bf16[272,128]{1,0:T(8,128)(2,1)S(1)}, u32[]{:S(2)}, u32[]{:S(2)}) collective-permute-start(bf16[272,128]{1,0:T(8,128)(2,1)S(1)} %fusion.4.refs_0_), channel_id=1, source_target_pairs={{0,1},{1,0},{2,3},{3,2},{4,5},{5,4},{6,7},{7,6},{8,9},{9,8},{10,11... | collective-permute-start | bytes 208904 | tf_op jit(solution)/shard_map/ppermute | solution.py:632
  57.7 6.6 %collective-permute-start.30 = (bf16[2,272,128]{2,1,0:T(8,128)(2,1)S(1)}, bf16[2,272,128]{2,1,0:T(8,128)(2,1)S(1)}, u32[]{:S(2)}, u32[]{:S(2)}) collective-permute-start(bf16[2,272,128]{2,1,0:T(8,128)(2,1)S(1)} %pad_maximum_fusion), channel_id=1, source_target_pairs={{0,1},{1,0},{2,3},{3,2},{4,5},{5,4},{6,7},{7,6},{8,9},{9,8},{10,11... | collective-permute-start | bytes 417800 | tf_op jit(solution)/shard_map/ppermute | solution.py:632
  60.0 4.3 %collective-permute-start.31 = (bf16[1,272,128]{2,1,0:T(8,128)(2,1)S(1)}, bf16[1,272,128]{2,1,0:T(8,128)(2,1)S(1)}, u32[]{:S(2)}, u32[]{:S(2)}) collective-permute-start(bf16[1,272,128]{2,1,0:T(8,128)(2,1)S(1)} %bitcast.30), channel_id=1, source_target_pairs={{0,1},{1,0},{2,3},{3,2},{4,5},{5,4},{6,7},{7,6},{8,9},{9,8},{10,11... | collective-permute-start | bytes 208904 | tf_op jit(solution)/shard_map/ppermute | solution.py:632
